TPU v7x, 128 devices: a whole 4x4x4 slice. The times are simulated.
128 devices in a mesh: dp: 16 (over y, x_lo, core), seq: 8 (over z, x_hi).
Axes of the slice: x: 4 (x_hi: 2, x_lo: 2; x = x_hi * 2 + x_lo), y: 4, z: 4, core: 2. Of those that a mesh axis runs over, the one named last changes fastest.
Arguments:
- tokens: bfloat16 [48, 1152, 768], P('dp', 'seq'), may hold values from -6 to 6
- view_counts: int32 [48], P('dp'), may hold values from 2 to 8, as said below
- ln1_gain: float32 [768], replicated, may hold values from 0.25 to 1.75
- ln1_shift: float32 [768], replicated, may hold values from -1.5 to 1.5
- qkv_weight: bfloat16 [768, 2304], replicated, may hold values from -0.21875 to 0.21875
- query_bias: float32 [768], replicated, may hold values from -2.5 to 2.5
- value_bias: float32 [768], replicated, may hold values from -2.5 to 2.5
- out_weight: bfloat16 [768, 768], replicated, may hold values from -1.75 to 1.75
- out_bias: float32 [768], replicated, may hold values from -1.5 to 1.5
- ln2_gain: float32 [768], replicated, may hold values from 0.25 to 1.75
- ln2_shift: float32 [768], replicated, may hold values from -1.5 to 1.5
- up_weight: bfloat16 [768, 3072], replicated, may hold values from -0.21875 to 0.21875
- up_bias: float32 [3072], replicated, may hold values from -2.5 to 2.5
- down_weight: bfloat16 [3072, 768], replicated, may hold values from -0.109375 to 0.109375
- down_bias: float32 [768], replicated, may hold values from -1.5 to 1.5
- cotangent: bfloat16 [48, 1152, 768], P('dp', 'seq'), may hold values from -6 to 6
Outputs:
- output: bfloat16 [48, 1152, 768], P('dp', 'seq')
- input_grad: bfloat16 [48, 1152, 768], P('dp', 'seq')
- ln1_gain_grad: float32 [768], replicated
- ln1_shift_grad: float32 [768], replicated
- qkv_weight_grad: float32 [768, 2304], replicated
- query_bias_grad: float32 [768], replicated
- value_bias_grad: float32 [768], replicated
- out_weight_grad: float32 [768, 768], replicated
- out_bias_grad: float32 [768], replicated
- ln2_gain_grad: float32 [768], replicated
- ln2_shift_grad: float32 [768], replicated
- up_weight_grad: float32 [768, 3072], replicated
- up_bias_grad: float32 [3072], replicated
- down_weight_grad: float32 [3072, 768], replicated
- down_bias_grad: float32 [768], replicated
Inputs may be any that keep to these rules, and one draw needn't show every extreme that they name: `view_counts`: each data group's 3 consecutive scenes include at least one with 8 input views.
All inputs are finite; a program needn't handle non-finite values.
Results may differ from a plain program's by a relative error of at most 0.018.
Values may be sent and summed in bfloat16 or wider, within the bound.
No kernel may reach another device: no remote copies, remote signals or barrier semaphores. Data moves between devices by JAX's collectives and lax.ppermute only.
A program may use at most 192 MiB of HBM per device.

v0:
```python
import jax
import jax.numpy as jnp
from jax import lax
from jax.sharding import PartitionSpec as P

HEADS = 12
HEAD_DIM = 64
VIEW_TOK = 128
VIEWS_MAX = 8


epsilon = 1e-05
masked_score = -1e30


def layer_norm(values_in, gain_vector, shift_vector):
    centred = values_in - jnp.mean(values_in, axis=-1, keepdims=True)
    spread = jnp.mean(centred * centred, axis=-1, keepdims=True)
    return centred * lax.rsqrt(spread + epsilon) * gain_vector + shift_vector


def gelu_tanh(values_in):
    return jax.nn.gelu(values_in, approximate=True)


def usable_keys(view_now, length):
    positions = jnp.arange(length, dtype=jnp.int32)
    return (positions < view_now * VIEW_TOK) | (positions >= VIEWS_MAX * VIEW_TOK)


def forward_step(running, pieces, queries, view_now):
    maxima, totals, accum = running
    key_rows, value_rows = pieces
    length = key_rows.shape[0]
    key_heads = key_rows.reshape(length, HEADS, HEAD_DIM)
    value_heads = value_rows.reshape(length, HEADS, HEAD_DIM)
    scores = (
        jnp.einsum("qhd,khd->hqk", queries, key_heads, preferred_element_type=jnp.float32) * 0.125
    )
    usable = usable_keys(view_now, length)[None, None, :]
    scores = jnp.where(usable, scores, masked_score)
    new_maxima = jnp.maximum(maxima, jnp.max(scores, axis=-1))
    weights = jnp.where(usable, jnp.exp(scores - new_maxima[..., None]), 0.0)
    totals = jnp.sum(weights, axis=-1)
    accum = jnp.einsum(
        "hqk,khd->hqd",
        weights.astype(jnp.bfloat16),
        value_heads,
        preferred_element_type=jnp.float32,
    )
    return (new_maxima, totals, accum)


def backward_step(pieces, queries, grad_heads, log_totals, delta, view_now):
    key_rows, value_rows = pieces
    length, model_width = key_rows.shape
    key_heads = key_rows.reshape(length, HEADS, HEAD_DIM)
    value_heads = value_rows.reshape(length, HEADS, HEAD_DIM)
    scores = (
        jnp.einsum("qhd,khd->hqk", queries, key_heads, preferred_element_type=jnp.float32) * 0.125
    )
    usable = usable_keys(view_now, length)[None, None, :]
    probs = jnp.where(usable, jnp.exp(scores - log_totals[..., None]), 0.0)
    grad_probs = jnp.einsum(
        "qhd,khd->hqk", grad_heads, value_heads, preferred_element_type=jnp.float32
    )
    grad_scores = (probs * (grad_probs - delta[..., None])).astype(jnp.bfloat16)
    grad_query = jnp.einsum(
        "hqk,khd->hqd", grad_scores, key_heads, preferred_element_type=jnp.float32
    )
    key_part = jnp.einsum(
        "hqk,qhd->khd", grad_scores, queries, preferred_element_type=jnp.float32
    ).reshape(length, model_width)
    value_part = jnp.einsum(
        "hqk,qhd->khd", probs.astype(jnp.bfloat16), grad_heads, preferred_element_type=jnp.float32
    ).reshape(length, model_width)
    return (grad_query, key_part, value_part)


def body(
    tokens,
    view_counts,
    ln1_gain,
    ln1_shift,
    qkv_weight,
    query_bias,
    value_bias,
    out_weight,
    out_bias,
    ln2_gain,
    ln2_shift,
    up_weight,
    up_bias,
    down_weight,
    down_bias,
    cotangent,
):
    micro_count, row_count, model_width = tokens.shape
    qkv_bias = jnp.concatenate([query_bias, jnp.zeros((model_width,), jnp.float32), value_bias])
    gradients = [
        jnp.zeros(member.shape, jnp.float32)
        for member in (
            ln1_gain,
            ln1_shift,
            qkv_weight,
            query_bias,
            value_bias,
            out_weight,
            out_bias,
            ln2_gain,
            ln2_shift,
            up_weight,
            up_bias,
            down_weight,
            down_bias,
        )
    ]
    outputs_list = []
    input_list = []
    for number in range(micro_count):
        source = tokens[number].astype(jnp.float32)
        view_now = view_counts[number]
        normed_f, ln1_back = jax.vjp(layer_norm, source, ln1_gain, ln1_shift)
        normed = normed_f.astype(jnp.bfloat16)
        joined = jnp.dot(normed, qkv_weight, preferred_element_type=jnp.float32) + qkv_bias
        queries = joined[:, :model_width].astype(jnp.bfloat16)
        key_rows = joined[:, model_width : 2 * model_width].astype(jnp.bfloat16)
        value_rows = joined[:, 2 * model_width :].astype(jnp.bfloat16)
        query_heads = queries.reshape(row_count, HEADS, HEAD_DIM)
        initial = (
            jnp.full((HEADS, row_count), masked_score, jnp.float32),
            jnp.zeros((HEADS, row_count), jnp.float32),
            jnp.zeros((HEADS, row_count, HEAD_DIM), jnp.float32),
        )
        maxima, totals, accum = forward_step(
            initial,
            (
                lax.all_gather(key_rows, "seq", axis=0, tiled=True),
                lax.all_gather(value_rows, "seq", axis=0, tiled=True),
            ),
            query_heads,
            view_now,
        )
        heads_out = accum / totals[..., None]
        log_totals = maxima + jnp.log(totals)
        attended = heads_out.transpose(1, 0, 2).reshape(row_count, model_width).astype(jnp.bfloat16)
        hidden = (
            source + jnp.dot(attended, out_weight, preferred_element_type=jnp.float32) + out_bias
        )
        normed2_f, ln2_back = jax.vjp(layer_norm, hidden, ln2_gain, ln2_shift)
        normed2 = normed2_f.astype(jnp.bfloat16)
        upward = jnp.dot(normed2, up_weight, preferred_element_type=jnp.float32) + up_bias
        active_f, gelu_back = jax.vjp(gelu_tanh, upward)
        active = active_f.astype(jnp.bfloat16)
        result = (
            hidden + jnp.dot(active, down_weight, preferred_element_type=jnp.float32) + down_bias
        )
        outputs_list.append(result.astype(jnp.bfloat16))
        grad_out_b = cotangent[number]
        grad_out = grad_out_b.astype(jnp.float32)
        grad_down_w = jnp.einsum(
            "tf,td->fd", active, grad_out_b, preferred_element_type=jnp.float32
        )
        grad_down_b = jnp.sum(grad_out, axis=0)
        grad_active = jnp.einsum(
            "td,fd->tf", grad_out_b, down_weight, preferred_element_type=jnp.float32
        )
        grad_up = gelu_back(grad_active)[0].astype(jnp.bfloat16)
        grad_up_w = jnp.einsum("td,tf->df", normed2, grad_up, preferred_element_type=jnp.float32)
        grad_up_b = jnp.sum(grad_up.astype(jnp.float32), axis=0)
        grad_normed2 = jnp.einsum(
            "tf,df->td", grad_up, up_weight, preferred_element_type=jnp.float32
        )
        grad_hidden_part, grad_ln2_gain, grad_ln2_shift = ln2_back(grad_normed2)
        grad_hidden = grad_out + grad_hidden_part
        grad_branch = grad_hidden.astype(jnp.bfloat16)
        grad_out_w = jnp.einsum(
            "td,te->de", attended, grad_branch, preferred_element_type=jnp.float32
        )
        grad_out_b_vec = jnp.sum(grad_hidden, axis=0)
        grad_att = jnp.einsum(
            "te,de->td", grad_branch, out_weight, preferred_element_type=jnp.float32
        ).astype(jnp.bfloat16)
        grad_heads = grad_att.reshape(row_count, HEADS, HEAD_DIM)
        delta = jnp.einsum("qhd,hqd->hq", grad_heads.astype(jnp.float32), heads_out)
        back_result = backward_step(
            (
                lax.all_gather(key_rows, "seq", axis=0, tiled=True),
                lax.all_gather(value_rows, "seq", axis=0, tiled=True),
            ),
            query_heads,
            grad_heads,
            log_totals,
            delta,
            view_now,
        )
        grad_query = back_result[0]
        grad_keys, grad_values = (
            lax.psum_scatter(
                back_result[1].astype(jnp.bfloat16), "seq", scatter_dimension=0, tiled=True
            ).astype(jnp.float32),
            lax.psum_scatter(
                back_result[2].astype(jnp.bfloat16), "seq", scatter_dimension=0, tiled=True
            ).astype(jnp.float32),
        )
        grad_q = (
            (grad_query * 0.125)
            .transpose(1, 0, 2)
            .reshape(row_count, model_width)
            .astype(jnp.bfloat16)
        )
        grad_k = (grad_keys * 0.125).astype(jnp.bfloat16)
        grad_v = grad_values.astype(jnp.bfloat16)
        grad_joined = jnp.concatenate([grad_q, grad_k, grad_v], axis=1)
        grad_qkv_w = jnp.einsum(
            "td,te->de", normed, grad_joined, preferred_element_type=jnp.float32
        )
        grad_query_b = jnp.sum(grad_q.astype(jnp.float32), axis=0)
        grad_value_b = jnp.sum(grad_v.astype(jnp.float32), axis=0)
        grad_normed = jnp.einsum(
            "te,de->td", grad_joined, qkv_weight, preferred_element_type=jnp.float32
        )
        grad_source_part, grad_ln1_gain, grad_ln1_shift = ln1_back(grad_normed)
        input_list.append((grad_hidden + grad_source_part).astype(jnp.bfloat16))
        fresh = (
            grad_ln1_gain,
            grad_ln1_shift,
            grad_qkv_w,
            grad_query_b,
            grad_value_b,
            grad_out_w,
            grad_out_b_vec,
            grad_ln2_gain,
            grad_ln2_shift,
            grad_up_w,
            grad_up_b,
            grad_down_w,
            grad_down_b,
        )
        gradients = [total + extra for total, extra in zip(gradients, fresh)]
    local_sums = tuple(gradients)
    summed = lax.psum(local_sums, ("dp", "seq"))
    return (
        jnp.stack(outputs_list),
        jnp.stack(input_list),
        summed[0],
        summed[1],
        summed[2],
        summed[3],
        summed[4],
        summed[5],
        summed[6],
        summed[7],
        summed[8],
        summed[9],
        summed[10],
        summed[11],
        summed[12],
    )


def solution(mesh):
    placed = (
        P("dp", "seq", None),
        P("dp"),
        P(),
        P(),
        P(),
        P(),
        P(),
        P(),
        P(),
        P(),
        P(),
        P(),
        P(),
        P(),
        P(),
        P("dp", "seq", None),
    )
    return jax.shard_map(
        body,
        mesh=mesh,
        in_specs=placed,
        out_specs=(
            P("dp", "seq", None),
            P("dp", "seq", None),
            P(),
            P(),
            P(),
            P(),
            P(),
            P(),
            P(),
            P(),
            P(),
            P(),
            P(),
            P(),
            P(),
        ),
        check_vma=False,
    )
```

profile of v0, /device:TPU:1, one launch (start us, length us, event | category | flops | bytes accessed | tf_op | source)
XLA Modules:
  0.0 1149.3 jit_solution(8478883831391110860)
XLA Ops:
  24.4 44.4 %all-gather.15.cloned.1.call-done = bf16[1152,768]{1,0:T(8,128)(2,1)} async-done(((bf16[144,768]{1,0:T(8,128)(2,1)}), bf16[1152,768]{1,0:T(8,128)(2,1)}) %all-gather.15.cloned.1.call-update) | async-done | bytes 1769488 | tf_op jit(solution)/shard_map/all_gather | solution.py:138
  81.7 39.5 %all-gather.11.cloned.1.call-done = bf16[1152,768]{1,0:T(8,128)(2,1)} async-done(((bf16[144,768]{1,0:T(8,128)(2,1)}), bf16[1152,768]{1,0:T(8,128)(2,1)}) %all-gather.11.cloned.1.call-update) | async-done | bytes 1769488 | tf_op jit(solution)/shard_map/all_gather | solution.py:138
  121.2 3.9 copy.71
  125.1 48.6 %all-gather.17.cloned.1.call-done = bf16[1152,768]{1,0:T(8,128)(2,1)} async-done(((bf16[144,768]{1,0:T(8,128)(2,1)}), bf16[1152,768]{1,0:T(8,128)(2,1)}) %all-gather.17.cloned.1.call-update) | async-done | bytes 1769488 | tf_op jit(solution)/shard_map/all_gather | solution.py:139
  177.5 6.7 fusion.87
  194.2 31.1 %all-gather.13.cloned.1.call-done = bf16[1152,768]{1,0:T(8,128)(2,1)} async-done(((bf16[144,768]{1,0:T(8,128)(2,1)}), bf16[1152,768]{1,0:T(8,128)(2,1)}) %all-gather.13.cloned.1.call-update) | async-done | bytes 1769488 | tf_op jit(solution)/shard_map/all_gather | solution.py:139
  225.3 4.3 copy.72
  229.7 6.8 fusion.88
  257.0 6.4 fusion.45
  263.5 3.9 copy.110
  268.8 6.5 multiply_convert_fusion
  277.9 3.9 copy.108
  289.8 6.6 multiply_convert_fusion.1
  302.9 6.4 fusion.42
  309.3 3.9 copy.106
  314.7 5.8 convert_reduce_fusion.6
  323.4 15.4 %reduce-scatter.29.cloned.1.call-done = bf16[144,768]{1,0:T(8,128)(2,1)} async-done(((bf16[1152,768]{1,0:T(8,128)(2,1)}), bf16[144,768]{1,0:T(8,128)(2,1)}) %reduce-scatter.29.cloned.1.call-update) | async-done | bytes 221200
  340.7 74.8 %reduce-scatter.27.cloned.1.call-done = bf16[144,768]{1,0:T(8,128)(2,1)} async-done(((bf16[1152,768]{1,0:T(8,128)(2,1)}), bf16[144,768]{1,0:T(8,128)(2,1)}) %reduce-scatter.27.cloned.1.call-update) | async-done | bytes 221200
  417.3 74.6 %reduce-scatter.23.cloned.1.call-done = bf16[144,768]{1,0:T(8,128)(2,1)} async-done(((bf16[1152,768]{1,0:T(8,128)(2,1)}), bf16[144,768]{1,0:T(8,128)(2,1)}) %reduce-scatter.23.cloned.1.call-update) | async-done | bytes 221200
  500.0 69.3 %reduce-scatter.25.cloned.1.call-done = bf16[144,768]{1,0:T(8,128)(2,1)} async-done(((bf16[1152,768]{1,0:T(8,128)(2,1)}), bf16[144,768]{1,0:T(8,128)(2,1)}) %reduce-scatter.25.cloned.1.call-update) | async-done | bytes 221200
  571.2 4.3 fusion.128
  581.9 47.2 %all-gather.7.cloned.1.call-done = bf16[1152,768]{1,0:T(8,128)(2,1)} async-done(((bf16[144,768]{1,0:T(8,128)(2,1)}), bf16[1152,768]{1,0:T(8,128)(2,1)}) %all-gather.7.cloned.1.call-update) | async-done | bytes 1769488 | tf_op jit(solution)/shard_map/all_gather | solution.py:138
  629.1 3.9 copy.68
  640.4 41.0 %all-gather.9.cloned.1.call-done = bf16[1152,768]{1,0:T(8,128)(2,1)} async-done(((bf16[144,768]{1,0:T(8,128)(2,1)}), bf16[1152,768]{1,0:T(8,128)(2,1)}) %all-gather.9.cloned.1.call-update) | async-done | bytes 1769488 | tf_op jit(solution)/shard_map/all_gather | solution.py:139
  681.4 4.1 copy.69
  685.5 6.8 fusion.89
  695.3 5.7 convert_reduce_fusion.2
  709.1 6.5 multiply_convert_fusion.2
  718.3 3.9 copy.100
  726.0 5.3 fusion.205
  731.4 6.4 fusion.139
  737.8 5.3 fusion.112
  746.0 3.9 copy.102
  753.2 5.1 convert_reduce_fusion.8
  758.6 4.9 add_add_fusion.3
  763.5 5.3 fusion.204
  770.5 12.7 %add_add_fusion.1 = f32[768,3072]{1,0:T(8,128)} fusion(f32[768,3072]{1,0:T(8,128)} %fusion.204, f32[768,3072]{1,0:T(8,128)} %fusion.205, bf16[144,3072]{1,0:T(8,128)(2,1)} %copy-done.46, f32[144,768]{1,0:T(8,128)S(1)} %copy-done.15, f32[144]{0:T(256)S(1)} %copy-done.119, f32[144]{0:T(256)S(1)} %copy-done.103, f32[768]{0:T(1024)S(1)} %copy-done.67, ...), kind=kOutput, calls=%fused_computation.1 | convolution fusion | flops 684748800 | bytes 29645952 | tf_op jit(solution)/shard_map/td,tf->df/dot_general | solution.py:169
  783.2 5.6 add_add_fusion
  788.8 4.9 reduce-scatter.19.cloned.1.call-done
  797.4 73.0 %reduce-scatter.21.cloned.1.call-done = bf16[144,768]{1,0:T(8,128)(2,1)} async-done(((bf16[1152,768]{1,0:T(8,128)(2,1)}), bf16[144,768]{1,0:T(8,128)(2,1)}) %reduce-scatter.21.cloned.1.call-update) | async-done | bytes 221200
  875.1 7.6 add_add_fusion.2
  883.4 4.9 fusion.83
  888.5 4.3 fusion.82
  897.8 4.6 fusion.81
  912.1 67.6 %all-reduce = (f32[768]{0:T(1024)}, f32[768]{0:T(1024)}, f32[768]{0:T(1024)}, f32[768]{0:T(1024)}, f32[768]{0:T(1024)}, /*index=5*/f32[768]{0:T(1024)}, f32[768]{0:T(1024)}, f32[3072]{0:T(1024)}, f32[768]{0:T(1024)}) all-reduce(f32[768]{0:T(1024)} %add_add_fusion.18, ...), channel_id=1, replica_groups=mesh['dp'=16,'seq'=8] {'dp','seq'}, use_global_device_ids=true, to_apply=%region_39.40 | all-reduce | flops 9216 | bytes 73728 | tf_op jit(solution)/shard_map/psum | solution.py:242
  984.3 137.2 %all-reduce.4.cloned.1.call-done = (f32[768,2304]{1,0:T(8,128)}, f32[768,768]{1,0:T(8,128)}, f32[768,3072]{1,0:T(8,128)}, f32[3072,768]{1,0:T(8,128)}) async-done(((f32[768,2304]{1,0:T(8,128)}, f32[768,768]{1,0:T(8,128)}, f32[768,3072]{1,0:T(8,128)}, f32[3072,768]{1,0:T(8,128)}), (f32[768,2304]{1,0:T(8,128)}, f32[768,768]{1,0:T(8,128)}, f32[768,3072]{1,0:T(8,128)}, ...) | async-done | bytes 28311568 | tf_op jit(solution)/shard_map/psum | solution.py:242
  1121.5 6.6 copy.119
  1129.5 9.3 copy.121
  (504 shorter events, 170.5 us)
Async XLA Ops:
  7.2 61.6 %all-gather.15.cloned.1.call-start = ((), (), s32[]{:S(2)}) async-start(), calls=%async_computation.10 | async-start | bytes 1990656 | tf_op jit(solution)/shard_map/all_gather | solution.py:138
  14.5 106.7 %all-gather.11.cloned.1.call-start = ((), (), s32[]{:S(2)}) async-start(), calls=%async_computation.8 | async-start | bytes 1990656 | tf_op jit(solution)/shard_map/all_gather | solution.py:138
  17.2 156.4 %all-gather.17.cloned.1.call-start = ((), (), s32[]{:S(2)}) async-start(), calls=%async_computation.11 | async-start | bytes 1990656 | tf_op jit(solution)/shard_map/all_gather | solution.py:139
  18.0 207.4 %all-gather.13.cloned.1.call-start = ((), (), s32[]{:S(2)}) async-start(), calls=%async_computation.9 | async-start | bytes 1990656 | tf_op jit(solution)/shard_map/all_gather | solution.py:139
  18.6 320.2 %reduce-scatter.29.cloned.1.call-start = ((), (), s32[]{:S(2)}) async-start(), calls=%async_computation.17 | async-start | bytes 1990656
  20.5 157.0 %copy-start.121 = (pred[1152]{0:T(1024)(128)(4,1)}, pred[1152]{0:T(1024)(128)(4,1)S(1)}, u32[]{:S(2)}) copy-start(pred[1152]{0:T(1024)(128)(4,1)S(1)} %fusion.165) | copy-start | bytes 3460
  20.6 209.1 %copy-start.120 = (pred[1152]{0:T(1024)(128)(4,1)}, pred[1152]{0:T(1024)(128)(4,1)S(1)}, u32[]{:S(2)}) copy-start(pred[1152]{0:T(1024)(128)(4,1)S(1)} %fusion.166) | copy-start | bytes 3460
  229.6 8.8 slice-start
  229.7 8.8 slice-start.1
  238.2 13.2 %copy-start.10 = (f32[144,768]{1,0:T(8,128)}, f32[144,768]{1,0:T(8,128)S(1)}, u32[]{:S(2)}) copy-start(f32[144,768]{1,0:T(8,128)S(1)} %get-tuple-element.100) | copy-start | bytes 1327108
  238.3 13.2 %copy-start.87 = (f32[144]{0:T(256)}, f32[144]{0:T(256)S(1)}, u32[]{:S(2)}) copy-start(f32[144]{0:T(256)S(1)} %broadcast_multiply_fusion.2) | copy-start | bytes 1732
  238.6 12.9 %copy-start.104 = (f32[144]{0:T(256)}, f32[144]{0:T(256)S(1)}, u32[]{:S(2)}) copy-start(f32[144]{0:T(256)S(1)} %fusion.171) | copy-start | bytes 1732
  267.4 148.1 %reduce-scatter.27.cloned.1.call-start = ((), (), s32[]{:S(2)}) async-start(), calls=%async_computation.16 | async-start | bytes 1990656
  281.8 210.2 %reduce-scatter.23.cloned.1.call-start = ((), (), s32[]{:S(2)}) async-start(), calls=%async_computation.14 | async-start | bytes 1990656
  302.8 266.5 %reduce-scatter.25.cloned.1.call-start = ((), (), s32[]{:S(2)}) async-start(), calls=%async_computation.15 | async-start | bytes 1990656
  313.2 315.9 %all-gather.7.cloned.1.call-start = ((), (), s32[]{:S(2)}) async-start(), calls=%async_computation.6 | async-start | bytes 1990656 | tf_op jit(solution)/shard_map/all_gather | solution.py:138
  578.1 103.3 %all-gather.9.cloned.1.call-start = ((), (), s32[]{:S(2)}) async-start(), calls=%async_computation.7 | async-start | bytes 1990656 | tf_op jit(solution)/shard_map/all_gather | solution.py:139
  578.7 215.0 %reduce-scatter.19.cloned.1.call-start = ((), (), s32[]{:S(2)}) async-start(), calls=%async_computation.12 | async-start | bytes 1990656
  685.5 8.7 slice-start.2
  685.5 8.7 slice-start.3
  693.9 9.5 copy-start.8
  694.0 9.5 copy-start.89
  694.2 9.2 copy-start.106
  722.2 148.2 %reduce-scatter.21.cloned.1.call-start = ((), (), s32[]{:S(2)}) async-start(), calls=%async_computation.13 | async-start | bytes 1990656
  726.0 17.0 %slice-start.7 = ((s8[7962624]{0:T(1024)(128)(4,1)}), s8[4194304]{0:T(1024)(128)(4,1)S(1)}, s32[]{:S(2)}) async-start(s8[7962624]{0:T(1024)(128)(4,1)} %bitcast.333), calls=%async_computation.26 | async-start | bytes 8388608
  731.3 11.7 %slice-start.8 = ((s8[7962624]{0:T(1024)(128)(4,1)}), s8[3768320]{0:T(1024)(128)(4,1)S(1)}, s32[]{:S(2)}) async-start(s8[7962624]{0:T(1024)(128)(4,1)} %bitcast.333), calls=%async_computation.27 | async-start | bytes 7536640
  758.3 363.2 %all-reduce.4.cloned.1.call-start = ((), (), s32[]{:S(2)}) async-start(), calls=%async_computation.18 | async-start | bytes 56623104 | tf_op jit(solution)/shard_map/psum | solution.py:242
  768.8 14.3 %slice-start.4 = ((s8[9437184]{0:T(1024)(128)(4,1)}), s8[4194304]{0:T(1024)(128)(4,1)S(1)}, s32[]{:S(2)}) async-start(s8[9437184]{0:T(1024)(128)(4,1)} %bitcast.331), calls=%async_computation.23 | async-start | bytes 8388608
  768.8 14.3 %slice-start.5 = ((s8[9437184]{0:T(1024)(128)(4,1)}), s8[4194304]{0:T(1024)(128)(4,1)S(1)}, s32[]{:S(2)}) async-start(s8[9437184]{0:T(1024)(128)(4,1)} %bitcast.331), calls=%async_computation.24 | async-start | bytes 8388608
  770.5 12.7 %slice-start.6 = ((s8[9437184]{0:T(1024)(128)(4,1)}), s8[1048576]{0:T(1024)(128)(4,1)S(1)}, s32[]{:S(2)}) async-start(s8[9437184]{0:T(1024)(128)(4,1)} %bitcast.331), calls=%async_computation.25 | async-start | bytes 2097152
  770.5 12.7 %copy-start.34 = (f32[144,3072]{1,0:T(8,128)S(1)}, f32[144,3072]{1,0:T(8,128)}, u32[]{:S(2)}) copy-start(f32[144,3072]{1,0:T(8,128)} %copy-done.33) | copy-start | bytes 5308420
  788.8 83.5 %copy-start.95 = (f32[144]{0:T(256)S(1)}, f32[144]{0:T(256)}, u32[]{:S(2)}) copy-start(f32[144]{0:T(256)} %broadcast_multiply_fusion.5) | copy-start | bytes 1732
  788.8 83.5 %copy-start.97 = (f32[144]{0:T(256)S(1)}, f32[144]{0:T(256)}, u32[]{:S(2)}) copy-start(f32[144]{0:T(256)} %copy-done.96) | copy-start | bytes 1732
  897.7 7.5 copy-start.45
  897.7 7.7 copy-start.7
  897.7 7.7 copy-start.56
  897.7 7.7 copy-start.68
  897.7 7.7 copy-start.69
  897.7 7.7 copy-start.71
  897.7 7.7 copy-start.100
  897.7 7.7 copy-start.114
  897.7 7.7 copy-start.117
  897.8 7.7 copy-start.132
  897.8 7.7 copy-start.153
  897.8 7.7 copy-start.154
  1128.1 10.7 slice-start.9
  1129.5 9.3 slice-start.10
  1129.5 9.3 slice-start.11
  (141 other events, 541.9 us)
Sparse Core Ops, SparseCore 0:
  14.7 54.0 all-gather.14
  71.7 49.5 all-gather.10
  124.1 49.5 all-gather.16
  175.8 49.5 all-gather.12
  267.5 71.2 reduce-scatter.28
  342.8 72.6 reduce-scatter.26
  419.2 72.6 reduce-scatter.22
  496.7 72.6 reduce-scatter.24
  578.2 50.8 all-gather.6
  631.8 49.5 all-gather.8
  722.3 71.3 reduce-scatter.18
  797.7 72.6 reduce-scatter.20
  882.9 238.5 all-reduce.3
where the time goes:
time: 1160 us; the launch traced here: 1150 us
  waiting for transfers between devices  703 us (61%)
  matrix products  207 us (18%)
  local copies, waits for them, and re-layouts  108 us (9%)
  blocking collectives  67.6 us (6%)
  other arithmetic  43.8 us (4%)
  between operations  18.2 us (2%)
    unnamed x19, waiting for transfers between devices  314 us
    psum x1, waiting for transfers between devices, body(): summed = lax.psum(local_sums, ('dp', 'seq'))  137 us
    all_gather x3, waiting for transfers between devices, body(): lax.all_gather(key_rows, 'seq', axis=0, tiled=True)  131 us
    all_gather x3, waiting for transfers between devices, body(): lax.all_gather(value_rows, 'seq', axis=0, tiled=True)  121 us
    unnamed x368, local copies, waits for them, and re-layouts  68.3 us
    psum x1, blocking collectives, body(): summed = lax.psum(local_sums, ('dp', 'seq'))  67.6 us
  transfers between devices with their start and end apart: 13, of which 13 were waited for; matrix products, arithmetic and copies ran while one was open for 19% of the time, Pallas kernels for 0%

commit v1 on v0

v1 whole, which is shorter than its diff:
```python
import itertools
import math

import jax
import jax.numpy as jnp
from jax import lax
from jax.experimental import pallas as pl
from jax.experimental.pallas import tpu as pltpu
from jax.sharding import Mesh
from jax.sharding import PartitionSpec as P

HEADS = 12
HEAD_DIM = 64
VIEW_TOK = 128
VIEWS_MAX = 8
D = 768
FF = 3072
BLK = 144
SLOTS = 4
ROWS = BLK * SLOTS
KEYS = 2 * ROWS
PAIRS = HEADS // 2
LANES = 128
FCHUNK = 768
NF = FF // FCHUNK

bf16 = jnp.bfloat16
f32 = jnp.float32
epsilon = 1e-05
masked_score = -1e30
GELU_C = math.sqrt(2.0 / math.pi)
GELU_A = 0.044715

AXES = ("y", "xl", "c", "z", "xh")
VMEM_LIMIT = 60 * 1024 * 1024


def mm(a, b):
    return lax.dot_general(a, b, (((1,), (0,)), ((), ())), preferred_element_type=f32)


def mm_nt(a, b):
    return lax.dot_general(a, b, (((1,), (1,)), ((), ())), preferred_element_type=f32)


def mm_tn(a, b):
    return lax.dot_general(a, b, (((0,), (0,)), ((), ())), preferred_element_type=f32)


def lane_row(at, first, last):
    lane = lax.broadcasted_iota(jnp.int32, (1, LANES), 1)
    return jnp.where((lane >= first) & (lane < last), 1.0, 0.0).astype(at)


def attention_forward_kernel(q_ref, ko_ref, vo_ref, ks_ref, vs_ref, mask_ref, p_ref, o_ref, linv_ref, att_ref):
    half = [lane_row(bf16, 0, 64), lane_row(bf16, 64, 128)]
    unit = [lane_row(bf16, 64, 65), lane_row(bf16, 0, 1)]
    q = q_ref[...]
    k = jnp.concatenate([ko_ref[...], ks_ref[...]], axis=0)
    v = jnp.concatenate([vo_ref[...], vs_ref[...]], axis=0)
    mask = mask_ref[...]
    lane = lax.broadcasted_iota(jnp.int32, (BLK, LANES), 1)
    q_now = [q * half[h] + unit[h] for h in range(2)]
    k_now = [k * half[h] + mask * unit[h] for h in range(2)]
    v_now = [v * half[h] + unit[h] for h in range(2)]
    for s in range(SLOTS):
        rows = slice(s * BLK, (s + 1) * BLK)
        outs, invs = [], []
        for h in range(2):
            scores = mm_nt(q_now[h][rows], k_now[h])
            top = jnp.max(scores, axis=1, keepdims=True)
            weights = jnp.exp((scores - top) * 0.125).astype(bf16)
            p_ref[h, rows, :] = weights
            out = mm(weights, v_now[h])
            total = out[:, 64:65] if h == 0 else out[:, 0:1]
            inv = 1.0 / total
            outs.append(out * inv)
            invs.append(jnp.broadcast_to(inv, (BLK, LANES)))
        out = jnp.where(lane < 64, outs[0], outs[1])
        o_ref[rows, :] = out
        att_ref[rows, :] = out.astype(bf16)
        linv_ref[rows, :] = jnp.where(lane < 64, invs[0], invs[1])


def attention_forward(joined, sibling, mask):
    col = lambda first: pl.BlockSpec((ROWS, LANES), lambda i, f=first: (0, f + i))
    return pl.pallas_call(
        attention_forward_kernel,
        grid=(PAIRS,),
        in_specs=[
            col(0), col(PAIRS), col(2 * PAIRS), col(0), col(PAIRS),
            pl.BlockSpec((KEYS, LANES), lambda i: (0, 0)),
        ],
        out_specs=[
            pl.BlockSpec((2, ROWS, KEYS), lambda i: (i, 0, 0)),
            col(0), col(0), col(0),
        ],
        out_shape=[
            jax.ShapeDtypeStruct((HEADS, ROWS, KEYS), bf16),
            jax.ShapeDtypeStruct((ROWS, D), f32),
            jax.ShapeDtypeStruct((ROWS, D), f32),
            jax.ShapeDtypeStruct((ROWS, D), bf16),
        ],
        compiler_params=pltpu.CompilerParams(vmem_limit_bytes=VMEM_LIMIT),
        cost_estimate=pl.CostEstimate(flops=16 * ROWS * KEYS * D, bytes_accessed=20_000_000, transcendentals=HEADS * ROWS * KEYS),
        name="attention_forward",
    )(joined, joined, joined, sibling, sibling, mask)


def attention_backward_kernel(
    q_ref, ko_ref, vo_ref, ks_ref, vs_ref, p_ref, o_ref, linv_ref, g_ref,
    gq_ref, gko_ref, gvo_ref, gks_ref, gvs_ref,
):
    half = [lane_row(bf16, 0, 64), lane_row(bf16, 64, 128)]
    two = [lane_row(bf16, 64, 66), lane_row(bf16, 0, 2)]
    q = q_ref[...]
    k = jnp.concatenate([ko_ref[...], ks_ref[...]], axis=0)
    v = jnp.concatenate([vo_ref[...], vs_ref[...]], axis=0)
    v_now = [v * half[h] + two[h] for h in range(2)]
    lane = lax.broadcasted_iota(jnp.int32, (ROWS, LANES), 1)
    gs = g_ref[...].astype(f32) * linv_ref[...]
    prod = gs * o_ref[...]
    gq, gk, gv = [], [], []
    for h in range(2):
        mine = (lane < 64) if h == 0 else (lane >= 64)
        base = 64 if h == 0 else 0
        delta = jnp.sum(jnp.where(mine, prod, 0.0), axis=1, keepdims=True)
        high = delta.astype(bf16).astype(f32)
        g_aug = jnp.where(
            mine, gs, jnp.where(lane == base, -high, jnp.where(lane == base + 1, high - delta, 0.0))
        ).astype(bf16)
        weights = p_ref[h]
        diff = mm_nt(g_aug, v_now[h])
        gscore = (weights.astype(f32) * diff).astype(bf16)
        gv.append(mm_tn(weights, g_aug))
        gk.append(mm_tn(gscore, q))
        gq.append(mm(gscore, k))
    gq_ref[...] = (jnp.where(lane < 64, gq[0], gq[1]) * 0.125).astype(bf16)
    lane_k = lax.broadcasted_iota(jnp.int32, (KEYS, LANES), 1)
    gk_all = jnp.where(lane_k < 64, gk[0], gk[1]) * 0.125
    gv_all = jnp.where(lane_k < 64, gv[0], gv[1])
    gko_ref[...] = gk_all[:ROWS]
    gvo_ref[...] = gv_all[:ROWS]
    gks_ref[...] = gk_all[ROWS:].astype(bf16)
    gvs_ref[...] = gv_all[ROWS:].astype(bf16)


def attention_backward(joined, sibling, weights, heads_out, linv, grad_att):
    col = lambda first: pl.BlockSpec((ROWS, LANES), lambda i, f=first: (0, f + i))
    return pl.pallas_call(
        attention_backward_kernel,
        grid=(PAIRS,),
        in_specs=[
            col(0), col(PAIRS), col(2 * PAIRS), col(0), col(PAIRS),
            pl.BlockSpec((2, ROWS, KEYS), lambda i: (i, 0, 0)),
            col(0), col(0), col(0),
        ],
        out_specs=[col(0), col(0), col(0), col(0), col(0)],
        out_shape=[
            jax.ShapeDtypeStruct((ROWS, D), bf16),
            jax.ShapeDtypeStruct((ROWS, D), f32),
            jax.ShapeDtypeStruct((ROWS, D), f32),
            jax.ShapeDtypeStruct((ROWS, D), bf16),
            jax.ShapeDtypeStruct((ROWS, D), bf16),
        ],
        compiler_params=pltpu.CompilerParams(vmem_limit_bytes=VMEM_LIMIT),
        cost_estimate=pl.CostEstimate(flops=32 * ROWS * KEYS * D, bytes_accessed=25_000_000, transcendentals=0),
        name="attention_backward",
    )(joined, joined, joined, sibling, sibling, weights, heads_out, linv, grad_att)


def feed_forward_kernel(
    att_ref, x_ref, g_ref, ow_ref, vec_ref, upb_ref, up_ref, down_ref,
    out_ref, gh_ref, gatt_ref, dout_ref, dup_ref, ddown_ref, vecg_ref, upbg_ref,
    hidden, xhat, rstd_s, normed2, y_acc, gn_acc,
):
    f = pl.program_id(0)
    out_bias, gain, shift, down_bias = (vec_ref[r : r + 1, :] for r in range(4))

    @pl.when(f == 0)
    def _():
        h = x_ref[...].astype(f32) + mm(att_ref[...], ow_ref[...]) + out_bias
        hidden[...] = h
        centred = h - jnp.mean(h, axis=1, keepdims=True)
        rstd = lax.rsqrt(jnp.mean(centred * centred, axis=1, keepdims=True) + epsilon)
        xh = centred * rstd
        xhat[...] = xh
        rstd_s[...] = jnp.broadcast_to(rstd, (ROWS, LANES))
        normed2[...] = (xh * gain + shift).astype(bf16)
        y_acc[...] = jnp.zeros_like(y_acc)
        gn_acc[...] = jnp.zeros_like(gn_acc)

    g = g_ref[...]
    n2 = normed2[...]
    u = mm(n2, up_ref[...]) + upb_ref[0]
    ga = mm_nt(g, down_ref[...])
    u2 = u * u
    t = jnp.tanh(u * (GELU_C + (GELU_C * GELU_A) * u2))
    hp = 0.5 + 0.5 * t
    active = (u * hp).astype(bf16)
    slope = hp + (0.5 * u) * (1.0 - t * t) * (GELU_C + (3.0 * GELU_C * GELU_A) * u2)
    gu = (ga * slope).astype(bf16)
    y_acc[...] += mm(active, down_ref[...])
    gn_acc[...] += mm_nt(gu, up_ref[...])
    ddown_ref[...] = mm_tn(active, g).astype(bf16)
    dup_ref[...] = mm_tn(n2, gu).astype(bf16)
    upbg_ref[0] = jnp.sum(gu.astype(f32), axis=0, keepdims=True)

    @pl.when(f == NF - 1)
    def _():
        out_ref[...] = (hidden[...] + y_acc[...] + down_bias).astype(bf16)
        gn = gn_acc[...]
        xh = xhat[...]
        gf = g_ref[...].astype(f32)
        vecg_ref[...] = jnp.zeros_like(vecg_ref)
        vecg_ref[1:2, :] = jnp.sum(gn * xh, axis=0, keepdims=True)
        vecg_ref[2:3, :] = jnp.sum(gn, axis=0, keepdims=True)
        vecg_ref[3:4, :] = jnp.sum(gf, axis=0, keepdims=True)
        gx = gn * gain
        mean1 = jnp.mean(gx, axis=1, keepdims=True)
        mean2 = jnp.mean(gx * xh, axis=1, keepdims=True)
        gh = gf + rstd_s[:, 0:1] * (gx - mean1 - xh * mean2)
        gh_ref[...] = gh
        vecg_ref[0:1, :] = jnp.sum(gh, axis=0, keepdims=True)
        gb = gh.astype(bf16)
        dout_ref[...] = mm_tn(att_ref[...], gb).astype(bf16)
        gatt_ref[...] = mm_nt(gb, ow_ref[...]).astype(bf16)


def feed_forward(attended, x, g, out_w, vecs, up_b, up_w, down_w):
    whole = lambda shape: pl.BlockSpec(shape, lambda f: (0,) * len(shape))
    return pl.pallas_call(
        feed_forward_kernel,
        grid=(NF,),
        in_specs=[
            whole((ROWS, D)), whole((ROWS, D)), whole((ROWS, D)), whole((D, D)), whole((8, D)),
            pl.BlockSpec((1, 1, FCHUNK), lambda f: (f, 0, 0)),
            pl.BlockSpec((D, FCHUNK), lambda f: (0, f)),
            pl.BlockSpec((FCHUNK, D), lambda f: (f, 0)),
        ],
        out_specs=[
            whole((ROWS, D)), whole((ROWS, D)), whole((ROWS, D)), whole((D, D)),
            pl.BlockSpec((D, FCHUNK), lambda f: (f, 0)),
            pl.BlockSpec((FCHUNK, D), lambda f: (f, 0)),
            whole((8, D)),
            pl.BlockSpec((1, 1, FCHUNK), lambda f: (f, 0, 0)),
        ],
        out_shape=[
            jax.ShapeDtypeStruct((ROWS, D), bf16),
            jax.ShapeDtypeStruct((ROWS, D), f32),
            jax.ShapeDtypeStruct((ROWS, D), bf16),
            jax.ShapeDtypeStruct((D, D), bf16),
            jax.ShapeDtypeStruct((NF * D, FCHUNK), bf16),
            jax.ShapeDtypeStruct((FF, D), bf16),
            jax.ShapeDtypeStruct((8, D), f32),
            jax.ShapeDtypeStruct((NF, 1, FCHUNK), f32),
        ],
        scratch_shapes=[
            pltpu.VMEM((ROWS, D), f32),
            pltpu.VMEM((ROWS, D), f32),
            pltpu.VMEM((ROWS, LANES), f32),
            pltpu.VMEM((ROWS, D), bf16),
            pltpu.VMEM((ROWS, D), f32),
            pltpu.VMEM((ROWS, D), f32),
        ],
        compiler_params=pltpu.CompilerParams(vmem_limit_bytes=VMEM_LIMIT),
        cost_estimate=pl.CostEstimate(flops=12 * ROWS * D * FF, bytes_accessed=30_000_000, transcendentals=ROWS * FF),
        name="feed_forward",
    )(attended, x, g, out_w, vecs, up_b, up_w, down_w)


def linear(y, xl, c, z, xh):
    return (((y * 2 + xl) * 2 + c) * 4 + z) * 2 + xh


def scene_pairs(slot):
    pairs = []
    for y in range(4):
        for xl in range(2):
            for z in range(4):
                for xh in range(2):
                    block = 2 * z + xh
                    scene = (slot - block) % 4
                    if scene < 3:
                        for c in range(2):
                            pairs.append((linear(y, xl, c, z, xh), linear(y, xl, block // 4, scene, c)))
    return pairs


def to_scene(values, block):
    pieces = []
    for slot in range(SLOTS):
        scene = jnp.minimum((slot - block) % 4, 2)
        pieces.append(lax.ppermute(lax.dynamic_index_in_dim(values, scene, 0, keepdims=False), AXES, scene_pairs(slot)))
    return jnp.concatenate(pieces, axis=0)


def from_scene(values, block):
    pieces = []
    for slot in range(SLOTS):
        back = [(target, source) for source, target in scene_pairs(slot)]
        pieces.append(lax.ppermute(values[slot * BLK : (slot + 1) * BLK], AXES, back))
    pieces = jnp.stack(pieces)
    return jnp.stack([lax.dynamic_index_in_dim(pieces, (m + block) % 4, 0, keepdims=False) for m in range(3)])


ORDERS = (("y", "z", "x"), ("z", "x", "y"), ("x", "y", "z"))
SWAP = ((0, 1), (1, 0))
STEPS = ((1, -1), (-1, 1), (2, 2))


def exchange(value, move):
    pairs = []
    for place in itertools.product(range(4), range(4), range(4), range(2)):
        ends = [linear(y, x % 2, c, z, x // 2) for x, y, z, c in (place, move(*place))]
        pairs.append(tuple(ends))
    return lax.ppermute(value, AXES, pairs)


def ring_exchange(value, axis, signs):
    def move(x, y, z, c):
        at = {"x": x, "y": y, "z": z}
        at[axis] = (at[axis] + signs[c]) % 4
        return at["x"], at["y"], at["z"], c

    return exchange(value, move)


def ring_place(axis):
    if axis == "x":
        return lax.axis_index("xh") * 2 + lax.axis_index("xl")
    return lax.axis_index(axis)


def reduce_stage(buffer, axis, core):
    place = ring_place(axis)
    blocks = buffer.reshape(4, buffer.shape[0] // 4, buffer.shape[1])
    total = lax.dynamic_index_in_dim(blocks, place, 0, keepdims=False).astype(f32)
    for signs in STEPS:
        step = jnp.where(core == 0, signs[0], signs[1])
        block = lax.dynamic_index_in_dim(blocks, (place + step) % 4, 0, keepdims=False)
        total = total + ring_exchange(block, axis, signs).astype(f32)
    return total.astype(bf16)


def gather_stage(block, axis, core):
    place = ring_place(axis)
    whole = jnp.zeros((4,) + block.shape, block.dtype)
    whole = lax.dynamic_update_index_in_dim(whole, block, place, 0)
    for signs in STEPS:
        step = jnp.where(core == 0, signs[0], signs[1])
        other = ring_exchange(block, axis, signs)
        whole = lax.dynamic_update_index_in_dim(whole, other, (place - step) % 4, 0)
    return whole.reshape(4 * block.shape[0], block.shape[1])


def sum_everywhere(grads, core):
    rows = grads.shape[0] // 3
    halves = grads.reshape(3, 2, rows // 2, grads.shape[1])
    parts = []
    for part in range(3):
        mine = lax.dynamic_index_in_dim(halves[part], core, 0, keepdims=False)
        other = lax.dynamic_index_in_dim(halves[part], 1 - core, 0, keepdims=False)
        parts.append((mine.astype(f32) + lax.ppermute(other, "c", SWAP).astype(f32)).astype(bf16))
    for stage in range(3):
        parts = [reduce_stage(parts[part], ORDERS[part][stage], core) for part in range(3)]
    for stage in (2, 1, 0):
        parts = [gather_stage(parts[part], ORDERS[part][stage], core) for part in range(3)]
    result = []
    for mine in parts:
        other = lax.ppermute(mine, "c", SWAP)
        result.append(jnp.where(core == 0, mine, other))
        result.append(jnp.where(core == 0, other, mine))
    return jnp.concatenate(result, axis=0)


def sum_small(values):
    values = values + lax.ppermute(values, "c", SWAP)
    for axis in "zyx":
        for bit in (1, 2):
            flip = lambda x, y, z, c: tuple(v ^ bit if n == axis else v for n, v in zip("xyz", (x, y, z))) + (c,)
            values = values + exchange(values, flip)
    return values


def body(
    tokens, view_counts, ln1_gain, ln1_shift, qkv_weight, query_bias, value_bias, out_weight, out_bias,
    ln2_gain, ln2_shift, up_weight, up_bias, down_weight, down_bias, cotangent,
):
    core, z, xh = lax.axis_index("c"), lax.axis_index("z"), lax.axis_index("xh")
    block = 2 * z + xh
    scene = jnp.minimum(z, 2)

    x = to_scene(tokens, block)
    views = view_counts.astype(f32)
    views_other = lax.ppermute(views, "c", SWAP)
    views = lax.dynamic_index_in_dim(jnp.where(core == xh, views, views_other), scene, 0, keepdims=False)
    g = to_scene(cotangent, block)

    slot = jnp.arange(ROWS, dtype=jnp.int32) // BLK
    inside = jnp.arange(ROWS, dtype=jnp.int32) % BLK
    offset = (slot - z) % 4 * BLK + inside
    place = jnp.concatenate([offset + core * ROWS, offset + (1 - core) * ROWS])
    usable = (place.astype(f32) < views * VIEW_TOK) | (place >= VIEWS_MAX * VIEW_TOK)
    mask = jnp.broadcast_to(jnp.where(usable, 0.0, masked_score).astype(bf16)[:, None], (KEYS, LANES))

    source = x.astype(f32)
    centred = source - jnp.mean(source, axis=1, keepdims=True)
    rstd = lax.rsqrt(jnp.mean(centred * centred, axis=1, keepdims=True) + epsilon)
    xhat = centred * rstd
    normed = (xhat * ln1_gain + ln1_shift).astype(bf16)
    qkv_bias = jnp.concatenate([query_bias, jnp.zeros((D,), f32), value_bias])
    joined = (jnp.dot(normed, qkv_weight, preferred_element_type=f32) + qkv_bias).astype(bf16)
    sibling = lax.ppermute(joined[:, D:], "c", SWAP)
    weights, heads_out, linv, attended = attention_forward(joined, sibling, mask)

    vecs = jnp.concatenate([jnp.stack([out_bias, ln2_gain, ln2_shift, down_bias]), jnp.zeros((4, D), f32)])
    output, grad_hidden, grad_att, d_out, d_up, d_down, vec_grads, up_b_grad = feed_forward(
        attended, x, g, out_weight, vecs, up_bias.reshape(NF, 1, FCHUNK), up_weight, down_weight
    )
    output = from_scene(output, block)
    ff_sum = sum_everywhere(jnp.concatenate([d_up, d_down], axis=0), core)

    grad_q, grad_k, grad_v, grad_k_other, grad_v_other = attention_backward(
        joined, sibling, weights, heads_out, linv, grad_att
    )
    swapped = lax.ppermute(jnp.concatenate([grad_k_other, grad_v_other], axis=1), "c", SWAP).astype(f32)
    grad_k = (grad_k + swapped[:, :D]).astype(bf16)
    grad_v = (grad_v + swapped[:, D:]).astype(bf16)

    d_qkv = [
        lax.dot_general(normed, part, (((0,), (0,)), ((), ())), preferred_element_type=f32).astype(bf16)
        for part in (grad_q, grad_k, grad_v)
    ]
    grad_joined = jnp.concatenate([grad_q, grad_k, grad_v], axis=1)
    grad_normed = lax.dot_general(grad_joined, qkv_weight, (((1,), (1,)), ((), ())), preferred_element_type=f32)
    gx = grad_normed * ln1_gain
    mean1 = jnp.mean(gx, axis=1, keepdims=True)
    mean2 = jnp.mean(gx * xhat, axis=1, keepdims=True)
    input_grad = (grad_hidden + rstd * (gx - mean1 - xhat * mean2)).astype(bf16)
    input_grad = from_scene(input_grad, block)
    small = jnp.concatenate(
        [
            vec_grads[0], vec_grads[1], vec_grads[2], vec_grads[3],
            jnp.sum(grad_normed * xhat, axis=0), jnp.sum(grad_normed, axis=0),
            jnp.sum(grad_q.astype(f32), axis=0), jnp.sum(grad_v.astype(f32), axis=0),
            up_b_grad.reshape(FF),
        ]
    ).reshape(-1, LANES)
    small = sum_small(small).reshape(-1)
    vector = lambda i: small[i * D : (i + 1) * D]
    qkvo_sum = sum_everywhere(jnp.concatenate(d_qkv + [d_out], axis=0), core)

    blocks = lambda a, n: jnp.concatenate([a[i * D : (i + 1) * D] for i in range(n)], axis=1).astype(f32)
    return (
        output, input_grad,
        vector(4), vector(5), blocks(qkvo_sum[: 3 * D], 3), vector(6), vector(7),
        qkvo_sum[3 * D :].astype(f32), vector(0), vector(1), vector(2),
        blocks(ff_sum[:FF], 4), small[8 * D :], ff_sum[FF:].astype(f32), vector(3),
    )


def solution(mesh):
    fine = Mesh(mesh.devices.reshape(4, 2, 2, 4, 2), AXES)
    rows = P(("y", "xl", "c"), ("z", "xh"), None)
    placed = (rows, P(("y", "xl", "c"))) + (P(),) * 13 + (rows,)
    return jax.shard_map(
        body, mesh=fine, in_specs=placed, out_specs=(rows, rows) + (P(),) * 13, check_vma=False
    )
```

time: 1160 us -> 542 us (0.47)
  waiting for transfers between devices: 703 us -> 97 us
  starting transfers between devices: 1.38 us -> 252 us
  matrix products: 207 us -> 9.35 us
  local copies, waits for them, and re-layouts: 108 us -> 23 us
  Pallas kernels: 0 us -> 78.7 us
  blocking collectives: 67.6 us -> 0 us
  other arithmetic: 43.8 us -> 72.3 us
  between operations: 18.2 us -> 3.88 us
    unnamed x19 -> x0, waiting for transfers between devices: 314 us -> none
    ppermute x0 -> x146, starting transfers between devices: none -> 252 us  [the longest x114 153 us: exchange(): return lax.ppermute(value, AXES, pairs)]
    all_gather x6 -> x0, waiting for transfers between devices: 252 us -> none  [the longest x3 131 us: body(): lax.all_gather(key_rows, 'seq', axis=0, tiled=True)]
    dot_general x54 -> x5, matrix products: 207 us -> 9.35 us  [the longest x3 4.26 us: body(): lax.dot_general(normed, part, (((0,), (0,)), ((), ())), preferred_element...]
    psum x1 -> x0, waiting for transfers between devices: 137 us -> none  [body(): summed = lax.psum(local_sums, ('dp', 'seq'))]
    ppermute x0 -> x146, waiting for transfers between devices: none -> 97 us  [the longest x114 68.4 us: exchange(): return lax.ppermute(value, AXES, pairs)]
    pallas_call x0 -> x3, Pallas kernels: none -> 78.7 us  [the longest x1 30.8 us: feed_forward(): pl.pallas_call(feed_forward_kernel, grid=(NF,), in_specs=[whole((ROWS, D)...]
    psum x1 -> x0, blocking collectives: 67.6 us -> none  [body(): summed = lax.psum(local_sums, ('dp', 'seq'))]
  transfers between devices with their start and end apart: 13 -> 146, of which waited for: 13 -> 61; matrix products, arithmetic and copies ran while one was open for 19% -> 16% of each run, Pallas kernels for 0% -> 4%
where the time goes in v1:
time: 542 us; the launch traced here: 537 us
  starting transfers between devices  252 us (46%)
  waiting for transfers between devices  97 us (18%)
  Pallas kernels  78.7 us (15%)
  other arithmetic  72.3 us (13%)
  local copies, waits for them, and re-layouts  23 us (4%)
  matrix products  9.35 us (2%)
    ppermute x114, starting transfers between devices, exchange(): return lax.ppermute(value, AXES, pairs)  153 us
    ppermute x114, waiting for transfers between devices, exchange(): return lax.ppermute(value, AXES, pairs)  68.4 us
    convert_element_type x2, other arithmetic, body(): jnp.concatenate([a[i * D:(i + 1) * D] for i in range(n)], axis=1)  41 us
    ppermute x8, starting transfers between devices, from_scene(): pieces.append(lax.ppermute(values[slot * BLK:(slot + 1) * BLK], AXES, back))  35.5 us
    pallas_call x1, Pallas kernels, feed_forward(): pl.pallas_call(feed_forward_kernel, grid=(NF,), in_specs=[whole((ROWS, D)...  30.8 us
    ppermute x6, starting transfers between devices, sum_everywhere(): other = lax.ppermute(mine, 'c', SWAP)  30.3 us
    ppermute x8, starting transfers between devices, to_scene(): lax.ppermute(lax.dynamic_index_in_dim(values, scene, 0, keepdims=False),...  27.9 us
    pallas_call x1, Pallas kernels, attention_forward(): pl.pallas_call(attention_forward_kernel, grid=(PAIRS,), in_specs=[col(0),...  25.5 us
  transfers between devices with their start and end apart: 146, of which 61 were waited for; matrix products, arithmetic and copies ran while one was open for 16% of the time, Pallas kernels for 4%

profile of v1, /device:TPU:1, one launch (start us, length us, event | category | flops | bytes accessed | tf_op | source)
XLA Modules:
  0.0 536.7 jit_solution(14187665468817542896)
XLA Ops:
  2.3 6.0 %collective-permute-start = (bf16[144,768]{1,0:T(8,128)(2,1)S(1)}, bf16[144,768]{1,0:T(8,128)(2,1)S(1)}, u32[]{:S(2)}, u32[]{:S(2)}) collective-permute-start(bf16[144,768]{1,0:T(8,128)(2,1)S(1)} %get-tuple-element.128), channel_id=1, source_target_pairs={{0,0},{8,1},{2,4},{10,5},{3,2},{11,3},{4,8},{12,9},{6,12},{14,13},... | collective-permute-start | bytes 663560 | tf_op jit(solution)/shard_map/ppermute | solution.py:294
  8.3 3.8 collective-permute-start.1
  12.1 5.7 %collective-permute-start.2 = (bf16[144,768]{1,0:T(8,128)(2,1)S(1)}, bf16[144,768]{1,0:T(8,128)(2,1)S(1)}, u32[]{:S(2)}, u32[]{:S(2)}) collective-permute-start(bf16[144,768]{1,0:T(8,128)(2,1)S(1)} %get-tuple-element.129), channel_id=1, source_target_pairs={{0,4},{8,5},{1,2},{9,3},{2,0},{10,1},{4,12},{12,13},{5,10},{13,11}... | collective-permute-start | bytes 663560 | tf_op jit(solution)/shard_map/ppermute | solution.py:294
  21.9 6.8 %collective-permute-done.3 = bf16[144,768]{1,0:T(8,128)(2,1)S(1)} collective-permute-done((bf16[144,768]{1,0:T(8,128)(2,1)S(1)}, bf16[144,768]{1,0:T(8,128)(2,1)S(1)}, u32[]{:S(2)}, u32[]{:S(2)}) %collective-permute-start.3) | collective-permute-done | bytes 221216 | tf_op jit(solution)/shard_map/ppermute | solution.py:294
  37.1 5.4 %collective-permute-start.8 = (bf16[144,768]{1,0:T(8,128)(2,1)}, bf16[144,768]{1,0:T(8,128)(2,1)}, u32[]{:S(2)}, u32[]{:S(2)}) collective-permute-start(bf16[144,768]{1,0:T(8,128)(2,1)} %get-tuple-element.125), channel_id=1, source_target_pairs={{0,4},{8,5},{1,2},{9,3},{2,0},{10,1},{4,12},{12,13},{5,10},{13,11}... | collective-permute-start | bytes 663560 | tf_op jit(solution)/shard_map/ppermute | solution.py:294
  42.5 2.5 collective-permute-start.7
  54.0 4.8 collective-permute-done.6
  61.9 25.5 %attention_forward.1 = (bf16[12,576,1152]{2,1,0:T(8,128)(2,1)}, f32[576,768]{1,0:T(8,128)}, f32[576,768]{1,0:T(8,128)}, bf16[576,768]{1,0:T(8,128)(2,1)}) custom-call(bf16[576,2304]{1,0:T(8,128)(2,1)} %copy-done.13, bf16[576,2304]{1,0:T(8,128)(2,1)} %copy-done.13, bf16[576,2304]{1,0:T(8,128)(2,1)} %copy-done.13, ...), custom_call_target="tpu_custom_call" | custom-call | flops 8153726976 | bytes 20000000 | tf_op jit(solution)/shard_map/attention_forward/pallas_call | solution.py:87
  87.4 30.8 %feed_forward.1 = (bf16[576,768]{1,0:T(8,128)(2,1)}, f32[576,768]{1,0:T(8,128)}, bf16[576,768]{1,0:T(8,128)(2,1)}, bf16[768,768]{1,0:T(8,128)(2,1)}, bf16[3072,7...) custom-call(bf16[576,768]{1,0:T(8,128)(2,1)} %get-tuple-element.32.att_ref, ...), custom_call_target="tpu_custom_call" | custom-call | flops 16307453952 | bytes 30000000 | tf_op jit(solution)/shard_map/feed_forward/pallas_call | solution.py:232
  120.3 4.1 collective-permute-start.13
  126.3 7.6 %collective-permute-start.11 = (bf16[144,768]{1,0:T(8,128)(2,1)}, bf16[144,768]{1,0:T(8,128)(2,1)}, u32[]{:S(2)}, u32[]{:S(2)}) collective-permute-start(bf16[144,768]{1,0:T(8,128)(2,1)} %get-tuple-element.112), channel_id=1, source_target_pairs={{2,0},{3,8},{0,1},{1,9},{4,3},{5,11},{10,4},{11,12},{8,5},{9,13},{... | collective-permute-start | bytes 663560 | tf_op jit(solution)/shard_map/ppermute | solution.py:302
  133.8 6.4 %fusion.142 = (bf16[2048,768]{1,0:T(8,128)(2,1)}, bf16[2048,768]{1,0:T(8,128)(2,1)S(1)}, bf16[2048,768]{1,0:T(8,128)(2,1)S(1)}) fusion(bf16[3072,768]{1,0:T(8,128)(2,1)} %get-tuple-element.48, bf16[3072,768]{1,0:T(8,128)(2,1)} %get-tuple-element.47), kind=kLoop, calls=%fused_computation.392 | loop fusion | flops 6291456 | bytes 25165824 | tf_op jit(solution)/shard_map/slice | solution.py:362
  143.9 22.4 %attention_backward.1 = (bf16[576,768]{1,0:T(8,128)(2,1)}, f32[576,768]{1,0:T(8,128)}, f32[576,768]{1,0:T(8,128)}, bf16[576,768]{1,0:T(8,128)(2,1)}, bf16[576,768]{1,0:T(8,128)(2,1)}) custom-call(bf16[576,2304]{1,0:T(8,128)(2,1)} %copy-done.13, bf16[576,2304]{1,0:T(8,128)(2,1)} %copy-done.13, bf16[576,2304]{1,0:T(8,128)(2,1)} %copy-done.13, ...), custom_call_target="tpu_custom_call" | custom-call | flops 16307453952 | bytes 25000000 | tf_op jit(solution)/shard_map/attention_backward/pallas_call | solution.py:150
  173.7 7.9 %collective-permute-done.10 = bf16[144,768]{1,0:T(8,128)(2,1)S(1)} collective-permute-done((bf16[144,768]{1,0:T(8,128)(2,1)S(1)}, bf16[144,768]{1,0:T(8,128)(2,1)S(1)}, u32[]{:S(2)}, u32[]{:S(2)}) %collective-permute-start.10) | collective-permute-done | bytes 221216 | tf_op jit(solution)/shard_map/ppermute | solution.py:302
  187.6 2.7 collective-permute-start.107
  192.2 3.2 collective-permute-start.89
  200.1 2.7 fusion.29
  205.2 2.7 collective-permute-done.20
  208.8 3.5 collective-permute-done.21
  215.7 3.8 collective-permute-done.23
  227.7 8.6 %collective-permute-start.18 = (bf16[144,768]{1,0:T(8,128)(2,1)S(1)}, bf16[144,768]{1,0:T(8,128)(2,1)S(1)}, u32[]{:S(2)}, u32[]{:S(2)}) collective-permute-start(bf16[144,768]{1,0:T(8,128)(2,1)S(1)} %get-tuple-element.103), channel_id=1, source_target_pairs={{4,1},{5,9},{2,2},{3,10},{0,3},{1,11},{12,5},{13,13},{10,6},{11,14... | collective-permute-start | bytes 663560 | tf_op jit(solution)/shard_map/ppermute | solution.py:302
  238.5 7.5 %collective-permute-start.16 = (bf16[144,768]{1,0:T(8,128)(2,1)S(1)}, bf16[144,768]{1,0:T(8,128)(2,1)S(1)}, u32[]{:S(2)}, u32[]{:S(2)}) collective-permute-start(bf16[144,768]{1,0:T(8,128)(2,1)S(1)} %get-tuple-element.105), channel_id=1, source_target_pairs={{2,0},{3,8},{0,1},{1,9},{4,3},{5,11},{10,4},{11,12},{8,5},{9,13},{... | collective-permute-start | bytes 663560 | tf_op jit(solution)/shard_map/ppermute | solution.py:302
  257.9 3.1 collective-permute-done.25
  266.8 2.8 collective-permute-done.92
  285.3 2.7 collective-permute-start.133
  289.5 4.2 collective-permute-start.26
  317.2 3.3 collective-permute-start.99
  332.1 3.0 collective-permute-start.122
  335.7 2.6 collective-permute-start.124
  340.9 3.1 collective-permute-done.122
  344.1 4.6 collective-permute-start.142
  350.9 2.8 collective-permute-done.103
  355.1 4.7 collective-permute-done.142
  359.8 3.4 collective-permute-start.67
  367.2 4.2 collective-permute-start.29
  371.6 7.8 %collective-permute-start.28 = (bf16[128,768]{1,0:T(8,128)(2,1)S(1)}, bf16[128,768]{1,0:T(8,128)(2,1)S(1)}, u32[]{:S(2)}, u32[]{:S(2)}) collective-permute-start(bf16[128,768]{1,0:T(8,128)(2,1)S(1)} %get-tuple-element.115), channel_id=1, source_target_pairs={{0,96},{8,40},{2,98},{10,42},{4,100},{12,44},{6,102},{14,46},{32,0... | collective-permute-start | bytes 589832 | tf_op jit(solution)/shard_map/ppermute | solution.py:317
  379.4 9.9 %collective-permute-start.125 = (bf16[1024,768]{1,0:T(8,128)(2,1)S(1)}, bf16[1024,768]{1,0:T(8,128)(2,1)S(1)}, u32[]{:S(2)}, u32[]{:S(2)}) collective-permute-start(bf16[1024,768]{1,0:T(8,128)(2,1)S(1)} %bitcast.492), channel_id=1, source_target_pairs={{0,8},{8,0},{1,9},{9,1},{2,10},{10,2},{3,11},{11,3},{4,12},{12,4},... | collective-permute-start | bytes 4718600 | tf_op jit(solution)/shard_map/ppermute | solution.py:371
  401.0 2.5 collective-permute-start.30
  405.0 2.7 collective-permute-start.73
  426.5 2.5 collective-permute-start.38
  448.9 3.8 collective-permute-start.63
  456.9 5.4 %collective-permute-start.43 = (bf16[128,768]{1,0:T(8,128)(2,1)S(1)}, bf16[128,768]{1,0:T(8,128)(2,1)S(1)}, u32[]{:S(2)}, u32[]{:S(2)}) collective-permute-start(bf16[128,768]{1,0:T(8,128)(2,1)S(1)} %bitcast.538), channel_id=1, source_target_pairs={{0,96},{8,40},{2,98},{10,42},{4,100},{12,44},{6,102},{14,46},{32,0... | collective-permute-start | bytes 589832 | tf_op jit(solution)/shard_map/ppermute | solution.py:317
  464.6 14.9 %collective-permute-start.85 = (bf16[512,768]{1,0:T(8,128)(2,1)S(1)}, bf16[512,768]{1,0:T(8,128)(2,1)S(1)}, u32[]{:S(2)}, u32[]{:S(2)}) collective-permute-start(bf16[512,768]{1,0:T(8,128)(2,1)S(1)} %bitcast.502), channel_id=1, source_target_pairs={{0,8},{8,0},{1,9},{9,1},{2,10},{10,2},{3,11},{11,3},{4,12},{12,4},... | collective-permute-start | bytes 2359304 | tf_op jit(solution)/shard_map/ppermute | solution.py:371
  479.7 4.5 collective-permute-start.105
  485.5 2.9 collective-permute-done.45
  488.5 18.4 %fusion.5 = f32[768,2304]{1,0:T(8,128)} fusion(bf16[512,768]{1,0:T(8,128)(2,1)S(1)} %get-tuple-element.91, bf16[512,768]{1,0:T(8,128)(2,1)S(1)} %get-tuple-element.95, bf16[512,768]{1,0:T(8,128)(2,1)S(1)} %get-tuple-element.94, bf16[512,768]{1,0:T(8,128)(2,1)S(1)} %get-tuple-element.93, bf16[512,768]{1,0:T(8,128)(2,1)S(1)} %get-tuple-element.92), kind=kLoop, calls=%fused_computation.10 | loop fusion | flops 21233664 | bytes 11010048 | tf_op jit(solution)/shard_map/convert_element_type | solution.py:454
  509.3 22.6 %fusion.2 = f32[768,3072]{1,0:T(8,128)} fusion(bf16[1024,768]{1,0:T(8,128)(2,1)S(1)} %get-tuple-element.76, bf16[1024,768]{1,0:T(8,128)(2,1)S(1)} %get-tuple-element.80, bf16[1024,768]{1,0:T(8,128)(2,1)S(1)} %get-tuple-element.79, bf16[768,768]{1,0:T(8,128)(2,1)S(1)} %slice.238, bf16[768,768]{1,0:T(8,128)(2,1)S(1)} %slice.237), kind=kLoop, calls=%fused_computation.4 | loop fusion | flops 28311552 | bytes 16515072 | tf_op jit(solution)/shard_map/convert_element_type | solution.py:454
  532.3 4.2 maximum_convert_fusion
  (521 shorter events, 211.7 us)
Async XLA Ops:
  2.3 16.9 %collective-permute-start = (bf16[144,768]{1,0:T(8,128)(2,1)S(1)}, bf16[144,768]{1,0:T(8,128)(2,1)S(1)}, u32[]{:S(2)}, u32[]{:S(2)}) collective-permute-start(bf16[144,768]{1,0:T(8,128)(2,1)S(1)} %get-tuple-element.128), channel_id=1, source_target_pairs={{0,0},{8,1},{2,4},{10,5},{3,2},{11,3},{4,8},{12,9},{6,12},{14,13},... | collective-permute-start | bytes 663560 | tf_op jit(solution)/shard_map/ppermute | solution.py:294
  8.3 11.3 %collective-permute-start.1 = (bf16[144,768]{1,0:T(8,128)(2,1)S(1)}, bf16[144,768]{1,0:T(8,128)(2,1)S(1)}, u32[]{:S(2)}, u32[]{:S(2)}) collective-permute-start(bf16[144,768]{1,0:T(8,128)(2,1)S(1)} %get-tuple-element.127), channel_id=1, source_target_pairs={{0,2},{8,3},{1,0},{9,1},{3,4},{11,5},{4,10},{12,11},{5,8},{13,9},{... | collective-permute-start | bytes 663560 | tf_op jit(solution)/shard_map/ppermute | solution.py:294
  17.8 10.9 %collective-permute-start.3 = (bf16[144,768]{1,0:T(8,128)(2,1)S(1)}, bf16[144,768]{1,0:T(8,128)(2,1)S(1)}, u32[]{:S(2)}, u32[]{:S(2)}) collective-permute-start(bf16[144,768]{1,0:T(8,128)(2,1)S(1)} %get-tuple-element.126), channel_id=1, source_target_pairs={{1,4},{9,5},{2,2},{10,3},{3,0},{11,1},{5,12},{13,13},{6,10},{14,11... | collective-permute-start | bytes 663560 | tf_op jit(solution)/shard_map/ppermute | solution.py:294
  33.9 27.1 %collective-permute-start.4 = (bf16[576,1536]{1,0:T(8,128)(2,1)}, bf16[576,1536]{1,0:T(8,128)(2,1)}, u32[]{:S(2)}, u32[]{:S(2)}) collective-permute-start(bf16[576,1536]{1,0:T(8,128)(2,1)} %slice.223), channel_id=1, source_target_pairs={{0,8},{8,0},{1,9},{9,1},{2,10},{10,2},{3,11},{11,3},{4,12},{12,4},... | collective-permute-start | bytes 5308424 | tf_op jit(solution)/shard_map/ppermute | solution.py:414
  34.4 15.4 %collective-permute-start.5 = (f32[3]{0:T(128)}, f32[3]{0:T(128)}, u32[]{:S(2)}, u32[]{:S(2)}) collective-permute-start(f32[3]{0:T(128)} %convert_element_type.465), channel_id=1, source_target_pairs={{0,8},{8,0},{1,9},{9,1},{2,10},{10,2},{3,11},{11,3},{4,12},{12,4},... | collective-permute-start | bytes 44 | tf_op jit(solution)/shard_map/ppermute | solution.py:396
  35.8 18.0 %collective-permute-start.9 = (bf16[144,768]{1,0:T(8,128)(2,1)}, bf16[144,768]{1,0:T(8,128)(2,1)}, u32[]{:S(2)}, u32[]{:S(2)}) collective-permute-start(bf16[144,768]{1,0:T(8,128)(2,1)} %get-tuple-element.124), channel_id=1, source_target_pairs={{1,4},{9,5},{2,2},{10,3},{3,0},{11,1},{5,12},{13,13},{6,10},{14,11... | collective-permute-start | bytes 663560 | tf_op jit(solution)/shard_map/ppermute | solution.py:294
  37.1 16.7 %collective-permute-start.8 = (bf16[144,768]{1,0:T(8,128)(2,1)}, bf16[144,768]{1,0:T(8,128)(2,1)}, u32[]{:S(2)}, u32[]{:S(2)}) collective-permute-start(bf16[144,768]{1,0:T(8,128)(2,1)} %get-tuple-element.125), channel_id=1, source_target_pairs={{0,4},{8,5},{1,2},{9,3},{2,0},{10,1},{4,12},{12,13},{5,10},{13,11}... | collective-permute-start | bytes 663560 | tf_op jit(solution)/shard_map/ppermute | solution.py:294
  42.5 11.5 %collective-permute-start.7 = (bf16[144,768]{1,0:T(8,128)(2,1)}, bf16[144,768]{1,0:T(8,128)(2,1)}, u32[]{:S(2)}, u32[]{:S(2)}) collective-permute-start(bf16[144,768]{1,0:T(8,128)(2,1)} %get-tuple-element.123), channel_id=1, source_target_pairs={{0,2},{8,3},{1,0},{9,1},{3,4},{11,5},{4,10},{12,11},{5,8},{13,9},{... | collective-permute-start | bytes 663560 | tf_op jit(solution)/shard_map/ppermute | solution.py:294
  120.3 50.7 %collective-permute-start.13 = (bf16[144,768]{1,0:T(8,128)(2,1)}, bf16[144,768]{1,0:T(8,128)(2,1)S(1)}, u32[]{:S(2)}, u32[]{:S(2)}) collective-permute-start(bf16[144,768]{1,0:T(8,128)(2,1)} %get-tuple-element.110), channel_id=1, source_target_pairs={{4,1},{5,9},{2,2},{3,10},{0,3},{1,11},{12,5},{13,13},{10,6},{11,14... | collective-permute-start | bytes 663560 | tf_op jit(solution)/shard_map/ppermute | solution.py:302
  124.3 47.2 %collective-permute-start.12 = (bf16[144,768]{1,0:T(8,128)(2,1)}, bf16[144,768]{1,0:T(8,128)(2,1)}, u32[]{:S(2)}, u32[]{:S(2)}) collective-permute-start(bf16[144,768]{1,0:T(8,128)(2,1)} %get-tuple-element.111), channel_id=1, source_target_pairs={{4,0},{5,8},{2,1},{3,9},{0,2},{1,10},{12,4},{13,12},{10,5},{11,13}... | collective-permute-start | bytes 663560 | tf_op jit(solution)/shard_map/ppermute | solution.py:302
  126.3 47.3 %collective-permute-start.11 = (bf16[144,768]{1,0:T(8,128)(2,1)}, bf16[144,768]{1,0:T(8,128)(2,1)}, u32[]{:S(2)}, u32[]{:S(2)}) collective-permute-start(bf16[144,768]{1,0:T(8,128)(2,1)} %get-tuple-element.112), channel_id=1, source_target_pairs={{2,0},{3,8},{0,1},{1,9},{4,3},{5,11},{10,4},{11,12},{8,5},{9,13},{... | collective-permute-start | bytes 663560 | tf_op jit(solution)/shard_map/ppermute | solution.py:302
  141.6 42.2 %collective-permute-start.106 = (bf16[1024,768]{1,0:T(8,128)(2,1)}, bf16[1024,768]{1,0:T(8,128)(2,1)}, u32[]{:S(2)}, u32[]{:S(2)}) collective-permute-start(bf16[1024,768]{1,0:T(8,128)(2,1)} %dynamic-slice_bitcast_fusion.1), channel_id=1, source_target_pairs={{0,8},{8,0},{1,9},{9,1},{2,10},{10,2},{3,11},{11,3},{4,12},{12,4},... | collective-permute-start | bytes 4718600 | tf_op jit(solution)/shard_map/ppermute | solution.py:364
  143.9 43.7 %collective-permute-start.86 = (bf16[1024,768]{1,0:T(8,128)(2,1)}, bf16[1024,768]{1,0:T(8,128)(2,1)}, u32[]{:S(2)}, u32[]{:S(2)}) collective-permute-start(bf16[1024,768]{1,0:T(8,128)(2,1)} %dynamic-slice_bitcast_fusion.2), channel_id=1, source_target_pairs={{0,8},{8,0},{1,9},{9,1},{2,10},{10,2},{3,11},{11,3},{4,12},{12,4},... | collective-permute-start | bytes 4718600 | tf_op jit(solution)/shard_map/ppermute | solution.py:364
  171.0 21.2 %collective-permute-start.126 = (bf16[1024,768]{1,0:T(8,128)(2,1)S(1)}, bf16[1024,768]{1,0:T(8,128)(2,1)S(1)}, u32[]{:S(2)}, u32[]{:S(2)}) collective-permute-start(bf16[1024,768]{1,0:T(8,128)(2,1)S(1)} %dynamic-slice_bitcast_fusion), channel_id=1, source_target_pairs={{0,8},{8,0},{1,9},{9,1},{2,10},{10,2},{3,11},{11,3},{4,12},{12,4},... | collective-permute-start | bytes 4718600 | tf_op jit(solution)/shard_map/ppermute | solution.py:364
  173.6 22.4 %collective-permute-start.14 = (bf16[576,1536]{1,0:T(8,128)(2,1)S(1)}, bf16[576,1536]{1,0:T(8,128)(2,1)S(1)}, u32[]{:S(2)}, u32[]{:S(2)}) collective-permute-start(bf16[576,1536]{1,0:T(8,128)(2,1)S(1)} %pad_maximum_fusion.6), channel_id=1, source_target_pairs={{0,8},{8,0},{1,9},{9,1},{2,10},{10,2},{3,11},{11,3},{4,12},{12,4},... | collective-permute-start | bytes 5308424 | tf_op jit(solution)/shard_map/ppermute | solution.py:427
  186.0 33.9 %collective-permute-start.109 = (bf16[256,768]{1,0:T(8,128)(2,1)S(1)}, bf16[256,768]{1,0:T(8,128)(2,1)S(1)}, u32[]{:S(2)}, u32[]{:S(2)}) collective-permute-start(bf16[256,768]{1,0:T(8,128)(2,1)S(1)} %get-tuple-element.88), channel_id=1, source_target_pairs={{0,4},{8,12},{2,6},{10,14},{4,0},{12,8},{6,2},{14,10},{32,36},{40,... | collective-permute-start | bytes 1179656 | tf_op jit(solution)/shard_map/ppermute | solution.py:317
  187.5 34.7 %collective-permute-start.108 = (bf16[256,768]{1,0:T(8,128)(2,1)S(1)}, bf16[256,768]{1,0:T(8,128)(2,1)S(1)}, u32[]{:S(2)}, u32[]{:S(2)}) collective-permute-start(bf16[256,768]{1,0:T(8,128)(2,1)S(1)} %get-tuple-element.89), channel_id=1, source_target_pairs={{0,6},{8,10},{2,0},{10,12},{4,2},{12,14},{6,4},{14,8},{32,38},{40,... | collective-permute-start | bytes 1179656 | tf_op jit(solution)/shard_map/ppermute | solution.py:317
  187.6 34.8 %collective-permute-start.107 = (bf16[256,768]{1,0:T(8,128)(2,1)S(1)}, bf16[256,768]{1,0:T(8,128)(2,1)S(1)}, u32[]{:S(2)}, u32[]{:S(2)}) collective-permute-start(bf16[256,768]{1,0:T(8,128)(2,1)S(1)} %get-tuple-element.87), channel_id=1, source_target_pairs={{0,2},{8,14},{2,4},{10,8},{4,6},{12,10},{6,0},{14,12},{32,34},{40,... | collective-permute-start | bytes 1179656 | tf_op jit(solution)/shard_map/ppermute | solution.py:317
  192.2 30.6 %collective-permute-start.89 = (bf16[256,768]{1,0:T(8,128)(2,1)S(1)}, bf16[256,768]{1,0:T(8,128)(2,1)S(1)}, u32[]{:S(2)}, u32[]{:S(2)}) collective-permute-start(bf16[256,768]{1,0:T(8,128)(2,1)S(1)} %get-tuple-element.85), channel_id=1, source_target_pairs={{0,64},{8,72},{2,66},{10,74},{4,68},{12,76},{6,70},{14,78},{32,96}... | collective-permute-start | bytes 1179656 | tf_op jit(solution)/shard_map/ppermute | solution.py:317
  219.9 16.4 %collective-permute-start.87 = (bf16[256,768]{1,0:T(8,128)(2,1)S(1)}, bf16[256,768]{1,0:T(8,128)(2,1)S(1)}, u32[]{:S(2)}, u32[]{:S(2)}) collective-permute-start(bf16[256,768]{1,0:T(8,128)(2,1)S(1)} %get-tuple-element.84), channel_id=1, source_target_pairs={{0,32},{8,104},{2,34},{10,106},{4,36},{12,108},{6,38},{14,110},{32... | collective-permute-start | bytes 1179656 | tf_op jit(solution)/shard_map/ppermute | solution.py:317
  222.2 16.2 %collective-permute-start.129 = (bf16[256,768]{1,0:T(8,128)(2,1)S(1)}, bf16[256,768]{1,0:T(8,128)(2,1)S(1)}, u32[]{:S(2)}, u32[]{:S(2)}) collective-permute-start(bf16[256,768]{1,0:T(8,128)(2,1)S(1)} %get-tuple-element.82), channel_id=1, source_target_pairs={{0,1},{8,9},{2,3},{10,11},{4,5},{12,13},{6,7},{14,15},{32,33},{40,... | collective-permute-start | bytes 1179656 | tf_op jit(solution)/shard_map/ppermute | solution.py:317
  222.3 23.7 %collective-permute-start.128 = (bf16[256,768]{1,0:T(8,128)(2,1)S(1)}, bf16[256,768]{1,0:T(8,128)(2,1)S(1)}, u32[]{:S(2)}, u32[]{:S(2)}) collective-permute-start(bf16[256,768]{1,0:T(8,128)(2,1)S(1)} %get-tuple-element.83), channel_id=1, source_target_pairs={{0,17},{8,24},{2,19},{10,26},{4,21},{12,28},{6,23},{14,30},{32,49}... | collective-permute-start | bytes 1179656 | tf_op jit(solution)/shard_map/ppermute | solution.py:317
  222.8 25.2 %collective-permute-start.127 = (bf16[256,768]{1,0:T(8,128)(2,1)S(1)}, bf16[256,768]{1,0:T(8,128)(2,1)S(1)}, u32[]{:S(2)}, u32[]{:S(2)}) collective-permute-start(bf16[256,768]{1,0:T(8,128)(2,1)S(1)} %get-tuple-element.81), channel_id=1, source_target_pairs={{0,16},{8,25},{2,18},{10,27},{4,20},{12,29},{6,22},{14,31},{32,48}... | collective-permute-start | bytes 1179656 | tf_op jit(solution)/shard_map/ppermute | solution.py:317
  227.7 20.7 %collective-permute-start.18 = (bf16[144,768]{1,0:T(8,128)(2,1)S(1)}, bf16[144,768]{1,0:T(8,128)(2,1)S(1)}, u32[]{:S(2)}, u32[]{:S(2)}) collective-permute-start(bf16[144,768]{1,0:T(8,128)(2,1)S(1)} %get-tuple-element.103), channel_id=1, source_target_pairs={{4,1},{5,9},{2,2},{3,10},{0,3},{1,11},{12,5},{13,13},{10,6},{11,14... | collective-permute-start | bytes 663560 | tf_op jit(solution)/shard_map/ppermute | solution.py:302
  236.3 12.6 %collective-permute-start.17 = (bf16[144,768]{1,0:T(8,128)(2,1)S(1)}, bf16[144,768]{1,0:T(8,128)(2,1)S(1)}, u32[]{:S(2)}, u32[]{:S(2)}) collective-permute-start(bf16[144,768]{1,0:T(8,128)(2,1)S(1)} %get-tuple-element.104), channel_id=1, source_target_pairs={{4,0},{5,8},{2,1},{3,9},{0,2},{1,10},{12,4},{13,12},{10,5},{11,13}... | collective-permute-start | bytes 663560 | tf_op jit(solution)/shard_map/ppermute | solution.py:302
  238.5 14.2 %collective-permute-start.16 = (bf16[144,768]{1,0:T(8,128)(2,1)S(1)}, bf16[144,768]{1,0:T(8,128)(2,1)S(1)}, u32[]{:S(2)}, u32[]{:S(2)}) collective-permute-start(bf16[144,768]{1,0:T(8,128)(2,1)S(1)} %get-tuple-element.105), channel_id=1, source_target_pairs={{2,0},{3,8},{0,1},{1,9},{4,3},{5,11},{10,4},{11,12},{8,5},{9,13},{... | collective-permute-start | bytes 663560 | tf_op jit(solution)/shard_map/ppermute | solution.py:302
  248.0 87.7 %collective-permute-start.66 = (bf16[512,768]{1,0:T(8,128)(2,1)S(1)}, bf16[512,768]{1,0:T(8,128)(2,1)S(1)}, u32[]{:S(2)}, u32[]{:S(2)}) collective-permute-start(bf16[512,768]{1,0:T(8,128)(2,1)S(1)} %dynamic-slice_bitcast_fusion.3), channel_id=1, source_target_pairs={{0,8},{8,0},{1,9},{9,1},{2,10},{10,2},{3,11},{11,3},{4,12},{12,4},... | collective-permute-start | bytes 2359304 | tf_op jit(solution)/shard_map/ppermute | solution.py:364
  248.4 90.2 %collective-permute-start.46 = (bf16[512,768]{1,0:T(8,128)(2,1)S(1)}, bf16[512,768]{1,0:T(8,128)(2,1)S(1)}, u32[]{:S(2)}, u32[]{:S(2)}) collective-permute-start(bf16[512,768]{1,0:T(8,128)(2,1)S(1)} %dynamic-slice_bitcast_fusion.4), channel_id=1, source_target_pairs={{0,8},{8,0},{1,9},{9,1},{2,10},{10,2},{3,11},{11,3},{4,12},{12,4},... | collective-permute-start | bytes 2359304 | tf_op jit(solution)/shard_map/ppermute | solution.py:364
  252.7 10.8 %collective-permute-start.112 = (bf16[64,768]{1,0:T(8,128)(2,1)S(1)}, bf16[64,768]{1,0:T(8,128)(2,1)S(1)}, u32[]{:S(2)}, u32[]{:S(2)}) collective-permute-start(bf16[64,768]{1,0:T(8,128)(2,1)S(1)} %get-tuple-element.137), channel_id=1, source_target_pairs={{0,1},{8,9},{2,3},{10,11},{4,5},{12,13},{6,7},{14,15},{32,33},{40,... | collective-permute-start | bytes 294920 | tf_op jit(solution)/shard_map/ppermute | solution.py:317
  289.5 51.0 %collective-permute-start.26 = (bf16[512,768]{1,0:T(8,128)(2,1)S(1)}, bf16[512,768]{1,0:T(8,128)(2,1)S(1)}, u32[]{:S(2)}, u32[]{:S(2)}) collective-permute-start(bf16[512,768]{1,0:T(8,128)(2,1)S(1)} %dynamic-slice_bitcast_fusion.5), channel_id=1, source_target_pairs={{0,8},{8,0},{1,9},{9,1},{2,10},{10,2},{3,11},{11,3},{4,12},{12,4},... | collective-permute-start | bytes 2359304 | tf_op jit(solution)/shard_map/ppermute | solution.py:364
  332.1 12.0 %collective-permute-start.122 = (bf16[256,768]{1,0:T(8,128)(2,1)S(1)}, bf16[256,768]{1,0:T(8,128)(2,1)S(1)}, u32[]{:S(2)}, u32[]{:S(2)}) collective-permute-start(bf16[256,768]{1,0:T(8,128)(2,1)S(1)} %bitcast.504), channel_id=1, source_target_pairs={{0,2},{8,14},{2,4},{10,8},{4,6},{12,10},{6,0},{14,12},{32,34},{40,... | collective-permute-start | bytes 1179656 | tf_op jit(solution)/shard_map/ppermute | solution.py:317
  335.7 13.0 %collective-permute-start.124 = (bf16[256,768]{1,0:T(8,128)(2,1)S(1)}, bf16[256,768]{1,0:T(8,128)(2,1)S(1)}, u32[]{:S(2)}, u32[]{:S(2)}) collective-permute-start(bf16[256,768]{1,0:T(8,128)(2,1)S(1)} %bitcast.507), channel_id=1, source_target_pairs={{0,4},{8,12},{2,6},{10,14},{4,0},{12,8},{6,2},{14,10},{32,36},{40,... | collective-permute-start | bytes 1179656 | tf_op jit(solution)/shard_map/ppermute | solution.py:317
  340.5 13.2 %collective-permute-start.103 = (bf16[256,768]{1,0:T(8,128)(2,1)S(1)}, bf16[256,768]{1,0:T(8,128)(2,1)S(1)}, u32[]{:S(2)}, u32[]{:S(2)}) collective-permute-start(bf16[256,768]{1,0:T(8,128)(2,1)S(1)} %bitcast.510), channel_id=1, source_target_pairs={{0,96},{8,40},{2,98},{10,42},{4,100},{12,44},{6,102},{14,46},{32,0... | collective-permute-start | bytes 1179656 | tf_op jit(solution)/shard_map/ppermute | solution.py:317
  344.1 15.7 %collective-permute-start.142 = (bf16[256,768]{1,0:T(8,128)(2,1)S(1)}, bf16[256,768]{1,0:T(8,128)(2,1)S(1)}, u32[]{:S(2)}, u32[]{:S(2)}) collective-permute-start(bf16[256,768]{1,0:T(8,128)(2,1)S(1)} %bitcast.513), channel_id=1, source_target_pairs={{0,16},{8,25},{2,18},{10,27},{4,20},{12,29},{6,22},{14,31},{32,48}... | collective-permute-start | bytes 1179656 | tf_op jit(solution)/shard_map/ppermute | solution.py:317
  348.8 14.5 %collective-permute-start.143 = (bf16[256,768]{1,0:T(8,128)(2,1)S(1)}, bf16[256,768]{1,0:T(8,128)(2,1)S(1)}, u32[]{:S(2)}, u32[]{:S(2)}) collective-permute-start(bf16[256,768]{1,0:T(8,128)(2,1)S(1)} %bitcast.514), channel_id=1, source_target_pairs={{0,17},{8,24},{2,19},{10,26},{4,21},{12,28},{6,23},{14,30},{32,49}... | collective-permute-start | bytes 1179656 | tf_op jit(solution)/shard_map/ppermute | solution.py:317
  348.9 135.3 %collective-permute-start.144 = (bf16[256,768]{1,0:T(8,128)(2,1)S(1)}, bf16[256,768]{1,0:T(8,128)(2,1)S(1)}, u32[]{:S(2)}, u32[]{:S(2)}) collective-permute-start(bf16[256,768]{1,0:T(8,128)(2,1)S(1)} %bitcast.515), channel_id=1, source_target_pairs={{0,1},{8,9},{2,3},{10,11},{4,5},{12,13},{6,7},{14,15},{32,33},{40,... | collective-permute-start | bytes 1179656 | tf_op jit(solution)/shard_map/ppermute | solution.py:317
  353.9 12.1 %collective-permute-start.68 = (bf16[128,768]{1,0:T(8,128)(2,1)S(1)}, bf16[128,768]{1,0:T(8,128)(2,1)S(1)}, u32[]{:S(2)}, u32[]{:S(2)}) collective-permute-start(bf16[128,768]{1,0:T(8,128)(2,1)S(1)} %get-tuple-element.121), channel_id=1, source_target_pairs={{0,17},{8,24},{2,19},{10,26},{4,21},{12,28},{6,23},{14,30},{32,49}... | collective-permute-start | bytes 589832 | tf_op jit(solution)/shard_map/ppermute | solution.py:317
  363.4 16.0 %collective-permute-start.48 = (bf16[128,768]{1,0:T(8,128)(2,1)S(1)}, bf16[128,768]{1,0:T(8,128)(2,1)S(1)}, u32[]{:S(2)}, u32[]{:S(2)}) collective-permute-start(bf16[128,768]{1,0:T(8,128)(2,1)S(1)} %get-tuple-element.118), channel_id=1, source_target_pairs={{0,6},{8,10},{2,0},{10,12},{4,2},{12,14},{6,4},{14,8},{32,38},{40,... | collective-permute-start | bytes 589832 | tf_op jit(solution)/shard_map/ppermute | solution.py:317
  366.0 13.4 %collective-permute-start.47 = (bf16[128,768]{1,0:T(8,128)(2,1)S(1)}, bf16[128,768]{1,0:T(8,128)(2,1)S(1)}, u32[]{:S(2)}, u32[]{:S(2)}) collective-permute-start(bf16[128,768]{1,0:T(8,128)(2,1)S(1)} %get-tuple-element.116), channel_id=1, source_target_pairs={{0,2},{8,14},{2,4},{10,8},{4,6},{12,10},{6,0},{14,12},{32,34},{40,... | collective-permute-start | bytes 589832 | tf_op jit(solution)/shard_map/ppermute | solution.py:317
  367.2 22.3 %collective-permute-start.29 = (bf16[128,768]{1,0:T(8,128)(2,1)S(1)}, bf16[128,768]{1,0:T(8,128)(2,1)S(1)}, u32[]{:S(2)}, u32[]{:S(2)}) collective-permute-start(bf16[128,768]{1,0:T(8,128)(2,1)S(1)} %get-tuple-element.114), channel_id=1, source_target_pairs={{0,64},{8,72},{2,66},{10,74},{4,68},{12,76},{6,70},{14,78},{32,96}... | collective-permute-start | bytes 589832 | tf_op jit(solution)/shard_map/ppermute | solution.py:317
  371.6 19.8 %collective-permute-start.28 = (bf16[128,768]{1,0:T(8,128)(2,1)S(1)}, bf16[128,768]{1,0:T(8,128)(2,1)S(1)}, u32[]{:S(2)}, u32[]{:S(2)}) collective-permute-start(bf16[128,768]{1,0:T(8,128)(2,1)S(1)} %get-tuple-element.115), channel_id=1, source_target_pairs={{0,96},{8,40},{2,98},{10,42},{4,100},{12,44},{6,102},{14,46},{32,0... | collective-permute-start | bytes 589832 | tf_op jit(solution)/shard_map/ppermute | solution.py:317
  379.4 13.1 %collective-permute-start.27 = (bf16[128,768]{1,0:T(8,128)(2,1)S(1)}, bf16[128,768]{1,0:T(8,128)(2,1)S(1)}, u32[]{:S(2)}, u32[]{:S(2)}) collective-permute-start(bf16[128,768]{1,0:T(8,128)(2,1)S(1)} %get-tuple-element.113), channel_id=1, source_target_pairs={{0,32},{8,104},{2,34},{10,106},{4,36},{12,108},{6,38},{14,110},{32... | collective-permute-start | bytes 589832 | tf_op jit(solution)/shard_map/ppermute | solution.py:317
  379.4 129.1 %collective-permute-start.125 = (bf16[1024,768]{1,0:T(8,128)(2,1)S(1)}, bf16[1024,768]{1,0:T(8,128)(2,1)S(1)}, u32[]{:S(2)}, u32[]{:S(2)}) collective-permute-start(bf16[1024,768]{1,0:T(8,128)(2,1)S(1)} %bitcast.492), channel_id=1, source_target_pairs={{0,8},{8,0},{1,9},{9,1},{2,10},{10,2},{3,11},{11,3},{4,12},{12,4},... | collective-permute-start | bytes 4718600 | tf_op jit(solution)/shard_map/ppermute | solution.py:371
  456.9 22.6 %collective-permute-start.43 = (bf16[128,768]{1,0:T(8,128)(2,1)S(1)}, bf16[128,768]{1,0:T(8,128)(2,1)S(1)}, u32[]{:S(2)}, u32[]{:S(2)}) collective-permute-start(bf16[128,768]{1,0:T(8,128)(2,1)S(1)} %bitcast.538), channel_id=1, source_target_pairs={{0,96},{8,40},{2,98},{10,42},{4,100},{12,44},{6,102},{14,46},{32,0... | collective-permute-start | bytes 589832 | tf_op jit(solution)/shard_map/ppermute | solution.py:317
  462.3 17.3 %collective-permute-start.44 = (bf16[128,768]{1,0:T(8,128)(2,1)S(1)}, bf16[128,768]{1,0:T(8,128)(2,1)S(1)}, u32[]{:S(2)}, u32[]{:S(2)}) collective-permute-start(bf16[128,768]{1,0:T(8,128)(2,1)S(1)} %bitcast.539), channel_id=1, source_target_pairs={{0,64},{8,72},{2,66},{10,74},{4,68},{12,76},{6,70},{14,78},{32,96}... | collective-permute-start | bytes 589832 | tf_op jit(solution)/shard_map/ppermute | solution.py:317
  464.6 19.8 %collective-permute-start.85 = (bf16[512,768]{1,0:T(8,128)(2,1)S(1)}, bf16[512,768]{1,0:T(8,128)(2,1)S(1)}, u32[]{:S(2)}, u32[]{:S(2)}) collective-permute-start(bf16[512,768]{1,0:T(8,128)(2,1)S(1)} %bitcast.502), channel_id=1, source_target_pairs={{0,8},{8,0},{1,9},{9,1},{2,10},{10,2},{3,11},{11,3},{4,12},{12,4},... | collective-permute-start | bytes 2359304 | tf_op jit(solution)/shard_map/ppermute | solution.py:371
  479.7 29.2 %collective-permute-start.105 = (bf16[1024,768]{1,0:T(8,128)(2,1)S(1)}, bf16[1024,768]{1,0:T(8,128)(2,1)S(1)}, u32[]{:S(2)}, u32[]{:S(2)}) collective-permute-start(bf16[1024,768]{1,0:T(8,128)(2,1)S(1)} %bitcast.493), channel_id=1, source_target_pairs={{0,8},{8,0},{1,9},{9,1},{2,10},{10,2},{3,11},{11,3},{4,12},{12,4},... | collective-permute-start | bytes 4718600 | tf_op jit(solution)/shard_map/ppermute | solution.py:371
  484.4 47.5 %collective-permute-start.145 = (bf16[1024,768]{1,0:T(8,128)(2,1)S(1)}, bf16[1024,768]{1,0:T(8,128)(2,1)S(1)}, u32[]{:S(2)}, u32[]{:S(2)}) collective-permute-start(bf16[1024,768]{1,0:T(8,128)(2,1)S(1)} %bitcast.494), channel_id=1, source_target_pairs={{0,8},{8,0},{1,9},{9,1},{2,10},{10,2},{3,11},{11,3},{4,12},{12,4},... | collective-permute-start | bytes 4718600 | tf_op jit(solution)/shard_map/ppermute | solution.py:371
  (129 other events, 706.7 us)

commit v2 on v1

--- a/solution.py
+++ b/solution.py
@@ -227,13 +227,16 @@
         gatt_ref[...] = mm_nt(gb, ow_ref[...]).astype(bf16)
 
 
-def feed_forward(attended, x, g, out_w, vecs, up_b, up_w, down_w):
+def feed_forward(attended, both, out_w, vecs, up_b, up_w, down_w):
     whole = lambda shape: pl.BlockSpec(shape, lambda f: (0,) * len(shape))
     return pl.pallas_call(
         feed_forward_kernel,
         grid=(NF,),
         in_specs=[
-            whole((ROWS, D)), whole((ROWS, D)), whole((ROWS, D)), whole((D, D)), whole((8, D)),
+            whole((ROWS, D)),
+            pl.BlockSpec((ROWS, D), lambda f: (0, 0)),
+            pl.BlockSpec((ROWS, D), lambda f: (0, 1)),
+            whole((D, D)), whole((8, D)),
             pl.BlockSpec((1, 1, FCHUNK), lambda f: (f, 0, 0)),
             pl.BlockSpec((D, FCHUNK), lambda f: (0, f)),
             pl.BlockSpec((FCHUNK, D), lambda f: (f, 0)),
@@ -266,7 +269,79 @@
         compiler_params=pltpu.CompilerParams(vmem_limit_bytes=VMEM_LIMIT),
         cost_estimate=pl.CostEstimate(flops=12 * ROWS * D * FF, bytes_accessed=30_000_000, transcendentals=ROWS * FF),
         name="feed_forward",
-    )(attended, x, g, out_w, vecs, up_b, up_w, down_w)
+    )(attended, both, both, out_w, vecs, up_b, up_w, down_w)
+
+
+def place_kernel(core_ref, mine_ref, other_ref, *out_refs):
+    step = pl.program_id(0)
+    lower = pl.num_programs(0) // 2
+    from_mine = (step >= lower).astype(jnp.int32) == core_ref[0]
+    for index, out_ref in enumerate(out_refs):
+        count = pl.num_programs(0)
+        first = 0 if index == 0 else count - 1
+        last = count - 1 if index == len(out_refs) - 1 else count - 2
+
+        @pl.when((step >= first) & (step <= last) & from_mine)
+        def _():
+            out_ref[...] = mine_ref[...].astype(f32)
+
+        @pl.when((step >= first) & (step <= last) & jnp.logical_not(from_mine))
+        def _():
+            out_ref[...] = other_ref[...].astype(f32)
+
+
+def place_rows(core, mine, other):
+    half = mine.shape[0] // D
+    source = pl.BlockSpec((D, D), lambda i, core_ref: (i % half, 0))
+    return pl.pallas_call(
+        place_kernel,
+        grid_spec=pltpu.PrefetchScalarGridSpec(
+            num_scalar_prefetch=1,
+            grid=(2 * half,),
+            in_specs=[source, source],
+            out_specs=pl.BlockSpec((D, D), lambda i, core_ref: (i, 0)),
+        ),
+        out_shape=jax.ShapeDtypeStruct((2 * mine.shape[0], D), f32),
+        compiler_params=pltpu.CompilerParams(vmem_limit_bytes=VMEM_LIMIT),
+        name="place_rows",
+    )(core, mine, other)
+
+
+def place_columns(core, mine, other):
+    half = mine.shape[0] // D
+    source = pl.BlockSpec((D, D), lambda i, core_ref: (i % half, 0))
+    return pl.pallas_call(
+        place_kernel,
+        grid_spec=pltpu.PrefetchScalarGridSpec(
+            num_scalar_prefetch=1,
+            grid=(2 * half,),
+            in_specs=[source, source],
+            out_specs=pl.BlockSpec((D, D), lambda i, core_ref: (0, i)),
+        ),
+        out_shape=jax.ShapeDtypeStruct((D, 2 * mine.shape[0]), f32),
+        compiler_params=pltpu.CompilerParams(vmem_limit_bytes=VMEM_LIMIT),
+        name="place_columns",
+    )(core, mine, other)
+
+
+def place_qkvo(core, mine, other):
+    half = mine.shape[0] // D
+    source = pl.BlockSpec((D, D), lambda i, core_ref: (i % half, 0))
+    return pl.pallas_call(
+        place_kernel,
+        grid_spec=pltpu.PrefetchScalarGridSpec(
+            num_scalar_prefetch=1,
+            grid=(4,),
+            in_specs=[source, source],
+            out_specs=[
+                pl.BlockSpec((D, D), lambda i, core_ref: (0, jnp.minimum(i, 2))),
+                pl.BlockSpec((D, D), lambda i, core_ref: (0, 0)),
+            ],
+        ),
+        out_shape=[jax.ShapeDtypeStruct((D, 3 * D), f32), jax.ShapeDtypeStruct((D, D), f32)],
+        compiler_params=pltpu.CompilerParams(vmem_limit_bytes=VMEM_LIMIT),
+        name="place_qkvo",
+    )(core, mine, other)
 
 
 def linear(y, xl, c, z, xh):
@@ -275,15 +350,12 @@
 
 def scene_pairs(slot):
     pairs = []
-    for y in range(4):
-        for xl in range(2):
-            for z in range(4):
-                for xh in range(2):
-                    block = 2 * z + xh
-                    scene = (slot - block) % 4
-                    if scene < 3:
-                        for c in range(2):
-                            pairs.append((linear(y, xl, c, z, xh), linear(y, xl, block // 4, scene, c)))
+    for y, xl, z, xh in itertools.product(range(4), range(2), range(4), range(2)):
+        block = 2 * z + xh
+        scene = (slot - block) % 4
+        if scene < 3:
+            for c in range(2):
+                pairs.append((linear(y, xl, c, z, xh), linear(y, xl, block // 4, scene, c)))
     return pairs
 
 
@@ -292,7 +364,7 @@
     for slot in range(SLOTS):
         scene = jnp.minimum((slot - block) % 4, 2)
         pieces.append(lax.ppermute(lax.dynamic_index_in_dim(values, scene, 0, keepdims=False), AXES, scene_pairs(slot)))
-    return jnp.concatenate(pieces, axis=0)
+    return pieces
 
 
 def from_scene(values, block):
@@ -304,9 +376,9 @@
     return jnp.stack([lax.dynamic_index_in_dim(pieces, (m + block) % 4, 0, keepdims=False) for m in range(3)])
 
 
-ORDERS = (("y", "z", "x"), ("z", "x", "y"), ("x", "y", "z"))
 SWAP = ((0, 1), (1, 0))
-STEPS = ((1, -1), (-1, 1), (2, 2))
+CHIPS = ("y", "xh", "xl", "z")
+MASKS = ((1, 3), (3, 1))
 
 
 def exchange(value, move):
@@ -317,10 +389,10 @@
     return lax.ppermute(value, AXES, pairs)
 
 
-def ring_exchange(value, axis, signs):
+def ring_exchange(value, axis, step):
     def move(x, y, z, c):
         at = {"x": x, "y": y, "z": z}
-        at[axis] = (at[axis] + signs[c]) % 4
+        at[axis] = at[axis] ^ MASKS[c][step]
         return at["x"], at["y"], at["z"], c
 
     return exchange(value, move)
@@ -332,46 +404,49 @@
     return lax.axis_index(axis)
 
 
-def reduce_stage(buffer, axis, core):
+def take(blocks, dim, index):
+    return lax.dynamic_slice_in_dim(blocks, index, 1, dim)
+
+
+def halve_stage(blocks, dim, axis, core):
     place = ring_place(axis)
-    blocks = buffer.reshape(4, buffer.shape[0] // 4, buffer.shape[1])
-    total = lax.dynamic_index_in_dim(blocks, place, 0, keepdims=False).astype(f32)
-    for signs in STEPS:
-        step = jnp.where(core == 0, signs[0], signs[1])
-        block = lax.dynamic_index_in_dim(blocks, (place + step) % 4, 0, keepdims=False)
-        total = total + ring_exchange(block, axis, signs).astype(f32)
-    return total.astype(bf16)
-
-
-def gather_stage(block, axis, core):
-    place = ring_place(axis)
-    whole = jnp.zeros((4,) + block.shape, block.dtype)
-    whole = lax.dynamic_update_index_in_dim(whole, block, place, 0)
-    for signs in STEPS:
-        step = jnp.where(core == 0, signs[0], signs[1])
-        other = ring_exchange(block, axis, signs)
-        whole = lax.dynamic_update_index_in_dim(whole, other, (place - step) % 4, 0)
-    return whole.reshape(4 * block.shape[0], block.shape[1])
-
-
-def sum_everywhere(grads, core):
-    rows = grads.shape[0] // 3
-    halves = grads.reshape(3, 2, rows // 2, grads.shape[1])
-    parts = []
-    for part in range(3):
-        mine = lax.dynamic_index_in_dim(halves[part], core, 0, keepdims=False)
-        other = lax.dynamic_index_in_dim(halves[part], 1 - core, 0, keepdims=False)
-        parts.append((mine.astype(f32) + lax.ppermute(other, "c", SWAP).astype(f32)).astype(bf16))
-    for stage in range(3):
-        parts = [reduce_stage(parts[part], ORDERS[part][stage], core) for part in range(3)]
-    for stage in (2, 1, 0):
-        parts = [gather_stage(parts[part], ORDERS[part][stage], core) for part in range(3)]
-    result = []
-    for mine in parts:
-        other = lax.ppermute(mine, "c", SWAP)
-        result.append(jnp.where(core == 0, mine, other))
-        result.append(jnp.where(core == 0, other, mine))
-    return jnp.concatenate(result, axis=0)
+    first = jnp.where(core == 0, 1, 3)
+    second = 4 - first
+    away = jnp.concatenate([take(blocks, dim, place ^ first), take(blocks, dim, place ^ 2)], axis=dim)
+    keep = jnp.concatenate([take(blocks, dim, place), take(blocks, dim, place ^ second)], axis=dim)
+    keep = keep + ring_exchange(away, axis, 0)
+    return lax.slice_in_dim(keep, 0, 1, axis=dim) + ring_exchange(lax.slice_in_dim(keep, 1, 2, axis=dim), axis, 1)
+
+
+def chip_gather(chunk):
+    return lax.all_gather(chunk, CHIPS, axis=0, tiled=True)
+
+
+def core_half(values, core):
+    half = values.shape[0] // 2
+    return lax.dynamic_slice_in_dim(values, core * half, half, 0)
+
+
+def sum_ff(d_up, d_down, core):
+    away = jnp.concatenate([core_half(d_up, 1 - core), core_half(d_down, 1 - core)], axis=0)
+    other = lax.ppermute(away, "c", SWAP)
+    half = FF // 2
+    up = (core_half(d_up, core) + other[:half]).reshape(4, 4, 4, half // 64, D)
+    down = (core_half(d_down, core) + other[half:]).reshape(4, 4, 4, half // 64, D)
+    dims = {"y": 0, "x": 1, "z": 2}
+    for axis_up, axis_down in zip("yxz", "zxy"):
+        up = halve_stage(up, dims[axis_up], axis_up, core)
+        down = halve_stage(down, dims[axis_down], axis_down, core)
+    up = chip_gather(up.reshape(half // 64, D))
+    down = chip_gather(down.reshape(half // 64, D))
+    return up, down
+
+
+def sum_qkvo(grads, core):
+    rows = grads.shape[0] // 2
+    mine = core_half(grads, core) + lax.ppermute(core_half(grads, 1 - core), "c", SWAP)
+    terms = lax.all_to_all(mine.reshape(64, rows // 64, D), CHIPS, 0, 0)
+    return chip_gather(jnp.sum(terms.astype(f32), axis=0).astype(bf16))
 
 
 def sum_small(values):
@@ -391,11 +466,11 @@
     block = 2 * z + xh
     scene = jnp.minimum(z, 2)
 
-    x = to_scene(tokens, block)
-    views = view_counts.astype(f32)
-    views_other = lax.ppermute(views, "c", SWAP)
-    views = lax.dynamic_index_in_dim(jnp.where(core == xh, views, views_other), scene, 0, keepdims=False)
-    g = to_scene(cotangent, block)
+    views = jnp.broadcast_to(view_counts.astype(bf16)[:, None, None], (3, BLK, LANES))
+    pieces = to_scene(jnp.concatenate([tokens, cotangent, views], axis=2), block)
+    both = jnp.concatenate([piece[:, : 2 * D] for piece in pieces], axis=0)
+    views = pieces[0][0, 2 * D].astype(f32)
+    x = both[:, :D]
 
     slot = jnp.arange(ROWS, dtype=jnp.int32) // BLK
     inside = jnp.arange(ROWS, dtype=jnp.int32) % BLK
@@ -416,10 +491,10 @@
 
     vecs = jnp.concatenate([jnp.stack([out_bias, ln2_gain, ln2_shift, down_bias]), jnp.zeros((4, D), f32)])
     output, grad_hidden, grad_att, d_out, d_up, d_down, vec_grads, up_b_grad = feed_forward(
-        attended, x, g, out_weight, vecs, up_bias.reshape(NF, 1, FCHUNK), up_weight, down_weight
+        attended, both, out_weight, vecs, up_bias.reshape(NF, 1, FCHUNK), up_weight, down_weight
     )
     output = from_scene(output, block)
-    ff_sum = sum_everywhere(jnp.concatenate([d_up, d_down], axis=0), core)
+    up_sum, down_sum = sum_ff(d_up, d_down, core)
 
     grad_q, grad_k, grad_v, grad_k_other, grad_v_other = attention_backward(
         joined, sibling, weights, heads_out, linv, grad_att
@@ -449,14 +524,14 @@
     ).reshape(-1, LANES)
     small = sum_small(small).reshape(-1)
     vector = lambda i: small[i * D : (i + 1) * D]
-    qkvo_sum = sum_everywhere(jnp.concatenate(d_qkv + [d_out], axis=0), core)
-
-    blocks = lambda a, n: jnp.concatenate([a[i * D : (i + 1) * D] for i in range(n)], axis=1).astype(f32)
+    qkvo_sum = sum_qkvo(jnp.concatenate(d_qkv + [d_out], axis=0), core)
+    up_other, down_other, qkvo_other = (lax.ppermute(v, "c", SWAP) for v in (up_sum, down_sum, qkvo_sum))
+    which = core.astype(jnp.int32).reshape(1)
+    d_qkv, d_out = place_qkvo(which, qkvo_sum, qkvo_other)
     return (
-        output, input_grad,
-        vector(4), vector(5), blocks(qkvo_sum[: 3 * D], 3), vector(6), vector(7),
-        qkvo_sum[3 * D :].astype(f32), vector(0), vector(1), vector(2),
-        blocks(ff_sum[:FF], 4), small[8 * D :], ff_sum[FF:].astype(f32), vector(3),
+        output, input_grad, vector(4), vector(5), d_qkv, vector(6), vector(7), d_out,
+        vector(0), vector(1), vector(2), place_columns(which, up_sum, up_other), small[8 * D :],
+        place_rows(which, down_sum, down_other), vector(3),
     )
 
 

time: 542 us -> 495 us (0.913)
  starting transfers between devices: 252 us -> 91.6 us
  waiting for transfers between devices: 97 us -> 195 us
  other arithmetic: 72.3 us -> 40 us
  Pallas kernels: 78.7 us -> 102 us
  between operations: 3.88 us -> 15.7 us
  local copies, waits for them, and re-layouts: 23 us -> 32.1 us
    ppermute x114 -> x18, starting transfers between devices: 153 us -> 13.7 us  [exchange(): return lax.ppermute(value, AXES, pairs)]
    convert_element_type x20 -> x1, other arithmetic: 53.4 us -> 0.81 us  [body(): view_counts.astype(bf16)[:, None, None]]
    all_gather x0 -> x3, waiting for transfers between devices: none -> 43.7 us  [chip_gather(): return lax.all_gather(chunk, CHIPS, axis=0, tiled=True)]
    ppermute x13 -> x5, starting transfers between devices: 36.2 us -> 3.16 us  [the longest x3 2.46 us: body(): lax.ppermute(v, 'c', SWAP)]
    all_to_all x0 -> x1, waiting for transfers between devices: none -> 30.1 us  [sum_qkvo(): terms = lax.all_to_all(mine.reshape(64, rows // 64, D), CHIPS, 0, 0)]
    ppermute x114 -> x18, waiting for transfers between devices: 68.4 us -> 92.4 us  [exchange(): return lax.ppermute(value, AXES, pairs)]
    pallas_call x0 -> x3, Pallas kernels: none -> 23.5 us  [the longest x1 8.3 us: place_qkvo(): pl.pallas_call(place_kernel, grid_spec=pltpu.PrefetchScalarGridSpec(num_s...]
    ppermute x1, starting transfers between devices: 0.09 us -> 18.3 us  [sum_small(): values = values + lax.ppermute(values, 'c', SWAP)]
  transfers between devices with their start and end apart: 146 -> 42, of which waited for: 61 -> 25; matrix products, arithmetic and copies ran while one was open for 16% -> 12% of each run, Pallas kernels for 4% -> 3%
where the time goes in v2:
time: 495 us; the launch traced here: 489 us
  waiting for transfers between devices  195 us (39%)
  Pallas kernels  102 us (21%)
  starting transfers between devices  91.6 us (19%)
  other arithmetic  40 us (8%)
  local copies, waits for them, and re-layouts  32.1 us (6%)
  between operations  15.7 us (3%)
  matrix products  13 us (3%)
    ppermute x18, waiting for transfers between devices, exchange(): return lax.ppermute(value, AXES, pairs)  92.4 us
    all_gather x3, waiting for transfers between devices, chip_gather(): return lax.all_gather(chunk, CHIPS, axis=0, tiled=True)  43.7 us
    pallas_call x1, Pallas kernels, feed_forward(): pl.pallas_call(feed_forward_kernel, grid=(NF,), in_specs=[whole((ROWS, D)...  30.8 us
    all_to_all x1, waiting for transfers between devices, sum_qkvo(): terms = lax.all_to_all(mine.reshape(64, rows // 64, D), CHIPS, 0, 0)  30.1 us
    ppermute x8, starting transfers between devices, from_scene(): pieces.append(lax.ppermute(values[slot * BLK:(slot + 1) * BLK], AXES, back))  29.7 us
    pallas_call x1, Pallas kernels, attention_forward(): pl.pallas_call(attention_forward_kernel, grid=(PAIRS,), in_specs=[col(0),...  25 us
    pallas_call x1, Pallas kernels, attention_backward(): pl.pallas_call(attention_backward_kernel, grid=(PAIRS,), in_specs=[col(0)...  22.8 us
    ppermute x1, starting transfers between devices, sum_small(): values = values + lax.ppermute(values, 'c', SWAP)  18.3 us
  transfers between devices with their start and end apart: 42, of which 25 were waited for; matrix products, arithmetic and copies ran while one was open for 12% of the time, Pallas kernels for 3%

profile of v2, /device:TPU:1, one launch (start us, length us, event | category | flops | bytes accessed | tf_op | source)
XLA Modules:
  0.0 489.4 jit_solution(6937285165625066896)
XLA Ops:
  11.3 10.0 %collective-permute-start.2 = (bf16[144,1664]{1,0:T(8,128)(2,1)S(1)}, bf16[144,1664]{1,0:T(8,128)(2,1)S(1)}, u32[]{:S(2)}, u32[]{:S(2)}) collective-permute-start(bf16[144,1664]{1,0:T(8,128)(2,1)S(1)} %get-tuple-element.76), channel_id=1, source_target_pairs={{0,4},{8,5},{1,2},{9,3},{2,0},{10,1},{4,12},{12,13},{5,10},{13,11}... | collective-permute-start | bytes 1437704 | tf_op jit(solution)/shard_map/ppermute | solution.py:366
  23.2 2.4 collective-permute-start
  25.7 4.1 collective-permute-done.2
  29.8 6.2 %collective-permute-done.1 = bf16[144,1664]{1,0:T(8,128)(2,1)S(1)} collective-permute-done((bf16[144,1664]{1,0:T(8,128)(2,1)S(1)}, bf16[144,1664]{1,0:T(8,128)(2,1)S(1)}, u32[]{:S(2)}, u32[]{:S(2)}) %collective-permute-start.1) | collective-permute-done | bytes 479264 | tf_op jit(solution)/shard_map/ppermute | solution.py:366
  36.1 4.2 collective-permute-done
  42.0 2.4 add_convert_fusion.q_ref.ko_ref.vo_ref
  46.6 3.0 collective-permute-start.4
  56.8 25.0 %attention_forward.1 = (bf16[12,576,1152]{2,1,0:T(8,128)(2,1)}, f32[576,768]{1,0:T(8,128)}, f32[576,768]{1,0:T(8,128)}, bf16[576,768]{1,0:T(8,128)(2,1)}) custom-call(bf16[576,2304]{1,0:T(8,128)(2,1)} %copy-done.9, bf16[576,2304]{1,0:T(8,128)(2,1)} %copy-done.9, bf16[576,2304]{1,0:T(8,128)(2,1)} %copy-done.9, ...), custom_call_target="tpu_custom_call" | custom-call | flops 8153726976 | bytes 20000000 | tf_op jit(solution)/shard_map/attention_forward/pallas_call | solution.py:87
  81.8 30.8 %feed_forward.1 = (bf16[576,768]{1,0:T(8,128)(2,1)}, f32[576,768]{1,0:T(8,128)}, bf16[576,768]{1,0:T(8,128)(2,1)}, bf16[768,768]{1,0:T(8,128)(2,1)}, bf16[3072,7...) custom-call(bf16[576,768]{1,0:T(8,128)(2,1)} %get-tuple-element.34.att_ref, ...), custom_call_target="tpu_custom_call" | custom-call | flops 16307453952 | bytes 30000000 | tf_op jit(solution)/shard_map/feed_forward/pallas_call | solution.py:232
  112.6 22.8 %attention_backward.1 = (bf16[576,768]{1,0:T(8,128)(2,1)}, f32[576,768]{1,0:T(8,128)}, f32[576,768]{1,0:T(8,128)}, bf16[576,768]{1,0:T(8,128)(2,1)}, bf16[576,768]{1,0:T(8,128)(2,1)}) custom-call(bf16[576,2304]{1,0:T(8,128)(2,1)} %copy-done.9, bf16[576,2304]{1,0:T(8,128)(2,1)} %copy-done.9, bf16[576,2304]{1,0:T(8,128)(2,1)} %copy-done.9, ...), custom_call_target="tpu_custom_call" | custom-call | flops 16307453952 | bytes 25000000 | tf_op jit(solution)/shard_map/attention_backward/pallas_call | solution.py:150
  135.4 2.8 pad_maximum_fusion.3
  152.4 2.5 pad_maximum_fusion.1
  156.8 4.4 dynamic-slice_add_fusion
  161.1 7.6 %all-to-all-start = ((bf16[64,24,768]{2,1,0:T(8,128)(2,1)}), bf16[64,24,768]{2,1,0:T(8,128)(2,1)}, u32[]{:S(2)}, u32[]{:S(2)}) async-start(bf16[64,24,768]{2,1,0:T(8,128)(2,1)} %bitcast.52), calls=%async_computation | async-start | bytes 4718592 | tf_op jit(solution)/shard_map/all_to_all | solution.py:448
  169.2 30.1 %all-to-all-done = bf16[64,24,768]{2,1,0:T(8,128)(2,1)} async-done(((bf16[64,24,768]{2,1,0:T(8,128)(2,1)}), bf16[64,24,768]{2,1,0:T(8,128)(2,1)}, u32[]{:S(2)}, u32[]{:S(2)}) %all-to-all-start) | async-done | bytes 2359328 | tf_op jit(solution)/shard_map/all_to_all | solution.py:448
  199.3 2.6 reduce_sum.92
  202.0 6.3 %slice_add_fusion = (bf16[1536,768]{1,0:T(8,128)(2,1)}, bf16[1536,768]{1,0:T(8,128)(2,1)S(1)}) fusion(bf16[3072,768]{1,0:T(8,128)(2,1)} %collective-permute-done.23, bf16[3072,768]{1,0:T(8,128)(2,1)} %get-tuple-element.52, s32[]{:T(128)S(6)} %select_n.189, bf16[3072,768]{1,0:T(8,128)(2,1)} %get-tuple-element.51), kind=kLoop, calls=%fused_computation.9 | loop fusion | flops 9437184 | bytes 14155780 | tf_op jit(solution)/shard_map/add | solution.py:435
  209.4 16.3 %collective-permute-done.24 = bf16[2,4,4,24,768]{4,3,2,1,0:T(8,128)(2,1)S(1)} collective-permute-done((bf16[2,4,4,24,768]{4,3,2,1,0:T(8,128)(2,1)S(1)}, bf16[2,4,4,24,768]{4,3,2,1,0:T(8,128)(2,1)S(1)}, u32[]{:S(2)}, u32[]{:S(2)}) %collective-permute-start.24) | collective-permute-done | bytes 1179680 | tf_op jit(solution)/shard_map/ppermute | solution.py:389
  227.7 9.9 %collective-permute-done.25 = bf16[1,4,4,24,768]{4,3,2,1,0:T(8,128)(2,1)} collective-permute-done((bf16[1,4,4,24,768]{4,3,2,1,0:T(8,128)(2,1)}, bf16[1,4,4,24,768]{4,3,2,1,0:T(8,128)(2,1)}, u32[]{:S(2)}, u32[]{:S(2)}) %collective-permute-start.25) | collective-permute-done | bytes 589856 | tf_op jit(solution)/shard_map/ppermute | solution.py:389
  239.7 6.7 %collective-permute-done.26 = bf16[1,2,4,24,768]{4,3,2,1,0:T(8,128)(2,1)S(1)} collective-permute-done((bf16[1,2,4,24,768]{4,3,2,1,0:T(8,128)(2,1)S(1)}, bf16[1,2,4,24,768]{4,3,2,1,0:T(8,128)(2,1)S(1)}, u32[]{:S(2)}, u32[]{:S(2)}) %collective-permute-start.26) | collective-permute-done | bytes 294944 | tf_op jit(solution)/shard_map/ppermute | solution.py:389
  247.9 4.3 collective-permute-done.27
  254.8 3.5 collective-permute-done.28
  258.4 3.2 collective-permute-done.29
  266.1 14.8 %collective-permute-done.31 = bf16[4,4,2,24,768]{4,3,2,1,0:T(8,128)(2,1)S(1)} collective-permute-done((bf16[4,4,2,24,768]{4,3,2,1,0:T(8,128)(2,1)S(1)}, bf16[4,4,2,24,768]{4,3,2,1,0:T(8,128)(2,1)S(1)}, u32[]{:S(2)}, u32[]{:S(2)}) %collective-permute-start.31) | collective-permute-done | bytes 1179680 | tf_op jit(solution)/shard_map/ppermute | solution.py:389
  281.2 14.3 %collective-permute-done.32 = bf16[4,4,1,24,768]{4,3,2,1,0:T(8,128)(2,1)S(1)} collective-permute-done((bf16[4,4,1,24,768]{4,3,2,1,0:T(8,128)(2,1)S(1)}, bf16[4,4,1,24,768]{4,3,2,1,0:T(8,128)(2,1)S(1)}, u32[]{:S(2)}, u32[]{:S(2)}) %collective-permute-start.32) | collective-permute-done | bytes 589856 | tf_op jit(solution)/shard_map/ppermute | solution.py:389
  295.8 7.6 %collective-permute-done.33 = bf16[4,2,1,24,768]{4,3,2,1,0:T(8,128)(2,1)S(1)} collective-permute-done((bf16[4,2,1,24,768]{4,3,2,1,0:T(8,128)(2,1)S(1)}, bf16[4,2,1,24,768]{4,3,2,1,0:T(8,128)(2,1)S(1)}, u32[]{:S(2)}, u32[]{:S(2)}) %collective-permute-start.33) | collective-permute-done | bytes 294944 | tf_op jit(solution)/shard_map/ppermute | solution.py:389
  303.6 4.4 collective-permute-done.34
  308.0 2.2 collective-permute-start.35
  310.2 2.3 collective-permute-done.35
  312.6 2.8 collective-permute-done.36
  323.6 6.4 %fusion.19 = (f32[768]{0:T(1024)S(1)}, f32[576]{0:T(1024)}, f32[576]{0:T(1024)}, f32[768]{0:T(1024)S(1)}, f32[576,768]{1,0:T(8,128)}) fusion(f32[576]{0:T(1024)S(1)} %copy-done.27, f32[576]{0:T(1024)S(1)} %broadcast_multiply_fusion.2, bf16[576,1536]{1,0:T(8,128)(2,1)} %copy-done.2, f32[768]{0:T(1024)} %param.18, bf16[768,2304]{1,0:T(8,128)(2,1)S(1)} %copy-done, ...), kind=kOutput, calls=%fused_computation.27 | convolution fusion | flops 2050815488 | bytes 8865792 | tf_op jit(solution)/shard_map/dot_general | solution.py:511
  330.1 18.3 %collective-permute-start.14 = (f32[72,128]{1,0:T(8,128)S(1)}, f32[72,128]{1,0:T(8,128)S(1)}, u32[]{:S(2)}, u32[]{:S(2)}) collective-permute-start(f32[72,128]{1,0:T(8,128)S(1)} %bitcast.66), channel_id=1, source_target_pairs={{0,8},{8,0},{1,9},{9,1},{2,10},{10,2},{3,11},{11,3},{4,12},{12,4},... | collective-permute-start | bytes 110600 | tf_op jit(solution)/shard_map/ppermute | solution.py:453
  350.2 2.7 collective-permute-start.8
  353.6 2.5 collective-permute-start.16
  356.9 43.7 %all-gather.10.cloned.1.call-done = bf16[1,1,1,1536,768]{4,3,2,1,0:T(8,128)(2,1)} async-done(((bf16[1,1,1,24,768]{4,3,2,1,0:T(8,128)(2,1)}), bf16[1,1,1,1536,768]{4,3,2,1,0:T(8,128)(2,1)}) %all-gather.10.cloned.1.call-update) | async-done | bytes 2359312 | tf_op jit(solution)/shard_map/all_gather | solution.py:422
  403.7 3.5 collective-permute-start.7
  407.2 6.1 %collective-permute-start.6 = (bf16[144,768]{1,0:T(8,128)(2,1)}, bf16[144,768]{1,0:T(8,128)(2,1)S(1)}, u32[]{:S(2)}, u32[]{:S(2)}) collective-permute-start(bf16[144,768]{1,0:T(8,128)(2,1)} %get-tuple-element.91), channel_id=1, source_target_pairs={{2,0},{3,8},{0,1},{1,9},{4,3},{5,11},{10,4},{11,12},{8,5},{9,13},{... | collective-permute-start | bytes 663560 | tf_op jit(solution)/shard_map/ppermute | solution.py:374
  413.4 2.9 fusion.18
  418.3 2.1 collective-permute-start.18
  421.3 4.8 collective-permute-done.5
  426.8 3.0 collective-permute-start.13
  434.3 7.1 %collective-permute-start.11 = (bf16[144,768]{1,0:T(8,128)(2,1)S(1)}, bf16[144,768]{1,0:T(8,128)(2,1)S(1)}, u32[]{:S(2)}, u32[]{:S(2)}) collective-permute-start(bf16[144,768]{1,0:T(8,128)(2,1)S(1)} %copy-done.18), channel_id=1, source_target_pairs={{2,0},{3,8},{0,1},{1,9},{4,3},{5,11},{10,4},{11,12},{8,5},{9,13},{... | collective-permute-start | bytes 663560 | tf_op jit(solution)/shard_map/ppermute | solution.py:374
  441.9 3.5 collective-permute-start.10
  446.7 5.6 %collective-permute-done.10 = bf16[144,768]{1,0:T(8,128)(2,1)S(1)} collective-permute-done((bf16[144,768]{1,0:T(8,128)(2,1)S(1)}, bf16[144,768]{1,0:T(8,128)(2,1)S(1)}, u32[]{:S(2)}, u32[]{:S(2)}) %collective-permute-start.10) | collective-permute-done | bytes 221216 | tf_op jit(solution)/shard_map/ppermute | solution.py:374
  455.7 2.3 collective-permute-done.20
  459.2 8.3 %place_qkvo.1 = (f32[768,2304]{1,0:T(8,128)}, f32[768,768]{1,0:T(8,128)}) custom-call(s32[1]{0:T(128)} %bitcast.18.core_ref, bf16[1536,768]{1,0:T(8,128)(2,1)} %all-gather.6.cloned.1.call-done.mine_ref, bf16[1536,768]{1,0:T(8,128)(2,1)} %collective-permute-done.22.other_ref), custom_call_target="tpu_custom_call" | custom-call | tf_op jit(solution)/shard_map/place_qkvo/pallas_call | solution.py:330
  467.5 7.6 %place_columns.1 = f32[768,3072]{1,0:T(8,128)} custom-call(s32[1]{0:T(128)} %bitcast.18.core_ref, bf16[1536,768]{1,0:T(8,128)(2,1)} %bitcast.58, bf16[1536,768]{1,0:T(8,128)(2,1)} %collective-permute-done.30.other_ref), custom_call_target="tpu_custom_call" | custom-call | tf_op jit(solution)/shard_map/place_columns/pallas_call | solution.py:313
  475.1 7.6 %place_rows.1 = f32[3072,768]{1,0:T(8,128)} custom-call(s32[1]{0:T(128)} %bitcast.18.core_ref, bf16[1536,768]{1,0:T(8,128)(2,1)} %bitcast.60, bf16[1536,768]{1,0:T(8,128)(2,1)} %collective-permute-done.37.other_ref), custom_call_target="tpu_custom_call" | custom-call | tf_op jit(solution)/shard_map/place_rows/pallas_call | solution.py:296
  (232 shorter events, 76.3 us)
Async XLA Ops:
  7.2 34.7 %copy-start = (bf16[768,2304]{1,0:T(8,128)(2,1)S(1)}, bf16[768,2304]{1,0:T(8,128)(2,1)}, u32[]{:S(2)}) copy-start(bf16[768,2304]{1,0:T(8,128)(2,1)} %param.20) | copy-start | bytes 10616836
  9.7 15.9 %copy-start.35 = (f32[768]{0:T(1024)S(1)}, f32[768]{0:T(1024)}, u32[]{:S(2)}) copy-start(f32[768]{0:T(1024)} %param.22) | copy-start | bytes 9220
  9.7 15.9 %copy-start.36 = (f32[768]{0:T(1024)S(1)}, f32[768]{0:T(1024)}, u32[]{:S(2)}) copy-start(f32[768]{0:T(1024)} %param.21) | copy-start | bytes 9220
  10.0 15.7 %collective-permute-start.3 = (bf16[144,1664]{1,0:T(8,128)(2,1)S(1)}, bf16[144,1664]{1,0:T(8,128)(2,1)S(1)}, u32[]{:S(2)}, u32[]{:S(2)}) collective-permute-start(bf16[144,1664]{1,0:T(8,128)(2,1)S(1)} %get-tuple-element.75), channel_id=1, source_target_pairs={{1,4},{9,5},{2,2},{10,3},{3,0},{11,1},{5,12},{13,13},{6,10},{14,11... | collective-permute-start | bytes 1437704 | tf_op jit(solution)/shard_map/ppermute | solution.py:366
  11.3 18.5 %collective-permute-start.2 = (bf16[144,1664]{1,0:T(8,128)(2,1)S(1)}, bf16[144,1664]{1,0:T(8,128)(2,1)S(1)}, u32[]{:S(2)}, u32[]{:S(2)}) collective-permute-start(bf16[144,1664]{1,0:T(8,128)(2,1)S(1)} %get-tuple-element.76), channel_id=1, source_target_pairs={{0,4},{8,5},{1,2},{9,3},{2,0},{10,1},{4,12},{12,13},{5,10},{13,11}... | collective-permute-start | bytes 1437704 | tf_op jit(solution)/shard_map/ppermute | solution.py:366
  21.2 14.8 %collective-permute-start.1 = (bf16[144,1664]{1,0:T(8,128)(2,1)S(1)}, bf16[144,1664]{1,0:T(8,128)(2,1)S(1)}, u32[]{:S(2)}, u32[]{:S(2)}) collective-permute-start(bf16[144,1664]{1,0:T(8,128)(2,1)S(1)} %get-tuple-element.77), channel_id=1, source_target_pairs={{0,2},{8,3},{1,0},{9,1},{3,4},{11,5},{4,10},{12,11},{5,8},{13,9},{... | collective-permute-start | bytes 1437704 | tf_op jit(solution)/shard_map/ppermute | solution.py:366
  23.2 17.2 %collective-permute-start = (bf16[144,1664]{1,0:T(8,128)(2,1)S(1)}, bf16[144,1664]{1,0:T(8,128)(2,1)S(1)}, u32[]{:S(2)}, u32[]{:S(2)}) collective-permute-start(bf16[144,1664]{1,0:T(8,128)(2,1)S(1)} %get-tuple-element.74), channel_id=1, source_target_pairs={{0,0},{8,1},{2,4},{10,5},{3,2},{11,3},{4,8},{12,9},{6,12},{14,13},... | collective-permute-start | bytes 1437704 | tf_op jit(solution)/shard_map/ppermute | solution.py:366
  46.6 9.3 %collective-permute-start.4 = (bf16[576,1536]{1,0:T(8,128)(2,1)}, bf16[576,1536]{1,0:T(8,128)(2,1)}, u32[]{:S(2)}, u32[]{:S(2)}) collective-permute-start(bf16[576,1536]{1,0:T(8,128)(2,1)} %slice.217), channel_id=1, source_target_pairs={{0,8},{8,0},{1,9},{9,1},{2,10},{10,2},{3,11},{11,3},{4,12},{12,4},... | collective-permute-start | bytes 5308424 | tf_op jit(solution)/shard_map/ppermute | solution.py:489
  138.2 4.0 collective-permute-start.9
  151.8 5.0 %collective-permute-start.21 = (bf16[1536,768]{1,0:T(8,128)(2,1)}, bf16[1536,768]{1,0:T(8,128)(2,1)}, u32[]{:S(2)}, u32[]{:S(2)}) collective-permute-start(bf16[1536,768]{1,0:T(8,128)(2,1)} %constant_dynamic-slice_fusion.26), channel_id=1, source_target_pairs={{0,8},{8,0},{1,9},{9,1},{2,10},{10,2},{3,11},{11,3},{4,12},{12,4},... | collective-permute-start | bytes 7077896 | tf_op jit(solution)/shard_map/ppermute | solution.py:447
  154.9 47.1 %collective-permute-start.23 = (bf16[3072,768]{1,0:T(8,128)(2,1)}, bf16[3072,768]{1,0:T(8,128)(2,1)}, u32[]{:S(2)}, u32[]{:S(2)}) collective-permute-start(bf16[3072,768]{1,0:T(8,128)(2,1)} %pad_maximum_fusion.1), channel_id=1, source_target_pairs={{0,8},{8,0},{1,9},{9,1},{2,10},{10,2},{3,11},{11,3},{4,12},{12,4},... | collective-permute-start | bytes 14155784 | tf_op jit(solution)/shard_map/ppermute | solution.py:432
  161.1 38.2 %all-to-all-start = ((bf16[64,24,768]{2,1,0:T(8,128)(2,1)}), bf16[64,24,768]{2,1,0:T(8,128)(2,1)}, u32[]{:S(2)}, u32[]{:S(2)}) async-start(bf16[64,24,768]{2,1,0:T(8,128)(2,1)} %bitcast.52), calls=%async_computation | async-start | bytes 4718592 | tf_op jit(solution)/shard_map/all_to_all | solution.py:448
  168.7 187.3 %all-gather.6.cloned.1.call-start = ((), (), s32[]{:S(2)}) async-start(), calls=%async_computation.1 | async-start | bytes 2396160 | tf_op jit(solution)/shard_map/all_gather | solution.py:422
  202.0 155.0 %all-gather.8.cloned.1.call-start = ((), (), s32[]{:S(2)}) async-start(), calls=%async_computation.2 | async-start | bytes 2396160 | tf_op jit(solution)/shard_map/all_gather | solution.py:422
  208.6 17.1 %collective-permute-start.24 = (bf16[2,4,4,24,768]{4,3,2,1,0:T(8,128)(2,1)S(1)}, bf16[2,4,4,24,768]{4,3,2,1,0:T(8,128)(2,1)S(1)}, u32[]{:S(2)}, u32[]{:S(2)}) collective-permute-start(bf16[2,4,4,24,768]{4,3,2,1,0:T(8,128)(2,1)S(1)} %pad_maximum_fusion.5), channel_id=1, source_target_pairs={{0,32},{8,104},{2,34},{10,106},{4,36},{12,108},{6,38},{14,110},{32... | collective-permute-start | bytes 3538952 | tf_op jit(solution)/shard_map/ppermute | solution.py:389
  227.7 9.9 %collective-permute-start.25 = (bf16[1,4,4,24,768]{4,3,2,1,0:T(8,128)(2,1)}, bf16[1,4,4,24,768]{4,3,2,1,0:T(8,128)(2,1)}, u32[]{:S(2)}, u32[]{:S(2)}) collective-permute-start(bf16[1,4,4,24,768]{4,3,2,1,0:T(8,128)(2,1)} %slice.234), channel_id=1, source_target_pairs={{0,96},{8,40},{2,98},{10,42},{4,100},{12,44},{6,102},{14,46},{32,6... | collective-permute-start | bytes 1769480 | tf_op jit(solution)/shard_map/ppermute | solution.py:389
  239.1 7.4 %collective-permute-start.26 = (bf16[1,2,4,24,768]{4,3,2,1,0:T(8,128)(2,1)S(1)}, bf16[1,2,4,24,768]{4,3,2,1,0:T(8,128)(2,1)S(1)}, u32[]{:S(2)}, u32[]{:S(2)}) collective-permute-start(bf16[1,2,4,24,768]{4,3,2,1,0:T(8,128)(2,1)S(1)} %pad_maximum_fusion.11), channel_id=1, source_target_pairs={{0,16},{8,25},{2,18},{10,27},{4,20},{12,29},{6,22},{14,31},{32,48}... | collective-permute-start | bytes 884744 | tf_op jit(solution)/shard_map/ppermute | solution.py:389
  247.9 4.3 collective-permute-start.27
  253.2 5.0 %collective-permute-start.28 = (bf16[1,1,2,24,768]{4,3,2,1,0:T(8,128)(2,1)S(1)}, bf16[1,1,2,24,768]{4,3,2,1,0:T(8,128)(2,1)S(1)}, u32[]{:S(2)}, u32[]{:S(2)}) collective-permute-start(bf16[1,1,2,24,768]{4,3,2,1,0:T(8,128)(2,1)S(1)} %pad_maximum_fusion.13), channel_id=1, source_target_pairs={{0,2},{8,14},{2,0},{10,12},{4,6},{12,10},{6,4},{14,8},{32,34},{40,... | collective-permute-start | bytes 221192 | tf_op jit(solution)/shard_map/ppermute | solution.py:389
  258.3 3.3 collective-permute-start.29
  262.2 138.4 %all-gather.10.cloned.1.call-start = ((), (), s32[]{:S(2)}) async-start(), calls=%async_computation.3 | async-start | bytes 2396160 | tf_op jit(solution)/shard_map/all_gather | solution.py:422
  264.2 16.7 %collective-permute-start.31 = (bf16[4,4,2,24,768]{4,3,2,1,0:T(8,128)(2,1)S(1)}, bf16[4,4,2,24,768]{4,3,2,1,0:T(8,128)(2,1)S(1)}, u32[]{:S(2)}, u32[]{:S(2)}) collective-permute-start(bf16[4,4,2,24,768]{4,3,2,1,0:T(8,128)(2,1)S(1)} %pad_maximum_fusion.6), channel_id=1, source_target_pairs={{0,2},{8,14},{2,0},{10,12},{4,6},{12,10},{6,4},{14,8},{32,34},{40,... | collective-permute-start | bytes 3538952 | tf_op jit(solution)/shard_map/ppermute | solution.py:389
  281.1 14.4 %collective-permute-start.32 = (bf16[4,4,1,24,768]{4,3,2,1,0:T(8,128)(2,1)S(1)}, bf16[4,4,1,24,768]{4,3,2,1,0:T(8,128)(2,1)S(1)}, u32[]{:S(2)}, u32[]{:S(2)}) collective-permute-start(bf16[4,4,1,24,768]{4,3,2,1,0:T(8,128)(2,1)S(1)} %slice.242), channel_id=1, source_target_pairs={{0,6},{8,10},{2,4},{10,8},{4,2},{12,14},{6,0},{14,12},{32,38},{40,... | collective-permute-start | bytes 1769480 | tf_op jit(solution)/shard_map/ppermute | solution.py:389
  295.7 7.7 %collective-permute-start.33 = (bf16[4,2,1,24,768]{4,3,2,1,0:T(8,128)(2,1)S(1)}, bf16[4,2,1,24,768]{4,3,2,1,0:T(8,128)(2,1)S(1)}, u32[]{:S(2)}, u32[]{:S(2)}) collective-permute-start(bf16[4,2,1,24,768]{4,3,2,1,0:T(8,128)(2,1)S(1)} %pad_maximum_fusion.12), channel_id=1, source_target_pairs={{0,16},{8,25},{2,18},{10,27},{4,20},{12,29},{6,22},{14,31},{32,48}... | collective-permute-start | bytes 884744 | tf_op jit(solution)/shard_map/ppermute | solution.py:389
  303.5 4.5 collective-permute-start.34
  308.0 4.5 collective-permute-start.35
  312.5 2.9 collective-permute-start.36
  323.6 25.7 %copy-start.10 = (bf16[576,768]{1,0:T(8,128)(2,1)S(1)}, bf16[576,768]{1,0:T(8,128)(2,1)}, u32[]{:S(2)}) copy-start(bf16[576,768]{1,0:T(8,128)(2,1)} %get-tuple-element.35) | copy-start | bytes 2654212
  330.0 72.2 %copy-start.34 = (f32[576]{0:T(1024)S(1)}, f32[576]{0:T(1024)}, u32[]{:S(2)}) copy-start(f32[576]{0:T(1024)} %get-tuple-element.54) | copy-start | bytes 6916
  330.1 19.2 %collective-permute-start.14 = (f32[72,128]{1,0:T(8,128)S(1)}, f32[72,128]{1,0:T(8,128)S(1)}, u32[]{:S(2)}, u32[]{:S(2)}) collective-permute-start(f32[72,128]{1,0:T(8,128)S(1)} %bitcast.66), channel_id=1, source_target_pairs={{0,8},{8,0},{1,9},{9,1},{2,10},{10,2},{3,11},{11,3},{4,12},{12,4},... | collective-permute-start | bytes 110600 | tf_op jit(solution)/shard_map/ppermute | solution.py:453
  349.3 3.7 collective-permute-start.15
  350.2 53.5 %collective-permute-start.8 = (bf16[144,768]{1,0:T(8,128)(2,1)}, bf16[144,768]{1,0:T(8,128)(2,1)}, u32[]{:S(2)}, u32[]{:S(2)}) collective-permute-start(bf16[144,768]{1,0:T(8,128)(2,1)} %get-tuple-element.89), channel_id=1, source_target_pairs={{4,1},{5,9},{2,2},{3,10},{0,3},{1,11},{12,5},{13,13},{10,6},{11,14... | collective-permute-start | bytes 663560 | tf_op jit(solution)/shard_map/ppermute | solution.py:374
  353.6 48.6 %collective-permute-start.16 = (f32[72,128]{1,0:T(8,128)}, f32[72,128]{1,0:T(8,128)}, u32[]{:S(2)}, u32[]{:S(2)}) collective-permute-start(f32[72,128]{1,0:T(8,128)} %fusion.48), channel_id=1, source_target_pairs={{0,4},{8,12},{2,6},{10,14},{4,0},{12,8},{6,2},{14,10},{32,36},{40,... | collective-permute-start | bytes 110600 | tf_op jit(solution)/shard_map/ppermute | solution.py:389
  356.0 103.2 %collective-permute-start.22 = (bf16[1536,768]{1,0:T(8,128)(2,1)}, bf16[1536,768]{1,0:T(8,128)(2,1)}, u32[]{:S(2)}, u32[]{:S(2)}) collective-permute-start(bf16[1536,768]{1,0:T(8,128)(2,1)} %all-gather.6.cloned.1.call-done.mine_ref), channel_id=1, source_target_pairs={{0,8},{8,0},{1,9},{9,1},{2,10},{10,2},{3,11},{11,3},{4,12},{12,4},... | collective-permute-start | bytes 7077896 | tf_op jit(solution)/shard_map/ppermute | solution.py:528
  356.9 110.6 %collective-permute-start.30 = (bf16[1536,768]{1,0:T(8,128)(2,1)}, bf16[1536,768]{1,0:T(8,128)(2,1)}, u32[]{:S(2)}, u32[]{:S(2)}) collective-permute-start(bf16[1536,768]{1,0:T(8,128)(2,1)} %bitcast.57), channel_id=1, source_target_pairs={{0,8},{8,0},{1,9},{9,1},{2,10},{10,2},{3,11},{11,3},{4,12},{12,4},... | collective-permute-start | bytes 7077896 | tf_op jit(solution)/shard_map/ppermute | solution.py:528
  400.6 74.5 %collective-permute-start.37 = (bf16[1536,768]{1,0:T(8,128)(2,1)}, bf16[1536,768]{1,0:T(8,128)(2,1)}, u32[]{:S(2)}, u32[]{:S(2)}) collective-permute-start(bf16[1536,768]{1,0:T(8,128)(2,1)} %bitcast.59), channel_id=1, source_target_pairs={{0,8},{8,0},{1,9},{9,1},{2,10},{10,2},{3,11},{11,3},{4,12},{12,4},... | collective-permute-start | bytes 7077896 | tf_op jit(solution)/shard_map/ppermute | solution.py:528
  403.0 4.2 collective-permute-start.17
  403.7 12.6 %collective-permute-start.7 = (bf16[144,768]{1,0:T(8,128)(2,1)}, bf16[144,768]{1,0:T(8,128)(2,1)S(1)}, u32[]{:S(2)}, u32[]{:S(2)}) collective-permute-start(bf16[144,768]{1,0:T(8,128)(2,1)} %get-tuple-element.90), channel_id=1, source_target_pairs={{4,0},{5,8},{2,1},{3,9},{0,2},{1,10},{12,4},{13,12},{10,5},{11,13}... | collective-permute-start | bytes 663560 | tf_op jit(solution)/shard_map/ppermute | solution.py:374
  407.2 11.0 %collective-permute-start.6 = (bf16[144,768]{1,0:T(8,128)(2,1)}, bf16[144,768]{1,0:T(8,128)(2,1)S(1)}, u32[]{:S(2)}, u32[]{:S(2)}) collective-permute-start(bf16[144,768]{1,0:T(8,128)(2,1)} %get-tuple-element.91), channel_id=1, source_target_pairs={{2,0},{3,8},{0,1},{1,9},{4,3},{5,11},{10,4},{11,12},{8,5},{9,13},{... | collective-permute-start | bytes 663560 | tf_op jit(solution)/shard_map/ppermute | solution.py:374
  416.3 13.5 %copy-start.21 = (f32[72,128]{1,0:T(8,128)}, f32[72,128]{1,0:T(8,128)S(1)}, u32[]{:S(2)}) copy-start(f32[72,128]{1,0:T(8,128)S(1)} %add.318) | copy-start | bytes 110596
  416.3 9.8 %collective-permute-start.5 = (bf16[144,768]{1,0:T(8,128)(2,1)S(1)}, bf16[144,768]{1,0:T(8,128)(2,1)S(1)}, u32[]{:S(2)}, u32[]{:S(2)}) collective-permute-start(bf16[144,768]{1,0:T(8,128)(2,1)S(1)} %copy-done.20), channel_id=1, source_target_pairs={{0,0},{1,8},{4,2},{5,10},{2,3},{3,11},{8,4},{9,12},{12,6},{13,14},... | collective-permute-start | bytes 663560 | tf_op jit(solution)/shard_map/ppermute | solution.py:374
  418.3 11.5 %collective-permute-start.18 = (f32[72,128]{1,0:T(8,128)S(1)}, f32[72,128]{1,0:T(8,128)S(1)}, u32[]{:S(2)}, u32[]{:S(2)}) collective-permute-start(f32[72,128]{1,0:T(8,128)S(1)} %add.318), channel_id=1, source_target_pairs={{0,64},{8,72},{2,66},{10,74},{4,68},{12,76},{6,70},{14,78},{32,96}... | collective-permute-start | bytes 110600 | tf_op jit(solution)/shard_map/ppermute | solution.py:389
  426.8 7.5 %collective-permute-start.13 = (bf16[144,768]{1,0:T(8,128)(2,1)}, bf16[144,768]{1,0:T(8,128)(2,1)}, u32[]{:S(2)}, u32[]{:S(2)}) collective-permute-start(bf16[144,768]{1,0:T(8,128)(2,1)} %get-tuple-element.82), channel_id=1, source_target_pairs={{4,1},{5,9},{2,2},{3,10},{0,3},{1,11},{12,5},{13,13},{10,6},{11,14... | collective-permute-start | bytes 663560 | tf_op jit(solution)/shard_map/ppermute | solution.py:374
  430.4 11.5 %collective-permute-start.12 = (bf16[144,768]{1,0:T(8,128)(2,1)}, bf16[144,768]{1,0:T(8,128)(2,1)}, u32[]{:S(2)}, u32[]{:S(2)}) collective-permute-start(bf16[144,768]{1,0:T(8,128)(2,1)} %get-tuple-element.83), channel_id=1, source_target_pairs={{4,0},{5,8},{2,1},{3,9},{0,2},{1,10},{12,4},{13,12},{10,5},{11,13}... | collective-permute-start | bytes 663560 | tf_op jit(solution)/shard_map/ppermute | solution.py:374
  434.3 12.1 %collective-permute-start.11 = (bf16[144,768]{1,0:T(8,128)(2,1)S(1)}, bf16[144,768]{1,0:T(8,128)(2,1)S(1)}, u32[]{:S(2)}, u32[]{:S(2)}) collective-permute-start(bf16[144,768]{1,0:T(8,128)(2,1)S(1)} %copy-done.18), channel_id=1, source_target_pairs={{2,0},{3,8},{0,1},{1,9},{4,3},{5,11},{10,4},{11,12},{8,5},{9,13},{... | collective-permute-start | bytes 663560 | tf_op jit(solution)/shard_map/ppermute | solution.py:374
  441.9 10.4 %collective-permute-start.10 = (bf16[144,768]{1,0:T(8,128)(2,1)S(1)}, bf16[144,768]{1,0:T(8,128)(2,1)S(1)}, u32[]{:S(2)}, u32[]{:S(2)}) collective-permute-start(bf16[144,768]{1,0:T(8,128)(2,1)S(1)} %copy-done.16), channel_id=1, source_target_pairs={{0,0},{1,8},{4,2},{5,10},{2,3},{3,11},{8,4},{9,12},{12,6},{13,14},... | collective-permute-start | bytes 663560 | tf_op jit(solution)/shard_map/ppermute | solution.py:374
  446.4 7.1 %collective-permute-start.19 = (f32[72,128]{1,0:T(8,128)S(1)}, f32[72,128]{1,0:T(8,128)S(1)}, u32[]{:S(2)}, u32[]{:S(2)}) collective-permute-start(f32[72,128]{1,0:T(8,128)S(1)} %add.319), channel_id=1, source_target_pairs={{0,16},{8,24},{2,18},{10,26},{4,20},{12,28},{6,22},{14,30},{32,48}... | collective-permute-start | bytes 110600 | tf_op jit(solution)/shard_map/ppermute | solution.py:389
  453.5 4.4 collective-permute-start.20
  (35 other events, 129.1 us)
Sparse Core Ops, SparseCore 0:
  202.1 64.1 all-gather.5
  269.1 63.6 all-gather.7
  335.6 64.9 all-gather.9

commit v3 on v1

v3 whole, which is shorter than its diff:
```python
import functools
import itertools
import math

import jax
import jax.numpy as jnp
from jax import lax
from jax.experimental import pallas as pl
from jax.experimental.pallas import tpu as pltpu
from jax.sharding import Mesh
from jax.sharding import PartitionSpec as P

HEADS = 12
HEAD_DIM = 64
VIEW_TOK = 128
VIEWS_MAX = 8
D = 768
FF = 3072
BLK = 144
SLOTS = 4
ROWS = BLK * SLOTS
KEYS = 2 * ROWS
PAIRS = HEADS // 2
LANES = 128
FCHUNK = 768
QUARTER = D // 4
NF = FF // FCHUNK

bf16 = jnp.bfloat16
f32 = jnp.float32
epsilon = 1e-05
masked_score = -1e30
GELU_C = math.sqrt(2.0 / math.pi)
GELU_A = 0.044715

AXES = ("y", "xl", "c", "z", "xh")
VMEM_LIMIT = 60 * 1024 * 1024


def mm(a, b):
    return lax.dot_general(a, b, (((1,), (0,)), ((), ())), preferred_element_type=f32)


def mm_nt(a, b):
    return lax.dot_general(a, b, (((1,), (1,)), ((), ())), preferred_element_type=f32)


def mm_tn(a, b):
    return lax.dot_general(a, b, (((0,), (0,)), ((), ())), preferred_element_type=f32)


def lane_row(at, first, last):
    lane = lax.broadcasted_iota(jnp.int32, (1, LANES), 1)
    return jnp.where((lane >= first) & (lane < last), 1.0, 0.0).astype(at)


def attention_forward_kernel(q_ref, ko_ref, vo_ref, ks_ref, vs_ref, mask_ref, p_ref, o_ref, linv_ref, att_ref):
    half = [lane_row(bf16, 0, 64), lane_row(bf16, 64, 128)]
    unit = [lane_row(bf16, 64, 65), lane_row(bf16, 0, 1)]
    q = q_ref[...]
    k = jnp.concatenate([ko_ref[...], ks_ref[...]], axis=0)
    v = jnp.concatenate([vo_ref[...], vs_ref[...]], axis=0)
    mask = mask_ref[...]
    lane = lax.broadcasted_iota(jnp.int32, (BLK, LANES), 1)
    q_now = [q * half[h] + unit[h] for h in range(2)]
    k_now = [k * half[h] + mask * unit[h] for h in range(2)]
    v_now = [v * half[h] + unit[h] for h in range(2)]
    for s in range(SLOTS):
        rows = slice(s * BLK, (s + 1) * BLK)
        outs, invs = [], []
        for h in range(2):
            scores = mm_nt(q_now[h][rows], k_now[h])
            top = jnp.max(scores, axis=1, keepdims=True)
            weights = jnp.exp((scores - top) * 0.125).astype(bf16)
            p_ref[h, rows, :] = weights
            out = mm(weights, v_now[h])
            total = out[:, 64:65] if h == 0 else out[:, 0:1]
            inv = 1.0 / total
            outs.append(out * inv)
            invs.append(jnp.broadcast_to(inv, (BLK, LANES)))
        out = jnp.where(lane < 64, outs[0], outs[1])
        o_ref[rows, :] = out
        att_ref[rows, :] = out.astype(bf16)
        linv_ref[rows, :] = jnp.where(lane < 64, invs[0], invs[1])


def attention_forward(joined, sibling, mask):
    col = lambda first: pl.BlockSpec((ROWS, LANES), lambda i, f=first: (0, f + i))
    return pl.pallas_call(
        attention_forward_kernel,
        grid=(PAIRS,),
        in_specs=[
            col(0), col(PAIRS), col(2 * PAIRS), col(0), col(PAIRS),
            pl.BlockSpec((KEYS, LANES), lambda i: (0, 0)),
        ],
        out_specs=[
            pl.BlockSpec((2, ROWS, KEYS), lambda i: (i, 0, 0)),
            col(0), col(0), col(0),
        ],
        out_shape=[
            jax.ShapeDtypeStruct((HEADS, ROWS, KEYS), bf16),
            jax.ShapeDtypeStruct((ROWS, D), f32),
            jax.ShapeDtypeStruct((ROWS, D), f32),
            jax.ShapeDtypeStruct((ROWS, D), bf16),
        ],
        compiler_params=pltpu.CompilerParams(vmem_limit_bytes=VMEM_LIMIT),
        cost_estimate=pl.CostEstimate(flops=16 * ROWS * KEYS * D, bytes_accessed=20_000_000, transcendentals=HEADS * ROWS * KEYS),
        name="attention_forward",
    )(joined, joined, joined, sibling, sibling, mask)


def attention_backward_kernel(
    q_ref, ko_ref, vo_ref, ks_ref, vs_ref, p_ref, o_ref, linv_ref, g_ref,
    gq_ref, gko_ref, gvo_ref, gks_ref, gvs_ref,
):
    half = [lane_row(bf16, 0, 64), lane_row(bf16, 64, 128)]
    two = [lane_row(bf16, 64, 66), lane_row(bf16, 0, 2)]
    q = q_ref[...]
    k = jnp.concatenate([ko_ref[...], ks_ref[...]], axis=0)
    v = jnp.concatenate([vo_ref[...], vs_ref[...]], axis=0)
    v_now = [v * half[h] + two[h] for h in range(2)]
    lane = lax.broadcasted_iota(jnp.int32, (ROWS, LANES), 1)
    gs = g_ref[...].astype(f32) * linv_ref[...]
    prod = gs * o_ref[...]
    gq, gk, gv = [], [], []
    for h in range(2):
        mine = (lane < 64) if h == 0 else (lane >= 64)
        base = 64 if h == 0 else 0
        delta = jnp.sum(jnp.where(mine, prod, 0.0), axis=1, keepdims=True)
        high = delta.astype(bf16).astype(f32)
        g_aug = jnp.where(
            mine, gs, jnp.where(lane == base, -high, jnp.where(lane == base + 1, high - delta, 0.0))
        ).astype(bf16)
        weights = p_ref[h]
        diff = mm_nt(g_aug, v_now[h])
        gscore = (weights.astype(f32) * diff).astype(bf16)
        gv.append(mm_tn(weights, g_aug))
        gk.append(mm_tn(gscore, q))
        gq.append(mm(gscore, k))
    gq_ref[...] = (jnp.where(lane < 64, gq[0], gq[1]) * 0.125).astype(bf16)
    lane_k = lax.broadcasted_iota(jnp.int32, (KEYS, LANES), 1)
    gk_all = jnp.where(lane_k < 64, gk[0], gk[1]) * 0.125
    gv_all = jnp.where(lane_k < 64, gv[0], gv[1])
    gko_ref[...] = gk_all[:ROWS]
    gvo_ref[...] = gv_all[:ROWS]
    gks_ref[...] = gk_all[ROWS:].astype(bf16)
    gvs_ref[...] = gv_all[ROWS:].astype(bf16)


def attention_backward(joined, sibling, weights, heads_out, linv, grad_att, first, count):
    col = lambda base: pl.BlockSpec((ROWS, LANES), lambda i, f=base + first: (0, f + i))
    own = pl.BlockSpec((ROWS, LANES), lambda i: (0, i))
    width = count * LANES
    return pl.pallas_call(
        attention_backward_kernel,
        grid=(count,),
        in_specs=[
            col(0), col(PAIRS), col(2 * PAIRS), col(0), col(PAIRS),
            pl.BlockSpec((2, ROWS, KEYS), lambda i: (first + i, 0, 0)),
            col(0), col(0), col(0),
        ],
        out_specs=[own] * 5,
        out_shape=[
            jax.ShapeDtypeStruct((ROWS, width), bf16),
            jax.ShapeDtypeStruct((ROWS, width), f32),
            jax.ShapeDtypeStruct((ROWS, width), f32),
            jax.ShapeDtypeStruct((ROWS, width), bf16),
            jax.ShapeDtypeStruct((ROWS, width), bf16),
        ],
        compiler_params=pltpu.CompilerParams(vmem_limit_bytes=VMEM_LIMIT),
        cost_estimate=pl.CostEstimate(flops=32 * ROWS * KEYS * width, bytes_accessed=12_000_000, transcendentals=0),
        name="attention_backward",
    )(joined, joined, joined, sibling, sibling, weights, heads_out, linv, grad_att)


def chunk_both_ways(g, n2, up, down, up_b):
    u = mm(n2, up) + up_b
    ga = mm_nt(g, down)
    u2 = u * u
    t = jnp.tanh(u * (GELU_C + (GELU_C * GELU_A) * u2))
    hp = 0.5 + 0.5 * t
    active = (u * hp).astype(bf16)
    slope = hp + (0.5 * u) * (1.0 - t * t) * (GELU_C + (3.0 * GELU_C * GELU_A) * u2)
    gu = (ga * slope).astype(bf16)
    return active, gu


def ff_first_kernel(
    at_ref, att_ref, x_ref, g_ref, ow_ref, vec_ref, upb_ref, up_ref, down_ref,
    y_ref, xhat_ref, rstd_ref, n2_ref, gn_ref, dup_ref, ddown_ref, upbg_ref,
):
    step = pl.program_id(0)
    out_bias, gain, shift, down_bias = (vec_ref[r : r + 1, :] for r in range(4))

    @pl.when(step == 0)
    def _():
        h = x_ref[...].astype(f32) + mm(att_ref[...], ow_ref[...]) + out_bias
        centred = h - jnp.mean(h, axis=1, keepdims=True)
        rstd = lax.rsqrt(jnp.mean(centred * centred, axis=1, keepdims=True) + epsilon)
        xh = centred * rstd
        xhat_ref[...] = xh
        rstd_ref[...] = jnp.broadcast_to(rstd, (ROWS, LANES))
        n2_ref[...] = (xh * gain + shift).astype(bf16)
        y_ref[...] = h + down_bias
        gn_ref[...] = jnp.zeros_like(gn_ref)

    g = g_ref[...]
    n2 = n2_ref[...]
    active, gu = chunk_both_ways(g, n2, up_ref[...], down_ref[...], upb_ref[0])
    ddown_ref[...] = mm_tn(active, g).astype(bf16)
    dup_ref[...] = mm_tn(n2, gu).astype(bf16)
    y_ref[...] += mm(active, down_ref[...])
    gn_ref[...] += mm_nt(gu, up_ref[...])
    upbg_ref[0] = jnp.sum(gu.astype(f32), axis=0, keepdims=True)


def quarters(buffer, place, core, keep_ref, away_ref):
    first = 1 + 2 * core
    for ref, index, block in (
        (keep_ref, 0, place), (keep_ref, 1, place ^ (4 - first)), (away_ref, 0, place ^ first), (away_ref, 1, place ^ 2),
    ):
        ref[index, 0] = buffer[pl.ds(pl.multiple_of(block * QUARTER, QUARTER), QUARTER), :]


def ff_second_kernel(
    at_ref, g_ref, ow_ref, vec_ref, upb_ref, up_ref, down_ref,
    y_ref, xhat_ref, rstd_ref, n2_ref, gn_in_ref,
    out_ref, gh_ref, gb_ref, gatt_ref, active_ref, gu_ref, vecg_ref, upbg_ref,
    y_acc, gn_acc,
):
    step = pl.program_id(0)
    gain = vec_ref[1:2, :]
    g = g_ref[...]
    active, gu = chunk_both_ways(g, n2_ref[...], up_ref[...], down_ref[...], upb_ref[0])
    active_ref[...] = active
    gu_ref[...] = gu
    upbg_ref[0] = jnp.sum(gu.astype(f32), axis=0, keepdims=True)
    y = mm(active, down_ref[...])
    gn = mm_nt(gu, up_ref[...])

    @pl.when(step == 0)
    def _():
        y_acc[...] = y + y_ref[...]
        gn_acc[...] = gn + gn_in_ref[...]

    @pl.when(step == 1)
    def _():
        out_ref[...] = (y_acc[...] + y).astype(bf16)
        gn_all = gn_acc[...] + gn
        xh = xhat_ref[...]
        gf = g.astype(f32)
        vecg_ref[...] = jnp.zeros_like(vecg_ref)
        vecg_ref[1:2, :] = jnp.sum(gn_all * xh, axis=0, keepdims=True)
        vecg_ref[2:3, :] = jnp.sum(gn_all, axis=0, keepdims=True)
        vecg_ref[3:4, :] = jnp.sum(gf, axis=0, keepdims=True)
        gx = gn_all * gain
        mean1 = jnp.mean(gx, axis=1, keepdims=True)
        mean2 = jnp.mean(gx * xh, axis=1, keepdims=True)
        gh = gf + rstd_ref[:, 0:1] * (gx - mean1 - xh * mean2)
        gh_ref[...] = gh
        vecg_ref[0:1, :] = jnp.sum(gh, axis=0, keepdims=True)
        gb = gh.astype(bf16)
        gb_ref[...] = gb
        gatt_ref[...] = mm_nt(gb, ow_ref[...]).astype(bf16)


def ff_grads_kernel(
    at_ref, active_ref, gu_ref, g_ref, n2_ref, dup_in_ref, ddown_in_ref,
    up_keep_ref, up_away_ref, down_keep_ref, down_away_ref, up_buf, down_buf,
):
    up_buf[...] = (mm_tn(n2_ref[...], gu_ref[...]) + dup_in_ref[...].astype(f32)).astype(bf16)
    quarters(up_buf, at_ref[1], at_ref[0], up_keep_ref, up_away_ref)
    down_buf[...] = (mm_tn(active_ref[...], g_ref[...]) + ddown_in_ref[...].astype(f32)).astype(bf16)
    quarters(down_buf, at_ref[2], at_ref[0], down_keep_ref, down_away_ref)


def whole(*shape):
    return pl.BlockSpec(shape, lambda s, at: (0,) * len(shape))


def ff_specs(chunk):
    return [
        pl.BlockSpec((1, 1, FCHUNK), lambda s, at: (chunk(s, at), 0, 0)),
        pl.BlockSpec((D, FCHUNK), lambda s, at: (0, chunk(s, at))),
        pl.BlockSpec((FCHUNK, D), lambda s, at: (chunk(s, at), 0)),
    ]


TOKEN_SPEC = pl.BlockSpec((ROWS, D), lambda s, at: (0, 0))
COTANGENT_SPEC = pl.BlockSpec((ROWS, D), lambda s, at: (0, 1))
STEP_ROWS = pl.BlockSpec((FCHUNK, D), lambda s, at: (s, 0))
QUARTERS = pl.BlockSpec((2, 1, QUARTER, D), lambda s, at: (0, s, 0, 0))
FF_COST = pl.CostEstimate(flops=6 * ROWS * D * FF, bytes_accessed=15_000_000, transcendentals=ROWS * FF // 2)


def ff_first(at, attended, both, out_w, vecs, up_b, up_w, down_w):
    shape = jax.ShapeDtypeStruct
    return pl.pallas_call(
        ff_first_kernel,
        grid_spec=pltpu.PrefetchScalarGridSpec(
            num_scalar_prefetch=1,
            grid=(NF // 2,),
            in_specs=[whole(ROWS, D), TOKEN_SPEC, COTANGENT_SPEC, whole(D, D), whole(8, D)]
            + ff_specs(lambda s, at: 2 * (1 - at[0]) + s),
            out_specs=[
                whole(ROWS, D), whole(ROWS, D), whole(ROWS, LANES), whole(ROWS, D), whole(ROWS, D),
                STEP_ROWS, STEP_ROWS, pl.BlockSpec((1, 1, FCHUNK), lambda s, at: (s, 0, 0)),
            ],
        ),
        out_shape=[
            shape((ROWS, D), f32), shape((ROWS, D), f32), shape((ROWS, LANES), f32), shape((ROWS, D), bf16),
            shape((ROWS, D), f32), shape((FF // 2, D), bf16), shape((FF // 2, D), bf16),
            shape((NF // 2, 1, FCHUNK), f32),
        ],
        compiler_params=pltpu.CompilerParams(vmem_limit_bytes=VMEM_LIMIT),
        cost_estimate=FF_COST,
        name="ff_first",
    )(at, attended, both, both, out_w, vecs, up_b, up_w, down_w)


def ff_second(at, both, out_w, vecs, up_b, up_w, down_w, kept):
    shape = jax.ShapeDtypeStruct
    step_columns = pl.BlockSpec((ROWS, FCHUNK), lambda s, at: (0, s))
    return pl.pallas_call(
        ff_second_kernel,
        grid_spec=pltpu.PrefetchScalarGridSpec(
            num_scalar_prefetch=1,
            grid=(NF // 2,),
            in_specs=[COTANGENT_SPEC, whole(D, D), whole(8, D)]
            + ff_specs(lambda s, at: 2 * at[0] + s)
            + [whole(ROWS, D), whole(ROWS, D), whole(ROWS, LANES), whole(ROWS, D), whole(ROWS, D)],
            out_specs=[whole(ROWS, D)] * 4
            + [step_columns, step_columns, whole(8, D), pl.BlockSpec((1, 1, FCHUNK), lambda s, at: (s, 0, 0))],
            scratch_shapes=[pltpu.VMEM((ROWS, D), f32), pltpu.VMEM((ROWS, D), f32)],
        ),
        out_shape=[
            shape((ROWS, D), bf16), shape((ROWS, D), f32), shape((ROWS, D), bf16), shape((ROWS, D), bf16),
            shape((ROWS, FF // 2), bf16), shape((ROWS, FF // 2), bf16),
            shape((8, D), f32), shape((NF // 2, 1, FCHUNK), f32),
        ],
        compiler_params=pltpu.CompilerParams(vmem_limit_bytes=VMEM_LIMIT),
        cost_estimate=FF_COST,
        name="ff_second",
    )(at, both, out_w, vecs, up_b, up_w, down_w, *kept)


def ff_grads(at, active, gu, both, n2, arrived):
    quarter_shape = jax.ShapeDtypeStruct((2, NF // 2, QUARTER, D), bf16)
    step_columns = pl.BlockSpec((ROWS, FCHUNK), lambda s, at: (0, s))
    return pl.pallas_call(
        ff_grads_kernel,
        grid_spec=pltpu.PrefetchScalarGridSpec(
            num_scalar_prefetch=1,
            grid=(NF // 2,),
            in_specs=[step_columns, step_columns, COTANGENT_SPEC, whole(ROWS, D), STEP_ROWS, STEP_ROWS],
            out_specs=[QUARTERS] * 4,
            scratch_shapes=[pltpu.VMEM((D, FCHUNK), bf16), pltpu.VMEM((FCHUNK, D), bf16)],
        ),
        out_shape=[quarter_shape] * 4,
        compiler_params=pltpu.CompilerParams(vmem_limit_bytes=VMEM_LIMIT),
        cost_estimate=pl.CostEstimate(flops=4 * ROWS * D * FF // 2, bytes_accessed=15_000_000, transcendentals=0),
        name="ff_grads",
    )(at, active, gu, both, n2, *arrived)


def square_kernel(at_ref, left_ref, right_ref, out_ref):
    out_ref[...] = mm_tn(left_ref[...], right_ref[...]).astype(bf16)


def square_sum_kernel(
    at_ref, left_ref, right_ref, other_ref, keep0_ref, away0_ref, keep1_ref, away1_ref, buf
):
    buf[...] = (mm_tn(left_ref[...], right_ref[...]) + other_ref[...].astype(f32)).astype(bf16)

    @pl.when(pl.program_id(0) == 0)
    def _():
        quarters(buf, at_ref[1], at_ref[0], keep0_ref, away0_ref)

    @pl.when(pl.program_id(0) == 1)
    def _():
        quarters(buf, at_ref[2], at_ref[0], keep1_ref, away1_ref)


def square_specs(mine):
    def number(s, at):
        return 2 * (at[0] if mine else 1 - at[0]) + s

    return [
        pl.BlockSpec((ROWS, D), lambda s, at: (0, jnp.maximum(number(s, at) - 2, 0))),
        pl.BlockSpec((ROWS, D), lambda s, at: (0, number(s, at))),
    ]


SQUARE_COST = pl.CostEstimate(flops=4 * ROWS * D * D, bytes_accessed=6_000_000, transcendentals=0)


def square_away(at, left, right):
    return pl.pallas_call(
        square_kernel,
        grid_spec=pltpu.PrefetchScalarGridSpec(
            num_scalar_prefetch=1, grid=(2,), in_specs=square_specs(False),
            out_specs=pl.BlockSpec((D, D), lambda s, at: (s, 0)),
        ),
        out_shape=jax.ShapeDtypeStruct((2 * D, D), bf16),
        compiler_params=pltpu.CompilerParams(vmem_limit_bytes=VMEM_LIMIT),
        cost_estimate=SQUARE_COST,
        name="square_away",
    )(at, left, right)


def square_mine(at, left, right, other):
    quarter_shape = jax.ShapeDtypeStruct((2, 1, QUARTER, D), bf16)
    return pl.pallas_call(
        square_sum_kernel,
        grid_spec=pltpu.PrefetchScalarGridSpec(
            num_scalar_prefetch=1, grid=(2,),
            in_specs=square_specs(True) + [pl.BlockSpec((D, D), lambda s, at: (s, 0))],
            out_specs=[whole(2, 1, QUARTER, D)] * 4,
            scratch_shapes=[pltpu.VMEM((D, D), bf16)],
        ),
        out_shape=[quarter_shape] * 4,
        compiler_params=pltpu.CompilerParams(vmem_limit_bytes=VMEM_LIMIT),
        cost_estimate=SQUARE_COST,
        name="square_mine",
    )(at, left, right, other)


def put_quarters(out_ref, place, core, own_ref, got_ref):
    first = 1 + 2 * core
    for ref, index, block in (
        (own_ref, 0, place), (own_ref, 1, place ^ (4 - first)), (got_ref, 0, place ^ first), (got_ref, 1, place ^ 2),
    ):
        out_ref[pl.ds(pl.multiple_of(block * QUARTER, QUARTER), QUARTER), :] = ref[index, 0].astype(f32)


def put_from(out_ref, at_ref, part, half, own, got, own_other, got_other):
    core, place = at_ref[0], at_ref[1 + part]

    @pl.when(core == half)
    def _():
        put_quarters(out_ref, place, core, own, got)

    @pl.when(core != half)
    def _():
        put_quarters(out_ref, place, 1 - core, own_other, got_other)


def place_ff_kernel(at_ref, *refs):
    half = pl.program_id(0) // 2
    put_from(refs[8], at_ref, 0, half, *refs[:4])
    put_from(refs[9], at_ref, 1, half, *refs[4:8])


def place_ff(at, first, second):
    source = pl.BlockSpec((2, 1, QUARTER, D), lambda s, at: (0, s % 2, 0, 0))
    return pl.pallas_call(
        place_ff_kernel,
        grid_spec=pltpu.PrefetchScalarGridSpec(
            num_scalar_prefetch=1, grid=(NF,), in_specs=[source] * 8,
            out_specs=[pl.BlockSpec((D, FCHUNK), lambda s, at: (0, s)), pl.BlockSpec((FCHUNK, D), lambda s, at: (s, 0))],
        ),
        out_shape=[jax.ShapeDtypeStruct((D, FF), f32), jax.ShapeDtypeStruct((FF, D), f32)],
        compiler_params=pltpu.CompilerParams(vmem_limit_bytes=VMEM_LIMIT),
        cost_estimate=pl.CostEstimate(flops=0, bytes_accessed=40_000_000, transcendentals=0),
        name="place_ff",
    )(at, *first, *second)


def place_squares_kernel(at_ref, *refs):
    for block in range(4):
        out_ref = refs[8] if block < 3 else refs[9]
        part = block % 2

        @pl.when(pl.program_id(0) == block)
        def _():
            put_from(out_ref, at_ref, part, block // 2, *refs[4 * part : 4 * part + 4])


def place_squares(at, first, second):
    return pl.pallas_call(
        place_squares_kernel,
        grid_spec=pltpu.PrefetchScalarGridSpec(
            num_scalar_prefetch=1, grid=(4,), in_specs=[whole(2, 1, QUARTER, D)] * 8,
            out_specs=[pl.BlockSpec((D, D), lambda s, at: (0, jnp.minimum(s, 2))), whole(D, D)],
        ),
        out_shape=[jax.ShapeDtypeStruct((D, 3 * D), f32), jax.ShapeDtypeStruct((D, D), f32)],
        compiler_params=pltpu.CompilerParams(vmem_limit_bytes=VMEM_LIMIT),
        cost_estimate=pl.CostEstimate(flops=0, bytes_accessed=20_000_000, transcendentals=0),
        name="place_squares",
    )(at, *first, *second)


def linear(y, xl, c, z, xh):
    return (((y * 2 + xl) * 2 + c) * 4 + z) * 2 + xh


def scene_pairs(slot):
    pairs = []
    for y, xl, z, xh in itertools.product(range(4), range(2), range(4), range(2)):
        block = 2 * z + xh
        scene = (slot - block) % 4
        if scene < 3:
            for c in range(2):
                pairs.append((linear(y, xl, c, z, xh), linear(y, xl, block // 4, scene, c)))
    return pairs


def to_scene(values, block):
    pieces = []
    for slot in range(SLOTS):
        scene = jnp.minimum((slot - block) % 4, 2)
        pieces.append(lax.ppermute(lax.dynamic_index_in_dim(values, scene, 0, keepdims=False), AXES, scene_pairs(slot)))
    return pieces


def send_from_scene(values):
    pieces = []
    for slot in range(SLOTS):
        back = [(target, source) for source, target in scene_pairs(slot)]
        pieces.append(lax.ppermute(values[slot * BLK : (slot + 1) * BLK], AXES, back))
    return pieces


def take_from_scene(pieces, block):
    pieces = jnp.stack(pieces)
    return jnp.stack([lax.dynamic_index_in_dim(pieces, (m + block) % 4, 0, keepdims=False) for m in range(3)])


SWAP = ((0, 1), (1, 0))
STEPS = ((1, -1), (-1, 1), (2, 2))
MASKS = ((1, 3), (3, 1))


def exchange(value, move):
    pairs = []
    for place in itertools.product(range(4), range(4), range(4), range(2)):
        ends = [linear(y, x % 2, c, z, x // 2) for x, y, z, c in (place, move(*place))]
        pairs.append(tuple(ends))
    return lax.ppermute(value, AXES, pairs)


def shift(value, axis, signs):
    def move(x, y, z, c):
        at = {"x": x, "y": y, "z": z}
        at[axis] = (at[axis] + signs[c]) % 4
        return at["x"], at["y"], at["z"], c

    return exchange(value, move)


def meet(value, axis, step):
    def move(x, y, z, c):
        at = {"x": x, "y": y, "z": z}
        at[axis] = at[axis] ^ MASKS[c][step]
        return at["x"], at["y"], at["z"], c

    return exchange(value, move)


def swap(value):
    return lax.ppermute(value, "c", SWAP)


class Sum:
    def __init__(self, core, x_place, keep, away):
        self.core, self.x_place = core, x_place
        self.keep, self.away = keep, away

    def send_half(self):
        return [meet(self.away[0], "y", 0), meet(self.away[1], "z", 0)]

    def take_half(self, arrived):
        self.keep = [k + a for k, a in zip(self.keep, arrived)]

    def send_quarter(self):
        return [meet(self.keep[0][1], "y", 1), meet(self.keep[1][1], "z", 1)]

    def take_quarter(self, arrived):
        total = jnp.stack([k[0] + a for k, a in zip(self.keep, arrived)])
        self.blocks = total.reshape(total.shape[:2] + (4, QUARTER // 4, D))

    def block(self, step):
        return lax.dynamic_index_in_dim(self.blocks, (self.x_place + step) % 4, 2, keepdims=False)

    def steps(self):
        return [jnp.where(self.core == 0, a, b) for a, b in STEPS]

    def send_x(self):
        return [shift(self.block(step), "x", signs) for step, signs in zip(self.steps(), STEPS)]

    def take_x(self, arrived):
        total = self.block(0).astype(f32)
        for term in arrived:
            total = total + term.astype(f32)
        self.ends = total.astype(bf16)

    def send_last(self, step):
        return [meet(self.ends[0], "z", step), meet(self.ends[1], "y", step)]

    def take_last(self, arrived):
        self.ends = self.ends + jnp.stack(arrived)

    def send_x_back(self):
        return [shift(self.ends, "x", signs) for signs in STEPS]

    def take_x_back(self, arrived):
        whole_x = jnp.zeros_like(self.blocks)
        for step, piece in zip([0] + self.steps(), [self.ends] + arrived):
            whole_x = lax.dynamic_update_index_in_dim(whole_x, piece, (self.x_place - step) % 4, 2)
        whole_x = whole_x.reshape(self.blocks.shape[:2] + (QUARTER, D))
        self.own = [whole_x[0], whole_x[1]]

    def send_quarter_back(self):
        return [meet(self.own[0], "y", 1), meet(self.own[1], "z", 1)]

    def take_quarter_back(self, arrived):
        self.own = [jnp.stack([o, a]) for o, a in zip(self.own, arrived)]

    def send_half_back(self):
        return [meet(self.own[0], "y", 0), meet(self.own[1], "z", 0)]

    def send_own(self):
        return [swap(self.own[0]), swap(self.own[1])]

    def pieces(self, got, own_other, got_other):
        return [[self.own[p], got[p], own_other[p], got_other[p]] for p in range(2)]


BITS = tuple((axis, bit) for axis in "czyx" for bit in ((1,) if axis == "c" else (1, 2)))


def send_small(values, number):
    axis, bit = BITS[number]
    flip = lambda x, y, z, c: tuple(v ^ bit if n == axis else v for n, v in zip("xyzc", (x, y, z, c)))
    return [exchange(values, flip)]


def hold(*values):
    return lax.optimization_barrier(values)


def body(
    tokens, view_counts, ln1_gain, ln1_shift, qkv_weight, query_bias, value_bias, out_weight, out_bias,
    ln2_gain, ln2_shift, up_weight, up_bias, down_weight, down_bias, cotangent,
):
    core, z, xh = lax.axis_index("c"), lax.axis_index("z"), lax.axis_index("xh")
    block = 2 * z + xh
    scene = jnp.minimum(z, 2)

    views = jnp.broadcast_to(view_counts.astype(bf16)[:, None, None], (3, BLK, LANES))
    pieces = to_scene(jnp.concatenate([tokens, cotangent, views], axis=2), block)
    both = jnp.concatenate([piece[:, : 2 * D] for piece in pieces], axis=0)
    views = pieces[0][0, 2 * D].astype(f32)
    x = both[:, :D]

    slot = jnp.arange(ROWS, dtype=jnp.int32) // BLK
    inside = jnp.arange(ROWS, dtype=jnp.int32) % BLK
    offset = (slot - z) % 4 * BLK + inside
    place = jnp.concatenate([offset + core * ROWS, offset + (1 - core) * ROWS])
    usable = (place.astype(f32) < views * VIEW_TOK) | (place >= VIEWS_MAX * VIEW_TOK)
    mask = jnp.broadcast_to(jnp.where(usable, 0.0, masked_score).astype(bf16)[:, None], (KEYS, LANES))

    source = x.astype(f32)
    centred = source - jnp.mean(source, axis=1, keepdims=True)
    rstd = lax.rsqrt(jnp.mean(centred * centred, axis=1, keepdims=True) + epsilon)
    xhat = centred * rstd
    normed = (xhat * ln1_gain + ln1_shift).astype(bf16)
    qkv_bias = jnp.concatenate([query_bias, jnp.zeros((D,), f32), value_bias])
    joined = (jnp.dot(normed, qkv_weight, preferred_element_type=f32) + qkv_bias).astype(bf16)
    sibling = lax.ppermute(joined[:, D:], "c", SWAP)
    weights, heads_out, linv, attended = attention_forward(joined, sibling, mask)

    vecs = jnp.concatenate([jnp.stack([out_bias, ln2_gain, ln2_shift, down_bias]), jnp.zeros((4, D), f32)])
    up_b = up_bias.reshape(NF, 1, FCHUNK)
    y = lax.axis_index("y")
    x_place = lax.axis_index("xh") * 2 + lax.axis_index("xl")
    at = jnp.stack([core, y, z]).astype(jnp.int32)
    *kept, up_away, down_away, up_b_first = ff_first(at, attended, both, out_weight, vecs, up_b, up_weight, down_weight)
    moving = [swap(up_away), swap(down_away)]
    output, grad_hidden, grad_branch, grad_att, active, grad_up, vec_grads, up_b_second = ff_second(
        at, both, out_weight, vecs, up_b, up_weight, down_weight, kept
    )

    moving, active = hold(moving, active)
    up_keep, up_away, down_keep, down_away = ff_grads(at, active, grad_up, both, kept[3], moving)
    ff = Sum(core, x_place, [up_keep, down_keep], [up_away, down_away])
    ff.away, grad_att = hold(ff.away, grad_att)
    moving = ff.send_half()
    one = attention_backward(joined, sibling, weights, heads_out, linv, grad_att, 0, PAIRS // 2)

    moving, one = hold(moving, one)
    ff.take_half(moving)
    ff.keep, grad_att = hold(ff.keep, grad_att)
    moving = ff.send_quarter()
    two = attention_backward(joined, sibling, weights, heads_out, linv, grad_att, PAIRS // 2, PAIRS // 2)

    grads = [jnp.concatenate([a, b], axis=1) for a, b in zip(one, two)]
    others = jnp.concatenate(grads[3:], axis=1)
    moving, others = hold(moving, others)
    swapped = swap(others)
    ff.take_quarter(moving)
    moving = ff.send_x()
    grad_q = grads[0]

    moving, swapped = hold(moving, swapped)
    swapped = swapped.astype(f32)
    grad_k = (grads[1] + swapped[:, :D]).astype(bf16)
    grad_v = (grads[2] + swapped[:, D:]).astype(bf16)
    right = jnp.concatenate([grad_q, grad_k, grad_v, grad_branch], axis=1)
    left = jnp.concatenate([normed, attended], axis=1)
    away = square_away(at, left, right)
    ff.take_x(moving)
    ff.ends, away = hold(ff.ends, away)
    moving2 = [swap(away)]
    moving = ff.send_last(0)
    grad_normed = lax.dot_general(
        right[:, : 3 * D], qkv_weight, (((1,), (1,)), ((), ())), preferred_element_type=f32
    )

    moving, moving2, grad_normed = hold(moving, moving2, grad_normed)
    ff.take_last(moving)
    ff.ends, moving2 = hold(ff.ends, moving2)
    moving = ff.send_last(1)
    keep0, away0, keep1, away1 = square_mine(at, left, right, moving2[0])
    squares = Sum(core, x_place, [keep0, keep1], [away0, away1])

    moving, squares.away, grad_normed = hold(moving, squares.away, grad_normed)
    ff.take_last(moving)
    moving2 = squares.send_half()
    moving = ff.send_x_back()
    gx = grad_normed * ln1_gain
    mean1 = jnp.mean(gx, axis=1, keepdims=True)
    mean2 = jnp.mean(gx * xhat, axis=1, keepdims=True)
    input_grad = (grad_hidden + rstd * (gx - mean1 - xhat * mean2)).astype(bf16)
    up_b_grad = jnp.where(
        core == 0, jnp.concatenate([up_b_second, up_b_first]), jnp.concatenate([up_b_first, up_b_second])
    )
    small = jnp.concatenate(
        [
            vec_grads[0], vec_grads[1], vec_grads[2], vec_grads[3],
            jnp.sum(grad_normed * xhat, axis=0), jnp.sum(grad_normed, axis=0),
            jnp.sum(grad_q.astype(f32), axis=0), jnp.sum(grad_v.astype(f32), axis=0),
            up_b_grad.reshape(FF),
        ]
    ).reshape(-1, LANES)

    moving, moving2, small, input_grad = hold(moving, moving2, small, input_grad)
    squares.take_half(moving2)
    ff.take_x_back(moving)
    squares.keep, ff.own, small = hold(squares.keep, ff.own, small)
    moving2 = squares.send_quarter()
    moving = ff.send_quarter_back()
    moving3 = send_small(small, 0)

    moving, moving2, moving3 = hold(moving, moving2, moving3)
    squares.take_quarter(moving2)
    ff.take_quarter_back(moving)
    small = small + moving3[0]
    squares.blocks, ff.own, small = hold(squares.blocks, ff.own, small)
    moving2 = squares.send_x()
    moving = ff.send_half_back()

    moving2, small = hold(moving2, small)
    squares.take_x(moving2)
    squares.ends, small, ff.own = hold(squares.ends, small, ff.own)
    moving2 = squares.send_last(0)
    moving3 = send_small(small, 1)
    own_other = ff.send_own()

    moving2, moving3 = hold(moving2, moving3)
    squares.take_last(moving2)
    small = small + moving3[0]
    squares.ends, small = hold(squares.ends, small)
    moving2 = squares.send_last(1)
    moving3 = send_small(small, 2)

    moving, moving2, moving3, own_other = hold(moving, moving2, moving3, own_other)
    squares.take_last(moving2)
    small = small + moving3[0]
    got = moving
    squares.ends, small, got, output = hold(squares.ends, small, got, output)
    moving2 = squares.send_x_back()
    got_other = [swap(v) for v in got]

    moving2, got_other, output = hold(moving2, got_other, output)
    squares.take_x_back(moving2)
    squares.own, small, output = hold(squares.own, small, output)
    moving2 = squares.send_quarter_back()
    moving3 = send_small(small, 3)
    d_up, d_down = place_ff(at, *ff.pieces(got, own_other, got_other))

    moving2, moving3, d_up, d_down = hold(moving2, moving3, d_up, d_down)
    squares.take_quarter_back(moving2)
    small = small + moving3[0]
    squares.own, small, output = hold(squares.own, small, output)
    moving2 = squares.send_half_back()
    own_other = squares.send_own()
    moving3 = send_small(small, 4)

    moving2, moving3, own_other, output, input_grad = hold(moving2, moving3, own_other, output, input_grad)
    small = small + moving3[0]
    got_other = [swap(v) for v in moving2]
    returned = send_from_scene(jnp.concatenate([output, input_grad], axis=1))
    got_other, small = hold(got_other, small)
    moving3 = send_small(small, 5)
    d_qkv, d_out = place_squares(at, *squares.pieces(moving2, own_other, got_other))
    small = small + moving3[0]
    small, returned = hold(small, returned)
    moving3 = send_small(small, 6)
    returned = take_from_scene(returned, block)
    output, input_grad = returned[:, :, :D], returned[:, :, D:]
    small = (small + moving3[0]).reshape(-1)
    vector = lambda i: small[i * D : (i + 1) * D]
    return (
        output, input_grad, vector(4), vector(5), d_qkv, vector(6), vector(7), d_out,
        vector(0), vector(1), vector(2), d_up, small[8 * D :], d_down, vector(3),
    )


def solution(mesh):
    fine = Mesh(mesh.devices.reshape(4, 2, 2, 4, 2), AXES)
    rows = P(("y", "xl", "c"), ("z", "xh"), None)
    placed = (rows, P(("y", "xl", "c"))) + (P(),) * 13 + (rows,)
    return jax.shard_map(
        body, mesh=fine, in_specs=placed, out_specs=(rows, rows) + (P(),) * 13, check_vma=False
    )
```

time: 542 us -> 401 us (0.74)
  starting transfers between devices: 252 us -> 104 us
  Pallas kernels: 78.7 us -> 127 us
  other arithmetic: 72.3 us -> 36.9 us
  waiting for transfers between devices: 97 us -> 85.1 us
  local copies, waits for them, and re-layouts: 23 us -> 32.4 us
    ppermute x114 -> x43, starting transfers between devices: 153 us -> 42.5 us  [exchange(): return lax.ppermute(value, AXES, pairs)]
    pallas_call x2 -> x9, Pallas kernels: 53.2 us -> 102 us  [the longest x2 25.5 us: attention_backward(): pl.pallas_call(attention_backward_kernel, grid=(count,), in_specs=[col(0)...]
    convert_element_type x21 -> x5, other arithmetic: 53.9 us -> 5.24 us  [the longest x2 2.12 us: take_x(): self.ends = total.astype(bf16)]
    ppermute x23 -> x16, starting transfers between devices: 71.8 us -> 43.1 us  [the longest x12 30.8 us: swap(): return lax.ppermute(value, 'c', SWAP)]
    ppermute x23 -> x16, waiting for transfers between devices: 14.1 us -> 0.5 us  [the longest x4 0.47 us: send_from_scene(): pieces.append(lax.ppermute(values[slot * BLK:(slot + 1) * BLK], AXES, back))]
    unnamed x73 -> x144, local copies, waits for them, and re-layouts: 4.08 us -> 15.6 us
    ppermute x8 -> x4, starting transfers between devices: 27.9 us -> 16.8 us  [to_scene(): lax.ppermute(lax.dynamic_index_in_dim(values, scene, 0, keepdims=False),...]
    add x7 -> x18, other arithmetic: 0.05 us -> 10.1 us  [the longest x4 4.31 us: take_half(): self.keep = [k + a for k, a in zip(self.keep, arrived)]]
  transfers between devices with their start and end apart: 146 -> 64, of which waited for: 61 -> 24; matrix products, arithmetic and copies ran while one was open for 16% -> 10% of each run, Pallas kernels for 4% -> 18%
where the time goes in v3:
time: 401 us; the launch traced here: 395 us
  Pallas kernels  127 us (32%)
  starting transfers between devices  104 us (26%)
  waiting for transfers between devices  85.1 us (21%)
  other arithmetic  36.9 us (9%)
  local copies, waits for them, and re-layouts  32.4 us (8%)
  matrix products  7.41 us (2%)
    ppermute x43, waiting for transfers between devices, exchange(): return lax.ppermute(value, AXES, pairs)  71.3 us
    ppermute x43, starting transfers between devices, exchange(): return lax.ppermute(value, AXES, pairs)  42.5 us
    ppermute x12, starting transfers between devices, swap(): return lax.ppermute(value, 'c', SWAP)  30.8 us
    pallas_call x2, Pallas kernels, attention_backward(): pl.pallas_call(attention_backward_kernel, grid=(count,), in_specs=[col(0)...  25.5 us
    pallas_call x1, Pallas kernels, attention_forward(): pl.pallas_call(attention_forward_kernel, grid=(PAIRS,), in_specs=[col(0),...  25 us
    pallas_call x1, Pallas kernels, ff_first(): pl.pallas_call(ff_first_kernel, grid_spec=pltpu.PrefetchScalarGridSpec(nu...  17.7 us
    ppermute x4, starting transfers between devices, to_scene(): lax.ppermute(lax.dynamic_index_in_dim(values, scene, 0, keepdims=False),...  16.8 us
    pallas_call x1, Pallas kernels, ff_second(): pl.pallas_call(ff_second_kernel, grid_spec=pltpu.PrefetchScalarGridSpec(n...  16.8 us
  transfers between devices with their start and end apart: 64, of which 24 were waited for; matrix products, arithmetic and copies ran while one was open for 10% of the time, Pallas kernels for 18%

profile of v3, /device:TPU:1, one launch (start us, length us, event | category | flops | bytes accessed | tf_op | source)
XLA Modules:
  0.0 395.4 jit_solution(2682777807313095596)
XLA Ops:
  3.4 6.0 %collective-permute-start = (bf16[144,1664]{1,0:T(8,128)(2,1)S(1)}, bf16[144,1664]{1,0:T(8,128)(2,1)S(1)}, u32[]{:S(2)}, u32[]{:S(2)}) collective-permute-start(bf16[144,1664]{1,0:T(8,128)(2,1)S(1)} %get-tuple-element.352), channel_id=1, source_target_pairs={{0,0},{8,1},{2,4},{10,5},{3,2},{11,3},{4,8},{12,9},{6,12},{14,13},... | collective-permute-start | bytes 1437704 | tf_op jit(solution)/shard_map/ppermute | solution.py:512
  9.5 3.7 collective-permute-start.1
  13.2 5.8 %collective-permute-start.2 = (bf16[144,1664]{1,0:T(8,128)(2,1)S(1)}, bf16[144,1664]{1,0:T(8,128)(2,1)S(1)}, u32[]{:S(2)}, u32[]{:S(2)}) collective-permute-start(bf16[144,1664]{1,0:T(8,128)(2,1)S(1)} %get-tuple-element.354), channel_id=1, source_target_pairs={{0,4},{8,5},{1,2},{9,3},{2,0},{10,1},{4,12},{12,13},{5,10},{13,11}... | collective-permute-start | bytes 1437704 | tf_op jit(solution)/shard_map/ppermute | solution.py:512
  20.4 3.1 collective-permute-done.1
  23.5 10.1 %collective-permute-done.2 = bf16[144,1664]{1,0:T(8,128)(2,1)S(1)} collective-permute-done((bf16[144,1664]{1,0:T(8,128)(2,1)S(1)}, bf16[144,1664]{1,0:T(8,128)(2,1)S(1)}, u32[]{:S(2)}, u32[]{:S(2)}) %collective-permute-start.2) | collective-permute-done | bytes 479264 | tf_op jit(solution)/shard_map/ppermute | solution.py:512
  35.9 2.2 add_convert_fusion.q_ref.ko_ref.vo_ref
  48.6 25.0 %attention_forward.1 = (bf16[12,576,1152]{2,1,0:T(8,128)(2,1)}, f32[576,768]{1,0:T(8,128)}, f32[576,768]{1,0:T(8,128)}, bf16[576,768]{1,0:T(8,128)(2,1)}) custom-call(bf16[576,2304]{1,0:T(8,128)(2,1)} %copy-done.1, bf16[576,2304]{1,0:T(8,128)(2,1)} %copy-done.1, bf16[576,2304]{1,0:T(8,128)(2,1)} %copy-done.1, ...), custom_call_target="tpu_custom_call" | custom-call | flops 8153726976 | bytes 20000000 | tf_op jit(solution)/shard_map/attention_forward/pallas_call | solution.py:89
  73.6 17.7 %ff_first.1 = (f32[576,768]{1,0:T(8,128)}, f32[576,768]{1,0:T(8,128)}, f32[576,128]{1,0:T(8,128)}, bf16[576,768]{1,0:T(8,128)(2,1)}, f32[576,768]{1,0:T(8,128)},...) custom-call(s32[3]{0:T(128)} %pad_add_fusion.1.at_ref, ...), custom_call_target="tpu_custom_call" | custom-call | flops 8153726976 | bytes 15000000 | tf_op jit(solution)/shard_map/ff_first/pallas_call | solution.py:298
  92.0 16.8 %ff_second.1 = (bf16[576,768]{1,0:T(8,128)(2,1)}, f32[576,768]{1,0:T(8,128)}, bf16[576,768]{1,0:T(8,128)(2,1)}, bf16[576,768]{1,0:T(8,128)(2,1)}, bf16[576,1536]...) custom-call(s32[3]{0:T(128)} %pad_add_fusion.1.at_ref, ...), custom_call_target="tpu_custom_call" | custom-call | flops 8153726976 | bytes 15000000 | tf_op jit(solution)/shard_map/ff_second/pallas_call | solution.py:324
  108.8 9.6 %ff_grads.1 = (bf16[2,2,192,768]{3,2,1,0:T(8,128)(2,1)}, bf16[2,2,192,768]{3,2,1,0:T(8,128)(2,1)}, bf16[2,2,192,768]{3,2,1,0:T(8,128)(2,1)}, bf16[2,2,192,768]{3,2,1,0:T(8,128)(2,1)}) custom-call(s32[3]{0:T(128)} %pad_add_fusion.1.at_ref, bf16[576,1536]{1,0:T(8,128)(2,1)} %get-tuple-element.182.active_ref, bf16[576,1536]{1,0:T(8,128)(2,1)} %get-tuple-element.183.gu_ref, ...), custom_call_target="tpu_custom_call" | custom-call | flops 2717908992 | bytes 15000000 | tf_op jit(solution)/shard_map/ff_grads/pallas_call | solution.py:350
  118.4 2.7 collective-permute-start.7
  121.1 12.8 %attention_backward.2 = (bf16[576,384]{1,0:T(8,128)(2,1)}, f32[576,384]{1,0:T(8,128)}, f32[576,384]{1,0:T(8,128)}, bf16[576,384]{1,0:T(8,128)(2,1)}, bf16[576,384]{1,0:T(8,128)(2,1)}) custom-call(bf16[576,2304]{1,0:T(8,128)(2,1)} %copy-done.1, bf16[576,2304]{1,0:T(8,128)(2,1)} %copy-done.1, bf16[576,2304]{1,0:T(8,128)(2,1)} %copy-done.1, ...), custom_call_target="tpu_custom_call" | custom-call | flops 8153726976 | bytes 12000000 | tf_op jit(solution)/shard_map/attention_backward/pallas_call | solution.py:154
  135.0 2.7 collective-permute-done.8
  143.8 12.7 %attention_backward.3 = (bf16[576,384]{1,0:T(8,128)(2,1)}, f32[576,384]{1,0:T(8,128)}, f32[576,384]{1,0:T(8,128)}, bf16[576,384]{1,0:T(8,128)(2,1)}, bf16[576,384]{1,0:T(8,128)(2,1)}) custom-call(bf16[576,2304]{1,0:T(8,128)(2,1)} %copy-done.1, bf16[576,2304]{1,0:T(8,128)(2,1)} %copy-done.1, bf16[576,2304]{1,0:T(8,128)(2,1)} %copy-done.1, ...), custom_call_target="tpu_custom_call" | custom-call | flops 8153726976 | bytes 12000000 | tf_op jit(solution)/shard_map/attention_backward/pallas_call | solution.py:154
  156.6 2.8 pad_maximum_fusion.2
  159.3 2.8 collective-permute-start.14
  165.9 4.3 %collective-permute-start.11 = (bf16[2,2,48,768]{3,2,1,0:T(8,128)(2,1)S(1)}, bf16[2,2,48,768]{3,2,1,0:T(8,128)(2,1)S(1)}, u32[]{:S(2)}, u32[]{:S(2)}) collective-permute-start(bf16[2,2,48,768]{3,2,1,0:T(8,128)(2,1)S(1)} %get-tuple-element.361), channel_id=1, source_target_pairs={{0,16},{8,25},{2,18},{10,27},{4,20},{12,29},{6,22},{14,31},{32,48}... | collective-permute-start | bytes 884744 | tf_op jit(solution)/shard_map/ppermute | solution.py:539
  174.5 8.3 %collective-permute-done.11 = bf16[2,2,48,768]{3,2,1,0:T(8,128)(2,1)S(1)} collective-permute-done((bf16[2,2,48,768]{3,2,1,0:T(8,128)(2,1)S(1)}, bf16[2,2,48,768]{3,2,1,0:T(8,128)(2,1)S(1)}, u32[]{:S(2)}, u32[]{:S(2)}) %collective-permute-start.11) | collective-permute-done | bytes 294944 | tf_op jit(solution)/shard_map/ppermute | solution.py:539
  182.7 2.2 collective-permute-done.13
  192.9 5.4 %square_away.1 = bf16[1536,768]{1,0:T(8,128)(2,1)} custom-call(s32[3]{0:T(128)} %pad_add_fusion.1.at_ref, bf16[576,1536]{1,0:T(8,128)(2,1)} %pad_maximum_fusion.1.left_ref, bf16[576,3072]{1,0:T(8,128)(2,1)} %constant_dynamic-update-slice_fusion.right_ref), custom_call_target="tpu_custom_call" | custom-call | flops 1358954496 | bytes 6000000 | tf_op jit(solution)/shard_map/square_away/pallas_call | solution.py:398
  211.1 5.2 %fusion = f32[576,768]{1,0:T(8,128)} fusion(bf16[768,2304]{1,0:T(8,128)(2,1)S(1)} %copy-done, bf16[576,768]{1,0:T(8,128)(2,1)} %copy-done.13, bf16[576,768]{1,0:T(8,128)(2,1)} %get-tuple-element.344, bf16[576,384]{1,0:T(8,128)(2,1)} %get-tuple-element.206, bf16[576,384]{1,0:T(8,128)(2,1)} %get-tuple-element.200), kind=kOutput, calls=%fused_computation.1 | convolution fusion | flops 2049048576 | bytes 7962624 | tf_op jit(solution)/shard_map/dot_general | solution.py:716
  219.1 6.4 %square_mine.1 = (bf16[2,1,192,768]{3,2,1,0:T(8,128)(2,1)}, bf16[2,1,192,768]{3,2,1,0:T(8,128)(2,1)}, bf16[2,1,192,768]{3,2,1,0:T(8,128)(2,1)}, bf16[2,1,192,768]{3,2,1,0:T(8,128)(2,1)}) custom-call(s32[3]{0:T(128)} %pad_add_fusion.1.at_ref, bf16[576,1536]{1,0:T(8,128)(2,1)} %pad_maximum_fusion.1.left_ref, ...), custom_call_target="tpu_custom_call" | custom-call | flops 1358954496 | bytes 6000000 | tf_op jit(solution)/shard_map/square_mine/pallas_call | solution.py:413
  225.8 2.6 collective-permute-start.20
  229.6 2.4 fusion.17
  235.6 3.1 fusion.21
  238.7 6.2 %collective-permute-done.21 = bf16[2,2,48,768]{3,2,1,0:T(8,128)(2,1)S(1)} collective-permute-done((bf16[2,2,48,768]{3,2,1,0:T(8,128)(2,1)S(1)}, bf16[2,2,48,768]{3,2,1,0:T(8,128)(2,1)S(1)}, u32[]{:S(2)}, u32[]{:S(2)}) %collective-permute-start.21) | collective-permute-done | bytes 294944 | tf_op jit(solution)/shard_map/ppermute | solution.py:539
  249.5 4.0 %collective-permute-start.29 = (f32[72,128]{1,0:T(8,128)S(1)}, f32[72,128]{1,0:T(8,128)S(1)}, u32[]{:S(2)}, u32[]{:S(2)}) collective-permute-start(f32[72,128]{1,0:T(8,128)S(1)} %bitcast.185), channel_id=1, source_target_pairs={{0,8},{8,0},{2,10},{10,2},{4,12},{12,4},{6,14},{14,6},{32,40},{40,... | collective-permute-start | bytes 110600 | tf_op jit(solution)/shard_map/ppermute | solution.py:539
  254.4 4.2 %collective-permute-done.27 = bf16[1,192,768]{2,1,0:T(8,128)(2,1)S(1)} collective-permute-done((bf16[1,192,768]{2,1,0:T(8,128)(2,1)S(1)}, bf16[1,192,768]{2,1,0:T(8,128)(2,1)S(1)}, u32[]{:S(2)}, u32[]{:S(2)}) %collective-permute-start.27) | collective-permute-done | bytes 294944 | tf_op jit(solution)/shard_map/ppermute | solution.py:539
  265.1 2.3 collective-permute-done.31
  267.5 6.4 %collective-permute-start.41 = (bf16[2,2,192,768]{3,2,1,0:T(8,128)(2,1)S(1)}, bf16[2,2,192,768]{3,2,1,0:T(8,128)(2,1)S(1)}, u32[]{:S(2)}, u32[]{:S(2)}) collective-permute-start(bf16[2,2,192,768]{3,2,1,0:T(8,128)(2,1)S(1)} %pad_maximum_fusion.6.refs_0_), channel_id=1, source_target_pairs={{0,8},{8,0},{1,9},{9,1},{2,10},{10,2},{3,11},{11,3},{4,12},{12,4},... | collective-permute-start | bytes 3538952 | tf_op jit(solution)/shard_map/ppermute | solution.py:561
  274.0 3.5 collective-permute-done.35
  279.0 2.9 collective-permute-done.33
  282.7 3.7 collective-permute-done.34
  286.8 4.3 %collective-permute-done.40 = f32[72,128]{1,0:T(8,128)S(1)} collective-permute-done((f32[72,128]{1,0:T(8,128)S(1)}, f32[72,128]{1,0:T(8,128)S(1)}, u32[]{:S(2)}, u32[]{:S(2)}) %collective-permute-start.40) | collective-permute-done | bytes 36896 | tf_op jit(solution)/shard_map/ppermute | solution.py:539
  291.1 3.5 collective-permute-done.38
  294.6 3.2 collective-permute-done.39
  298.7 14.5 %collective-permute-start.46 = (bf16[2,2,192,768]{3,2,1,0:T(8,128)(2,1)S(1)}, bf16[2,2,192,768]{3,2,1,0:T(8,128)(2,1)S(1)}, u32[]{:S(2)}, u32[]{:S(2)}) collective-permute-start(bf16[2,2,192,768]{3,2,1,0:T(8,128)(2,1)S(1)} %collective-permute-done.36.refs_1_), channel_id=1, source_target_pairs={{0,8},{8,0},{1,9},{9,1},{2,10},{10,2},{3,11},{11,3},{4,12},{12,4},... | collective-permute-start | bytes 3538952 | tf_op jit(solution)/shard_map/ppermute | solution.py:561
  318.3 6.1 %collective-permute-done.44 = bf16[2,1,48,768]{3,2,0,1:T(8,128)(2,1)S(1)} collective-permute-done((bf16[2,1,48,768]{3,2,0,1:T(8,128)(2,1)S(1)}, bf16[2,1,48,768]{3,2,0,1:T(8,128)(2,1)S(1)}, u32[]{:S(2)}, u32[]{:S(2)}) %collective-permute-start.44) | collective-permute-done | bytes 147488 | tf_op jit(solution)/shard_map/ppermute | solution.py:539
  327.5 13.2 %place_ff.1 = (f32[768,3072]{1,0:T(8,128)}, f32[3072,768]{1,0:T(8,128)}) custom-call(s32[3]{0:T(128)} %pad_add_fusion.1.at_ref, bf16[2,2,192,768]{3,2,1,0:T(8,128)(2,1)} %copy-done.7, bf16[2,2,192,768]{3,2,1,0:T(8,128)(2,1)} %copy-done.22, bf16[2,2,192,768]{3,2,1,0:T(8,128)(2,1)} %copy-done.24, bf16[2,2,192,768]{3,2,1,0:T(8,128)(2,1)} %copy-done.26, ...), custom_call_target="tpu_custom_call" | custom-call | bytes 40000000 | tf_op jit(solution)/shard_map/place_ff/pallas_call | solution.py:456
  347.0 2.2 collective-permute-start.53
  349.2 2.5 collective-permute-done.53
  351.7 2.6 collective-permute-done.51.refs_1_
  354.4 3.6 collective-permute-start.56
  359.6 2.2 collective-permute-start.59
  361.9 6.1 %collective-permute-start.60 = (bf16[144,1536]{1,0:T(8,128)(2,1)}, bf16[144,1536]{1,0:T(8,128)(2,1)}, u32[]{:S(2)}, u32[]{:S(2)}) collective-permute-start(bf16[144,1536]{1,0:T(8,128)(2,1)} %get-tuple-element.350), channel_id=1, source_target_pairs={{2,0},{3,8},{0,1},{1,9},{4,3},{5,11},{10,4},{11,12},{8,5},{9,13},{... | collective-permute-start | bytes 1327112 | tf_op jit(solution)/shard_map/ppermute | solution.py:520
  369.9 2.1 collective-permute-start.62
  373.5 7.7 %place_squares.1 = (f32[768,2304]{1,0:T(8,128)}, f32[768,768]{1,0:T(8,128)}) custom-call(s32[3]{0:T(128)} %pad_add_fusion.1.at_ref, bf16[2,1,192,768]{3,2,1,0:T(8,128)(2,1)} %copy-done.17, bf16[2,1,192,768]{3,2,1,0:T(8,128)(2,1)} %copy-done.36, bf16[2,1,192,768]{3,2,1,0:T(8,128)(2,1)} %copy-done.38, bf16[2,1,192,768]{3,2,1,0:T(8,128)(2,1)} %copy-done.40, ...), custom_call_target="tpu_custom_call" | custom-call | bytes 20000000 | tf_op jit(solution)/shard_map/place_squares/pallas_call | solution.py:480
  381.2 7.3 %collective-permute-done.58 = f32[72,128]{1,0:T(8,128)} collective-permute-done((f32[72,128]{1,0:T(8,128)}, f32[72,128]{1,0:T(8,128)}, u32[]{:S(2)}, u32[]{:S(2)}) %collective-permute-start.58) | collective-permute-done | bytes 36896 | tf_op jit(solution)/shard_map/ppermute | solution.py:539
  (334 shorter events, 102.0 us)
Async XLA Ops:
  3.4 16.9 %collective-permute-start = (bf16[144,1664]{1,0:T(8,128)(2,1)S(1)}, bf16[144,1664]{1,0:T(8,128)(2,1)S(1)}, u32[]{:S(2)}, u32[]{:S(2)}) collective-permute-start(bf16[144,1664]{1,0:T(8,128)(2,1)S(1)} %get-tuple-element.352), channel_id=1, source_target_pairs={{0,0},{8,1},{2,4},{10,5},{3,2},{11,3},{4,8},{12,9},{6,12},{14,13},... | collective-permute-start | bytes 1437704 | tf_op jit(solution)/shard_map/ppermute | solution.py:512
  9.5 14.0 %collective-permute-start.1 = (bf16[144,1664]{1,0:T(8,128)(2,1)S(1)}, bf16[144,1664]{1,0:T(8,128)(2,1)S(1)}, u32[]{:S(2)}, u32[]{:S(2)}) collective-permute-start(bf16[144,1664]{1,0:T(8,128)(2,1)S(1)} %get-tuple-element.355), channel_id=1, source_target_pairs={{0,2},{8,3},{1,0},{9,1},{3,4},{11,5},{4,10},{12,11},{5,8},{13,9},{... | collective-permute-start | bytes 1437704 | tf_op jit(solution)/shard_map/ppermute | solution.py:512
  13.2 20.5 %collective-permute-start.2 = (bf16[144,1664]{1,0:T(8,128)(2,1)S(1)}, bf16[144,1664]{1,0:T(8,128)(2,1)S(1)}, u32[]{:S(2)}, u32[]{:S(2)}) collective-permute-start(bf16[144,1664]{1,0:T(8,128)(2,1)S(1)} %get-tuple-element.354), channel_id=1, source_target_pairs={{0,4},{8,5},{1,2},{9,3},{2,0},{10,1},{4,12},{12,13},{5,10},{13,11}... | collective-permute-start | bytes 1437704 | tf_op jit(solution)/shard_map/ppermute | solution.py:512
  19.0 14.7 %collective-permute-start.3 = (bf16[144,1664]{1,0:T(8,128)(2,1)S(1)}, bf16[144,1664]{1,0:T(8,128)(2,1)S(1)}, u32[]{:S(2)}, u32[]{:S(2)}) collective-permute-start(bf16[144,1664]{1,0:T(8,128)(2,1)S(1)} %get-tuple-element.353), channel_id=1, source_target_pairs={{1,4},{9,5},{2,2},{10,3},{3,0},{11,1},{5,12},{13,13},{6,10},{14,11... | collective-permute-start | bytes 1437704 | tf_op jit(solution)/shard_map/ppermute | solution.py:512
  40.3 7.4 %collective-permute-start.4 = (bf16[576,1536]{1,0:T(8,128)(2,1)}, bf16[576,1536]{1,0:T(8,128)(2,1)}, u32[]{:S(2)}, u32[]{:S(2)}) collective-permute-start(bf16[576,1536]{1,0:T(8,128)(2,1)} %slice.239), channel_id=1, source_target_pairs={{0,8},{8,0},{1,9},{9,1},{2,10},{10,2},{3,11},{11,3},{4,12},{12,4},... | collective-permute-start | bytes 5308424 | tf_op jit(solution)/shard_map/ppermute | solution.py:670
  91.3 17.5 %collective-permute-start.5 = (bf16[1536,768]{1,0:T(8,128)(2,1)}, bf16[1536,768]{1,0:T(8,128)(2,1)}, u32[]{:S(2)}, u32[]{:S(2)}) collective-permute-start(bf16[1536,768]{1,0:T(8,128)(2,1)} %get-tuple-element.174), channel_id=1, source_target_pairs={{0,8},{8,0},{1,9},{9,1},{2,10},{10,2},{3,11},{11,3},{4,12},{12,4},... | collective-permute-start | bytes 7077896 | tf_op jit(solution)/shard_map/ppermute | solution.py:561
  91.4 17.4 %collective-permute-start.6 = (bf16[1536,768]{1,0:T(8,128)(2,1)}, bf16[1536,768]{1,0:T(8,128)(2,1)}, u32[]{:S(2)}, u32[]{:S(2)}) collective-permute-start(bf16[1536,768]{1,0:T(8,128)(2,1)} %get-tuple-element.175), channel_id=1, source_target_pairs={{0,8},{8,0},{1,9},{9,1},{2,10},{10,2},{3,11},{11,3},{4,12},{12,4},... | collective-permute-start | bytes 7077896 | tf_op jit(solution)/shard_map/ppermute | solution.py:561
  118.4 16.6 %collective-permute-start.7 = (bf16[2,2,192,768]{3,2,1,0:T(8,128)(2,1)}, bf16[2,2,192,768]{3,2,1,0:T(8,128)(2,1)}, u32[]{:S(2)}, u32[]{:S(2)}) collective-permute-start(bf16[2,2,192,768]{3,2,1,0:T(8,128)(2,1)} %get-tuple-element.189), channel_id=1, source_target_pairs={{0,32},{8,104},{2,34},{10,106},{4,36},{12,108},{6,38},{14,110},{32... | collective-permute-start | bytes 3538952 | tf_op jit(solution)/shard_map/ppermute | solution.py:539
  121.1 16.6 %collective-permute-start.8 = (bf16[2,2,192,768]{3,2,1,0:T(8,128)(2,1)}, bf16[2,2,192,768]{3,2,1,0:T(8,128)(2,1)}, u32[]{:S(2)}, u32[]{:S(2)}) collective-permute-start(bf16[2,2,192,768]{3,2,1,0:T(8,128)(2,1)} %get-tuple-element.190), channel_id=1, source_target_pairs={{0,2},{8,14},{2,0},{10,12},{4,6},{12,10},{6,4},{14,8},{32,34},{40,... | collective-permute-start | bytes 3538952 | tf_op jit(solution)/shard_map/ppermute | solution.py:539
  141.8 17.5 %collective-permute-start.10 = (bf16[2,192,768]{2,1,0:T(8,128)(2,1)S(1)}, bf16[2,192,768]{2,1,0:T(8,128)(2,1)}, u32[]{:S(2)}, u32[]{:S(2)}) collective-permute-start(bf16[2,192,768]{2,1,0:T(8,128)(2,1)S(1)} %slice_bitcast_fusion), channel_id=1, source_target_pairs={{0,6},{8,10},{2,4},{10,8},{4,2},{12,14},{6,0},{14,12},{32,38},{40,... | collective-permute-start | bytes 1769480 | tf_op jit(solution)/shard_map/ppermute | solution.py:539
  143.6 15.7 %collective-permute-start.9 = (bf16[2,192,768]{2,1,0:T(8,128)(2,1)}, bf16[2,192,768]{2,1,0:T(8,128)(2,1)}, u32[]{:S(2)}, u32[]{:S(2)}) collective-permute-start(bf16[2,192,768]{2,1,0:T(8,128)(2,1)} %slice_bitcast_fusion.1), channel_id=1, source_target_pairs={{0,96},{8,40},{2,98},{10,42},{4,100},{12,44},{6,102},{14,46},{32,6... | collective-permute-start | bytes 1769480 | tf_op jit(solution)/shard_map/ppermute | solution.py:539
  159.3 26.3 %collective-permute-start.14 = (bf16[576,1536]{1,0:T(8,128)(2,1)}, bf16[576,1536]{1,0:T(8,128)(2,1)}, u32[]{:S(2)}, u32[]{:S(2)}) collective-permute-start(bf16[576,1536]{1,0:T(8,128)(2,1)} %pad_maximum_fusion.2), channel_id=1, source_target_pairs={{0,8},{8,0},{1,9},{9,1},{2,10},{10,2},{3,11},{11,3},{4,12},{12,4},... | collective-permute-start | bytes 5308424 | tf_op jit(solution)/shard_map/ppermute | solution.py:561
  165.9 16.8 %collective-permute-start.11 = (bf16[2,2,48,768]{3,2,1,0:T(8,128)(2,1)S(1)}, bf16[2,2,48,768]{3,2,1,0:T(8,128)(2,1)S(1)}, u32[]{:S(2)}, u32[]{:S(2)}) collective-permute-start(bf16[2,2,48,768]{3,2,1,0:T(8,128)(2,1)S(1)} %get-tuple-element.361), channel_id=1, source_target_pairs={{0,16},{8,25},{2,18},{10,27},{4,20},{12,29},{6,22},{14,31},{32,48}... | collective-permute-start | bytes 884744 | tf_op jit(solution)/shard_map/ppermute | solution.py:539
  170.2 12.6 %collective-permute-start.12 = (bf16[2,2,48,768]{3,2,1,0:T(8,128)(2,1)S(1)}, bf16[2,2,48,768]{3,2,1,0:T(8,128)(2,1)S(1)}, u32[]{:S(2)}, u32[]{:S(2)}) collective-permute-start(bf16[2,2,48,768]{3,2,1,0:T(8,128)(2,1)S(1)} %get-tuple-element.362), channel_id=1, source_target_pairs={{0,17},{8,24},{2,19},{10,26},{4,21},{12,28},{6,23},{14,30},{32,49}... | collective-permute-start | bytes 884744 | tf_op jit(solution)/shard_map/ppermute | solution.py:539
  170.2 14.7 %collective-permute-start.13 = (bf16[2,2,48,768]{3,2,1,0:T(8,128)(2,1)S(1)}, bf16[2,2,48,768]{3,2,1,0:T(8,128)(2,1)S(1)}, u32[]{:S(2)}, u32[]{:S(2)}) collective-permute-start(bf16[2,2,48,768]{3,2,1,0:T(8,128)(2,1)S(1)} %get-tuple-element.360), channel_id=1, source_target_pairs={{0,1},{8,9},{2,3},{10,11},{4,5},{12,13},{6,7},{14,15},{32,33},{40,... | collective-permute-start | bytes 884744 | tf_op jit(solution)/shard_map/ppermute | solution.py:539
  200.3 16.0 %collective-permute-start.17 = (bf16[1536,768]{1,0:T(8,128)(2,1)}, bf16[1536,768]{1,0:T(8,128)(2,1)}, u32[]{:S(2)}, u32[]{:S(2)}) collective-permute-start(bf16[1536,768]{1,0:T(8,128)(2,1)} %square_away.1), channel_id=1, source_target_pairs={{0,8},{8,0},{1,9},{9,1},{2,10},{10,2},{3,11},{11,3},{4,12},{12,4},... | collective-permute-start | bytes 7077896 | tf_op jit(solution)/shard_map/ppermute | solution.py:561
  217.2 8.3 %collective-permute-start.18 = (bf16[2,48,768]{2,1,0:T(8,128)(2,1)}, bf16[2,48,768]{2,1,0:T(8,128)(2,1)S(1)}, u32[]{:S(2)}, u32[]{:S(2)}) collective-permute-start(bf16[2,48,768]{2,1,0:T(8,128)(2,1)} %get-tuple-element.369), channel_id=1, source_target_pairs={{0,6},{8,10},{2,4},{10,8},{4,2},{12,14},{6,0},{14,12},{32,38},{40,... | collective-permute-start | bytes 442376 | tf_op jit(solution)/shard_map/ppermute | solution.py:539
  225.8 12.9 %collective-permute-start.20 = (bf16[2,2,48,768]{3,2,1,0:T(8,128)(2,1)S(1)}, bf16[2,2,48,768]{3,2,1,0:T(8,128)(2,1)S(1)}, u32[]{:S(2)}, u32[]{:S(2)}) collective-permute-start(bf16[2,2,48,768]{3,2,1,0:T(8,128)(2,1)S(1)} %get-tuple-element.340), channel_id=1, source_target_pairs={{0,16},{8,25},{2,18},{10,27},{4,20},{12,29},{6,22},{14,31},{32,48}... | collective-permute-start | bytes 884744 | tf_op jit(solution)/shard_map/ppermute | solution.py:539
  228.3 16.5 %collective-permute-start.21 = (bf16[2,2,48,768]{3,2,1,0:T(8,128)(2,1)S(1)}, bf16[2,2,48,768]{3,2,1,0:T(8,128)(2,1)S(1)}, u32[]{:S(2)}, u32[]{:S(2)}) collective-permute-start(bf16[2,2,48,768]{3,2,1,0:T(8,128)(2,1)S(1)} %get-tuple-element.340), channel_id=1, source_target_pairs={{0,17},{8,24},{2,19},{10,26},{4,21},{12,28},{6,23},{14,30},{32,49}... | collective-permute-start | bytes 884744 | tf_op jit(solution)/shard_map/ppermute | solution.py:539
  228.3 16.5 %collective-permute-start.22 = (bf16[2,2,48,768]{3,2,1,0:T(8,128)(2,1)S(1)}, bf16[2,2,48,768]{3,2,1,0:T(8,128)(2,1)S(1)}, u32[]{:S(2)}, u32[]{:S(2)}) collective-permute-start(bf16[2,2,48,768]{3,2,1,0:T(8,128)(2,1)S(1)} %get-tuple-element.340), channel_id=1, source_target_pairs={{0,1},{8,9},{2,3},{10,11},{4,5},{12,13},{6,7},{14,15},{32,33},{40,... | collective-permute-start | bytes 884744 | tf_op jit(solution)/shard_map/ppermute | solution.py:539
  232.0 12.8 %collective-permute-start.23 = (bf16[2,1,192,768]{3,2,1,0:T(8,128)(2,1)S(1)}, bf16[2,1,192,768]{3,2,1,0:T(8,128)(2,1)S(1)}, u32[]{:S(2)}, u32[]{:S(2)}) collective-permute-start(bf16[2,1,192,768]{3,2,1,0:T(8,128)(2,1)S(1)} %copy-done.65), channel_id=1, source_target_pairs={{0,32},{8,104},{2,34},{10,106},{4,36},{12,108},{6,38},{14,110},{32... | collective-permute-start | bytes 1769480 | tf_op jit(solution)/shard_map/ppermute | solution.py:539
  234.0 10.8 %collective-permute-start.24 = (bf16[2,1,192,768]{3,2,1,0:T(8,128)(2,1)S(1)}, bf16[2,1,192,768]{3,2,1,0:T(8,128)(2,1)S(1)}, u32[]{:S(2)}, u32[]{:S(2)}) collective-permute-start(bf16[2,1,192,768]{3,2,1,0:T(8,128)(2,1)S(1)} %copy-done.64), channel_id=1, source_target_pairs={{0,2},{8,14},{2,0},{10,12},{4,6},{12,10},{6,4},{14,8},{32,34},{40,... | collective-permute-start | bytes 1769480 | tf_op jit(solution)/shard_map/ppermute | solution.py:539
  246.3 13.0 %collective-permute-start.25 = (bf16[2,192,768]{2,1,0:T(8,128)(2,1)S(1)}, bf16[2,192,768]{2,1,0:T(8,128)(2,1)S(1)}, u32[]{:S(2)}, u32[]{:S(2)}) collective-permute-start(bf16[2,192,768]{2,1,0:T(8,128)(2,1)S(1)} %bitcast.164), channel_id=1, source_target_pairs={{0,96},{8,40},{2,98},{10,42},{4,100},{12,44},{6,102},{14,46},{32,6... | collective-permute-start | bytes 1769480 | tf_op jit(solution)/shard_map/ppermute | solution.py:539
  247.1 12.2 %collective-permute-start.26 = (bf16[2,192,768]{2,1,0:T(8,128)(2,1)S(1)}, bf16[2,192,768]{2,1,0:T(8,128)(2,1)S(1)}, u32[]{:S(2)}, u32[]{:S(2)}) collective-permute-start(bf16[2,192,768]{2,1,0:T(8,128)(2,1)S(1)} %bitcast.166), channel_id=1, source_target_pairs={{0,6},{8,10},{2,4},{10,8},{4,2},{12,14},{6,0},{14,12},{32,38},{40,... | collective-permute-start | bytes 1769480 | tf_op jit(solution)/shard_map/ppermute | solution.py:539
  247.1 11.5 %collective-permute-start.27 = (bf16[1,192,768]{2,1,0:T(8,128)(2,1)S(1)}, bf16[1,192,768]{2,1,0:T(8,128)(2,1)S(1)}, u32[]{:S(2)}, u32[]{:S(2)}) collective-permute-start(bf16[1,192,768]{2,1,0:T(8,128)(2,1)S(1)} %slice_bitcast_fusion.3), channel_id=1, source_target_pairs={{0,96},{8,40},{2,98},{10,42},{4,100},{12,44},{6,102},{14,46},{32,6... | collective-permute-start | bytes 884744 | tf_op jit(solution)/shard_map/ppermute | solution.py:539
  248.0 11.3 %collective-permute-start.28 = (bf16[1,192,768]{2,1,0:T(8,128)(2,1)S(1)}, bf16[1,192,768]{2,1,0:T(8,128)(2,1)S(1)}, u32[]{:S(2)}, u32[]{:S(2)}) collective-permute-start(bf16[1,192,768]{2,1,0:T(8,128)(2,1)S(1)} %slice_bitcast_fusion.2), channel_id=1, source_target_pairs={{0,6},{8,10},{2,4},{10,8},{4,2},{12,14},{6,0},{14,12},{32,38},{40,... | collective-permute-start | bytes 884744 | tf_op jit(solution)/shard_map/ppermute | solution.py:539
  262.9 35.0 %collective-permute-start.36 = (bf16[2,2,192,768]{3,2,1,0:T(8,128)(2,1)S(1)}, bf16[2,2,192,768]{3,2,1,0:T(8,128)(2,1)S(1)}, u32[]{:S(2)}, u32[]{:S(2)}) collective-permute-start(bf16[2,2,192,768]{3,2,1,0:T(8,128)(2,1)S(1)} %pad_maximum_fusion.6.refs_0_), channel_id=1, source_target_pairs={{0,32},{8,104},{2,34},{10,106},{4,36},{12,108},{6,38},{14,110},{32... | collective-permute-start | bytes 3538952 | tf_op jit(solution)/shard_map/ppermute | solution.py:539
  263.6 34.2 %collective-permute-start.37 = (bf16[2,2,192,768]{3,2,1,0:T(8,128)(2,1)S(1)}, bf16[2,2,192,768]{3,2,1,0:T(8,128)(2,1)S(1)}, u32[]{:S(2)}, u32[]{:S(2)}) collective-permute-start(bf16[2,2,192,768]{3,2,1,0:T(8,128)(2,1)S(1)} %pad_maximum_fusion.7.refs_4_), channel_id=1, source_target_pairs={{0,2},{8,14},{2,0},{10,12},{4,6},{12,10},{6,4},{14,8},{32,34},{40,... | collective-permute-start | bytes 3538952 | tf_op jit(solution)/shard_map/ppermute | solution.py:539
  267.5 30.4 %collective-permute-start.41 = (bf16[2,2,192,768]{3,2,1,0:T(8,128)(2,1)S(1)}, bf16[2,2,192,768]{3,2,1,0:T(8,128)(2,1)S(1)}, u32[]{:S(2)}, u32[]{:S(2)}) collective-permute-start(bf16[2,2,192,768]{3,2,1,0:T(8,128)(2,1)S(1)} %pad_maximum_fusion.6.refs_0_), channel_id=1, source_target_pairs={{0,8},{8,0},{1,9},{9,1},{2,10},{10,2},{3,11},{11,3},{4,12},{12,4},... | collective-permute-start | bytes 3538952 | tf_op jit(solution)/shard_map/ppermute | solution.py:561
  273.9 24.0 %collective-permute-start.42 = (bf16[2,2,192,768]{3,2,1,0:T(8,128)(2,1)S(1)}, bf16[2,2,192,768]{3,2,1,0:T(8,128)(2,1)S(1)}, u32[]{:S(2)}, u32[]{:S(2)}) collective-permute-start(bf16[2,2,192,768]{3,2,1,0:T(8,128)(2,1)S(1)} %pad_maximum_fusion.7.refs_4_), channel_id=1, source_target_pairs={{0,8},{8,0},{1,9},{9,1},{2,10},{10,2},{3,11},{11,3},{4,12},{12,4},... | collective-permute-start | bytes 3538952 | tf_op jit(solution)/shard_map/ppermute | solution.py:561
  298.7 25.7 %collective-permute-start.46 = (bf16[2,2,192,768]{3,2,1,0:T(8,128)(2,1)S(1)}, bf16[2,2,192,768]{3,2,1,0:T(8,128)(2,1)S(1)}, u32[]{:S(2)}, u32[]{:S(2)}) collective-permute-start(bf16[2,2,192,768]{3,2,1,0:T(8,128)(2,1)S(1)} %collective-permute-done.36.refs_1_), channel_id=1, source_target_pairs={{0,8},{8,0},{1,9},{9,1},{2,10},{10,2},{3,11},{11,3},{4,12},{12,4},... | collective-permute-start | bytes 3538952 | tf_op jit(solution)/shard_map/ppermute | solution.py:561
  313.2 11.2 %collective-permute-start.47 = (bf16[2,2,192,768]{3,2,1,0:T(8,128)(2,1)S(1)}, bf16[2,2,192,768]{3,2,1,0:T(8,128)(2,1)S(1)}, u32[]{:S(2)}, u32[]{:S(2)}) collective-permute-start(bf16[2,2,192,768]{3,2,1,0:T(8,128)(2,1)S(1)} %collective-permute-done.37.refs_5_), channel_id=1, source_target_pairs={{0,8},{8,0},{1,9},{9,1},{2,10},{10,2},{3,11},{11,3},{4,12},{12,4},... | collective-permute-start | bytes 3538952 | tf_op jit(solution)/shard_map/ppermute | solution.py:561
  314.1 10.2 %collective-permute-start.44 = (bf16[2,1,48,768]{3,2,0,1:T(8,128)(2,1)S(1)}, bf16[2,1,48,768]{3,2,0,1:T(8,128)(2,1)S(1)}, u32[]{:S(2)}, u32[]{:S(2)}) collective-permute-start(bf16[2,1,48,768]{3,2,0,1:T(8,128)(2,1)S(1)} %maximum_add_fusion.3), channel_id=1, source_target_pairs={{0,17},{8,24},{2,19},{10,26},{4,21},{12,28},{6,23},{14,30},{32,49}... | collective-permute-start | bytes 442376 | tf_op jit(solution)/shard_map/ppermute | solution.py:539
  314.7 9.6 %collective-permute-start.45 = (bf16[2,1,48,768]{3,2,0,1:T(8,128)(2,1)S(1)}, bf16[2,1,48,768]{3,2,0,1:T(8,128)(2,1)S(1)}, u32[]{:S(2)}, u32[]{:S(2)}) collective-permute-start(bf16[2,1,48,768]{3,2,0,1:T(8,128)(2,1)S(1)} %maximum_add_fusion.3), channel_id=1, source_target_pairs={{0,1},{8,9},{2,3},{10,11},{4,5},{12,13},{6,7},{14,15},{32,33},{40,... | collective-permute-start | bytes 442376 | tf_op jit(solution)/shard_map/ppermute | solution.py:539
  325.9 14.9 %collective-permute-start.48 = (bf16[1,192,768]{2,1,0:T(8,128)(2,1)S(1)}, bf16[1,192,768]{2,1,0:T(8,128)(2,1)}, u32[]{:S(2)}, u32[]{:S(2)}) collective-permute-start(bf16[1,192,768]{2,1,0:T(8,128)(2,1)S(1)} %bitcast.170), channel_id=1, source_target_pairs={{0,96},{8,40},{2,98},{10,42},{4,100},{12,44},{6,102},{14,46},{32,6... | collective-permute-start | bytes 884744 | tf_op jit(solution)/shard_map/ppermute | solution.py:539
  325.9 14.9 %collective-permute-start.49 = (bf16[1,192,768]{2,1,0:T(8,128)(2,1)S(1)}, bf16[1,192,768]{2,1,0:T(8,128)(2,1)}, u32[]{:S(2)}, u32[]{:S(2)}) collective-permute-start(bf16[1,192,768]{2,1,0:T(8,128)(2,1)S(1)} %bitcast.172), channel_id=1, source_target_pairs={{0,6},{8,10},{2,4},{10,8},{4,2},{12,14},{6,0},{14,12},{32,38},{40,... | collective-permute-start | bytes 884744 | tf_op jit(solution)/shard_map/ppermute | solution.py:539
  325.9 14.8 %collective-permute-start.50 = (f32[72,128]{1,0:T(8,128)}, f32[72,128]{1,0:T(8,128)}, u32[]{:S(2)}, u32[]{:S(2)}) collective-permute-start(f32[72,128]{1,0:T(8,128)} %add.364), channel_id=1, source_target_pairs={{0,32},{8,40},{2,34},{10,42},{4,36},{12,44},{6,38},{14,46},{32,0},... | collective-permute-start | bytes 110600 | tf_op jit(solution)/shard_map/ppermute | solution.py:539
  343.9 10.4 %collective-permute-start.51 = (bf16[2,1,192,768]{3,2,1,0:T(8,128)(2,1)S(1)}, bf16[2,1,192,768]{3,2,1,0:T(8,128)(2,1)S(1)}, u32[]{:S(2)}, u32[]{:S(2)}) collective-permute-start(bf16[2,1,192,768]{3,2,1,0:T(8,128)(2,1)S(1)} %pad_maximum_fusion.9.refs_0_), channel_id=1, source_target_pairs={{0,32},{8,104},{2,34},{10,106},{4,36},{12,108},{6,38},{14,110},{32... | collective-permute-start | bytes 1769480 | tf_op jit(solution)/shard_map/ppermute | solution.py:539
  344.0 10.3 %collective-permute-start.52 = (bf16[2,1,192,768]{3,2,1,0:T(8,128)(2,1)S(1)}, bf16[2,1,192,768]{3,2,1,0:T(8,128)(2,1)S(1)}, u32[]{:S(2)}, u32[]{:S(2)}) collective-permute-start(bf16[2,1,192,768]{3,2,1,0:T(8,128)(2,1)S(1)} %pad_maximum_fusion.10.refs_4_), channel_id=1, source_target_pairs={{0,2},{8,14},{2,0},{10,12},{4,6},{12,10},{6,4},{14,8},{32,34},{40,... | collective-permute-start | bytes 1769480 | tf_op jit(solution)/shard_map/ppermute | solution.py:539
  345.4 8.9 %collective-permute-start.54 = (bf16[2,1,192,768]{3,2,1,0:T(8,128)(2,1)S(1)}, bf16[2,1,192,768]{3,2,1,0:T(8,128)(2,1)S(1)}, u32[]{:S(2)}, u32[]{:S(2)}) collective-permute-start(bf16[2,1,192,768]{3,2,1,0:T(8,128)(2,1)S(1)} %pad_maximum_fusion.9.refs_0_), channel_id=1, source_target_pairs={{0,8},{8,0},{1,9},{9,1},{2,10},{10,2},{3,11},{11,3},{4,12},{12,4},... | collective-permute-start | bytes 1769480 | tf_op jit(solution)/shard_map/ppermute | solution.py:561
  347.0 7.3 %collective-permute-start.55 = (bf16[2,1,192,768]{3,2,1,0:T(8,128)(2,1)S(1)}, bf16[2,1,192,768]{3,2,1,0:T(8,128)(2,1)S(1)}, u32[]{:S(2)}, u32[]{:S(2)}) collective-permute-start(bf16[2,1,192,768]{3,2,1,0:T(8,128)(2,1)S(1)} %pad_maximum_fusion.10.refs_4_), channel_id=1, source_target_pairs={{0,8},{8,0},{1,9},{9,1},{2,10},{10,2},{3,11},{11,3},{4,12},{12,4},... | collective-permute-start | bytes 1769480 | tf_op jit(solution)/shard_map/ppermute | solution.py:561
  354.4 15.5 %collective-permute-start.56 = (bf16[2,1,192,768]{3,2,1,0:T(8,128)(2,1)S(1)}, bf16[2,1,192,768]{3,2,1,0:T(8,128)(2,1)S(1)}, u32[]{:S(2)}, u32[]{:S(2)}) collective-permute-start(bf16[2,1,192,768]{3,2,1,0:T(8,128)(2,1)S(1)} %collective-permute-done.51.refs_1_), channel_id=1, source_target_pairs={{0,8},{8,0},{1,9},{9,1},{2,10},{10,2},{3,11},{11,3},{4,12},{12,4},... | collective-permute-start | bytes 1769480 | tf_op jit(solution)/shard_map/ppermute | solution.py:561
  358.0 14.6 %collective-permute-start.57 = (bf16[2,1,192,768]{3,2,1,0:T(8,128)(2,1)S(1)}, bf16[2,1,192,768]{3,2,1,0:T(8,128)(2,1)S(1)}, u32[]{:S(2)}, u32[]{:S(2)}) collective-permute-start(bf16[2,1,192,768]{3,2,1,0:T(8,128)(2,1)S(1)} %collective-permute-done.52.refs_5_), channel_id=1, source_target_pairs={{0,8},{8,0},{1,9},{9,1},{2,10},{10,2},{3,11},{11,3},{4,12},{12,4},... | collective-permute-start | bytes 1769480 | tf_op jit(solution)/shard_map/ppermute | solution.py:561
  359.6 29.6 %collective-permute-start.59 = (bf16[144,1536]{1,0:T(8,128)(2,1)}, bf16[144,1536]{1,0:T(8,128)(2,1)}, u32[]{:S(2)}, u32[]{:S(2)}) collective-permute-start(bf16[144,1536]{1,0:T(8,128)(2,1)} %get-tuple-element.351), channel_id=1, source_target_pairs={{0,0},{1,8},{4,2},{5,10},{2,3},{3,11},{8,4},{9,12},{12,6},{13,14},... | collective-permute-start | bytes 1327112 | tf_op jit(solution)/shard_map/ppermute | solution.py:520
  361.9 27.4 %collective-permute-start.60 = (bf16[144,1536]{1,0:T(8,128)(2,1)}, bf16[144,1536]{1,0:T(8,128)(2,1)}, u32[]{:S(2)}, u32[]{:S(2)}) collective-permute-start(bf16[144,1536]{1,0:T(8,128)(2,1)} %get-tuple-element.350), channel_id=1, source_target_pairs={{2,0},{3,8},{0,1},{1,9},{4,3},{5,11},{10,4},{11,12},{8,5},{9,13},{... | collective-permute-start | bytes 1327112 | tf_op jit(solution)/shard_map/ppermute | solution.py:520
  368.0 21.7 %collective-permute-start.61 = (bf16[144,1536]{1,0:T(8,128)(2,1)}, bf16[144,1536]{1,0:T(8,128)(2,1)}, u32[]{:S(2)}, u32[]{:S(2)}) collective-permute-start(bf16[144,1536]{1,0:T(8,128)(2,1)} %get-tuple-element.349), channel_id=1, source_target_pairs={{4,0},{5,8},{2,1},{3,9},{0,2},{1,10},{12,4},{13,12},{10,5},{11,13}... | collective-permute-start | bytes 1327112 | tf_op jit(solution)/shard_map/ppermute | solution.py:520
  369.9 19.8 %collective-permute-start.62 = (bf16[144,1536]{1,0:T(8,128)(2,1)}, bf16[144,1536]{1,0:T(8,128)(2,1)}, u32[]{:S(2)}, u32[]{:S(2)}) collective-permute-start(bf16[144,1536]{1,0:T(8,128)(2,1)} %get-tuple-element.348), channel_id=1, source_target_pairs={{4,1},{5,9},{2,2},{3,10},{0,3},{1,11},{12,5},{13,13},{10,6},{11,14... | collective-permute-start | bytes 1327112 | tf_op jit(solution)/shard_map/ppermute | solution.py:520
  373.5 15.0 %collective-permute-start.58 = (f32[72,128]{1,0:T(8,128)}, f32[72,128]{1,0:T(8,128)}, u32[]{:S(2)}, u32[]{:S(2)}) collective-permute-start(f32[72,128]{1,0:T(8,128)} %add.366), channel_id=1, source_target_pairs={{0,16},{8,24},{2,18},{10,26},{4,20},{12,28},{6,22},{14,30},{32,48}... | collective-permute-start | bytes 110600 | tf_op jit(solution)/shard_map/ppermute | solution.py:539
  (82 other events, 555.6 us)

commit v4 on v1

v4 whole, which is shorter than its diff:
```python
import functools
import itertools
import math

import jax
import jax.numpy as jnp
from jax import lax
from jax.experimental import pallas as pl
from jax.experimental.pallas import tpu as pltpu
from jax.sharding import Mesh
from jax.sharding import PartitionSpec as P

HEADS = 12
HEAD_DIM = 64
VIEW_TOK = 128
VIEWS_MAX = 8
D = 768
FF = 3072
BLK = 144
SLOTS = 4
ROWS = BLK * SLOTS
KEYS = 2 * ROWS
PAIRS = HEADS // 2
LANES = 128
FCHUNK = 768
QROWS = 288
QUARTER = D // 4
NF = FF // FCHUNK

bf16 = jnp.bfloat16
f32 = jnp.float32
epsilon = 1e-05
masked_score = -1e30
GELU_C = math.sqrt(2.0 / math.pi)
GELU_A = 0.044715

AXES = ("y", "xl", "c", "z", "xh")
VMEM_LIMIT = 60 * 1024 * 1024


def mm(a, b):
    return lax.dot_general(a, b, (((1,), (0,)), ((), ())), preferred_element_type=f32)


def mm_nt(a, b):
    return lax.dot_general(a, b, (((1,), (1,)), ((), ())), preferred_element_type=f32)


def mm_tn(a, b):
    return lax.dot_general(a, b, (((0,), (0,)), ((), ())), preferred_element_type=f32)


def lane_row(at, first, last):
    lane = lax.broadcasted_iota(jnp.int32, (1, LANES), 1)
    return jnp.where((lane >= first) & (lane < last), 1.0, 0.0).astype(at)


def attention_forward_kernel(q_ref, ko_ref, vo_ref, ks_ref, vs_ref, mask_ref, p_ref, o_ref, linv_ref, att_ref):
    half = [lane_row(bf16, 0, 64), lane_row(bf16, 64, 128)]
    unit = [lane_row(bf16, 64, 65), lane_row(bf16, 0, 1)]
    q = q_ref[...]
    k = jnp.concatenate([ko_ref[...], ks_ref[...]], axis=0)
    v = jnp.concatenate([vo_ref[...], vs_ref[...]], axis=0)
    mask = mask_ref[...]
    lane = lax.broadcasted_iota(jnp.int32, (QROWS, LANES), 1)
    q_now = [q * half[h] + unit[h] for h in range(2)]
    k_now = [k * half[h] + mask * unit[h] for h in range(2)]
    v_now = [v * half[h] + unit[h] for h in range(2)]
    items = [(slice(s * QROWS, (s + 1) * QROWS), h) for s in range(ROWS // QROWS) for h in range(2)]
    done = {}

    def product(number, weights):
        rows, h = items[number]
        out = mm(weights, v_now[h])
        inv = 1.0 / (out[:, 64:65] if h == 0 else out[:, 0:1])
        done[h] = (out * inv, jnp.broadcast_to(inv, (QROWS, LANES)))
        if h == 1:
            out = jnp.where(lane < 64, done[0][0], done[1][0])
            o_ref[rows, :] = out
            att_ref[rows, :] = out.astype(bf16)
            linv_ref[rows, :] = jnp.where(lane < 64, done[0][1], done[1][1])

    scores = mm_nt(q_now[0][items[0][0]], k_now[0])
    before = None
    for number, (rows, h) in enumerate(items):
        following = None
        if number + 1 < len(items):
            next_rows, next_h = items[number + 1]
            following = mm_nt(q_now[next_h][next_rows], k_now[next_h])
        top = jnp.max(scores, axis=1, keepdims=True)
        weights = jnp.exp((scores - top) * 0.125).astype(bf16)
        p_ref[h, rows, :] = weights
        if before is not None:
            product(number - 1, before)
        before, scores = weights, following
    product(len(items) - 1, before)


def head_columns(base):
    return pl.BlockSpec((ROWS, LANES), lambda i, f=base: (0, f + i))


def attention_forward(queries, own, sibling, mask):
    col = head_columns
    return pl.pallas_call(
        attention_forward_kernel,
        grid=(PAIRS,),
        in_specs=[col(0), col(0), col(PAIRS), col(0), col(PAIRS), pl.BlockSpec((KEYS, LANES), lambda i: (0, 0))],
        out_specs=[pl.BlockSpec((2, ROWS, KEYS), lambda i: (i, 0, 0)), col(0), col(0), col(0)],
        out_shape=[
            jax.ShapeDtypeStruct((HEADS, ROWS, KEYS), bf16),
            jax.ShapeDtypeStruct((ROWS, D), f32),
            jax.ShapeDtypeStruct((ROWS, D), f32),
            jax.ShapeDtypeStruct((ROWS, D), bf16),
        ],
        compiler_params=pltpu.CompilerParams(vmem_limit_bytes=VMEM_LIMIT),
        cost_estimate=pl.CostEstimate(flops=16 * ROWS * KEYS * D, bytes_accessed=20_000_000, transcendentals=HEADS * ROWS * KEYS),
        name="attention_forward",
    )(queries, own, own, sibling, sibling, mask)


def attention_backward_kernel(
    at_ref, q_ref, ko_ref, vo_ref, ks_ref, vs_ref, p_ref, o_ref, linv_ref, g_ref, gq_ref, gown_ref, sent_ref
):
    half = [lane_row(bf16, 0, 64), lane_row(bf16, 64, 128)]
    two = [lane_row(bf16, 64, 66), lane_row(bf16, 0, 2)]
    lane = lax.broadcasted_iota(jnp.int32, (ROWS, LANES), 1)
    k = jnp.concatenate([ko_ref[...], ks_ref[...]], axis=0)
    v = jnp.concatenate([vo_ref[...], vs_ref[...]], axis=0)
    gs = g_ref[...].astype(f32) * linv_ref[...]
    prod = gs * o_ref[...]
    g_now, v_now = [], []
    for h in range(2):
        mine = (lane < 64) if h == 0 else (lane >= 64)
        base = 64 if h == 0 else 0
        delta = jnp.sum(jnp.where(mine, prod, 0.0), axis=1, keepdims=True)
        high = delta.astype(bf16).astype(f32)
        columns = jnp.where(lane == base, -high, jnp.where(lane == base + 1, high - delta, 0.0))
        g_now.append(jnp.where(mine, gs, columns).astype(bf16))
        v_now.append(v * half[h] + two[h])
    g_turned, q_turned = gs.astype(bf16).T, q_ref[...].T
    head = lambda turned, h: turned[64 * h : 64 * h + 64]
    grad_score = lambda h, diff: (p_ref[h].astype(f32) * diff).astype(bf16)
    diff = mm_nt(g_now[0], v_now[0])
    gv0 = mm(head(g_turned, 0), p_ref[0])
    gs0 = grad_score(0, diff)
    diff = mm_nt(g_now[1], v_now[1])
    gv1 = mm(head(g_turned, 1), p_ref[1])
    gs1 = grad_score(1, diff)
    gk0, gq0 = mm(head(q_turned, 0), gs0), mm(gs0, k)
    gk1, gq1 = mm(head(q_turned, 1), gs1), mm(gs1, k)
    gq = (jnp.where(lane < 64, gq0, gq1) * 0.125).astype(bf16)
    gk = (jnp.concatenate([gk0, gk1], axis=0) * 0.125).T.astype(bf16)
    gv = jnp.concatenate([gv0, gv1], axis=0).T.astype(bf16)
    gq_ref[...] = gq
    gown_ref[0], gown_ref[1] = gk[:ROWS], gv[:ROWS]
    sent_ref[0], sent_ref[1] = gk[ROWS:], gv[ROWS:]
    sent_ref[2] = jnp.where(at_ref[0] == 0, gv[:ROWS], gk[:ROWS])
    sent_ref[3] = gq


def attention_backward(at, queries, own, sibling, weights, heads_out, linv, grad_att):
    col = lambda base: pl.BlockSpec((ROWS, LANES), lambda i, at: (0, base + i))
    several = lambda count: pl.BlockSpec((count, ROWS, LANES), lambda i, at: (0, 0, i))
    return pl.pallas_call(
        attention_backward_kernel,
        grid_spec=pltpu.PrefetchScalarGridSpec(
            num_scalar_prefetch=1, grid=(PAIRS,),
            in_specs=[
                col(0), col(0), col(PAIRS), col(0), col(PAIRS),
                pl.BlockSpec((2, ROWS, KEYS), lambda i, at: (i, 0, 0)),
                col(0), col(0), col(0),
            ],
            out_specs=[col(0), several(2), several(4)],
        ),
        out_shape=[jax.ShapeDtypeStruct(shape, bf16) for shape in ((ROWS, D), (2, ROWS, D), (4, ROWS, D))],
        compiler_params=pltpu.CompilerParams(vmem_limit_bytes=VMEM_LIMIT),
        cost_estimate=pl.CostEstimate(flops=32 * ROWS * KEYS * D, bytes_accessed=25_000_000, transcendentals=0),
        name="attention_backward",
    )(at, queries, own, own, sibling, sibling, weights, heads_out, linv, grad_att)


def quarter_blocks(place, core):
    first = 1 + 2 * core
    return place, place ^ (4 - first), place ^ first, place ^ 2


def quarter_rows(block):
    return pl.ds(pl.multiple_of(block * QUARTER, QUARTER), QUARTER)


def put_quarters(ref, buffer, place, core):
    for index, block in enumerate(quarter_blocks(place, core)):
        ref[index, 0] = buffer[quarter_rows(block), :]


def feed_forward_kernel(
    at_ref, att_ref, x_ref, g_ref, ow_ref, vec_ref, upb_ref, up_ref, down_ref,
    out_ref, gh_ref, gb_ref, gatt_ref, up_other_ref, up_mine_ref, down_other_ref, down_mine_ref, vecg_ref, upbg_ref,
    hidden, xhat, rstd_s, normed2, y_acc, gn_acc, buffer,
):
    step = pl.program_id(0)
    out_bias, gain, shift, down_bias = (vec_ref[r : r + 1, :] for r in range(4))

    @pl.when(step == 0)
    def _():
        h = x_ref[...].astype(f32) + mm(att_ref[...], ow_ref[...]) + out_bias
        hidden[...] = h
        centred = h - jnp.mean(h, axis=1, keepdims=True)
        rstd = lax.rsqrt(jnp.mean(centred * centred, axis=1, keepdims=True) + epsilon)
        xh = centred * rstd
        xhat[...] = xh
        rstd_s[...] = jnp.broadcast_to(rstd, (ROWS, LANES))
        normed2[...] = (xh * gain + shift).astype(bf16)
        y_acc[...] = jnp.zeros_like(y_acc)
        gn_acc[...] = jnp.zeros_like(gn_acc)

    g = g_ref[...]
    n2 = normed2[...]
    u = mm(n2, up_ref[...]) + upb_ref[0]
    ga = mm_nt(g, down_ref[...])
    u2 = u * u
    t = jnp.tanh(u * (GELU_C + (GELU_C * GELU_A) * u2))
    hp = 0.5 + 0.5 * t
    active = (u * hp).astype(bf16)
    slope = hp + (0.5 * u) * (1.0 - t * t) * (GELU_C + (3.0 * GELU_C * GELU_A) * u2)
    gu = (ga * slope).astype(bf16)
    y_acc[...] += mm(active, down_ref[...])
    gn_acc[...] += mm_nt(gu, up_ref[...])
    upbg_ref[0] = jnp.sum(gu.astype(f32), axis=0, keepdims=True)
    for part, value, other_ref, mine_ref in (
        (0, mm_tn(n2, gu), up_other_ref, up_mine_ref), (1, mm_tn(active, g), down_other_ref, down_mine_ref),
    ):
        buffer[...] = value.astype(bf16)

        @pl.when(step < NF // 2)
        def _():
            put_quarters(other_ref, buffer, at_ref[1 + part], 1 - at_ref[0])

        @pl.when(step >= NF // 2)
        def _():
            put_quarters(mine_ref, buffer, at_ref[1 + part], at_ref[0])

    @pl.when(step == NF - 1)
    def _():
        out_ref[...] = (hidden[...] + y_acc[...] + down_bias).astype(bf16)
        gn = gn_acc[...]
        xh = xhat[...]
        gf = g_ref[...].astype(f32)
        vecg_ref[...] = jnp.zeros_like(vecg_ref)
        vecg_ref[1:2, :] = jnp.sum(gn * xh, axis=0, keepdims=True)
        vecg_ref[2:3, :] = jnp.sum(gn, axis=0, keepdims=True)
        vecg_ref[3:4, :] = jnp.sum(gf, axis=0, keepdims=True)
        gx = gn * gain
        mean1 = jnp.mean(gx, axis=1, keepdims=True)
        mean2 = jnp.mean(gx * xh, axis=1, keepdims=True)
        gh = gf + rstd_s[:, 0:1] * (gx - mean1 - xh * mean2)
        gh_ref[...] = gh
        vecg_ref[0:1, :] = jnp.sum(gh, axis=0, keepdims=True)
        gb = gh.astype(bf16)
        gb_ref[...] = gb
        gatt_ref[...] = mm_nt(gb, ow_ref[...]).astype(bf16)


def whole(*shape):
    return pl.BlockSpec(shape, lambda s, at: (0,) * len(shape))


TOKEN_SPEC = pl.BlockSpec((ROWS, D), lambda s, at: (0, 0))
COTANGENT_SPEC = pl.BlockSpec((ROWS, D), lambda s, at: (0, 1))


def feed_forward(at, attended, both, out_w, vecs, up_b, up_w, down_w):
    shape = jax.ShapeDtypeStruct
    chunk = lambda s, at: (2 * (1 - at[0]) + s) % NF
    other = pl.BlockSpec((4, 1, QUARTER, D), lambda s, at: (0, jnp.minimum(s, NF // 2 - 1), 0, 0))
    mine = pl.BlockSpec((4, 1, QUARTER, D), lambda s, at: (0, jnp.maximum(s - NF // 2, 0), 0, 0))
    return pl.pallas_call(
        feed_forward_kernel,
        grid_spec=pltpu.PrefetchScalarGridSpec(
            num_scalar_prefetch=1,
            grid=(NF,),
            in_specs=[
                whole(ROWS, D), TOKEN_SPEC, COTANGENT_SPEC, whole(D, D), whole(8, D),
                pl.BlockSpec((1, 1, FCHUNK), lambda s, at: (chunk(s, at), 0, 0)),
                pl.BlockSpec((D, FCHUNK), lambda s, at: (0, chunk(s, at))),
                pl.BlockSpec((FCHUNK, D), lambda s, at: (chunk(s, at), 0)),
            ],
            out_specs=[whole(ROWS, D)] * 4
            + [other, mine, other, mine, whole(8, D), pl.BlockSpec((1, 1, FCHUNK), lambda s, at: (chunk(s, at), 0, 0))],
            scratch_shapes=[
                pltpu.VMEM((ROWS, D), f32), pltpu.VMEM((ROWS, D), f32), pltpu.VMEM((ROWS, LANES), f32),
                pltpu.VMEM((ROWS, D), bf16), pltpu.VMEM((ROWS, D), f32), pltpu.VMEM((ROWS, D), f32),
                pltpu.VMEM((D, D), bf16),
            ],
        ),
        out_shape=[
            shape((ROWS, D), bf16), shape((ROWS, D), f32), shape((ROWS, D), bf16), shape((ROWS, D), bf16),
        ]
        + [shape((4, NF // 2, QUARTER, D), bf16)] * 4
        + [shape((8, D), f32), shape((NF, 1, FCHUNK), f32)],
        compiler_params=pltpu.CompilerParams(vmem_limit_bytes=VMEM_LIMIT),
        cost_estimate=pl.CostEstimate(flops=12 * ROWS * D * FF, bytes_accessed=30_000_000, transcendentals=ROWS * FF),
        name="feed_forward",
    )(at, attended, both, both, out_w, vecs, up_b, up_w, down_w)


def squares_kernel(
    at_ref, gq_ref, own_ref, other_ref, arrived_ref, arrived_own_ref, arrived_gq_ref, gb_ref, gb_other_ref,
    normed_ref, normed_other_ref, att_ref, att_other_ref, keep0_ref, away0_ref, keep1_ref, away1_ref,
    joined, joined_other, buffer,
):
    core = at_ref[0]

    def product(part, left, left_other, right, right_other):
        buffer[...] = (mm_tn(left[...], right[...]) + mm_tn(left_other[...], right_other[...])).astype(bf16)
        keep_ref, away_ref = ((keep0_ref, away0_ref), (keep1_ref, away1_ref))[part]
        for index, block in enumerate(quarter_blocks(at_ref[1 + part], core)):
            (keep_ref if index < 2 else away_ref)[index % 2, 0] = buffer[quarter_rows(block), :]

    joined[...] = own_ref[0] + arrived_ref[0]
    joined_other[...] = arrived_own_ref[0] + other_ref[0]

    @pl.when(core == 0)
    def _():
        product(0, normed_ref, normed_other_ref, gq_ref, arrived_gq_ref.at[0])
        product(1, normed_ref, normed_other_ref, joined, joined_other)

    @pl.when(core != 0)
    def _():
        product(0, normed_ref, normed_other_ref, joined, joined_other)
        product(1, att_ref, att_other_ref, gb_ref, gb_other_ref)


def squares(at, gq, own, sent, arrived, *pairs):
    rows = whole(ROWS, D)
    pick = pl.BlockSpec((1, ROWS, D), lambda s, at: (at[0], 0, 0))
    number = lambda n: pl.BlockSpec((1, ROWS, D), lambda s, at: (n, 0, 0))
    return pl.pallas_call(
        squares_kernel,
        grid_spec=pltpu.PrefetchScalarGridSpec(
            num_scalar_prefetch=1, grid=(1,),
            in_specs=[rows, pick, pick, pick, number(2), number(3)] + [rows] * 6,
            out_specs=[whole(2, 1, QUARTER, D)] * 4,
            scratch_shapes=[pltpu.VMEM((ROWS, D), bf16), pltpu.VMEM((ROWS, D), bf16), pltpu.VMEM((D, D), bf16)],
        ),
        out_shape=[jax.ShapeDtypeStruct((2, 1, QUARTER, D), bf16)] * 4,
        compiler_params=pltpu.CompilerParams(vmem_limit_bytes=VMEM_LIMIT),
        cost_estimate=pl.CostEstimate(flops=8 * ROWS * D * D, bytes_accessed=13_000_000, transcendentals=0),
        name="squares",
    )(at, gq, own, sent, arrived, arrived, arrived, *pairs)


def input_grad_kernel(
    gq_ref, own_ref, swapped_ref, w_ref, x_ref, gh_ref, gain_ref, vecg_ref, upbg_ref, out_ref, small_ref, right
):
    step = pl.program_id(0)
    right[:, :D] = gq_ref[...]
    right[:, D : 2 * D] = own_ref[0] + swapped_ref[0]
    right[:, 2 * D :] = own_ref[1] + swapped_ref[1]
    grad_normed = mm_nt(right[...], w_ref[...])
    source = x_ref[...].astype(f32)
    centred = source - jnp.mean(source, axis=1, keepdims=True)
    rstd = lax.rsqrt(jnp.mean(centred * centred, axis=1, keepdims=True) + epsilon)
    xhat = centred * rstd
    gx = grad_normed * gain_ref[0:1, :]
    mean1 = jnp.mean(gx, axis=1, keepdims=True)
    mean2 = jnp.mean(gx * xhat, axis=1, keepdims=True)
    out_ref[...] = (gh_ref[...] + rstd * (gx - mean1 - xhat * mean2)).astype(bf16)

    @pl.when(step == 0)
    def _():
        small_ref[...] = jnp.zeros_like(small_ref)
        small_ref[0:4, :] = vecg_ref[0:4, :]
        for f in range(NF):
            small_ref[8 + f : 9 + f, :] = upbg_ref[f]

    small_ref[4:5, :] += jnp.sum(grad_normed * xhat, axis=0, keepdims=True)
    small_ref[5:6, :] += jnp.sum(grad_normed, axis=0, keepdims=True)
    small_ref[6:7, :] += jnp.sum(right[:, :D].astype(f32), axis=0, keepdims=True)
    small_ref[7:8, :] += jnp.sum(right[:, 2 * D :].astype(f32), axis=0, keepdims=True)


def input_gradient(gq, own, swapped, qkv_w, both, grad_hidden, gain, vec_grads, up_b_grad):
    steps = 3
    length = ROWS // steps
    rows = pl.BlockSpec((length, D), lambda s: (s, 0))
    pair = pl.BlockSpec((2, length, D), lambda s: (0, s, 0))
    fixed = lambda *shape: pl.BlockSpec(shape, lambda s: (0,) * len(shape))
    return pl.pallas_call(
        input_grad_kernel,
        grid=(steps,),
        in_specs=[rows, pair, pair, fixed(D, 3 * D), rows, rows, fixed(8, D), fixed(8, D), fixed(NF, 1, FCHUNK)],
        out_specs=[rows, fixed(16, D)],
        out_shape=[jax.ShapeDtypeStruct((ROWS, D), bf16), jax.ShapeDtypeStruct((16, D), f32)],
        scratch_shapes=[pltpu.VMEM((length, 3 * D), bf16)],
        compiler_params=pltpu.CompilerParams(vmem_limit_bytes=VMEM_LIMIT),
        cost_estimate=pl.CostEstimate(flops=6 * ROWS * D * D, bytes_accessed=10_000_000, transcendentals=0),
        name="input_gradient",
    )(gq, own, swapped, qkv_w, both, grad_hidden, gain, vec_grads, up_b_grad)


def place_kernel(mine, late, at_ref, source0_ref, source1_ref, *refs):
    up_ref, down_ref, qkv_ref, out_ref, tiles, sems = refs[-6:]
    half = at_ref[0] if mine else 1 - at_ref[0]
    sources = (source0_ref, source1_ref)
    copies = []

    def send(source, target, condition=None):
        number = len(copies)
        copies.append(None)
        tiles[number] = source.astype(f32)

        def start(to):
            copy = pltpu.make_async_copy(tiles.at[number], to, sems.at[number])
            copy.start()

        if condition is None:
            start(target[0])
        else:
            pl.when(condition)(lambda: start(target[0]))
            pl.when(jnp.logical_not(condition))(lambda: start(target[1]))

    for j in range(2):
        block = 2 * half + j
        columns = pl.ds(pl.multiple_of(block * D, D), D)
        for s in range(2):
            rows = [
                quarter_rows(quarter_blocks(at_ref[1 + part], half)[s + (2 if late else 0)]) for part in range(2)
            ]
            send(sources[0][s, j], [up_ref.at[rows[0], columns]])
            down_rows = pl.ds(pl.multiple_of(block * D + rows[1].start, QUARTER), QUARTER)
            send(sources[1][s, j], [down_ref.at[down_rows, :]])
            if j == 0:
                send(sources[j][s, 2], [qkv_ref.at[rows[j], columns]])
            else:
                columns_qkv = pl.ds(pl.multiple_of(D, D), D)
                send(sources[j][s, 2], [qkv_ref.at[rows[j], columns_qkv], out_ref.at[rows[j], :]], half == 0)
    for number in range(len(copies)):
        pltpu.make_async_copy(tiles.at[number], up_ref.at[pl.ds(0, QUARTER), pl.ds(0, D)], sems.at[number]).wait()


def place(at, pieces, mine, late, before=()):
    shape = jax.ShapeDtypeStruct
    anywhere = pl.BlockSpec(memory_space=pl.ANY)
    return pl.pallas_call(
        functools.partial(place_kernel, mine, late),
        grid_spec=pltpu.PrefetchScalarGridSpec(
            num_scalar_prefetch=1, grid=(1,),
            in_specs=[whole(2, NF // 2 + 1, QUARTER, D)] * 2 + [anywhere] * len(before),
            out_specs=[anywhere] * 4,
            scratch_shapes=[pltpu.VMEM((12, QUARTER, D), f32), pltpu.SemaphoreType.DMA((12,))],
        ),
        out_shape=[shape((D, FF), f32), shape((FF, D), f32), shape((D, 3 * D), f32), shape((D, D), f32)],
        input_output_aliases={3 + index: index for index in range(len(before))},
        compiler_params=pltpu.CompilerParams(vmem_limit_bytes=VMEM_LIMIT),
        cost_estimate=pl.CostEstimate(flops=0, bytes_accessed=11_000_000, transcendentals=0),
        name="place_late" if late else "place_early",
    )(at, *pieces, *before)


def linear(y, xl, c, z, xh):
    return (((y * 2 + xl) * 2 + c) * 4 + z) * 2 + xh


def scene_pairs(slot):
    pairs = []
    for y, xl, z, xh in itertools.product(range(4), range(2), range(4), range(2)):
        block = 2 * z + xh
        scene = (slot - block) % 4
        if scene < 3:
            for c in range(2):
                pairs.append((linear(y, xl, c, z, xh), linear(y, xl, block // 4, scene, c)))
    return pairs


def to_scene(values, block):
    pieces = []
    for slot in range(SLOTS):
        scene = jnp.minimum((slot - block) % 4, 2)
        pieces.append(lax.ppermute(lax.dynamic_index_in_dim(values, scene, 0, keepdims=False), AXES, scene_pairs(slot)))
    return pieces


def send_from_scene(values):
    pieces = []
    for slot in range(SLOTS):
        back = [(target, source) for source, target in scene_pairs(slot)]
        pieces.append(lax.ppermute(values[slot * BLK : (slot + 1) * BLK], AXES, back))
    return pieces


def take_from_scene(pieces, block):
    pieces = jnp.stack(pieces)
    return jnp.stack([lax.dynamic_index_in_dim(pieces, (m + block) % 4, 0, keepdims=False) for m in range(3)])


SWAP = ((0, 1), (1, 0))
MASKS = ((1, 3), (3, 1))


def exchange(value, move):
    pairs = []
    for place in itertools.product(range(4), range(4), range(4), range(2)):
        ends = [linear(y, x % 2, c, z, x // 2) for x, y, z, c in (place, move(*place))]
        pairs.append(tuple(ends))
    return lax.ppermute(value, AXES, pairs)


def meet(value, axis, step):
    def move(x, y, z, c):
        at = {"x": x, "y": y, "z": z}
        at[axis] = at[axis] ^ MASKS[c][step]
        return at["x"], at["y"], at["z"], c

    return exchange(value, move)


def swap(value):
    return lax.ppermute(value, "c", SWAP)


ORDERS = ("yxz", "zyx")


def meet_parts(values, stage, step):
    return [meet(value, ORDERS[part][stage], step) for part, value in enumerate(values)]


def add(*terms):
    return functools.reduce(jnp.add, [term.astype(f32) for term in terms]).astype(bf16)


def block_of(blocks, index):
    return lax.dynamic_index_in_dim(blocks, index, 1, keepdims=False)


def put_block(blocks, value, index):
    return lax.dynamic_update_index_in_dim(blocks, value, index, 1)


SMALL = 16


def meet_with(value, small, axis, step):
    high = lax.reduce_precision(small, 8, 7)
    low = lax.reduce_precision(small - high, 8, 7)
    rows = value.reshape(-1, D)
    message = jnp.concatenate([rows, high.astype(bf16), low.astype(bf16)], axis=0)
    arrived = meet(message, axis, step)
    count = rows.shape[0]
    other = arrived[count : count + SMALL].astype(f32) + arrived[count + SMALL :].astype(f32)
    return arrived[:count].reshape(value.shape), (high + low) + other


def hold(*values):
    return lax.optimization_barrier(values)


def body(
    tokens, view_counts, ln1_gain, ln1_shift, qkv_weight, query_bias, value_bias, out_weight, out_bias,
    ln2_gain, ln2_shift, up_weight, up_bias, down_weight, down_bias, cotangent,
):
    core, z, xh = lax.axis_index("c"), lax.axis_index("z"), lax.axis_index("xh")

    block = 2 * z + xh
    views = jnp.broadcast_to(view_counts.astype(bf16)[:, None, None], (3, BLK, LANES))
    pieces = to_scene(jnp.concatenate([tokens, cotangent, views], axis=2), block)
    both = jnp.concatenate([piece[:, : 2 * D] for piece in pieces], axis=0)
    views = pieces[0][0, 2 * D].astype(f32)
    x = both[:, :D]

    row = jnp.arange(ROWS, dtype=jnp.int32)
    offset = (row // BLK - z) % 4 * BLK + row % BLK
    position = jnp.concatenate([offset + core * ROWS, offset + (1 - core) * ROWS])
    usable = (position.astype(f32) < views * VIEW_TOK) | (position >= VIEWS_MAX * VIEW_TOK)
    mask = jnp.broadcast_to(jnp.where(usable, 0.0, masked_score).astype(bf16)[:, None], (KEYS, LANES))

    source = x.astype(f32)
    centred = source - jnp.mean(source, axis=1, keepdims=True)
    rstd = lax.rsqrt(jnp.mean(centred * centred, axis=1, keepdims=True) + epsilon)
    normed = (centred * rstd * ln1_gain + ln1_shift).astype(bf16)
    product = lambda weight: jnp.dot(normed, weight, preferred_element_type=f32)
    kv_bias = jnp.concatenate([jnp.zeros((D,), f32), value_bias])
    own = (product(qkv_weight[:, D:]) + kv_bias).astype(bf16)
    sibling = swap(own)
    normed_other = swap(normed)
    queries = (product(qkv_weight[:, :D]) + query_bias).astype(bf16)
    weights, heads_out, linv, attended = attention_forward(queries, own, sibling, mask)

    vecs = jnp.concatenate([jnp.stack([out_bias, ln2_gain, ln2_shift, down_bias]), jnp.zeros((4, D), f32)])
    up_b = up_bias.reshape(NF, 1, FCHUNK)
    y = lax.axis_index("y")
    x_place = lax.axis_index("xh") * 2 + lax.axis_index("xl")
    at = jnp.stack([core, y, z]).astype(jnp.int32)
    output, grad_hidden, grad_branch, grad_att, up_other, up_mine, down_other, down_mine, vec_grads, up_b_grad = (
        feed_forward(at, attended, both, out_weight, vecs, up_b, up_weight, down_weight)
    )

    moving = [swap(up_other), swap(down_other)]
    attended_other, branch_other = swap(attended), swap(grad_branch)
    grad_q, grad_own, sent = attention_backward(at, queries, own, sibling, weights, heads_out, linv, grad_att)

    moving, attended_other, branch_other, sent = hold(moving, attended_other, branch_other, sent)
    arrived = swap(sent)
    pieces = [(up_mine, moving[0]), (down_mine, moving[1])]
    away = [add(mine[2:], other[2:]) for mine, other in pieces]
    arrived, away = hold(arrived, away)
    halved = meet_parts(away, 0, 0)
    keep0, away0, keep1, away1 = squares(
        at, grad_q, grad_own, sent, arrived, grad_branch, branch_other, normed, normed_other, attended, attended_other
    )

    away, grad_hidden = hold([away0, away1], grad_hidden)
    square_halved = meet_parts(away, 0, 0)
    gains = jnp.broadcast_to(ln1_gain[None, :], (8, D))
    input_grad, small = input_gradient(
        grad_q, grad_own, arrived, qkv_weight, both, grad_hidden, gains, vec_grads, up_b_grad
    )

    halved, square_halved, small, input_grad = hold(halved, square_halved, small, input_grad)
    away = [add(mine[1], other[1], half[1]) for (mine, other), half in zip(pieces, halved)]
    square_away = [add(keep[1], half[1]) for keep, half in zip((keep0, keep1), square_halved)]
    square_quartered = meet_parts(square_away, 0, 1)
    quartered = meet_parts(away, 0, 1)

    def ring_sum(pieces, halved, quartered):
        return [
            add(mine[0], other[0], half[0], quarter)
            for (mine, other), half, quarter in zip(pieces, halved, quartered)
        ]

    ff_own = ring_sum(pieces, halved, quartered)
    square_quartered, ff_own, small = hold(square_quartered, ff_own, small)
    owns = [add(k[0], h[0], q) for k, h, q in zip((keep0, keep1), square_halved, square_quartered)]
    blocks = [
        jnp.concatenate([f, o], axis=0).reshape(NF // 2 + 1, 4, QUARTER // 4, D) for f, o in zip(ff_own, owns)
    ]
    places = [x_place, y]
    first = 1 + 2 * core
    keep = [(block_of(b, p), block_of(b, p ^ (4 - first))) for b, p in zip(blocks, places)]
    away = [jnp.stack([block_of(b, p ^ first), block_of(b, p ^ 2)]) for b, p in zip(blocks, places)]
    keep, away, small = hold(keep, away, small)
    one_way = meet(away[0], "x", 0)
    other_way, small = meet_with(away[1], small, "y", 0)

    one_way, other_way, small = hold(one_way, other_way, small)
    halved = [one_way, other_way]
    away, small = hold([add(k[1], h[1]) for k, h in zip(keep, halved)], small)
    one_way = meet(away[0], "x", 1)
    other_way, small = meet_with(away[1], small, "y", 1)

    one_way, other_way, small = hold(one_way, other_way, small)
    quartered = [one_way, other_way]
    ends = [add(k[0], h[0], q) for k, h, q in zip(keep, halved, quartered)]
    for step in range(2):
        ends, small = hold(ends, small)
        one_way, small = meet_with(ends[0], small, "z", step)
        other_way = meet(ends[1], "x", step)
        one_way, other_way, small = hold(one_way, other_way, small)
        ends = [ends[0] + one_way, ends[1] + other_way]

    ends, small, output, input_grad = hold(ends, small, output, input_grad)
    one_way, small = meet_with(ends[0], small, "x", 1)
    other_way = meet(ends[1], "y", 1)

    one_way, other_way, small = hold(one_way, other_way, small)
    pairs = [jnp.stack([ends[0], one_way]), jnp.stack([ends[1], other_way])]
    pairs, small = hold(pairs, small)
    one_way, small = meet_with(pairs[0], small, "x", 0)
    other_way = meet(pairs[1], "y", 0)

    one_way, other_way, small = hold(one_way, other_way, small)
    owns = []
    for pair, more, p, empty in zip(pairs, (one_way, other_way), places, blocks):
        full = jnp.zeros_like(empty)
        for value, index in ((pair[0], p), (pair[1], p ^ (4 - first)), (more[0], p ^ first), (more[1], p ^ 2)):
            full = put_block(full, value, index)
        owns.append(full.reshape(NF // 2 + 1, QUARTER, D))
    owns, small, output, input_grad = hold(owns, small, output, input_grad)
    arrived = meet_parts(owns, 0, 1)
    returned = send_from_scene(jnp.concatenate([output, input_grad], axis=1))

    arrived, returned = hold(arrived, returned)
    pairs = [jnp.stack([o, a]) for o, a in zip(owns, arrived)]
    pairs, small = hold(pairs, small)
    got = meet_parts(pairs, 0, 0)
    own_other = [swap(v) for v in pairs]
    small_other = swap(small)
    placed = place(at, pairs, True, False)
    returned = take_from_scene(returned, block)

    own_other, small_other, placed = hold(own_other, small_other, placed)
    small = small + small_other
    placed = place(at, own_other, False, False, placed)
    got, placed, returned = hold(got, placed, returned)
    got_other = [swap(v) for v in got]
    placed = place(at, got, True, True, placed)
    d_up, d_down, d_qkv, d_out = place(at, got_other, False, True, placed)
    return (
        returned[:, :, :D], returned[:, :, D:], small[4], small[5], d_qkv, small[6], small[7], d_out,
        small[0], small[1], small[2], d_up, small[8:12].reshape(FF), d_down, small[3],
    )


def solution(mesh):
    fine = Mesh(mesh.devices.reshape(4, 2, 2, 4, 2), AXES)
    rows = P(("y", "xl", "c"), ("z", "xh"), None)
    placed = (rows, P(("y", "xl", "c"))) + (P(),) * 13 + (rows,)
    return jax.shard_map(
        body, mesh=fine, in_specs=placed, out_specs=(rows, rows) + (P(),) * 13, check_vma=False
    )
```

time: 542 us -> 319 us (0.59)
  starting transfers between devices: 252 us -> 77.9 us
  other arithmetic: 72.3 us -> 21.3 us
  Pallas kernels: 78.7 us -> 110 us
  waiting for transfers between devices: 97 us -> 78.1 us
    ppermute x114 -> x24, starting transfers between devices: 153 us -> 27.3 us  [exchange(): return lax.ppermute(value, AXES, pairs)]
    pallas_call x2 -> x8, Pallas kernels: 53.2 us -> 94.6 us  [the longest x1 33.1 us: feed_forward(): pl.pallas_call(feed_forward_kernel, grid_spec=pltpu.PrefetchScalarGridSpe...]
    convert_element_type x22, other arithmetic: 54.5 us -> 13.7 us  [the longest x14 12.6 us: add(): functools.reduce(jnp.add, [term.astype(f32) for term in terms]).astype(bf16)]
    ppermute x24 -> x16, starting transfers between devices: 71.8 us -> 33.7 us  [the longest x4 26.8 us: send_from_scene(): pieces.append(lax.ppermute(values[slot * BLK:(slot + 1) * BLK], AXES, back))]
    ppermute x114 -> x24, waiting for transfers between devices: 68.4 us -> 45.9 us  [exchange(): return lax.ppermute(value, AXES, pairs)]
    ppermute x8 -> x4, starting transfers between devices: 27.9 us -> 16.9 us  [to_scene(): lax.ppermute(lax.dynamic_index_in_dim(values, scene, 0, keepdims=False),...]
    pallas_call x1, Pallas kernels: 25.5 us -> 15.8 us  [attention_forward(): pl.pallas_call(attention_forward_kernel, grid=(PAIRS,), in_specs=[col(0),...]
    slice x1 -> x0, other arithmetic: 6.39 us -> none  [sum_everywhere(): mine = lax.dynamic_index_in_dim(halves[part], core, 0, keepdims=False)]
  transfers between devices with their start and end apart: 146 -> 44, of which waited for: 61 -> 19; matrix products, arithmetic and copies ran while one was open for 16% -> 8% of each run, Pallas kernels for 4% -> 18%
where the time goes in v4:
time: 319 us; the launch traced here: 314 us
  Pallas kernels  110 us (34%)
  waiting for transfers between devices  78.1 us (24%)
  starting transfers between devices  77.9 us (24%)
  other arithmetic  21.3 us (7%)
  local copies, waits for them, and re-layouts  17.7 us (6%)
  matrix products  5.73 us (2%)
    ppermute x24, waiting for transfers between devices, exchange(): return lax.ppermute(value, AXES, pairs)  45.9 us
    pallas_call x1, Pallas kernels, feed_forward(): pl.pallas_call(feed_forward_kernel, grid_spec=pltpu.PrefetchScalarGridSpe...  33.1 us
    ppermute x24, starting transfers between devices, exchange(): return lax.ppermute(value, AXES, pairs)  27.3 us
    ppermute x4, starting transfers between devices, send_from_scene(): pieces.append(lax.ppermute(values[slot * BLK:(slot + 1) * BLK], AXES, back))  26.8 us
    pallas_call x4, Pallas kernels, place(): pl.pallas_call(functools.partial(place_kernel, mine, late), grid_spec=plt...  23.1 us
    pallas_call x1, Pallas kernels, attention_backward(): pl.pallas_call(attention_backward_kernel, grid_spec=pltpu.PrefetchScalarG...  19.4 us
    ppermute x4, starting transfers between devices, to_scene(): lax.ppermute(lax.dynamic_index_in_dim(values, scene, 0, keepdims=False),...  16.9 us
    ppermute x4, waiting for transfers between devices, send_from_scene(): pieces.append(lax.ppermute(values[slot * BLK:(slot + 1) * BLK], AXES, back))  16.3 us
  transfers between devices with their start and end apart: 44, of which 19 were waited for; matrix products, arithmetic and copies ran while one was open for 8% of the time, Pallas kernels for 18%

profile of v4, /device:TPU:1, one launch (start us, length us, event | category | flops | bytes accessed | tf_op | source)
XLA Modules:
  0.0 313.7 jit_solution(11710397590113845094)
XLA Ops:
  3.2 6.0 %collective-permute-start = (bf16[144,1664]{1,0:T(8,128)(2,1)S(1)}, bf16[144,1664]{1,0:T(8,128)(2,1)S(1)}, u32[]{:S(2)}, u32[]{:S(2)}) collective-permute-start(bf16[144,1664]{1,0:T(8,128)(2,1)S(1)} %get-tuple-element.292), channel_id=1, source_target_pairs={{0,0},{8,1},{2,4},{10,5},{3,2},{11,3},{4,8},{12,9},{6,12},{14,13},... | collective-permute-start | bytes 1437704 | tf_op jit(solution)/shard_map/ppermute | solution.py:481
  10.5 7.6 %collective-permute-start.2 = (bf16[144,1664]{1,0:T(8,128)(2,1)S(1)}, bf16[144,1664]{1,0:T(8,128)(2,1)S(1)}, u32[]{:S(2)}, u32[]{:S(2)}) collective-permute-start(bf16[144,1664]{1,0:T(8,128)(2,1)S(1)} %get-tuple-element.294), channel_id=1, source_target_pairs={{0,4},{8,5},{1,2},{9,3},{2,0},{10,1},{4,12},{12,13},{5,10},{13,11}... | collective-permute-start | bytes 1437704 | tf_op jit(solution)/shard_map/ppermute | solution.py:481
  18.1 1.9 collective-permute-start.1
  20.2 4.1 %collective-permute-done.3 = bf16[144,1664]{1,0:T(8,128)(2,1)S(1)} collective-permute-done((bf16[144,1664]{1,0:T(8,128)(2,1)S(1)}, bf16[144,1664]{1,0:T(8,128)(2,1)S(1)}, u32[]{:S(2)}, u32[]{:S(2)}) %collective-permute-start.3) | collective-permute-done | bytes 479264 | tf_op jit(solution)/shard_map/ppermute | solution.py:481
  24.2 5.3 %collective-permute-done.2 = bf16[144,1664]{1,0:T(8,128)(2,1)S(1)} collective-permute-done((bf16[144,1664]{1,0:T(8,128)(2,1)S(1)}, bf16[144,1664]{1,0:T(8,128)(2,1)S(1)}, u32[]{:S(2)}, u32[]{:S(2)}) %collective-permute-start.2) | collective-permute-done | bytes 479264 | tf_op jit(solution)/shard_map/ppermute | solution.py:481
  29.6 5.1 %collective-permute-done.1 = bf16[144,1664]{1,0:T(8,128)(2,1)S(1)} collective-permute-done((bf16[144,1664]{1,0:T(8,128)(2,1)S(1)}, bf16[144,1664]{1,0:T(8,128)(2,1)S(1)}, u32[]{:S(2)}, u32[]{:S(2)}) %collective-permute-start.1) | collective-permute-done | bytes 479264 | tf_op jit(solution)/shard_map/ppermute | solution.py:481
  37.5 2.8 add_convert_fusion.ko_ref.vo_ref
  47.8 3.0 add_convert_fusion.3.q_ref
  51.6 15.8 %attention_forward.1 = (bf16[12,576,1152]{2,1,0:T(8,128)(2,1)}, f32[576,768]{1,0:T(8,128)}, f32[576,768]{1,0:T(8,128)}, bf16[576,768]{1,0:T(8,128)(2,1)}) custom-call(bf16[576,768]{1,0:T(8,128)(2,1)} %add_convert_fusion.3.q_ref, bf16[576,1536]{1,0:T(8,128)(2,1)} %add_convert_fusion.ko_ref.vo_ref, bf16[576,1536]{1,0:T(8,128)(2,1)} %add_convert_fusion.ko_ref.vo_ref, ...), custom_call_target="tpu_custom_call" | custom-call | flops 8153726976 | bytes 20000000 | tf_op jit(solution)/shard_map/attention_forward/pallas_call | solution.py:105
  67.5 33.1 %feed_forward.1 = (bf16[576,768]{1,0:T(8,128)(2,1)}, f32[576,768]{1,0:T(8,128)}, bf16[576,768]{1,0:T(8,128)(2,1)}, bf16[576,768]{1,0:T(8,128)(2,1)}, bf16[4,2,19...) custom-call(s32[3]{0:T(128)} %pad_add_fusion.1.at_ref, ...), custom_call_target="tpu_custom_call" | custom-call | flops 16307453952 | bytes 30000000 | tf_op jit(solution)/shard_map/feed_forward/pallas_call | solution.py:278
  101.8 19.4 %attention_backward.1 = (bf16[576,768]{1,0:T(8,128)(2,1)}, bf16[2,576,768]{2,1,0:T(8,128)(2,1)}, bf16[4,576,768]{2,1,0:T(8,128)(2,1)}) custom-call(s32[3]{0:T(128)} %pad_add_fusion.1.at_ref, bf16[576,768]{1,0:T(8,128)(2,1)} %add_convert_fusion.3.q_ref, bf16[576,1536]{1,0:T(8,128)(2,1)} %add_convert_fusion.ko_ref.vo_ref, ...), custom_call_target="tpu_custom_call" | custom-call | flops 16307453952 | bytes 25000000 | tf_op jit(solution)/shard_map/attention_backward/pallas_call | solution.py:165
  123.4 3.1 add_convert_fusion.2
  126.5 2.6 add_convert_fusion.1
  129.1 1.5 collective-permute-done.9.arrived_ref.arrived_own_ref.arrived_gq_ref.swapped_ref
  130.6 2.7 collective-permute-start.11
  133.3 10.3 %squares.1 = (bf16[2,1,192,768]{3,2,1,0:T(8,128)(2,1)}, bf16[2,1,192,768]{3,2,1,0:T(8,128)(2,1)}, bf16[2,1,192,768]{3,2,1,0:T(8,128)(2,1)}, bf16[2,1,192,768]{3,2,1,0:T(8,128)(2,1)}) custom-call(s32[3]{0:T(128)} %pad_add_fusion.1.at_ref, bf16[576,768]{1,0:T(8,128)(2,1)} %get-tuple-element.151.gq_ref, bf16[2,576,768]{2,1,0:T(8,128)(2,1)} %get-tuple-element.152.own_ref, ...), custom_call_target="tpu_custom_call" | custom-call | flops 2717908992 | bytes 13000000 | tf_op jit(solution)/shard_map/squares/pallas_call | solution.py:339
  143.6 1.9 collective-permute-start.13
  147.5 8.8 %input_gradient.1 = (bf16[576,768]{1,0:T(8,128)(2,1)}, f32[16,768]{1,0:T(8,128)}) custom-call(bf16[576,768]{1,0:T(8,128)(2,1)} %get-tuple-element.151.gq_ref, bf16[2,576,768]{2,1,0:T(8,128)(2,1)} %get-tuple-element.152.own_ref, bf16[4,576,768]{2,1,0:T(8,128)(2,1)} %copy-done, bf16[768,2304]{1,0:T(8,128)(2,1)} %w_ref.1, bf16[576,1536]{1,0:T(8,128)(2,1)} %copy-done.1, ...), custom_call_target="tpu_custom_call" | custom-call | flops 2038431744 | bytes 10000000 | tf_op jit(solution)/shard_map/input_gradient/pallas_call | solution.py:390
  156.4 1.8 fusion.11
  161.4 1.5 collective-permute-start.15
  163.0 4.3 %collective-permute-done.18 = bf16[2,192,768]{2,1,0:T(8,128)(2,1)S(1)} collective-permute-done((bf16[2,192,768]{2,1,0:T(8,128)(2,1)S(1)}, bf16[2,192,768]{2,1,0:T(8,128)(2,1)S(1)}, u32[]{:S(2)}, u32[]{:S(2)}) %collective-permute-start.18) | collective-permute-done | bytes 589856 | tf_op jit(solution)/shard_map/ppermute | solution.py:507
  167.3 1.7 fusion.7
  171.3 1.8 collective-permute-done.15
  174.5 2.4 collective-permute-start.20
  176.9 4.5 %collective-permute-start.19 = (bf16[2,3,48,768]{3,2,1,0:T(8,128)(2,1)S(1)}, bf16[2,3,48,768]{3,2,1,0:T(8,128)(2,1)S(1)}, u32[]{:S(2)}, u32[]{:S(2)}) collective-permute-start(bf16[2,3,48,768]{3,2,1,0:T(8,128)(2,1)S(1)} %pad_maximum_fusion.10), channel_id=1, source_target_pairs={{0,16},{8,25},{2,18},{10,27},{4,20},{12,29},{6,22},{14,31},{32,48}... | collective-permute-start | bytes 1327112 | tf_op jit(solution)/shard_map/ppermute | solution.py:507
  181.4 2.1 collective-permute-done.20
  183.6 3.6 %collective-permute-done.19 = bf16[2,3,48,768]{3,2,1,0:T(8,128)(2,1)S(1)} collective-permute-done((bf16[2,3,48,768]{3,2,1,0:T(8,128)(2,1)S(1)}, bf16[2,3,48,768]{3,2,1,0:T(8,128)(2,1)S(1)}, u32[]{:S(2)}, u32[]{:S(2)}) %collective-permute-start.19) | collective-permute-done | bytes 442400 | tf_op jit(solution)/shard_map/ppermute | solution.py:507
  187.5 5.5 %collective-permute-done.22 = bf16[176,768]{1,0:T(8,128)(2,1)S(1)} collective-permute-done((bf16[176,768]{1,0:T(8,128)(2,1)S(1)}, bf16[176,768]{1,0:T(8,128)(2,1)S(1)}, u32[]{:S(2)}, u32[]{:S(2)}) %collective-permute-start.22) | collective-permute-done | bytes 270368 | tf_op jit(solution)/shard_map/ppermute | solution.py:507
  194.0 2.4 collective-permute-start.24
  196.4 3.5 %collective-permute-done.23 = bf16[176,768]{1,0:T(8,128)(2,1)S(1)} collective-permute-done((bf16[176,768]{1,0:T(8,128)(2,1)S(1)}, bf16[176,768]{1,0:T(8,128)(2,1)S(1)}, u32[]{:S(2)}, u32[]{:S(2)}) %collective-permute-start.23) | collective-permute-done | bytes 270368 | tf_op jit(solution)/shard_map/ppermute | solution.py:507
  200.4 5.2 %collective-permute-done.25 = bf16[176,768]{1,0:T(8,128)(2,1)S(1)} collective-permute-done((bf16[176,768]{1,0:T(8,128)(2,1)S(1)}, bf16[176,768]{1,0:T(8,128)(2,1)S(1)}, u32[]{:S(2)}, u32[]{:S(2)}) %collective-permute-start.25) | collective-permute-done | bytes 270368 | tf_op jit(solution)/shard_map/ppermute | solution.py:507
  206.8 4.6 %collective-permute-done.27 = bf16[176,768]{1,0:T(8,128)(2,1)S(1)} collective-permute-done((bf16[176,768]{1,0:T(8,128)(2,1)S(1)}, bf16[176,768]{1,0:T(8,128)(2,1)S(1)}, u32[]{:S(2)}, u32[]{:S(2)}) %collective-permute-start.27) | collective-permute-done | bytes 270368 | tf_op jit(solution)/shard_map/ppermute | solution.py:507
  211.6 1.8 collective-permute-start.30
  213.6 2.5 collective-permute-start.29
  216.2 9.2 %collective-permute-done.29 = bf16[320,768]{1,0:T(8,128)(2,1)S(1)} collective-permute-done((bf16[320,768]{1,0:T(8,128)(2,1)S(1)}, bf16[320,768]{1,0:T(8,128)(2,1)S(1)}, u32[]{:S(2)}, u32[]{:S(2)}) %collective-permute-start.29) | collective-permute-done | bytes 491552 | tf_op jit(solution)/shard_map/ppermute | solution.py:507
  227.5 14.1 %collective-permute-start.36 = (bf16[144,1536]{1,0:T(8,128)(2,1)S(1)}, bf16[144,1536]{1,0:T(8,128)(2,1)S(1)}, u32[]{:S(2)}, u32[]{:S(2)}) collective-permute-start(bf16[144,1536]{1,0:T(8,128)(2,1)S(1)} %get-tuple-element.288), channel_id=1, source_target_pairs={{4,1},{5,9},{2,2},{3,10},{0,3},{1,11},{12,5},{13,13},{10,6},{11,14... | collective-permute-start | bytes 1327112 | tf_op jit(solution)/shard_map/ppermute | solution.py:489
  243.0 5.5 %collective-permute-start.35 = (bf16[144,1536]{1,0:T(8,128)(2,1)S(1)}, bf16[144,1536]{1,0:T(8,128)(2,1)S(1)}, u32[]{:S(2)}, u32[]{:S(2)}) collective-permute-start(bf16[144,1536]{1,0:T(8,128)(2,1)S(1)} %get-tuple-element.289), channel_id=1, source_target_pairs={{4,0},{5,8},{2,1},{3,9},{0,2},{1,10},{12,4},{13,12},{10,5},{11,13}... | collective-permute-start | bytes 1327112 | tf_op jit(solution)/shard_map/ppermute | solution.py:489
  248.4 4.0 %collective-permute-start.34 = (bf16[144,1536]{1,0:T(8,128)(2,1)S(1)}, bf16[144,1536]{1,0:T(8,128)(2,1)S(1)}, u32[]{:S(2)}, u32[]{:S(2)}) collective-permute-start(bf16[144,1536]{1,0:T(8,128)(2,1)S(1)} %get-tuple-element.290), channel_id=1, source_target_pairs={{2,0},{3,8},{0,1},{1,9},{4,3},{5,11},{10,4},{11,12},{8,5},{9,13},{... | collective-permute-start | bytes 1327112 | tf_op jit(solution)/shard_map/ppermute | solution.py:489
  252.5 3.2 %collective-permute-start.33 = (bf16[144,1536]{1,0:T(8,128)(2,1)S(1)}, bf16[144,1536]{1,0:T(8,128)(2,1)S(1)}, u32[]{:S(2)}, u32[]{:S(2)}) collective-permute-start(bf16[144,1536]{1,0:T(8,128)(2,1)S(1)} %get-tuple-element.291), channel_id=1, source_target_pairs={{0,0},{1,8},{4,2},{5,10},{2,3},{3,11},{8,4},{9,12},{12,6},{13,14},... | collective-permute-start | bytes 1327112 | tf_op jit(solution)/shard_map/ppermute | solution.py:489
  255.7 6.8 %collective-permute-done.35 = bf16[144,1536]{1,0:T(8,128)(2,1)S(1)} collective-permute-done((bf16[144,1536]{1,0:T(8,128)(2,1)S(1)}, bf16[144,1536]{1,0:T(8,128)(2,1)S(1)}, u32[]{:S(2)}, u32[]{:S(2)}) %collective-permute-start.35) | collective-permute-done | bytes 442400 | tf_op jit(solution)/shard_map/ppermute | solution.py:489
  262.5 9.5 %collective-permute-done.33 = bf16[144,1536]{1,0:T(8,128)(2,1)S(1)} collective-permute-done((bf16[144,1536]{1,0:T(8,128)(2,1)S(1)}, bf16[144,1536]{1,0:T(8,128)(2,1)S(1)}, u32[]{:S(2)}, u32[]{:S(2)}) %collective-permute-start.33) | collective-permute-done | bytes 442400 | tf_op jit(solution)/shard_map/ppermute | solution.py:489
  275.1 2.6 collective-permute-start.41
  277.7 1.6 pad_maximum_fusion.3
  280.7 5.7 %place_early.2 = (f32[768,3072]{1,0:T(8,128)}, f32[3072,768]{1,0:T(8,128)}, f32[768,2304]{1,0:T(8,128)}, f32[768,768]{1,0:T(8,128)}) custom-call(s32[3]{0:T(128)} %pad_add_fusion.1.at_ref, bf16[2,3,192,768]{3,2,1,0:T(8,128)(2,1)} %copy-done.3, bf16[2,3,192,768]{3,2,1,0:T(8,128)(2,1)} %copy-done.2), custom_call_target="tpu_custom_call" | custom-call | bytes 11000000 | tf_op jit(solution)/shard_map/place_early/pallas_call | solution.py:446
  286.5 5.8 %place_early.3 = (f32[768,3072]{1,0:T(8,128)}, f32[3072,768]{1,0:T(8,128)}, f32[768,2304]{1,0:T(8,128)}, f32[768,768]{1,0:T(8,128)}) custom-call(s32[3]{0:T(128)} %pad_add_fusion.1.at_ref, bf16[2,3,192,768]{3,2,1,0:T(8,128)(2,1)} %collective-permute-done.39.source0_ref, ...), custom_call_target="tpu_custom_call", output_to_operand_aliasing={{0}: (3, {}), {1}: (4, {}), {2}: (5, {}), {3}: (6, {})} | custom-call | bytes 11000000 | tf_op jit(solution)/shard_map/place_early/pallas_call | solution.py:446
  292.3 4.5 %collective-permute-done.37.source0_ref = bf16[2,3,192,768]{3,2,1,0:T(8,128)(2,1)} collective-permute-done((bf16[2,3,192,768]{3,2,1,0:T(8,128)(2,1)S(1)}, bf16[2,3,192,768]{3,2,1,0:T(8,128)(2,1)}, u32[]{:S(2)}, u32[]{:S(2)}) %collective-permute-start.37) | collective-permute-done | bytes 1769504 | tf_op jit(solution)/shard_map/ppermute | solution.py:507
  299.0 5.8 %place_late.2 = (f32[768,3072]{1,0:T(8,128)}, f32[3072,768]{1,0:T(8,128)}, f32[768,2304]{1,0:T(8,128)}, f32[768,768]{1,0:T(8,128)}) custom-call(s32[3]{0:T(128)} %pad_add_fusion.1.at_ref, bf16[2,3,192,768]{3,2,1,0:T(8,128)(2,1)} %collective-permute-done.37.source0_ref, ...), custom_call_target="tpu_custom_call", output_to_operand_aliasing={{0}: (3, {}), {1}: (4, {}), {2}: (5, {}), {3}: (6, {})} | custom-call | bytes 11000000 | tf_op jit(solution)/shard_map/place_late/pallas_call | solution.py:446
  307.8 5.7 %place_late.3 = (f32[768,3072]{1,0:T(8,128)}, f32[3072,768]{1,0:T(8,128)}, f32[768,2304]{1,0:T(8,128)}, f32[768,768]{1,0:T(8,128)}) custom-call(s32[3]{0:T(128)} %pad_add_fusion.1.at_ref, bf16[2,3,192,768]{3,2,1,0:T(8,128)(2,1)} %copy-done.11, ...), custom_call_target="tpu_custom_call", output_to_operand_aliasing={{0}: (3, {}), {1}: (4, {}), {2}: (5, {}), {3}: (6, {})} | custom-call | bytes 11000000 | tf_op jit(solution)/shard_map/place_late/pallas_call | solution.py:446
  (215 shorter events, 43.1 us)
Async XLA Ops:
  2.9 17.2 %copy-start.28 = (f32[768]{0:T(1024)S(1)}, f32[768]{0:T(1024)}, u32[]{:S(2)}) copy-start(f32[768]{0:T(1024)} %param.22) | copy-start | bytes 9220
  3.2 16.9 %collective-permute-start = (bf16[144,1664]{1,0:T(8,128)(2,1)S(1)}, bf16[144,1664]{1,0:T(8,128)(2,1)S(1)}, u32[]{:S(2)}, u32[]{:S(2)}) collective-permute-start(bf16[144,1664]{1,0:T(8,128)(2,1)S(1)} %get-tuple-element.292), channel_id=1, source_target_pairs={{0,0},{8,1},{2,4},{10,5},{3,2},{11,3},{4,8},{12,9},{6,12},{14,13},... | collective-permute-start | bytes 1437704 | tf_op jit(solution)/shard_map/ppermute | solution.py:481
  9.2 15.0 %collective-permute-start.3 = (bf16[144,1664]{1,0:T(8,128)(2,1)S(1)}, bf16[144,1664]{1,0:T(8,128)(2,1)S(1)}, u32[]{:S(2)}, u32[]{:S(2)}) collective-permute-start(bf16[144,1664]{1,0:T(8,128)(2,1)S(1)} %get-tuple-element.293), channel_id=1, source_target_pairs={{1,4},{9,5},{2,2},{10,3},{3,0},{11,1},{5,12},{13,13},{6,10},{14,11... | collective-permute-start | bytes 1437704 | tf_op jit(solution)/shard_map/ppermute | solution.py:481
  10.5 19.0 %collective-permute-start.2 = (bf16[144,1664]{1,0:T(8,128)(2,1)S(1)}, bf16[144,1664]{1,0:T(8,128)(2,1)S(1)}, u32[]{:S(2)}, u32[]{:S(2)}) collective-permute-start(bf16[144,1664]{1,0:T(8,128)(2,1)S(1)} %get-tuple-element.294), channel_id=1, source_target_pairs={{0,4},{8,5},{1,2},{9,3},{2,0},{10,1},{4,12},{12,13},{5,10},{13,11}... | collective-permute-start | bytes 1437704 | tf_op jit(solution)/shard_map/ppermute | solution.py:481
  18.1 16.5 %collective-permute-start.1 = (bf16[144,1664]{1,0:T(8,128)(2,1)S(1)}, bf16[144,1664]{1,0:T(8,128)(2,1)S(1)}, u32[]{:S(2)}, u32[]{:S(2)}) collective-permute-start(bf16[144,1664]{1,0:T(8,128)(2,1)S(1)} %get-tuple-element.295), channel_id=1, source_target_pairs={{0,2},{8,3},{1,0},{9,1},{3,4},{11,5},{4,10},{12,11},{5,8},{13,9},{... | collective-permute-start | bytes 1437704 | tf_op jit(solution)/shard_map/ppermute | solution.py:481
  20.1 14.6 %copy-start.22 = (bf16[144,1664]{1,0:T(8,128)(2,1)}, bf16[144,1664]{1,0:T(8,128)(2,1)S(1)}, u32[]{:S(2)}) copy-start(bf16[144,1664]{1,0:T(8,128)(2,1)S(1)} %collective-permute-done) | copy-start | bytes 1437700
  40.3 10.4 %collective-permute-start.4 = (bf16[576,1536]{1,0:T(8,128)(2,1)}, bf16[576,1536]{1,0:T(8,128)(2,1)}, u32[]{:S(2)}, u32[]{:S(2)}) collective-permute-start(bf16[576,1536]{1,0:T(8,128)(2,1)} %add_convert_fusion.ko_ref.vo_ref), channel_id=1, source_target_pairs={{0,8},{8,0},{1,9},{9,1},{2,10},{10,2},{3,11},{11,3},{4,12},{12,4},... | collective-permute-start | bytes 5308424 | tf_op jit(solution)/shard_map/ppermute | solution.py:520
  67.5 33.7 %copy-start.14 = (bf16[576,768]{1,0:T(8,128)(2,1)S(1)}, bf16[576,768]{1,0:T(8,128)(2,1)}, u32[]{:S(2)}) copy-start(bf16[576,768]{1,0:T(8,128)(2,1)} %get-tuple-element.149.att_ref) | copy-start | bytes 2654212
  100.5 20.7 %collective-permute-start.5 = (bf16[4,2,192,768]{3,2,1,0:T(8,128)(2,1)}, bf16[4,2,192,768]{3,2,1,0:T(8,128)(2,1)S(1)}, u32[]{:S(2)}, u32[]{:S(2)}) collective-permute-start(bf16[4,2,192,768]{3,2,1,0:T(8,128)(2,1)} %get-tuple-element.153), channel_id=1, source_target_pairs={{0,8},{8,0},{1,9},{9,1},{2,10},{10,2},{3,11},{11,3},{4,12},{12,4},... | collective-permute-start | bytes 7077896 | tf_op jit(solution)/shard_map/ppermute | solution.py:520
  100.7 20.6 %collective-permute-start.6 = (bf16[4,2,192,768]{3,2,1,0:T(8,128)(2,1)}, bf16[4,2,192,768]{3,2,1,0:T(8,128)(2,1)}, u32[]{:S(2)}, u32[]{:S(2)}) collective-permute-start(bf16[4,2,192,768]{3,2,1,0:T(8,128)(2,1)} %get-tuple-element.154), channel_id=1, source_target_pairs={{0,8},{8,0},{1,9},{9,1},{2,10},{10,2},{3,11},{11,3},{4,12},{12,4},... | collective-permute-start | bytes 7077896 | tf_op jit(solution)/shard_map/ppermute | solution.py:520
  101.1 20.1 %collective-permute-start.7 = (bf16[576,768]{1,0:T(8,128)(2,1)S(1)}, bf16[576,768]{1,0:T(8,128)(2,1)S(1)}, u32[]{:S(2)}, u32[]{:S(2)}) collective-permute-start(bf16[576,768]{1,0:T(8,128)(2,1)S(1)} %copy-done.14), channel_id=1, source_target_pairs={{0,8},{8,0},{1,9},{9,1},{2,10},{10,2},{3,11},{11,3},{4,12},{12,4},... | collective-permute-start | bytes 2654216 | tf_op jit(solution)/shard_map/ppermute | solution.py:520
  101.4 19.8 %collective-permute-start.8 = (bf16[576,768]{1,0:T(8,128)(2,1)}, bf16[576,768]{1,0:T(8,128)(2,1)}, u32[]{:S(2)}, u32[]{:S(2)}) collective-permute-start(bf16[576,768]{1,0:T(8,128)(2,1)} %get-tuple-element.155.gb_ref), channel_id=1, source_target_pairs={{0,8},{8,0},{1,9},{9,1},{2,10},{10,2},{3,11},{11,3},{4,12},{12,4},... | collective-permute-start | bytes 2654216 | tf_op jit(solution)/shard_map/ppermute | solution.py:520
  122.9 7.7 %collective-permute-start.9 = (bf16[4,576,768]{2,1,0:T(8,128)(2,1)}, bf16[4,576,768]{2,1,0:T(8,128)(2,1)S(1)}, u32[]{:S(2)}, u32[]{:S(2)}) collective-permute-start(bf16[4,576,768]{2,1,0:T(8,128)(2,1)} %get-tuple-element.157.other_ref), channel_id=1, source_target_pairs={{0,8},{8,0},{1,9},{9,1},{2,10},{10,2},{3,11},{11,3},{4,12},{12,4},... | collective-permute-start | bytes 10616840 | tf_op jit(solution)/shard_map/ppermute | solution.py:520
  123.0 10.3 %collective-permute-start.10 = (bf16[576,768]{1,0:T(8,128)(2,1)}, bf16[576,768]{1,0:T(8,128)(2,1)}, u32[]{:S(2)}, u32[]{:S(2)}) collective-permute-start(bf16[576,768]{1,0:T(8,128)(2,1)} %copy-done.6), channel_id=1, source_target_pairs={{0,8},{8,0},{1,9},{9,1},{2,10},{10,2},{3,11},{11,3},{4,12},{12,4},... | collective-permute-start | bytes 2654216 | tf_op jit(solution)/shard_map/ppermute | solution.py:520
  130.6 25.8 %collective-permute-start.11 = (bf16[2,2,192,768]{3,2,1,0:T(8,128)(2,1)}, bf16[2,2,192,768]{3,2,1,0:T(8,128)(2,1)}, u32[]{:S(2)}, u32[]{:S(2)}) collective-permute-start(bf16[2,2,192,768]{3,2,1,0:T(8,128)(2,1)} %add_convert_fusion.2), channel_id=1, source_target_pairs={{0,32},{8,104},{2,34},{10,106},{4,36},{12,108},{6,38},{14,110},{32... | collective-permute-start | bytes 3538952 | tf_op jit(solution)/shard_map/ppermute | solution.py:507
  133.3 23.0 %collective-permute-start.12 = (bf16[2,2,192,768]{3,2,1,0:T(8,128)(2,1)}, bf16[2,2,192,768]{3,2,1,0:T(8,128)(2,1)}, u32[]{:S(2)}, u32[]{:S(2)}) collective-permute-start(bf16[2,2,192,768]{3,2,1,0:T(8,128)(2,1)} %add_convert_fusion.1), channel_id=1, source_target_pairs={{0,2},{8,14},{2,0},{10,12},{4,6},{12,10},{6,4},{14,8},{32,34},{40,... | collective-permute-start | bytes 3538952 | tf_op jit(solution)/shard_map/ppermute | solution.py:507
  143.6 12.7 %collective-permute-start.13 = (bf16[2,1,192,768]{3,2,1,0:T(8,128)(2,1)}, bf16[2,1,192,768]{3,2,1,0:T(8,128)(2,1)S(1)}, u32[]{:S(2)}, u32[]{:S(2)}) collective-permute-start(bf16[2,1,192,768]{3,2,1,0:T(8,128)(2,1)} %get-tuple-element.171), channel_id=1, source_target_pairs={{0,32},{8,104},{2,34},{10,106},{4,36},{12,108},{6,38},{14,110},{32... | collective-permute-start | bytes 1769480 | tf_op jit(solution)/shard_map/ppermute | solution.py:507
  145.5 10.8 %collective-permute-start.14 = (bf16[2,1,192,768]{3,2,1,0:T(8,128)(2,1)}, bf16[2,1,192,768]{3,2,1,0:T(8,128)(2,1)S(1)}, u32[]{:S(2)}, u32[]{:S(2)}) collective-permute-start(bf16[2,1,192,768]{3,2,1,0:T(8,128)(2,1)} %get-tuple-element.172), channel_id=1, source_target_pairs={{0,2},{8,14},{2,0},{10,12},{4,6},{12,10},{6,4},{14,8},{32,34},{40,... | collective-permute-start | bytes 1769480 | tf_op jit(solution)/shard_map/ppermute | solution.py:507
  158.2 9.1 %collective-permute-start.18 = (bf16[2,192,768]{2,1,0:T(8,128)(2,1)S(1)}, bf16[2,192,768]{2,1,0:T(8,128)(2,1)S(1)}, u32[]{:S(2)}, u32[]{:S(2)}) collective-permute-start(bf16[2,192,768]{2,1,0:T(8,128)(2,1)S(1)} %fusion.11), channel_id=1, source_target_pairs={{0,6},{8,10},{2,4},{10,8},{4,2},{12,14},{6,0},{14,12},{32,38},{40,... | collective-permute-start | bytes 1769480 | tf_op jit(solution)/shard_map/ppermute | solution.py:507
  160.8 9.1 %collective-permute-start.17 = (bf16[2,192,768]{2,1,0:T(8,128)(2,1)S(1)}, bf16[2,192,768]{2,1,0:T(8,128)(2,1)S(1)}, u32[]{:S(2)}, u32[]{:S(2)}) collective-permute-start(bf16[2,192,768]{2,1,0:T(8,128)(2,1)S(1)} %fusion.10), channel_id=1, source_target_pairs={{0,96},{8,40},{2,98},{10,42},{4,100},{12,44},{6,102},{14,46},{32,6... | collective-permute-start | bytes 1769480 | tf_op jit(solution)/shard_map/ppermute | solution.py:507
  161.0 10.3 %collective-permute-start.16 = (bf16[1,192,768]{2,1,0:T(8,128)(2,1)S(1)}, bf16[1,192,768]{2,1,0:T(8,128)(2,1)S(1)}, u32[]{:S(2)}, u32[]{:S(2)}) collective-permute-start(bf16[1,192,768]{2,1,0:T(8,128)(2,1)S(1)} %fusion.21), channel_id=1, source_target_pairs={{0,6},{8,10},{2,4},{10,8},{4,2},{12,14},{6,0},{14,12},{32,38},{40,... | collective-permute-start | bytes 884744 | tf_op jit(solution)/shard_map/ppermute | solution.py:507
  161.4 11.7 %collective-permute-start.15 = (bf16[1,192,768]{2,1,0:T(8,128)(2,1)S(1)}, bf16[1,192,768]{2,1,0:T(8,128)(2,1)S(1)}, u32[]{:S(2)}, u32[]{:S(2)}) collective-permute-start(bf16[1,192,768]{2,1,0:T(8,128)(2,1)S(1)} %fusion.20), channel_id=1, source_target_pairs={{0,96},{8,40},{2,98},{10,42},{4,100},{12,44},{6,102},{14,46},{32,6... | collective-permute-start | bytes 884744 | tf_op jit(solution)/shard_map/ppermute | solution.py:507
  174.5 9.0 %collective-permute-start.20 = (bf16[320,768]{1,0:T(8,128)(2,1)S(1)}, bf16[320,768]{1,0:T(8,128)(2,1)S(1)}, u32[]{:S(2)}, u32[]{:S(2)}) collective-permute-start(bf16[320,768]{1,0:T(8,128)(2,1)S(1)} %pad_maximum_fusion.8), channel_id=1, source_target_pairs={{0,32},{8,104},{2,34},{10,106},{4,36},{12,108},{6,38},{14,110},{32... | collective-permute-start | bytes 1474568 | tf_op jit(solution)/shard_map/ppermute | solution.py:507
  176.9 10.2 %collective-permute-start.19 = (bf16[2,3,48,768]{3,2,1,0:T(8,128)(2,1)S(1)}, bf16[2,3,48,768]{3,2,1,0:T(8,128)(2,1)S(1)}, u32[]{:S(2)}, u32[]{:S(2)}) collective-permute-start(bf16[2,3,48,768]{3,2,1,0:T(8,128)(2,1)S(1)} %pad_maximum_fusion.10), channel_id=1, source_target_pairs={{0,16},{8,25},{2,18},{10,27},{4,20},{12,29},{6,22},{14,31},{32,48}... | collective-permute-start | bytes 1327112 | tf_op jit(solution)/shard_map/ppermute | solution.py:507
  187.3 5.7 %collective-permute-start.22 = (bf16[176,768]{1,0:T(8,128)(2,1)S(1)}, bf16[176,768]{1,0:T(8,128)(2,1)S(1)}, u32[]{:S(2)}, u32[]{:S(2)}) collective-permute-start(bf16[176,768]{1,0:T(8,128)(2,1)S(1)} %pad_maximum_fusion.14), channel_id=1, source_target_pairs={{0,96},{8,40},{2,98},{10,42},{4,100},{12,44},{6,102},{14,46},{32,6... | collective-permute-start | bytes 811016 | tf_op jit(solution)/shard_map/ppermute | solution.py:507
  187.4 5.6 %collective-permute-start.21 = (bf16[3,48,768]{2,1,0:T(8,128)(2,1)S(1)}, bf16[3,48,768]{2,1,0:T(8,128)(2,1)S(1)}, u32[]{:S(2)}, u32[]{:S(2)}) collective-permute-start(bf16[3,48,768]{2,1,0:T(8,128)(2,1)S(1)} %fusion.17), channel_id=1, source_target_pairs={{0,17},{8,24},{2,19},{10,26},{4,21},{12,28},{6,23},{14,30},{32,49}... | collective-permute-start | bytes 663560 | tf_op jit(solution)/shard_map/ppermute | solution.py:507
  193.2 6.6 %collective-permute-start.23 = (bf16[176,768]{1,0:T(8,128)(2,1)S(1)}, bf16[176,768]{1,0:T(8,128)(2,1)S(1)}, u32[]{:S(2)}, u32[]{:S(2)}) collective-permute-start(bf16[176,768]{1,0:T(8,128)(2,1)S(1)} %pad_maximum_fusion.15), channel_id=1, source_target_pairs={{0,2},{8,14},{2,0},{10,12},{4,6},{12,10},{6,4},{14,8},{32,34},{40,... | collective-permute-start | bytes 811016 | tf_op jit(solution)/shard_map/ppermute | solution.py:507
  194.0 6.0 %collective-permute-start.24 = (bf16[3,48,768]{2,1,0:T(8,128)(2,1)S(1)}, bf16[3,48,768]{2,1,0:T(8,128)(2,1)S(1)}, u32[]{:S(2)}, u32[]{:S(2)}) collective-permute-start(bf16[3,48,768]{2,1,0:T(8,128)(2,1)S(1)} %fusion.15), channel_id=1, source_target_pairs={{0,16},{8,25},{2,18},{10,27},{4,20},{12,29},{6,22},{14,31},{32,48}... | collective-permute-start | bytes 663560 | tf_op jit(solution)/shard_map/ppermute | solution.py:507
  200.2 5.4 %collective-permute-start.25 = (bf16[176,768]{1,0:T(8,128)(2,1)S(1)}, bf16[176,768]{1,0:T(8,128)(2,1)S(1)}, u32[]{:S(2)}, u32[]{:S(2)}) collective-permute-start(bf16[176,768]{1,0:T(8,128)(2,1)S(1)} %pad_maximum_fusion.16), channel_id=1, source_target_pairs={{0,6},{8,10},{2,4},{10,8},{4,2},{12,14},{6,0},{14,12},{32,38},{40,... | collective-permute-start | bytes 811016 | tf_op jit(solution)/shard_map/ppermute | solution.py:507
  200.3 5.4 %collective-permute-start.26 = (bf16[3,48,768]{2,1,0:T(8,128)(2,1)S(1)}, bf16[3,48,768]{2,1,0:T(8,128)(2,1)S(1)}, u32[]{:S(2)}, u32[]{:S(2)}) collective-permute-start(bf16[3,48,768]{2,1,0:T(8,128)(2,1)S(1)} %add.452), channel_id=1, source_target_pairs={{0,17},{8,24},{2,19},{10,26},{4,21},{12,28},{6,23},{14,30},{32,49}... | collective-permute-start | bytes 663560 | tf_op jit(solution)/shard_map/ppermute | solution.py:507
  205.8 5.7 %collective-permute-start.27 = (bf16[176,768]{1,0:T(8,128)(2,1)S(1)}, bf16[176,768]{1,0:T(8,128)(2,1)S(1)}, u32[]{:S(2)}, u32[]{:S(2)}) collective-permute-start(bf16[176,768]{1,0:T(8,128)(2,1)S(1)} %pad_maximum_fusion.17), channel_id=1, source_target_pairs={{0,17},{8,24},{2,19},{10,26},{4,21},{12,28},{6,23},{14,30},{32,49}... | collective-permute-start | bytes 811016 | tf_op jit(solution)/shard_map/ppermute | solution.py:507
  205.9 5.6 %collective-permute-start.28 = (bf16[3,48,768]{2,1,0:T(8,128)(2,1)S(1)}, bf16[3,48,768]{2,1,0:T(8,128)(2,1)S(1)}, u32[]{:S(2)}, u32[]{:S(2)}) collective-permute-start(bf16[3,48,768]{2,1,0:T(8,128)(2,1)S(1)} %add.457), channel_id=1, source_target_pairs={{0,96},{8,40},{2,98},{10,42},{4,100},{12,44},{6,102},{14,46},{32,6... | collective-permute-start | bytes 663560 | tf_op jit(solution)/shard_map/ppermute | solution.py:507
  211.6 14.5 %collective-permute-start.30 = (bf16[2,3,48,768]{3,2,1,0:T(8,128)(2,1)S(1)}, bf16[2,3,48,768]{3,2,1,0:T(8,128)(2,1)S(1)}, u32[]{:S(2)}, u32[]{:S(2)}) collective-permute-start(bf16[2,3,48,768]{3,2,1,0:T(8,128)(2,1)S(1)} %pad_maximum_fusion.13), channel_id=1, source_target_pairs={{0,32},{8,104},{2,34},{10,106},{4,36},{12,108},{6,38},{14,110},{32... | collective-permute-start | bytes 1327112 | tf_op jit(solution)/shard_map/ppermute | solution.py:507
  213.6 11.9 %collective-permute-start.29 = (bf16[320,768]{1,0:T(8,128)(2,1)S(1)}, bf16[320,768]{1,0:T(8,128)(2,1)S(1)}, u32[]{:S(2)}, u32[]{:S(2)}) collective-permute-start(bf16[320,768]{1,0:T(8,128)(2,1)S(1)} %pad_maximum_fusion.9), channel_id=1, source_target_pairs={{0,16},{8,25},{2,18},{10,27},{4,20},{12,29},{6,22},{14,31},{32,48}... | collective-permute-start | bytes 1474568 | tf_op jit(solution)/shard_map/ppermute | solution.py:507
  227.5 25.0 %collective-permute-start.36 = (bf16[144,1536]{1,0:T(8,128)(2,1)S(1)}, bf16[144,1536]{1,0:T(8,128)(2,1)S(1)}, u32[]{:S(2)}, u32[]{:S(2)}) collective-permute-start(bf16[144,1536]{1,0:T(8,128)(2,1)S(1)} %get-tuple-element.288), channel_id=1, source_target_pairs={{4,1},{5,9},{2,2},{3,10},{0,3},{1,11},{12,5},{13,13},{10,6},{11,14... | collective-permute-start | bytes 1327112 | tf_op jit(solution)/shard_map/ppermute | solution.py:489
  241.6 30.4 %collective-permute-start.31 = (bf16[3,192,768]{2,1,0:T(8,128)(2,1)S(1)}, bf16[3,192,768]{2,1,0:T(8,128)(2,1)S(1)}, u32[]{:S(2)}, u32[]{:S(2)}) collective-permute-start(bf16[3,192,768]{2,1,0:T(8,128)(2,1)S(1)} %bitcast.122), channel_id=1, source_target_pairs={{0,96},{8,40},{2,98},{10,42},{4,100},{12,44},{6,102},{14,46},{32,6... | collective-permute-start | bytes 2654216 | tf_op jit(solution)/shard_map/ppermute | solution.py:507
  243.0 29.0 %collective-permute-start.32 = (bf16[3,192,768]{2,1,0:T(8,128)(2,1)S(1)}, bf16[3,192,768]{2,1,0:T(8,128)(2,1)S(1)}, u32[]{:S(2)}, u32[]{:S(2)}) collective-permute-start(bf16[3,192,768]{2,1,0:T(8,128)(2,1)S(1)} %bitcast.124), channel_id=1, source_target_pairs={{0,6},{8,10},{2,4},{10,8},{4,2},{12,14},{6,0},{14,12},{32,38},{40,... | collective-permute-start | bytes 2654216 | tf_op jit(solution)/shard_map/ppermute | solution.py:507
  243.0 19.5 %collective-permute-start.35 = (bf16[144,1536]{1,0:T(8,128)(2,1)S(1)}, bf16[144,1536]{1,0:T(8,128)(2,1)S(1)}, u32[]{:S(2)}, u32[]{:S(2)}) collective-permute-start(bf16[144,1536]{1,0:T(8,128)(2,1)S(1)} %get-tuple-element.289), channel_id=1, source_target_pairs={{4,0},{5,8},{2,1},{3,9},{0,2},{1,10},{12,4},{13,12},{10,5},{11,13}... | collective-permute-start | bytes 1327112 | tf_op jit(solution)/shard_map/ppermute | solution.py:489
  248.4 14.1 %collective-permute-start.34 = (bf16[144,1536]{1,0:T(8,128)(2,1)S(1)}, bf16[144,1536]{1,0:T(8,128)(2,1)S(1)}, u32[]{:S(2)}, u32[]{:S(2)}) collective-permute-start(bf16[144,1536]{1,0:T(8,128)(2,1)S(1)} %get-tuple-element.290), channel_id=1, source_target_pairs={{2,0},{3,8},{0,1},{1,9},{4,3},{5,11},{10,4},{11,12},{8,5},{9,13},{... | collective-permute-start | bytes 1327112 | tf_op jit(solution)/shard_map/ppermute | solution.py:489
  252.4 19.5 %copy-start.18 = (bf16[144,1536]{1,0:T(8,128)(2,1)}, bf16[144,1536]{1,0:T(8,128)(2,1)S(1)}, u32[]{:S(2)}) copy-start(bf16[144,1536]{1,0:T(8,128)(2,1)S(1)} %collective-permute-done.36) | copy-start | bytes 1327108
  252.5 19.5 %collective-permute-start.33 = (bf16[144,1536]{1,0:T(8,128)(2,1)S(1)}, bf16[144,1536]{1,0:T(8,128)(2,1)S(1)}, u32[]{:S(2)}, u32[]{:S(2)}) collective-permute-start(bf16[144,1536]{1,0:T(8,128)(2,1)S(1)} %get-tuple-element.291), channel_id=1, source_target_pairs={{0,0},{1,8},{4,2},{5,10},{2,3},{3,11},{8,4},{9,12},{12,6},{13,14},... | collective-permute-start | bytes 1327112 | tf_op jit(solution)/shard_map/ppermute | solution.py:489
  273.1 13.4 %collective-permute-start.39 = (bf16[2,3,192,768]{3,2,1,0:T(8,128)(2,1)S(1)}, bf16[2,3,192,768]{3,2,1,0:T(8,128)(2,1)}, u32[]{:S(2)}, u32[]{:S(2)}) collective-permute-start(bf16[2,3,192,768]{3,2,1,0:T(8,128)(2,1)S(1)} %pad_maximum_fusion.1.source0_ref), channel_id=1, source_target_pairs={{0,8},{8,0},{1,9},{9,1},{2,10},{10,2},{3,11},{11,3},{4,12},{12,4},... | collective-permute-start | bytes 5308424 | tf_op jit(solution)/shard_map/ppermute | solution.py:520
  273.2 13.3 %collective-permute-start.40 = (bf16[2,3,192,768]{3,2,1,0:T(8,128)(2,1)S(1)}, bf16[2,3,192,768]{3,2,1,0:T(8,128)(2,1)}, u32[]{:S(2)}, u32[]{:S(2)}) collective-permute-start(bf16[2,3,192,768]{3,2,1,0:T(8,128)(2,1)S(1)} %pad_maximum_fusion.2.source1_ref), channel_id=1, source_target_pairs={{0,8},{8,0},{1,9},{9,1},{2,10},{10,2},{3,11},{11,3},{4,12},{12,4},... | collective-permute-start | bytes 5308424 | tf_op jit(solution)/shard_map/ppermute | solution.py:520
  274.2 22.7 %collective-permute-start.37 = (bf16[2,3,192,768]{3,2,1,0:T(8,128)(2,1)S(1)}, bf16[2,3,192,768]{3,2,1,0:T(8,128)(2,1)}, u32[]{:S(2)}, u32[]{:S(2)}) collective-permute-start(bf16[2,3,192,768]{3,2,1,0:T(8,128)(2,1)S(1)} %pad_maximum_fusion.1.source0_ref), channel_id=1, source_target_pairs={{0,32},{8,104},{2,34},{10,106},{4,36},{12,108},{6,38},{14,110},{32... | collective-permute-start | bytes 5308424 | tf_op jit(solution)/shard_map/ppermute | solution.py:507
  274.5 22.8 %collective-permute-start.38 = (bf16[2,3,192,768]{3,2,1,0:T(8,128)(2,1)S(1)}, bf16[2,3,192,768]{3,2,1,0:T(8,128)(2,1)}, u32[]{:S(2)}, u32[]{:S(2)}) collective-permute-start(bf16[2,3,192,768]{3,2,1,0:T(8,128)(2,1)S(1)} %pad_maximum_fusion.2.source1_ref), channel_id=1, source_target_pairs={{0,2},{8,14},{2,0},{10,12},{4,6},{12,10},{6,4},{14,8},{32,34},{40,... | collective-permute-start | bytes 5308424 | tf_op jit(solution)/shard_map/ppermute | solution.py:507
  275.1 11.3 %collective-permute-start.41 = (f32[16,768]{1,0:T(8,128)}, f32[16,768]{1,0:T(8,128)S(1)}, u32[]{:S(2)}, u32[]{:S(2)}) collective-permute-start(f32[16,768]{1,0:T(8,128)} %fusion.39), channel_id=1, source_target_pairs={{0,8},{8,0},{1,9},{9,1},{2,10},{10,2},{3,11},{11,3},{4,12},{12,4},... | collective-permute-start | bytes 147464 | tf_op jit(solution)/shard_map/ppermute | solution.py:520
  297.4 9.2 %collective-permute-start.42 = (bf16[2,3,192,768]{3,2,1,0:T(8,128)(2,1)}, bf16[2,3,192,768]{3,2,1,0:T(8,128)(2,1)S(1)}, u32[]{:S(2)}, u32[]{:S(2)}) collective-permute-start(bf16[2,3,192,768]{3,2,1,0:T(8,128)(2,1)} %collective-permute-done.37.source0_ref), channel_id=1, source_target_pairs={{0,8},{8,0},{1,9},{9,1},{2,10},{10,2},{3,11},{11,3},{4,12},{12,4},... | collective-permute-start | bytes 5308424 | tf_op jit(solution)/shard_map/ppermute | solution.py:520
  298.3 8.3 %collective-permute-start.43 = (bf16[2,3,192,768]{3,2,1,0:T(8,128)(2,1)}, bf16[2,3,192,768]{3,2,1,0:T(8,128)(2,1)}, u32[]{:S(2)}, u32[]{:S(2)}) collective-permute-start(bf16[2,3,192,768]{3,2,1,0:T(8,128)(2,1)} %collective-permute-done.38.source1_ref), channel_id=1, source_target_pairs={{0,8},{8,0},{1,9},{9,1},{2,10},{10,2},{3,11},{11,3},{4,12},{12,4},... | collective-permute-start | bytes 5308424 | tf_op jit(solution)/shard_map/ppermute | solution.py:520
  (28 other events, 122.5 us)

commit v5 on v4

--- a/solution.py
+++ b/solution.py
@@ -401,26 +401,10 @@
 
 
 def place_kernel(mine, late, at_ref, source0_ref, source1_ref, *refs):
-    up_ref, down_ref, qkv_ref, out_ref, tiles, sems = refs[-6:]
+    up_ref, down_ref, qkv_ref, out_ref, pieces, tiles, in_sems, out_sems = refs[-8:]
     half = at_ref[0] if mine else 1 - at_ref[0]
     sources = (source0_ref, source1_ref)
-    copies = []
-
-    def send(source, target, condition=None):
-        number = len(copies)
-        copies.append(None)
-        tiles[number] = source.astype(f32)
-
-        def start(to):
-            copy = pltpu.make_async_copy(tiles.at[number], to, sems.at[number])
-            copy.start()
-
-        if condition is None:
-            start(target[0])
-        else:
-            pl.when(condition)(lambda: start(target[0]))
-            pl.when(jnp.logical_not(condition))(lambda: start(target[1]))
-
+    plan = []
     for j in range(2):
         block = 2 * half + j
         columns = pl.ds(pl.multiple_of(block * D, D), D)
@@ -428,16 +412,30 @@
             rows = [
                 quarter_rows(quarter_blocks(at_ref[1 + part], half)[s + (2 if late else 0)]) for part in range(2)
             ]
-            send(sources[0][s, j], [up_ref.at[rows[0], columns]])
             down_rows = pl.ds(pl.multiple_of(block * D + rows[1].start, QUARTER), QUARTER)
-            send(sources[1][s, j], [down_ref.at[down_rows, :]])
-            if j == 0:
-                send(sources[j][s, 2], [qkv_ref.at[rows[j], columns]])
-            else:
-                columns_qkv = pl.ds(pl.multiple_of(D, D), D)
-                send(sources[j][s, 2], [qkv_ref.at[rows[j], columns_qkv], out_ref.at[rows[j], :]], half == 0)
-    for number in range(len(copies)):
-        pltpu.make_async_copy(tiles.at[number], up_ref.at[pl.ds(0, QUARTER), pl.ds(0, D)], sems.at[number]).wait()
+            plan.append((sources[0].at[s, j], up_ref.at[rows[0], columns], None))
+            plan.append((sources[1].at[s, j], down_ref.at[down_rows, :], None))
+            last = out_ref.at[rows[j], :] if j == 1 else None
+            square_columns = columns if j == 0 else pl.ds(D, D)
+            plan.append((sources[j].at[s, 2], qkv_ref.at[rows[j], square_columns], last))
+    loads = []
+    for number, (source, _, _) in enumerate(plan):
+        loads.append(pltpu.make_async_copy(source, pieces.at[number], in_sems.at[number]))
+        loads[-1].start()
+    for number, (_, target, last) in enumerate(plan):
+        loads[number].wait()
+        tiles[number] = pieces[number].astype(f32)
+
+        def start(to, number=number):
+            pltpu.make_async_copy(tiles.at[number], to, out_sems.at[number]).start()
+
+        if last is None:
+            start(target)
+        else:
+            pl.when(half == 0)(lambda: start(target))
+            pl.when(half != 0)(lambda: start(last))
+    for number, (_, target, _) in enumerate(plan):
+        pltpu.make_async_copy(tiles.at[number], target, out_sems.at[number]).wait()
 
 
 def place(at, pieces, mine, late, before=()):
@@ -447,9 +445,12 @@
         functools.partial(place_kernel, mine, late),
         grid_spec=pltpu.PrefetchScalarGridSpec(
             num_scalar_prefetch=1, grid=(1,),
-            in_specs=[whole(2, NF // 2 + 1, QUARTER, D)] * 2 + [anywhere] * len(before),
+            in_specs=[anywhere] * (2 + len(before)),
             out_specs=[anywhere] * 4,
-            scratch_shapes=[pltpu.VMEM((12, QUARTER, D), f32), pltpu.SemaphoreType.DMA((12,))],
+            scratch_shapes=[
+                pltpu.VMEM((12, QUARTER, D), bf16), pltpu.VMEM((12, QUARTER, D), f32),
+                pltpu.SemaphoreType.DMA((12,)), pltpu.SemaphoreType.DMA((12,)),
+            ],
         ),
         out_shape=[shape((D, FF), f32), shape((FF, D), f32), shape((D, 3 * D), f32), shape((D, D), f32)],
         input_output_aliases={3 + index: index for index in range(len(before))},
@@ -566,6 +567,10 @@
     block = 2 * z + xh
     views = jnp.broadcast_to(view_counts.astype(bf16)[:, None, None], (3, BLK, LANES))
     pieces = to_scene(jnp.concatenate([tokens, cotangent, views], axis=2), block)
+    vecs = jnp.concatenate([jnp.stack([out_bias, ln2_gain, ln2_shift, down_bias]), jnp.zeros((4, D), f32)])
+    gains = jnp.broadcast_to(ln1_gain[None, :], (8, D))
+    weight_q, weight_kv = qkv_weight[:, :D], qkv_weight[:, D:]
+    pieces, vecs, gains, weight_q, weight_kv = hold(pieces, vecs, gains, weight_q, weight_kv)
     both = jnp.concatenate([piece[:, : 2 * D] for piece in pieces], axis=0)
     views = pieces[0][0, 2 * D].astype(f32)
     x = both[:, :D]
@@ -582,13 +587,12 @@
     normed = (centred * rstd * ln1_gain + ln1_shift).astype(bf16)
     product = lambda weight: jnp.dot(normed, weight, preferred_element_type=f32)
     kv_bias = jnp.concatenate([jnp.zeros((D,), f32), value_bias])
-    own = (product(qkv_weight[:, D:]) + kv_bias).astype(bf16)
+    own = (product(weight_kv) + kv_bias).astype(bf16)
     sibling = swap(own)
     normed_other = swap(normed)
-    queries = (product(qkv_weight[:, :D]) + query_bias).astype(bf16)
+    queries = (product(weight_q) + query_bias).astype(bf16)
     weights, heads_out, linv, attended = attention_forward(queries, own, sibling, mask)
 
-    vecs = jnp.concatenate([jnp.stack([out_bias, ln2_gain, ln2_shift, down_bias]), jnp.zeros((4, D), f32)])
     up_b = up_bias.reshape(NF, 1, FCHUNK)
     y = lax.axis_index("y")
     x_place = lax.axis_index("xh") * 2 + lax.axis_index("xl")
@@ -605,15 +609,14 @@
     arrived = swap(sent)
     pieces = [(up_mine, moving[0]), (down_mine, moving[1])]
     away = [add(mine[2:], other[2:]) for mine, other in pieces]
+    halved = meet_parts(away, 0, 0)
     arrived, away = hold(arrived, away)
-    halved = meet_parts(away, 0, 0)
     keep0, away0, keep1, away1 = squares(
         at, grad_q, grad_own, sent, arrived, grad_branch, branch_other, normed, normed_other, attended, attended_other
     )
 
     away, grad_hidden = hold([away0, away1], grad_hidden)
     square_halved = meet_parts(away, 0, 0)
-    gains = jnp.broadcast_to(ln1_gain[None, :], (8, D))
     input_grad, small = input_gradient(
         grad_q, grad_own, arrived, qkv_weight, both, grad_hidden, gains, vec_grads, up_b_grad
     )
@@ -689,16 +692,17 @@
     small_other = swap(small)
     placed = place(at, pairs, True, False)
     returned = take_from_scene(returned, block)
-
-    own_other, small_other, placed = hold(own_other, small_other, placed)
+    output, input_grad = returned[:, :, :D], returned[:, :, D:]
+
+    own_other, small_other, placed, output, input_grad = hold(own_other, small_other, placed, output, input_grad)
     small = small + small_other
     placed = place(at, own_other, False, False, placed)
-    got, placed, returned = hold(got, placed, returned)
+    got, placed = hold(got, placed)
     got_other = [swap(v) for v in got]
     placed = place(at, got, True, True, placed)
     d_up, d_down, d_qkv, d_out = place(at, got_other, False, True, placed)
     return (
-        returned[:, :, :D], returned[:, :, D:], small[4], small[5], d_qkv, small[6], small[7], d_out,
+        output, input_grad, small[4], small[5], d_qkv, small[6], small[7], d_out,
         small[0], small[1], small[2], d_up, small[8:12].reshape(FF), d_down, small[3],
     )
 

time: 319 us -> 310 us (0.972)
  starting transfers between devices: 77.9 us -> 66.6 us
  waiting for transfers between devices: 78.1 us -> 85.2 us
    ppermute x24, waiting for transfers between devices: 45.9 us -> 55.5 us  [exchange(): return lax.ppermute(value, AXES, pairs)]
    ppermute x24, starting transfers between devices: 27.3 us -> 18.2 us  [exchange(): return lax.ppermute(value, AXES, pairs)]
    pallas_call x4, Pallas kernels: 23.1 us -> 19.4 us  [place(): pl.pallas_call(functools.partial(place_kernel, mine, late), grid_spec=plt...]
    unnamed x65 -> x69, local copies, waits for them, and re-layouts: 7.5 us -> 9.99 us
  transfers between devices with their start and end apart: 44 -> 44, of which waited for: 19 -> 17; matrix products, arithmetic and copies ran while one was open for 8% -> 7% of each run, Pallas kernels for 18% -> 17%
where the time goes in v5:
time: 310 us; the launch traced here: 306 us
  Pallas kernels  107 us (35%)
  waiting for transfers between devices  85.2 us (27%)
  starting transfers between devices  66.6 us (21%)
  other arithmetic  20.1 us (6%)
  local copies, waits for them, and re-layouts  18.8 us (6%)
  matrix products  5.69 us (2%)
    ppermute x24, waiting for transfers between devices, exchange(): return lax.ppermute(value, AXES, pairs)  55.5 us
    pallas_call x1, Pallas kernels, feed_forward(): pl.pallas_call(feed_forward_kernel, grid_spec=pltpu.PrefetchScalarGridSpe...  33.1 us
    ppermute x4, starting transfers between devices, send_from_scene(): pieces.append(lax.ppermute(values[slot * BLK:(slot + 1) * BLK], AXES, back))  25.6 us
    pallas_call x1, Pallas kernels, attention_backward(): pl.pallas_call(attention_backward_kernel, grid_spec=pltpu.PrefetchScalarG...  19.4 us
    pallas_call x4, Pallas kernels, place(): pl.pallas_call(functools.partial(place_kernel, mine, late), grid_spec=plt...  19.4 us
    ppermute x24, starting transfers between devices, exchange(): return lax.ppermute(value, AXES, pairs)  18.2 us
    ppermute x4, waiting for transfers between devices, send_from_scene(): pieces.append(lax.ppermute(values[slot * BLK:(slot + 1) * BLK], AXES, back))  16.4 us
    pallas_call x1, Pallas kernels, attention_forward(): pl.pallas_call(attention_forward_kernel, grid=(PAIRS,), in_specs=[col(0),...  15.8 us
  transfers between devices with their start and end apart: 44, of which 17 were waited for; matrix products, arithmetic and copies ran while one was open for 7% of the time, Pallas kernels for 17%

profile of v5, /device:TPU:1, one launch (start us, length us, event | category | flops | bytes accessed | tf_op | source)
XLA Modules:
  0.0 305.8 jit_solution(2151453660787447258)
XLA Ops:
  1.5 1.4 pad_maximum_fusion.4
  4.5 9.9 %collective-permute-start.2 = (bf16[144,1664]{1,0:T(8,128)(2,1)S(1)}, bf16[144,1664]{1,0:T(8,128)(2,1)S(1)}, u32[]{:S(2)}, u32[]{:S(2)}) collective-permute-start(bf16[144,1664]{1,0:T(8,128)(2,1)S(1)} %get-tuple-element.307), channel_id=1, source_target_pairs={{0,4},{8,5},{1,2},{9,3},{2,0},{10,1},{4,12},{12,13},{5,10},{13,11}... | collective-permute-start | bytes 1437704 | tf_op jit(solution)/shard_map/ppermute | solution.py:482
  14.4 1.9 collective-permute-start.1
  16.3 2.5 collective-permute-start
  20.2 2.8 collective-permute-done.2
  23.0 6.3 %collective-permute-done.1 = bf16[144,1664]{1,0:T(8,128)(2,1)} collective-permute-done((bf16[144,1664]{1,0:T(8,128)(2,1)S(1)}, bf16[144,1664]{1,0:T(8,128)(2,1)}, u32[]{:S(2)}, u32[]{:S(2)}) %collective-permute-start.1) | collective-permute-done | bytes 479264 | tf_op jit(solution)/shard_map/ppermute | solution.py:482
  29.3 4.2 %collective-permute-done = bf16[144,1664]{1,0:T(8,128)(2,1)S(1)} collective-permute-done((bf16[144,1664]{1,0:T(8,128)(2,1)S(1)}, bf16[144,1664]{1,0:T(8,128)(2,1)S(1)}, u32[]{:S(2)}, u32[]{:S(2)}) %collective-permute-start) | collective-permute-done | bytes 479264 | tf_op jit(solution)/shard_map/ppermute | solution.py:482
  37.7 2.7 add_convert_fusion.ko_ref.vo_ref
  40.5 2.9 collective-permute-start.4
  45.3 3.0 add_convert_fusion.3.q_ref
  49.7 15.8 %attention_forward.1 = (bf16[12,576,1152]{2,1,0:T(8,128)(2,1)}, f32[576,768]{1,0:T(8,128)}, f32[576,768]{1,0:T(8,128)}, bf16[576,768]{1,0:T(8,128)(2,1)}) custom-call(bf16[576,768]{1,0:T(8,128)(2,1)} %add_convert_fusion.3.q_ref, bf16[576,1536]{1,0:T(8,128)(2,1)} %add_convert_fusion.ko_ref.vo_ref, bf16[576,1536]{1,0:T(8,128)(2,1)} %add_convert_fusion.ko_ref.vo_ref, ...), custom_call_target="tpu_custom_call" | custom-call | flops 8153726976 | bytes 20000000 | tf_op jit(solution)/shard_map/attention_forward/pallas_call | solution.py:105
  65.5 33.1 %feed_forward.1 = (bf16[576,768]{1,0:T(8,128)(2,1)}, f32[576,768]{1,0:T(8,128)}, bf16[576,768]{1,0:T(8,128)(2,1)}, bf16[576,768]{1,0:T(8,128)(2,1)}, bf16[4,2,19...) custom-call(s32[3]{0:T(128)} %pad_add_fusion.1.at_ref, ...), custom_call_target="tpu_custom_call" | custom-call | flops 16307453952 | bytes 30000000 | tf_op jit(solution)/shard_map/feed_forward/pallas_call | solution.py:278
  99.8 19.4 %attention_backward.1 = (bf16[576,768]{1,0:T(8,128)(2,1)}, bf16[2,576,768]{2,1,0:T(8,128)(2,1)}, bf16[4,576,768]{2,1,0:T(8,128)(2,1)}) custom-call(s32[3]{0:T(128)} %pad_add_fusion.1.at_ref, bf16[576,768]{1,0:T(8,128)(2,1)} %add_convert_fusion.3.q_ref, bf16[576,1536]{1,0:T(8,128)(2,1)} %add_convert_fusion.ko_ref.vo_ref, ...), custom_call_target="tpu_custom_call" | custom-call | flops 16307453952 | bytes 25000000 | tf_op jit(solution)/shard_map/attention_backward/pallas_call | solution.py:165
  121.5 3.1 %add_convert_fusion.1 = bf16[2,2,192,768]{3,2,1,0:T(8,128)(2,1)} fusion(bf16[4,2,192,768]{3,2,1,0:T(8,128)(2,1)} %collective-permute-done.6, bf16[4,2,192,768]{3,2,1,0:T(8,128)(2,1)} %get-tuple-element.174), kind=kLoop, calls=%fused_computation.1 | loop fusion | flops 2359296 | bytes 3538944 | tf_op jit(solution)/shard_map/convert_element_type | solution.py:532
  124.5 2.6 add_convert_fusion.2
  127.2 2.7 collective-permute-start.11
  129.9 1.8 copy-done
  131.7 10.3 %squares.1 = (bf16[2,1,192,768]{3,2,1,0:T(8,128)(2,1)}, bf16[2,1,192,768]{3,2,1,0:T(8,128)(2,1)}, bf16[2,1,192,768]{3,2,1,0:T(8,128)(2,1)}, bf16[2,1,192,768]{3,2,1,0:T(8,128)(2,1)}) custom-call(s32[3]{0:T(128)} %pad_add_fusion.1.at_ref, bf16[576,768]{1,0:T(8,128)(2,1)} %get-tuple-element.165.gq_ref, bf16[2,576,768]{2,1,0:T(8,128)(2,1)} %get-tuple-element.166.own_ref, ...), custom_call_target="tpu_custom_call" | custom-call | flops 2717908992 | bytes 13000000 | tf_op jit(solution)/shard_map/squares/pallas_call | solution.py:339
  141.9 1.5 collective-permute-start.13
  143.4 1.7 collective-permute-start.14
  145.1 8.8 %input_gradient.1 = (bf16[576,768]{1,0:T(8,128)(2,1)}, f32[16,768]{1,0:T(8,128)}) custom-call(bf16[576,768]{1,0:T(8,128)(2,1)} %get-tuple-element.165.gq_ref, bf16[2,576,768]{2,1,0:T(8,128)(2,1)} %get-tuple-element.166.own_ref, bf16[4,576,768]{2,1,0:T(8,128)(2,1)} %copy-done, bf16[768,2304]{1,0:T(8,128)(2,1)} %w_ref.1, bf16[576,1536]{1,0:T(8,128)(2,1)} %copy-done.1, ...), custom_call_target="tpu_custom_call" | custom-call | flops 2038431744 | bytes 10000000 | tf_op jit(solution)/shard_map/input_gradient/pallas_call | solution.py:390
  154.0 1.8 fusion.9
  159.0 1.5 collective-permute-start.15
  160.5 4.4 %collective-permute-done.18 = bf16[2,192,768]{2,1,0:T(8,128)(2,1)S(1)} collective-permute-done((bf16[2,192,768]{2,1,0:T(8,128)(2,1)S(1)}, bf16[2,192,768]{2,1,0:T(8,128)(2,1)S(1)}, u32[]{:S(2)}, u32[]{:S(2)}) %collective-permute-start.18) | collective-permute-done | bytes 589856 | tf_op jit(solution)/shard_map/ppermute | solution.py:508
  164.9 1.7 fusion.6
  168.7 1.8 collective-permute-done.15
  171.9 2.7 collective-permute-start.20
  174.6 6.3 %collective-permute-done.20 = bf16[320,768]{1,0:T(8,128)(2,1)S(1)} collective-permute-done((bf16[320,768]{1,0:T(8,128)(2,1)S(1)}, bf16[320,768]{1,0:T(8,128)(2,1)S(1)}, u32[]{:S(2)}, u32[]{:S(2)}) %collective-permute-start.20) | collective-permute-done | bytes 491552 | tf_op jit(solution)/shard_map/ppermute | solution.py:508
  180.9 2.0 collective-permute-done.19
  183.3 5.5 %collective-permute-done.22 = bf16[176,768]{1,0:T(8,128)(2,1)S(1)} collective-permute-done((bf16[176,768]{1,0:T(8,128)(2,1)S(1)}, bf16[176,768]{1,0:T(8,128)(2,1)S(1)}, u32[]{:S(2)}, u32[]{:S(2)}) %collective-permute-start.22) | collective-permute-done | bytes 270368 | tf_op jit(solution)/shard_map/ppermute | solution.py:508
  189.8 5.8 %collective-permute-done.23 = bf16[176,768]{1,0:T(8,128)(2,1)S(1)} collective-permute-done((bf16[176,768]{1,0:T(8,128)(2,1)S(1)}, bf16[176,768]{1,0:T(8,128)(2,1)S(1)}, u32[]{:S(2)}, u32[]{:S(2)}) %collective-permute-start.23) | collective-permute-done | bytes 270368 | tf_op jit(solution)/shard_map/ppermute | solution.py:508
  196.3 5.3 %collective-permute-done.25 = bf16[176,768]{1,0:T(8,128)(2,1)S(1)} collective-permute-done((bf16[176,768]{1,0:T(8,128)(2,1)S(1)}, bf16[176,768]{1,0:T(8,128)(2,1)S(1)}, u32[]{:S(2)}, u32[]{:S(2)}) %collective-permute-start.25) | collective-permute-done | bytes 270368 | tf_op jit(solution)/shard_map/ppermute | solution.py:508
  202.7 4.9 %collective-permute-done.27 = bf16[176,768]{1,0:T(8,128)(2,1)S(1)} collective-permute-done((bf16[176,768]{1,0:T(8,128)(2,1)S(1)}, bf16[176,768]{1,0:T(8,128)(2,1)S(1)}, u32[]{:S(2)}, u32[]{:S(2)}) %collective-permute-start.27) | collective-permute-done | bytes 270368 | tf_op jit(solution)/shard_map/ppermute | solution.py:508
  209.0 11.0 %collective-permute-done.29 = bf16[320,768]{1,0:T(8,128)(2,1)S(1)} collective-permute-done((bf16[320,768]{1,0:T(8,128)(2,1)S(1)}, bf16[320,768]{1,0:T(8,128)(2,1)S(1)}, u32[]{:S(2)}, u32[]{:S(2)}) %collective-permute-start.29) | collective-permute-done | bytes 491552 | tf_op jit(solution)/shard_map/ppermute | solution.py:508
  222.1 13.1 %collective-permute-start.36 = (bf16[144,1536]{1,0:T(8,128)(2,1)S(1)}, bf16[144,1536]{1,0:T(8,128)(2,1)S(1)}, u32[]{:S(2)}, u32[]{:S(2)}) collective-permute-start(bf16[144,1536]{1,0:T(8,128)(2,1)S(1)} %get-tuple-element.302), channel_id=1, source_target_pairs={{4,1},{5,9},{2,2},{3,10},{0,3},{1,11},{12,5},{13,13},{10,6},{11,14... | collective-permute-start | bytes 1327112 | tf_op jit(solution)/shard_map/ppermute | solution.py:490
  235.2 1.8 collective-permute-start.31
  237.6 2.7 collective-permute-start.35
  240.4 6.7 %collective-permute-start.34 = (bf16[144,1536]{1,0:T(8,128)(2,1)S(1)}, bf16[144,1536]{1,0:T(8,128)(2,1)S(1)}, u32[]{:S(2)}, u32[]{:S(2)}) collective-permute-start(bf16[144,1536]{1,0:T(8,128)(2,1)S(1)} %get-tuple-element.304), channel_id=1, source_target_pairs={{2,0},{3,8},{0,1},{1,9},{4,3},{5,11},{10,4},{11,12},{8,5},{9,13},{... | collective-permute-start | bytes 1327112 | tf_op jit(solution)/shard_map/ppermute | solution.py:490
  247.1 3.0 collective-permute-start.33
  250.1 5.9 %collective-permute-done.35 = bf16[144,1536]{1,0:T(8,128)(2,1)S(1)} collective-permute-done((bf16[144,1536]{1,0:T(8,128)(2,1)S(1)}, bf16[144,1536]{1,0:T(8,128)(2,1)S(1)}, u32[]{:S(2)}, u32[]{:S(2)}) %collective-permute-start.35) | collective-permute-done | bytes 442400 | tf_op jit(solution)/shard_map/ppermute | solution.py:490
  256.1 10.5 %collective-permute-done.33 = bf16[144,1536]{1,0:T(8,128)(2,1)S(1)} collective-permute-done((bf16[144,1536]{1,0:T(8,128)(2,1)S(1)}, bf16[144,1536]{1,0:T(8,128)(2,1)S(1)}, u32[]{:S(2)}, u32[]{:S(2)}) %collective-permute-start.33) | collective-permute-done | bytes 442400 | tf_op jit(solution)/shard_map/ppermute | solution.py:490
  269.6 1.4 collective-permute-start.39
  271.1 1.6 pad_maximum_fusion.3
  274.1 4.8 %place_early.2 = (f32[768,3072]{1,0:T(8,128)}, f32[3072,768]{1,0:T(8,128)}, f32[768,2304]{1,0:T(8,128)}, f32[768,768]{1,0:T(8,128)}) custom-call(s32[3]{0:T(128)} %pad_add_fusion.1.at_ref, bf16[2,3,192,768]{3,2,1,0:T(8,128)(2,1)} %copy-done.3, bf16[2,3,192,768]{3,2,1,0:T(8,128)(2,1)} %copy-done.2), custom_call_target="tpu_custom_call" | custom-call | bytes 11000000 | tf_op jit(solution)/shard_map/place_early/pallas_call | solution.py:444
  278.9 4.9 %place_early.3 = (f32[768,3072]{1,0:T(8,128)}, f32[3072,768]{1,0:T(8,128)}, f32[768,2304]{1,0:T(8,128)}, f32[768,768]{1,0:T(8,128)}) custom-call(s32[3]{0:T(128)} %pad_add_fusion.1.at_ref, bf16[2,3,192,768]{3,2,1,0:T(8,128)(2,1)} %collective-permute-done.37.source0_ref, ...), custom_call_target="tpu_custom_call", output_to_operand_aliasing={{0}: (3, {}), {1}: (4, {}), {2}: (5, {}), {3}: (6, {})} | custom-call | bytes 11000000 | tf_op jit(solution)/shard_map/place_early/pallas_call | solution.py:444
  283.9 7.6 %collective-permute-done.40.source0_ref = bf16[2,3,192,768]{3,2,1,0:T(8,128)(2,1)} collective-permute-done((bf16[2,3,192,768]{3,2,1,0:T(8,128)(2,1)S(1)}, bf16[2,3,192,768]{3,2,1,0:T(8,128)(2,1)}, u32[]{:S(2)}, u32[]{:S(2)}) %collective-permute-start.40) | collective-permute-done | bytes 1769504 | tf_op jit(solution)/shard_map/ppermute | solution.py:508
  293.4 4.9 %place_late.2 = (f32[768,3072]{1,0:T(8,128)}, f32[3072,768]{1,0:T(8,128)}, f32[768,2304]{1,0:T(8,128)}, f32[768,768]{1,0:T(8,128)}) custom-call(s32[3]{0:T(128)} %pad_add_fusion.1.at_ref, bf16[2,3,192,768]{3,2,1,0:T(8,128)(2,1)} %collective-permute-done.40.source0_ref, ...), custom_call_target="tpu_custom_call", output_to_operand_aliasing={{0}: (3, {}), {1}: (4, {}), {2}: (5, {}), {3}: (6, {})} | custom-call | bytes 11000000 | tf_op jit(solution)/shard_map/place_late/pallas_call | solution.py:444
  300.8 4.8 %place_late.3 = (f32[768,3072]{1,0:T(8,128)}, f32[3072,768]{1,0:T(8,128)}, f32[768,2304]{1,0:T(8,128)}, f32[768,768]{1,0:T(8,128)}) custom-call(s32[3]{0:T(128)} %pad_add_fusion.1.at_ref, bf16[2,3,192,768]{3,2,1,0:T(8,128)(2,1)} %copy-done.9, ...), custom_call_target="tpu_custom_call", output_to_operand_aliasing={{0}: (3, {}), {1}: (4, {}), {2}: (5, {}), {3}: (6, {})} | custom-call | bytes 11000000 | tf_op jit(solution)/shard_map/place_late/pallas_call | solution.py:444
  (223 shorter events, 36.4 us)
Async XLA Ops:
  3.2 17.1 %collective-permute-start.3 = (bf16[144,1664]{1,0:T(8,128)(2,1)S(1)}, bf16[144,1664]{1,0:T(8,128)(2,1)S(1)}, u32[]{:S(2)}, u32[]{:S(2)}) collective-permute-start(bf16[144,1664]{1,0:T(8,128)(2,1)S(1)} %get-tuple-element.306), channel_id=1, source_target_pairs={{1,4},{9,5},{2,2},{10,3},{3,0},{11,1},{5,12},{13,13},{6,10},{14,11... | collective-permute-start | bytes 1437704 | tf_op jit(solution)/shard_map/ppermute | solution.py:482
  4.5 18.5 %collective-permute-start.2 = (bf16[144,1664]{1,0:T(8,128)(2,1)S(1)}, bf16[144,1664]{1,0:T(8,128)(2,1)S(1)}, u32[]{:S(2)}, u32[]{:S(2)}) collective-permute-start(bf16[144,1664]{1,0:T(8,128)(2,1)S(1)} %get-tuple-element.307), channel_id=1, source_target_pairs={{0,4},{8,5},{1,2},{9,3},{2,0},{10,1},{4,12},{12,13},{5,10},{13,11}... | collective-permute-start | bytes 1437704 | tf_op jit(solution)/shard_map/ppermute | solution.py:482
  14.4 14.9 %collective-permute-start.1 = (bf16[144,1664]{1,0:T(8,128)(2,1)S(1)}, bf16[144,1664]{1,0:T(8,128)(2,1)}, u32[]{:S(2)}, u32[]{:S(2)}) collective-permute-start(bf16[144,1664]{1,0:T(8,128)(2,1)S(1)} %get-tuple-element.308), channel_id=1, source_target_pairs={{0,2},{8,3},{1,0},{9,1},{3,4},{11,5},{4,10},{12,11},{5,8},{13,9},{... | collective-permute-start | bytes 1437704 | tf_op jit(solution)/shard_map/ppermute | solution.py:482
  16.3 17.2 %collective-permute-start = (bf16[144,1664]{1,0:T(8,128)(2,1)S(1)}, bf16[144,1664]{1,0:T(8,128)(2,1)S(1)}, u32[]{:S(2)}, u32[]{:S(2)}) collective-permute-start(bf16[144,1664]{1,0:T(8,128)(2,1)S(1)} %get-tuple-element.309), channel_id=1, source_target_pairs={{0,0},{8,1},{2,4},{10,5},{3,2},{11,3},{4,8},{12,9},{6,12},{14,13},... | collective-permute-start | bytes 1437704 | tf_op jit(solution)/shard_map/ppermute | solution.py:482
  18.9 14.7 %copy-start.25 = (f32[768]{0:T(1024)S(1)}, f32[768]{0:T(1024)}, u32[]{:S(2)}) copy-start(f32[768]{0:T(1024)} %param.18) | copy-start | bytes 9220
  40.5 7.8 %collective-permute-start.4 = (bf16[576,1536]{1,0:T(8,128)(2,1)}, bf16[576,1536]{1,0:T(8,128)(2,1)S(1)}, u32[]{:S(2)}, u32[]{:S(2)}) collective-permute-start(bf16[576,1536]{1,0:T(8,128)(2,1)} %add_convert_fusion.ko_ref.vo_ref), channel_id=1, source_target_pairs={{0,8},{8,0},{1,9},{9,1},{2,10},{10,2},{3,11},{11,3},{4,12},{12,4},... | collective-permute-start | bytes 5308424 | tf_op jit(solution)/shard_map/ppermute | solution.py:521
  65.5 33.7 %copy-start.13 = (bf16[576,768]{1,0:T(8,128)(2,1)S(1)}, bf16[576,768]{1,0:T(8,128)(2,1)}, u32[]{:S(2)}) copy-start(bf16[576,768]{1,0:T(8,128)(2,1)} %get-tuple-element.162.att_ref) | copy-start | bytes 2654212
  98.5 20.7 %collective-permute-start.5 = (bf16[4,2,192,768]{3,2,1,0:T(8,128)(2,1)}, bf16[4,2,192,768]{3,2,1,0:T(8,128)(2,1)S(1)}, u32[]{:S(2)}, u32[]{:S(2)}) collective-permute-start(bf16[4,2,192,768]{3,2,1,0:T(8,128)(2,1)} %get-tuple-element.167), channel_id=1, source_target_pairs={{0,8},{8,0},{1,9},{9,1},{2,10},{10,2},{3,11},{11,3},{4,12},{12,4},... | collective-permute-start | bytes 7077896 | tf_op jit(solution)/shard_map/ppermute | solution.py:521
  98.7 20.6 %collective-permute-start.6 = (bf16[4,2,192,768]{3,2,1,0:T(8,128)(2,1)}, bf16[4,2,192,768]{3,2,1,0:T(8,128)(2,1)}, u32[]{:S(2)}, u32[]{:S(2)}) collective-permute-start(bf16[4,2,192,768]{3,2,1,0:T(8,128)(2,1)} %get-tuple-element.168), channel_id=1, source_target_pairs={{0,8},{8,0},{1,9},{9,1},{2,10},{10,2},{3,11},{11,3},{4,12},{12,4},... | collective-permute-start | bytes 7077896 | tf_op jit(solution)/shard_map/ppermute | solution.py:521
  99.1 20.1 %collective-permute-start.7 = (bf16[576,768]{1,0:T(8,128)(2,1)S(1)}, bf16[576,768]{1,0:T(8,128)(2,1)S(1)}, u32[]{:S(2)}, u32[]{:S(2)}) collective-permute-start(bf16[576,768]{1,0:T(8,128)(2,1)S(1)} %copy-done.13), channel_id=1, source_target_pairs={{0,8},{8,0},{1,9},{9,1},{2,10},{10,2},{3,11},{11,3},{4,12},{12,4},... | collective-permute-start | bytes 2654216 | tf_op jit(solution)/shard_map/ppermute | solution.py:521
  99.4 19.8 %collective-permute-start.8 = (bf16[576,768]{1,0:T(8,128)(2,1)}, bf16[576,768]{1,0:T(8,128)(2,1)}, u32[]{:S(2)}, u32[]{:S(2)}) collective-permute-start(bf16[576,768]{1,0:T(8,128)(2,1)} %get-tuple-element.169.gb_ref), channel_id=1, source_target_pairs={{0,8},{8,0},{1,9},{9,1},{2,10},{10,2},{3,11},{11,3},{4,12},{12,4},... | collective-permute-start | bytes 2654216 | tf_op jit(solution)/shard_map/ppermute | solution.py:521
  121.0 8.9 %collective-permute-start.9 = (bf16[4,576,768]{2,1,0:T(8,128)(2,1)}, bf16[4,576,768]{2,1,0:T(8,128)(2,1)S(1)}, u32[]{:S(2)}, u32[]{:S(2)}) collective-permute-start(bf16[4,576,768]{2,1,0:T(8,128)(2,1)} %get-tuple-element.171.other_ref), channel_id=1, source_target_pairs={{0,8},{8,0},{1,9},{9,1},{2,10},{10,2},{3,11},{11,3},{4,12},{12,4},... | collective-permute-start | bytes 10616840 | tf_op jit(solution)/shard_map/ppermute | solution.py:521
  121.0 8.8 %collective-permute-start.10 = (bf16[576,768]{1,0:T(8,128)(2,1)}, bf16[576,768]{1,0:T(8,128)(2,1)}, u32[]{:S(2)}, u32[]{:S(2)}) collective-permute-start(bf16[576,768]{1,0:T(8,128)(2,1)} %copy-done.4), channel_id=1, source_target_pairs={{0,8},{8,0},{1,9},{9,1},{2,10},{10,2},{3,11},{11,3},{4,12},{12,4},... | collective-permute-start | bytes 2654216 | tf_op jit(solution)/shard_map/ppermute | solution.py:521
  124.5 29.4 %collective-permute-start.12 = (bf16[2,2,192,768]{3,2,1,0:T(8,128)(2,1)}, bf16[2,2,192,768]{3,2,1,0:T(8,128)(2,1)}, u32[]{:S(2)}, u32[]{:S(2)}) collective-permute-start(bf16[2,2,192,768]{3,2,1,0:T(8,128)(2,1)} %add_convert_fusion.1), channel_id=1, source_target_pairs={{0,2},{8,14},{2,0},{10,12},{4,6},{12,10},{6,4},{14,8},{32,34},{40,... | collective-permute-start | bytes 3538952 | tf_op jit(solution)/shard_map/ppermute | solution.py:508
  127.2 26.8 %collective-permute-start.11 = (bf16[2,2,192,768]{3,2,1,0:T(8,128)(2,1)}, bf16[2,2,192,768]{3,2,1,0:T(8,128)(2,1)}, u32[]{:S(2)}, u32[]{:S(2)}) collective-permute-start(bf16[2,2,192,768]{3,2,1,0:T(8,128)(2,1)} %add_convert_fusion.2), channel_id=1, source_target_pairs={{0,32},{8,104},{2,34},{10,106},{4,36},{12,108},{6,38},{14,110},{32... | collective-permute-start | bytes 3538952 | tf_op jit(solution)/shard_map/ppermute | solution.py:508
  141.9 12.0 %collective-permute-start.13 = (bf16[2,1,192,768]{3,2,1,0:T(8,128)(2,1)}, bf16[2,1,192,768]{3,2,1,0:T(8,128)(2,1)S(1)}, u32[]{:S(2)}, u32[]{:S(2)}) collective-permute-start(bf16[2,1,192,768]{3,2,1,0:T(8,128)(2,1)} %get-tuple-element.183), channel_id=1, source_target_pairs={{0,32},{8,104},{2,34},{10,106},{4,36},{12,108},{6,38},{14,110},{32... | collective-permute-start | bytes 1769480 | tf_op jit(solution)/shard_map/ppermute | solution.py:508
  143.4 10.5 %collective-permute-start.14 = (bf16[2,1,192,768]{3,2,1,0:T(8,128)(2,1)}, bf16[2,1,192,768]{3,2,1,0:T(8,128)(2,1)S(1)}, u32[]{:S(2)}, u32[]{:S(2)}) collective-permute-start(bf16[2,1,192,768]{3,2,1,0:T(8,128)(2,1)} %get-tuple-element.184), channel_id=1, source_target_pairs={{0,2},{8,14},{2,0},{10,12},{4,6},{12,10},{6,4},{14,8},{32,34},{40,... | collective-permute-start | bytes 1769480 | tf_op jit(solution)/shard_map/ppermute | solution.py:508
  155.8 9.1 %collective-permute-start.18 = (bf16[2,192,768]{2,1,0:T(8,128)(2,1)S(1)}, bf16[2,192,768]{2,1,0:T(8,128)(2,1)S(1)}, u32[]{:S(2)}, u32[]{:S(2)}) collective-permute-start(bf16[2,192,768]{2,1,0:T(8,128)(2,1)S(1)} %fusion.9), channel_id=1, source_target_pairs={{0,6},{8,10},{2,4},{10,8},{4,2},{12,14},{6,0},{14,12},{32,38},{40,... | collective-permute-start | bytes 1769480 | tf_op jit(solution)/shard_map/ppermute | solution.py:508
  158.2 9.1 %collective-permute-start.17 = (bf16[2,192,768]{2,1,0:T(8,128)(2,1)S(1)}, bf16[2,192,768]{2,1,0:T(8,128)(2,1)S(1)}, u32[]{:S(2)}, u32[]{:S(2)}) collective-permute-start(bf16[2,192,768]{2,1,0:T(8,128)(2,1)S(1)} %fusion.8), channel_id=1, source_target_pairs={{0,96},{8,40},{2,98},{10,42},{4,100},{12,44},{6,102},{14,46},{32,6... | collective-permute-start | bytes 1769480 | tf_op jit(solution)/shard_map/ppermute | solution.py:508
  158.4 10.3 %collective-permute-start.16 = (bf16[1,192,768]{2,1,0:T(8,128)(2,1)S(1)}, bf16[1,192,768]{2,1,0:T(8,128)(2,1)S(1)}, u32[]{:S(2)}, u32[]{:S(2)}) collective-permute-start(bf16[1,192,768]{2,1,0:T(8,128)(2,1)S(1)} %fusion.19), channel_id=1, source_target_pairs={{0,6},{8,10},{2,4},{10,8},{4,2},{12,14},{6,0},{14,12},{32,38},{40,... | collective-permute-start | bytes 884744 | tf_op jit(solution)/shard_map/ppermute | solution.py:508
  159.0 11.5 %collective-permute-start.15 = (bf16[1,192,768]{2,1,0:T(8,128)(2,1)S(1)}, bf16[1,192,768]{2,1,0:T(8,128)(2,1)S(1)}, u32[]{:S(2)}, u32[]{:S(2)}) collective-permute-start(bf16[1,192,768]{2,1,0:T(8,128)(2,1)S(1)} %fusion.18), channel_id=1, source_target_pairs={{0,96},{8,40},{2,98},{10,42},{4,100},{12,44},{6,102},{14,46},{32,6... | collective-permute-start | bytes 884744 | tf_op jit(solution)/shard_map/ppermute | solution.py:508
  171.9 9.0 %collective-permute-start.20 = (bf16[320,768]{1,0:T(8,128)(2,1)S(1)}, bf16[320,768]{1,0:T(8,128)(2,1)S(1)}, u32[]{:S(2)}, u32[]{:S(2)}) collective-permute-start(bf16[320,768]{1,0:T(8,128)(2,1)S(1)} %pad_maximum_fusion.8), channel_id=1, source_target_pairs={{0,32},{8,104},{2,34},{10,106},{4,36},{12,108},{6,38},{14,110},{32... | collective-permute-start | bytes 1474568 | tf_op jit(solution)/shard_map/ppermute | solution.py:508
  174.6 8.4 %collective-permute-start.19 = (bf16[2,3,48,768]{3,2,1,0:T(8,128)(2,1)S(1)}, bf16[2,3,48,768]{3,2,1,0:T(8,128)(2,1)S(1)}, u32[]{:S(2)}, u32[]{:S(2)}) collective-permute-start(bf16[2,3,48,768]{3,2,1,0:T(8,128)(2,1)S(1)} %pad_maximum_fusion.10), channel_id=1, source_target_pairs={{0,16},{8,25},{2,18},{10,27},{4,20},{12,29},{6,22},{14,31},{32,48}... | collective-permute-start | bytes 1327112 | tf_op jit(solution)/shard_map/ppermute | solution.py:508
  183.1 5.7 %collective-permute-start.22 = (bf16[176,768]{1,0:T(8,128)(2,1)S(1)}, bf16[176,768]{1,0:T(8,128)(2,1)S(1)}, u32[]{:S(2)}, u32[]{:S(2)}) collective-permute-start(bf16[176,768]{1,0:T(8,128)(2,1)S(1)} %pad_maximum_fusion.14), channel_id=1, source_target_pairs={{0,96},{8,40},{2,98},{10,42},{4,100},{12,44},{6,102},{14,46},{32,6... | collective-permute-start | bytes 811016 | tf_op jit(solution)/shard_map/ppermute | solution.py:508
  183.2 5.6 %collective-permute-start.21 = (bf16[3,48,768]{2,1,0:T(8,128)(2,1)S(1)}, bf16[3,48,768]{2,1,0:T(8,128)(2,1)S(1)}, u32[]{:S(2)}, u32[]{:S(2)}) collective-permute-start(bf16[3,48,768]{2,1,0:T(8,128)(2,1)S(1)} %fusion.15), channel_id=1, source_target_pairs={{0,17},{8,24},{2,19},{10,26},{4,21},{12,28},{6,23},{14,30},{32,49}... | collective-permute-start | bytes 663560 | tf_op jit(solution)/shard_map/ppermute | solution.py:508
  189.1 6.6 %collective-permute-start.23 = (bf16[176,768]{1,0:T(8,128)(2,1)S(1)}, bf16[176,768]{1,0:T(8,128)(2,1)S(1)}, u32[]{:S(2)}, u32[]{:S(2)}) collective-permute-start(bf16[176,768]{1,0:T(8,128)(2,1)S(1)} %pad_maximum_fusion.15), channel_id=1, source_target_pairs={{0,2},{8,14},{2,0},{10,12},{4,6},{12,10},{6,4},{14,8},{32,34},{40,... | collective-permute-start | bytes 811016 | tf_op jit(solution)/shard_map/ppermute | solution.py:508
  189.5 6.2 %collective-permute-start.24 = (bf16[3,48,768]{2,1,0:T(8,128)(2,1)S(1)}, bf16[3,48,768]{2,1,0:T(8,128)(2,1)S(1)}, u32[]{:S(2)}, u32[]{:S(2)}) collective-permute-start(bf16[3,48,768]{2,1,0:T(8,128)(2,1)S(1)} %fusion.13), channel_id=1, source_target_pairs={{0,16},{8,25},{2,18},{10,27},{4,20},{12,29},{6,22},{14,31},{32,48}... | collective-permute-start | bytes 663560 | tf_op jit(solution)/shard_map/ppermute | solution.py:508
  195.9 5.7 %collective-permute-start.25 = (bf16[176,768]{1,0:T(8,128)(2,1)S(1)}, bf16[176,768]{1,0:T(8,128)(2,1)S(1)}, u32[]{:S(2)}, u32[]{:S(2)}) collective-permute-start(bf16[176,768]{1,0:T(8,128)(2,1)S(1)} %pad_maximum_fusion.16), channel_id=1, source_target_pairs={{0,6},{8,10},{2,4},{10,8},{4,2},{12,14},{6,0},{14,12},{32,38},{40,... | collective-permute-start | bytes 811016 | tf_op jit(solution)/shard_map/ppermute | solution.py:508
  196.3 5.3 %collective-permute-start.26 = (bf16[3,48,768]{2,1,0:T(8,128)(2,1)S(1)}, bf16[3,48,768]{2,1,0:T(8,128)(2,1)S(1)}, u32[]{:S(2)}, u32[]{:S(2)}) collective-permute-start(bf16[3,48,768]{2,1,0:T(8,128)(2,1)S(1)} %add.452), channel_id=1, source_target_pairs={{0,17},{8,24},{2,19},{10,26},{4,21},{12,28},{6,23},{14,30},{32,49}... | collective-permute-start | bytes 663560 | tf_op jit(solution)/shard_map/ppermute | solution.py:508
  201.8 5.7 %collective-permute-start.27 = (bf16[176,768]{1,0:T(8,128)(2,1)S(1)}, bf16[176,768]{1,0:T(8,128)(2,1)S(1)}, u32[]{:S(2)}, u32[]{:S(2)}) collective-permute-start(bf16[176,768]{1,0:T(8,128)(2,1)S(1)} %pad_maximum_fusion.17), channel_id=1, source_target_pairs={{0,17},{8,24},{2,19},{10,26},{4,21},{12,28},{6,23},{14,30},{32,49}... | collective-permute-start | bytes 811016 | tf_op jit(solution)/shard_map/ppermute | solution.py:508
  201.9 5.6 %collective-permute-start.28 = (bf16[3,48,768]{2,1,0:T(8,128)(2,1)S(1)}, bf16[3,48,768]{2,1,0:T(8,128)(2,1)S(1)}, u32[]{:S(2)}, u32[]{:S(2)}) collective-permute-start(bf16[3,48,768]{2,1,0:T(8,128)(2,1)S(1)} %add.457), channel_id=1, source_target_pairs={{0,96},{8,40},{2,98},{10,42},{4,100},{12,44},{6,102},{14,46},{32,6... | collective-permute-start | bytes 663560 | tf_op jit(solution)/shard_map/ppermute | solution.py:508
  207.7 13.0 %collective-permute-start.30 = (bf16[2,3,48,768]{3,2,1,0:T(8,128)(2,1)S(1)}, bf16[2,3,48,768]{3,2,1,0:T(8,128)(2,1)S(1)}, u32[]{:S(2)}, u32[]{:S(2)}) collective-permute-start(bf16[2,3,48,768]{3,2,1,0:T(8,128)(2,1)S(1)} %pad_maximum_fusion.13), channel_id=1, source_target_pairs={{0,32},{8,104},{2,34},{10,106},{4,36},{12,108},{6,38},{14,110},{32... | collective-permute-start | bytes 1327112 | tf_op jit(solution)/shard_map/ppermute | solution.py:508
  208.6 11.4 %collective-permute-start.29 = (bf16[320,768]{1,0:T(8,128)(2,1)S(1)}, bf16[320,768]{1,0:T(8,128)(2,1)S(1)}, u32[]{:S(2)}, u32[]{:S(2)}) collective-permute-start(bf16[320,768]{1,0:T(8,128)(2,1)S(1)} %pad_maximum_fusion.9), channel_id=1, source_target_pairs={{0,16},{8,25},{2,18},{10,27},{4,20},{12,29},{6,22},{14,31},{32,48}... | collective-permute-start | bytes 1474568 | tf_op jit(solution)/shard_map/ppermute | solution.py:508
  222.1 25.0 %collective-permute-start.36 = (bf16[144,1536]{1,0:T(8,128)(2,1)S(1)}, bf16[144,1536]{1,0:T(8,128)(2,1)S(1)}, u32[]{:S(2)}, u32[]{:S(2)}) collective-permute-start(bf16[144,1536]{1,0:T(8,128)(2,1)S(1)} %get-tuple-element.302), channel_id=1, source_target_pairs={{4,1},{5,9},{2,2},{3,10},{0,3},{1,11},{12,5},{13,13},{10,6},{11,14... | collective-permute-start | bytes 1327112 | tf_op jit(solution)/shard_map/ppermute | solution.py:490
  235.2 31.4 %collective-permute-start.31 = (bf16[3,192,768]{2,1,0:T(8,128)(2,1)S(1)}, bf16[3,192,768]{2,1,0:T(8,128)(2,1)S(1)}, u32[]{:S(2)}, u32[]{:S(2)}) collective-permute-start(bf16[3,192,768]{2,1,0:T(8,128)(2,1)S(1)} %bitcast.124), channel_id=1, source_target_pairs={{0,96},{8,40},{2,98},{10,42},{4,100},{12,44},{6,102},{14,46},{32,6... | collective-permute-start | bytes 2654216 | tf_op jit(solution)/shard_map/ppermute | solution.py:508
  237.0 29.6 %collective-permute-start.32 = (bf16[3,192,768]{2,1,0:T(8,128)(2,1)S(1)}, bf16[3,192,768]{2,1,0:T(8,128)(2,1)S(1)}, u32[]{:S(2)}, u32[]{:S(2)}) collective-permute-start(bf16[3,192,768]{2,1,0:T(8,128)(2,1)S(1)} %bitcast.126), channel_id=1, source_target_pairs={{0,6},{8,10},{2,4},{10,8},{4,2},{12,14},{6,0},{14,12},{32,38},{40,... | collective-permute-start | bytes 2654216 | tf_op jit(solution)/shard_map/ppermute | solution.py:508
  237.6 18.4 %collective-permute-start.35 = (bf16[144,1536]{1,0:T(8,128)(2,1)S(1)}, bf16[144,1536]{1,0:T(8,128)(2,1)S(1)}, u32[]{:S(2)}, u32[]{:S(2)}) collective-permute-start(bf16[144,1536]{1,0:T(8,128)(2,1)S(1)} %get-tuple-element.303), channel_id=1, source_target_pairs={{4,0},{5,8},{2,1},{3,9},{0,2},{1,10},{12,4},{13,12},{10,5},{11,13}... | collective-permute-start | bytes 1327112 | tf_op jit(solution)/shard_map/ppermute | solution.py:490
  240.4 15.7 %collective-permute-start.34 = (bf16[144,1536]{1,0:T(8,128)(2,1)S(1)}, bf16[144,1536]{1,0:T(8,128)(2,1)S(1)}, u32[]{:S(2)}, u32[]{:S(2)}) collective-permute-start(bf16[144,1536]{1,0:T(8,128)(2,1)S(1)} %get-tuple-element.304), channel_id=1, source_target_pairs={{2,0},{3,8},{0,1},{1,9},{4,3},{5,11},{10,4},{11,12},{8,5},{9,13},{... | collective-permute-start | bytes 1327112 | tf_op jit(solution)/shard_map/ppermute | solution.py:490
  247.1 19.5 %copy-start.17 = (bf16[144,1536]{1,0:T(8,128)(2,1)}, bf16[144,1536]{1,0:T(8,128)(2,1)S(1)}, u32[]{:S(2)}) copy-start(bf16[144,1536]{1,0:T(8,128)(2,1)S(1)} %collective-permute-done.36) | copy-start | bytes 1327108
  247.1 19.5 %collective-permute-start.33 = (bf16[144,1536]{1,0:T(8,128)(2,1)S(1)}, bf16[144,1536]{1,0:T(8,128)(2,1)S(1)}, u32[]{:S(2)}, u32[]{:S(2)}) collective-permute-start(bf16[144,1536]{1,0:T(8,128)(2,1)S(1)} %get-tuple-element.305), channel_id=1, source_target_pairs={{0,0},{1,8},{4,2},{5,10},{2,3},{3,11},{8,4},{9,12},{12,6},{13,14},... | collective-permute-start | bytes 1327112 | tf_op jit(solution)/shard_map/ppermute | solution.py:490
  267.7 11.2 %collective-permute-start.37 = (bf16[2,3,192,768]{3,2,1,0:T(8,128)(2,1)S(1)}, bf16[2,3,192,768]{3,2,1,0:T(8,128)(2,1)}, u32[]{:S(2)}, u32[]{:S(2)}) collective-permute-start(bf16[2,3,192,768]{3,2,1,0:T(8,128)(2,1)S(1)} %pad_maximum_fusion.1.source0_ref), channel_id=1, source_target_pairs={{0,8},{8,0},{1,9},{9,1},{2,10},{10,2},{3,11},{11,3},{4,12},{12,4},... | collective-permute-start | bytes 5308424 | tf_op jit(solution)/shard_map/ppermute | solution.py:521
  267.8 11.1 %collective-permute-start.38 = (bf16[2,3,192,768]{3,2,1,0:T(8,128)(2,1)S(1)}, bf16[2,3,192,768]{3,2,1,0:T(8,128)(2,1)}, u32[]{:S(2)}, u32[]{:S(2)}) collective-permute-start(bf16[2,3,192,768]{3,2,1,0:T(8,128)(2,1)S(1)} %pad_maximum_fusion.2.source1_ref), channel_id=1, source_target_pairs={{0,8},{8,0},{1,9},{9,1},{2,10},{10,2},{3,11},{11,3},{4,12},{12,4},... | collective-permute-start | bytes 5308424 | tf_op jit(solution)/shard_map/ppermute | solution.py:521
  268.8 22.7 %collective-permute-start.40 = (bf16[2,3,192,768]{3,2,1,0:T(8,128)(2,1)S(1)}, bf16[2,3,192,768]{3,2,1,0:T(8,128)(2,1)}, u32[]{:S(2)}, u32[]{:S(2)}) collective-permute-start(bf16[2,3,192,768]{3,2,1,0:T(8,128)(2,1)S(1)} %pad_maximum_fusion.1.source0_ref), channel_id=1, source_target_pairs={{0,32},{8,104},{2,34},{10,106},{4,36},{12,108},{6,38},{14,110},{32... | collective-permute-start | bytes 5308424 | tf_op jit(solution)/shard_map/ppermute | solution.py:508
  268.8 22.8 %collective-permute-start.41 = (bf16[2,3,192,768]{3,2,1,0:T(8,128)(2,1)S(1)}, bf16[2,3,192,768]{3,2,1,0:T(8,128)(2,1)}, u32[]{:S(2)}, u32[]{:S(2)}) collective-permute-start(bf16[2,3,192,768]{3,2,1,0:T(8,128)(2,1)S(1)} %pad_maximum_fusion.2.source1_ref), channel_id=1, source_target_pairs={{0,2},{8,14},{2,0},{10,12},{4,6},{12,10},{6,4},{14,8},{32,34},{40,... | collective-permute-start | bytes 5308424 | tf_op jit(solution)/shard_map/ppermute | solution.py:508
  269.6 9.3 %collective-permute-start.39 = (f32[16,768]{1,0:T(8,128)}, f32[16,768]{1,0:T(8,128)S(1)}, u32[]{:S(2)}, u32[]{:S(2)}) collective-permute-start(f32[16,768]{1,0:T(8,128)} %fusion.37), channel_id=1, source_target_pairs={{0,8},{8,0},{1,9},{9,1},{2,10},{10,2},{3,11},{11,3},{4,12},{12,4},... | collective-permute-start | bytes 147464 | tf_op jit(solution)/shard_map/ppermute | solution.py:521
  278.9 13.2 %copy-start.22 = (f32[16,768]{1,0:T(8,128)S(1)}, f32[16,768]{1,0:T(8,128)}, u32[]{:S(2)}) copy-start(f32[16,768]{1,0:T(8,128)} %fusion.37) | copy-start | bytes 147460
  291.6 7.3 %collective-permute-start.42 = (bf16[2,3,192,768]{3,2,1,0:T(8,128)(2,1)}, bf16[2,3,192,768]{3,2,1,0:T(8,128)(2,1)S(1)}, u32[]{:S(2)}, u32[]{:S(2)}) collective-permute-start(bf16[2,3,192,768]{3,2,1,0:T(8,128)(2,1)} %collective-permute-done.40.source0_ref), channel_id=1, source_target_pairs={{0,8},{8,0},{1,9},{9,1},{2,10},{10,2},{3,11},{11,3},{4,12},{12,4},... | collective-permute-start | bytes 5308424 | tf_op jit(solution)/shard_map/ppermute | solution.py:521
  291.7 7.3 %collective-permute-start.43 = (bf16[2,3,192,768]{3,2,1,0:T(8,128)(2,1)}, bf16[2,3,192,768]{3,2,1,0:T(8,128)(2,1)S(1)}, u32[]{:S(2)}, u32[]{:S(2)}) collective-permute-start(bf16[2,3,192,768]{3,2,1,0:T(8,128)(2,1)} %collective-permute-done.41.source1_ref), channel_id=1, source_target_pairs={{0,8},{8,0},{1,9},{9,1},{2,10},{10,2},{3,11},{11,3},{4,12},{12,4},... | collective-permute-start | bytes 5308424 | tf_op jit(solution)/shard_map/ppermute | solution.py:521
  (32 other events, 105.6 us)

commit v6 on v5

--- a/solution.py
+++ b/solution.py
@@ -35,7 +35,7 @@
 GELU_A = 0.044715
 
 AXES = ("y", "xl", "c", "z", "xh")
-VMEM_LIMIT = 60 * 1024 * 1024
+MIB = 1024 * 1024
 
 
 def mm(a, b):
@@ -113,7 +113,7 @@
             jax.ShapeDtypeStruct((ROWS, D), f32),
             jax.ShapeDtypeStruct((ROWS, D), bf16),
         ],
-        compiler_params=pltpu.CompilerParams(vmem_limit_bytes=VMEM_LIMIT),
+        compiler_params=pltpu.CompilerParams(vmem_limit_bytes=60 * MIB),
         cost_estimate=pl.CostEstimate(flops=16 * ROWS * KEYS * D, bytes_accessed=20_000_000, transcendentals=HEADS * ROWS * KEYS),
         name="attention_forward",
     )(queries, own, own, sibling, sibling, mask)
@@ -174,7 +174,7 @@
             out_specs=[col(0), several(2), several(4)],
         ),
         out_shape=[jax.ShapeDtypeStruct(shape, bf16) for shape in ((ROWS, D), (2, ROWS, D), (4, ROWS, D))],
-        compiler_params=pltpu.CompilerParams(vmem_limit_bytes=VMEM_LIMIT),
+        compiler_params=pltpu.CompilerParams(vmem_limit_bytes=60 * MIB),
         cost_estimate=pl.CostEstimate(flops=32 * ROWS * KEYS * D, bytes_accessed=25_000_000, transcendentals=0),
         name="attention_backward",
     )(at, queries, own, own, sibling, sibling, weights, heads_out, linv, grad_att)
@@ -299,7 +299,7 @@
         ]
         + [shape((4, NF // 2, QUARTER, D), bf16)] * 4
         + [shape((8, D), f32), shape((NF, 1, FCHUNK), f32)],
-        compiler_params=pltpu.CompilerParams(vmem_limit_bytes=VMEM_LIMIT),
+        compiler_params=pltpu.CompilerParams(vmem_limit_bytes=60 * MIB),
         cost_estimate=pl.CostEstimate(flops=12 * ROWS * D * FF, bytes_accessed=30_000_000, transcendentals=ROWS * FF),
         name="feed_forward",
     )(at, attended, both, both, out_w, vecs, up_b, up_w, down_w)
@@ -345,7 +345,7 @@
             scratch_shapes=[pltpu.VMEM((ROWS, D), bf16), pltpu.VMEM((ROWS, D), bf16), pltpu.VMEM((D, D), bf16)],
         ),
         out_shape=[jax.ShapeDtypeStruct((2, 1, QUARTER, D), bf16)] * 4,
-        compiler_params=pltpu.CompilerParams(vmem_limit_bytes=VMEM_LIMIT),
+        compiler_params=pltpu.CompilerParams(vmem_limit_bytes=44 * MIB),
         cost_estimate=pl.CostEstimate(flops=8 * ROWS * D * D, bytes_accessed=13_000_000, transcendentals=0),
         name="squares",
     )(at, gq, own, sent, arrived, arrived, arrived, *pairs)
@@ -394,7 +394,7 @@
         out_specs=[rows, fixed(16, D)],
         out_shape=[jax.ShapeDtypeStruct((ROWS, D), bf16), jax.ShapeDtypeStruct((16, D), f32)],
         scratch_shapes=[pltpu.VMEM((length, 3 * D), bf16)],
-        compiler_params=pltpu.CompilerParams(vmem_limit_bytes=VMEM_LIMIT),
+        compiler_params=pltpu.CompilerParams(vmem_limit_bytes=60 * MIB),
         cost_estimate=pl.CostEstimate(flops=6 * ROWS * D * D, bytes_accessed=10_000_000, transcendentals=0),
         name="input_gradient",
     )(gq, own, swapped, qkv_w, both, grad_hidden, gain, vec_grads, up_b_grad)
@@ -454,7 +454,7 @@
         ),
         out_shape=[shape((D, FF), f32), shape((FF, D), f32), shape((D, 3 * D), f32), shape((D, D), f32)],
         input_output_aliases={3 + index: index for index in range(len(before))},
-        compiler_params=pltpu.CompilerParams(vmem_limit_bytes=VMEM_LIMIT),
+        compiler_params=pltpu.CompilerParams(vmem_limit_bytes=16 * MIB),
         cost_estimate=pl.CostEstimate(flops=0, bytes_accessed=11_000_000, transcendentals=0),
         name="place_late" if late else "place_early",
     )(at, *pieces, *before)
@@ -466,34 +466,36 @@
 
 def scene_pairs(slot):
     pairs = []
-    for y, xl, z, xh in itertools.product(range(4), range(2), range(4), range(2)):
-        block = 2 * z + xh
-        scene = (slot - block) % 4
-        if scene < 3:
-            for c in range(2):
-                pairs.append((linear(y, xl, c, z, xh), linear(y, xl, block // 4, scene, c)))
+    for y, xl, c, z, xh in itertools.product(range(4), range(2), range(2), range(4), range(2)):
+        target = z ^ slot ^ (0 if xh == c else 2)
+        if target < 3:
+            pairs.append((linear(y, xl, c, z, xh), linear(y, xl, xh, target, c)))
     return pairs
 
 
-def to_scene(values, block):
+def to_scene(values, z, flip):
     pieces = []
     for slot in range(SLOTS):
-        scene = jnp.minimum((slot - block) % 4, 2)
+        scene = jnp.minimum(z ^ slot ^ flip, 2)
         pieces.append(lax.ppermute(lax.dynamic_index_in_dim(values, scene, 0, keepdims=False), AXES, scene_pairs(slot)))
     return pieces
 
 
-def send_from_scene(values):
-    pieces = []
-    for slot in range(SLOTS):
-        back = [(target, source) for source, target in scene_pairs(slot)]
-        pieces.append(lax.ppermute(values[slot * BLK : (slot + 1) * BLK], AXES, back))
-    return pieces
-
-
-def take_from_scene(pieces, block):
-    pieces = jnp.stack(pieces)
-    return jnp.stack([lax.dynamic_index_in_dim(pieces, (m + block) % 4, 0, keepdims=False) for m in range(3)])
+def turn(values):
+    pairs = [
+        (linear(y, xl, c, z, xh), linear(y, xl, xh, z, c))
+        for y, xl, c, z, xh in itertools.product(range(4), range(2), range(2), range(4), range(2))
+    ]
+    return lax.ppermute(values, AXES, pairs)
+
+
+def slot_block(values, offset, flip):
+    return lax.dynamic_slice_in_dim(values, (offset ^ flip) * BLK, BLK, 0)
+
+
+def for_home(stayed, first, second, both, z, core):
+    pieces = jnp.stack([stayed, jnp.where(core == 0, first, second), both, jnp.where(core == 0, second, first)])
+    return jnp.stack([lax.dynamic_index_in_dim(pieces, z ^ scene, 0, keepdims=False) for scene in range(3)])
 
 
 SWAP = ((0, 1), (1, 0))
@@ -564,9 +566,9 @@
 ):
     core, z, xh = lax.axis_index("c"), lax.axis_index("z"), lax.axis_index("xh")
 
-    block = 2 * z + xh
+    flip = jnp.where(xh == core, 0, 2)
     views = jnp.broadcast_to(view_counts.astype(bf16)[:, None, None], (3, BLK, LANES))
-    pieces = to_scene(jnp.concatenate([tokens, cotangent, views], axis=2), block)
+    pieces = to_scene(jnp.concatenate([tokens, cotangent, views], axis=2), z, flip)
     vecs = jnp.concatenate([jnp.stack([out_bias, ln2_gain, ln2_shift, down_bias]), jnp.zeros((4, D), f32)])
     gains = jnp.broadcast_to(ln1_gain[None, :], (8, D))
     weight_q, weight_kv = qkv_weight[:, :D], qkv_weight[:, D:]
@@ -576,8 +578,11 @@
     x = both[:, :D]
 
     row = jnp.arange(ROWS, dtype=jnp.int32)
-    offset = (row // BLK - z) % 4 * BLK + row % BLK
-    position = jnp.concatenate([offset + core * ROWS, offset + (1 - core) * ROWS])
+    slot = row // BLK
+    position = jnp.concatenate([
+        (2 * (z ^ slot ^ flip) + core) * BLK + row % BLK,
+        (2 * (z ^ slot ^ (2 - flip)) + 1 - core) * BLK + row % BLK,
+    ])
     usable = (position.astype(f32) < views * VIEW_TOK) | (position >= VIEWS_MAX * VIEW_TOK)
     mask = jnp.broadcast_to(jnp.where(usable, 0.0, masked_score).astype(bf16)[:, None], (KEYS, LANES))
 
@@ -643,7 +648,11 @@
     first = 1 + 2 * core
     keep = [(block_of(b, p), block_of(b, p ^ (4 - first))) for b, p in zip(blocks, places)]
     away = [jnp.stack([block_of(b, p ^ first), block_of(b, p ^ 2)]) for b, p in zip(blocks, places)]
-    keep, away, small = hold(keep, away, small)
+    second = 4 - first
+    back = jnp.concatenate([output, input_grad], axis=1)
+    over = jnp.concatenate([slot_block(back, first, flip), slot_block(back, 2, flip)], axis=0)
+    keep, away, small, over, back = hold(keep, away, small, over, back)
+    over = meet(over, "z", 0)
     one_way = meet(away[0], "x", 0)
     other_way, small = meet_with(away[1], small, "y", 0)
 
@@ -663,7 +672,10 @@
         one_way, other_way, small = hold(one_way, other_way, small)
         ends = [ends[0] + one_way, ends[1] + other_way]
 
-    ends, small, output, input_grad = hold(ends, small, output, input_grad)
+    over_first = over[:BLK]
+    over = jnp.concatenate([slot_block(back, second, flip), over[BLK:]], axis=0)
+    ends, small, over, over_first = hold(ends, small, over, over_first)
+    over = meet(over, "z", 1)
     one_way, small = meet_with(ends[0], small, "x", 1)
     other_way = meet(ends[1], "y", 1)
 
@@ -680,18 +692,18 @@
         for value, index in ((pair[0], p), (pair[1], p ^ (4 - first)), (more[0], p ^ first), (more[1], p ^ 2)):
             full = put_block(full, value, index)
         owns.append(full.reshape(NF // 2 + 1, QUARTER, D))
-    owns, small, output, input_grad = hold(owns, small, output, input_grad)
+    returned = for_home(slot_block(back, 0, flip), over_first, over[:BLK], over[BLK:], z, core)
+    owns, small, returned = hold(owns, small, returned)
     arrived = meet_parts(owns, 0, 1)
-    returned = send_from_scene(jnp.concatenate([output, input_grad], axis=1))
-
-    arrived, returned = hold(arrived, returned)
+    returned = turn(returned)
+
+    arrived, small, returned = hold(arrived, small, returned)
     pairs = [jnp.stack([o, a]) for o, a in zip(owns, arrived)]
     pairs, small = hold(pairs, small)
     got = meet_parts(pairs, 0, 0)
     own_other = [swap(v) for v in pairs]
     small_other = swap(small)
     placed = place(at, pairs, True, False)
-    returned = take_from_scene(returned, block)
     output, input_grad = returned[:, :, :D], returned[:, :, D:]
 
     own_other, small_other, placed, output, input_grad = hold(own_other, small_other, placed, output, input_grad)

time: 310 us -> 304 us (0.981)
  waiting for transfers between devices: 85.2 us -> 77 us
  Pallas kernels: 107 us -> 102 us
    ppermute x24 -> x26, starting transfers between devices: 18.2 us -> 34.5 us  [exchange(): return lax.ppermute(value, AXES, pairs)]
    ppermute x4 -> x1, waiting for transfers between devices: 16.4 us -> 2.92 us  [turn(): return lax.ppermute(values, AXES, pairs)]
    ppermute x4 -> x1, starting transfers between devices: 25.6 us -> 13.1 us  [turn(): return lax.ppermute(values, AXES, pairs)]
    ppermute x24 -> x26, waiting for transfers between devices: 55.5 us -> 63.5 us  [exchange(): return lax.ppermute(value, AXES, pairs)]
    ppermute x12, starting transfers between devices: 7.19 us -> 3.14 us  [swap(): return lax.ppermute(value, 'c', SWAP)]
    ppermute x4, waiting for transfers between devices: 13.3 us -> 10.2 us  [to_scene(): lax.ppermute(lax.dynamic_index_in_dim(values, scene, 0, keepdims=False),...]
    unnamed x69 -> x65, local copies, waits for them, and re-layouts: 9.99 us -> 9.26 us
  transfers between devices with their start and end apart: 44 -> 43, of which waited for: 17 -> 18; matrix products, arithmetic and copies ran while one was open for 7% -> 8% of each run, Pallas kernels for 17% -> 16%
where the time goes in v6:
time: 304 us; the launch traced here: 299 us
  Pallas kernels  102 us (34%)
  waiting for transfers between devices  77 us (25%)
  starting transfers between devices  68.7 us (23%)
  other arithmetic  22.5 us (7%)
  local copies, waits for them, and re-layouts  20.9 us (7%)
  matrix products  4.58 us (2%)
    ppermute x26, waiting for transfers between devices, exchange(): return lax.ppermute(value, AXES, pairs)  63.5 us
    ppermute x26, starting transfers between devices, exchange(): return lax.ppermute(value, AXES, pairs)  34.5 us
    pallas_call x1, Pallas kernels, feed_forward(): pl.pallas_call(feed_forward_kernel, grid_spec=pltpu.PrefetchScalarGridSpe...  32.9 us
    pallas_call x1, Pallas kernels, attention_backward(): pl.pallas_call(attention_backward_kernel, grid_spec=pltpu.PrefetchScalarG...  19.4 us
    pallas_call x4, Pallas kernels, place(): pl.pallas_call(functools.partial(place_kernel, mine, late), grid_spec=plt...  17.9 us
    ppermute x4, starting transfers between devices, to_scene(): lax.ppermute(lax.dynamic_index_in_dim(values, scene, 0, keepdims=False),...  17.9 us
    pallas_call x1, Pallas kernels, attention_forward(): pl.pallas_call(attention_forward_kernel, grid=(PAIRS,), in_specs=[col(0),...  15.8 us
    convert_element_type x14, other arithmetic, add(): functools.reduce(jnp.add, [term.astype(f32) for term in terms]).astype(bf16)  15.1 us
  transfers between devices with their start and end apart: 43, of which 18 were waited for; matrix products, arithmetic and copies ran while one was open for 8% of the time, Pallas kernels for 16%

profile of v6, /device:TPU:1, one launch (start us, length us, event | category | flops | bytes accessed | tf_op | source)
XLA Modules:
  0.0 298.6 jit_solution(11179148128090973220)
XLA Ops:
  3.0 7.4 %collective-permute-start.3 = (bf16[144,1664]{1,0:T(8,128)(2,1)S(1)}, bf16[144,1664]{1,0:T(8,128)(2,1)S(1)}, u32[]{:S(2)}, u32[]{:S(2)}) collective-permute-start(bf16[144,1664]{1,0:T(8,128)(2,1)S(1)} %get-tuple-element.304), channel_id=1, source_target_pairs={{1,10},{2,4},{3,8},{4,2},{6,0},{7,12},{8,3},{10,1},{11,13},{13,11}... | collective-permute-start | bytes 1437704 | tf_op jit(solution)/shard_map/ppermute | solution.py:480
  10.4 1.9 collective-permute-start.2
  13.7 7.3 %collective-permute-start = (bf16[144,1664]{1,0:T(8,128)(2,1)S(1)}, bf16[144,1664]{1,0:T(8,128)(2,1)S(1)}, u32[]{:S(2)}, u32[]{:S(2)}) collective-permute-start(bf16[144,1664]{1,0:T(8,128)(2,1)S(1)} %get-tuple-element.307), channel_id=1, source_target_pairs={{0,0},{1,12},{2,2},{4,4},{5,8},{7,10},{8,5},{9,9},{11,11},{12,1},{... | collective-permute-start | bytes 1437704 | tf_op jit(solution)/shard_map/ppermute | solution.py:480
  22.4 3.8 %collective-permute-done.1 = bf16[144,1664]{1,0:T(8,128)(2,1)} collective-permute-done((bf16[144,1664]{1,0:T(8,128)(2,1)S(1)}, bf16[144,1664]{1,0:T(8,128)(2,1)}, u32[]{:S(2)}, u32[]{:S(2)}) %collective-permute-start.1) | collective-permute-done | bytes 479264 | tf_op jit(solution)/shard_map/ppermute | solution.py:480
  26.2 6.4 %collective-permute-done = bf16[144,1664]{1,0:T(8,128)(2,1)S(1)} collective-permute-done((bf16[144,1664]{1,0:T(8,128)(2,1)S(1)}, bf16[144,1664]{1,0:T(8,128)(2,1)S(1)}, u32[]{:S(2)}, u32[]{:S(2)}) %collective-permute-start) | collective-permute-done | bytes 479264 | tf_op jit(solution)/shard_map/ppermute | solution.py:480
  37.8 2.8 add_convert_fusion.ko_ref.vo_ref
  42.6 1.8 add_convert_fusion.3.q_ref
  45.7 15.8 %attention_forward.1 = (bf16[12,576,1152]{2,1,0:T(8,128)(2,1)}, f32[576,768]{1,0:T(8,128)}, f32[576,768]{1,0:T(8,128)}, bf16[576,768]{1,0:T(8,128)(2,1)}) custom-call(bf16[576,768]{1,0:T(8,128)(2,1)} %add_convert_fusion.3.q_ref, bf16[576,1536]{1,0:T(8,128)(2,1)} %add_convert_fusion.ko_ref.vo_ref, bf16[576,1536]{1,0:T(8,128)(2,1)} %add_convert_fusion.ko_ref.vo_ref, ...), custom_call_target="tpu_custom_call" | custom-call | flops 8153726976 | bytes 20000000 | tf_op jit(solution)/shard_map/attention_forward/pallas_call | solution.py:105
  61.5 32.9 %feed_forward.1 = (bf16[576,768]{1,0:T(8,128)(2,1)}, f32[576,768]{1,0:T(8,128)}, bf16[576,768]{1,0:T(8,128)(2,1)}, bf16[576,768]{1,0:T(8,128)(2,1)}, bf16[4,2,19...) custom-call(s32[3]{0:T(128)} %pad_add_fusion.1.at_ref, ...), custom_call_target="tpu_custom_call" | custom-call | flops 16307453952 | bytes 30000000 | tf_op jit(solution)/shard_map/feed_forward/pallas_call | solution.py:278
  95.8 19.4 %attention_backward.1 = (bf16[576,768]{1,0:T(8,128)(2,1)}, bf16[2,576,768]{2,1,0:T(8,128)(2,1)}, bf16[4,576,768]{2,1,0:T(8,128)(2,1)}) custom-call(s32[3]{0:T(128)} %pad_add_fusion.1.at_ref, bf16[576,768]{1,0:T(8,128)(2,1)} %add_convert_fusion.3.q_ref, bf16[576,1536]{1,0:T(8,128)(2,1)} %add_convert_fusion.ko_ref.vo_ref, ...), custom_call_target="tpu_custom_call" | custom-call | flops 16307453952 | bytes 25000000 | tf_op jit(solution)/shard_map/attention_backward/pallas_call | solution.py:165
  115.8 3.1 %add_convert_fusion.1 = bf16[2,2,192,768]{3,2,1,0:T(8,128)(2,1)} fusion(bf16[4,2,192,768]{3,2,1,0:T(8,128)(2,1)} %collective-permute-done.6, bf16[4,2,192,768]{3,2,1,0:T(8,128)(2,1)} %get-tuple-element.173), kind=kLoop, calls=%fused_computation.1 | loop fusion | flops 2359296 | bytes 3538944 | tf_op jit(solution)/shard_map/convert_element_type | solution.py:534
  118.8 6.4 %collective-permute-start.12 = (bf16[2,2,192,768]{3,2,1,0:T(8,128)(2,1)}, bf16[2,2,192,768]{3,2,1,0:T(8,128)(2,1)}, u32[]{:S(2)}, u32[]{:S(2)}) collective-permute-start(bf16[2,2,192,768]{3,2,1,0:T(8,128)(2,1)} %add_convert_fusion.1), channel_id=1, source_target_pairs={{0,2},{8,14},{2,0},{10,12},{4,6},{12,10},{6,4},{14,8},{32,34},{40,... | collective-permute-start | bytes 3538952 | tf_op jit(solution)/shard_map/ppermute | solution.py:510
  125.2 2.7 add_convert_fusion.2
  128.0 2.7 collective-permute-start.11
  130.7 1.8 copy-done.14
  134.9 7.7 %squares.1 = (bf16[2,1,192,768]{3,2,1,0:T(8,128)(2,1)S(1)}, bf16[2,1,192,768]{3,2,1,0:T(8,128)(2,1)}, bf16[2,1,192,768]{3,2,1,0:T(8,128)(2,1)S(1)}, bf16[2,1,192,768]{3,2,1,0:T(8,128)(2,1)}) custom-call(s32[3]{0:T(128)S(1)} %copy-done.13, bf16[576,768]{1,0:T(8,128)(2,1)S(1)} %copy-done.1, bf16[2,576,768]{2,1,0:T(8,128)(2,1)S(1)} %copy-done, ...), custom_call_target="tpu_custom_call" | custom-call | flops 2717908992 | bytes 13000000 | tf_op jit(solution)/shard_map/squares/pallas_call | solution.py:339
  144.2 1.8 collective-permute-start.14
  147.2 8.8 %input_gradient.1 = (bf16[576,768]{1,0:T(8,128)(2,1)}, f32[16,768]{1,0:T(8,128)}) custom-call(bf16[576,768]{1,0:T(8,128)(2,1)} %get-tuple-element.164.gq_ref, bf16[2,576,768]{2,1,0:T(8,128)(2,1)} %get-tuple-element.165.own_ref, bf16[4,576,768]{2,1,0:T(8,128)(2,1)} %copy-done.14, bf16[768,2304]{1,0:T(8,128)(2,1)} %w_ref.1, bf16[576,1536]{1,0:T(8,128)(2,1)} %copy-done.15, ...), custom_call_target="tpu_custom_call" | custom-call | flops 2038431744 | bytes 10000000 | tf_op jit(solution)/shard_map/input_gradient/pallas_call | solution.py:390
  157.3 1.8 collective-permute-start.16
  159.3 1.7 fusion.8
  161.0 1.5 fusion.9
  165.1 6.4 %collective-permute-done.18 = bf16[2,192,768]{2,1,0:T(8,128)(2,1)S(1)} collective-permute-done((bf16[2,192,768]{2,1,0:T(8,128)(2,1)S(1)}, bf16[2,192,768]{2,1,0:T(8,128)(2,1)S(1)}, u32[]{:S(2)}, u32[]{:S(2)}) %collective-permute-start.18) | collective-permute-done | bytes 589856 | tf_op jit(solution)/shard_map/ppermute | solution.py:510
  171.6 1.6 fusion.6
  173.2 1.8 fusion.7
  177.4 1.5 collective-permute-start.20
  178.8 2.1 collective-permute-start.19
  180.9 5.4 %collective-permute-done.20 = bf16[320,768]{1,0:T(8,128)(2,1)S(1)} collective-permute-done((bf16[320,768]{1,0:T(8,128)(2,1)S(1)}, bf16[320,768]{1,0:T(8,128)(2,1)S(1)}, u32[]{:S(2)}, u32[]{:S(2)}) %collective-permute-start.20) | collective-permute-done | bytes 491552 | tf_op jit(solution)/shard_map/ppermute | solution.py:510
  188.2 2.0 collective-permute-start.27
  190.5 2.5 collective-permute-done.22
  193.1 1.9 collective-permute-done.21
  196.0 2.2 collective-permute-start.24
  198.2 6.3 %collective-permute-done.23 = bf16[176,768]{1,0:T(8,128)(2,1)} collective-permute-done((bf16[176,768]{1,0:T(8,128)(2,1)S(1)}, bf16[176,768]{1,0:T(8,128)(2,1)}, u32[]{:S(2)}, u32[]{:S(2)}) %collective-permute-start.23) | collective-permute-done | bytes 270368 | tf_op jit(solution)/shard_map/ppermute | solution.py:510
  208.2 3.6 %collective-permute-done.25 = bf16[176,768]{1,0:T(8,128)(2,1)S(1)} collective-permute-done((bf16[176,768]{1,0:T(8,128)(2,1)S(1)}, bf16[176,768]{1,0:T(8,128)(2,1)S(1)}, u32[]{:S(2)}, u32[]{:S(2)}) %collective-permute-start.25) | collective-permute-done | bytes 270368 | tf_op jit(solution)/shard_map/ppermute | solution.py:510
  215.5 3.0 %collective-permute-done.28 = bf16[176,768]{1,0:T(8,128)(2,1)S(1)} collective-permute-done((bf16[176,768]{1,0:T(8,128)(2,1)S(1)}, bf16[176,768]{1,0:T(8,128)(2,1)S(1)}, u32[]{:S(2)}, u32[]{:S(2)}) %collective-permute-start.28) | collective-permute-done | bytes 270368 | tf_op jit(solution)/shard_map/ppermute | solution.py:510
  218.7 1.5 collective-permute-start.31
  220.4 2.0 collective-permute-start.30
  222.5 10.0 %collective-permute-done.30 = bf16[320,768]{1,0:T(8,128)(2,1)S(1)} collective-permute-done((bf16[320,768]{1,0:T(8,128)(2,1)S(1)}, bf16[320,768]{1,0:T(8,128)(2,1)S(1)}, u32[]{:S(2)}, u32[]{:S(2)}) %collective-permute-start.30) | collective-permute-done | bytes 491552 | tf_op jit(solution)/shard_map/ppermute | solution.py:510
  233.4 13.1 %collective-permute-start.35 = (bf16[3,144,1536]{2,1,0:T(8,128)(2,1)S(1)}, bf16[3,144,1536]{2,1,0:T(8,128)(2,1)S(1)}, u32[]{:S(2)}, u32[]{:S(2)}) collective-permute-start(bf16[3,144,1536]{2,1,0:T(8,128)(2,1)S(1)} %pad_maximum_fusion.5), channel_id=1, source_target_pairs={{0,0},{1,8},{2,2},{3,10},{4,4},{5,12},{6,6},{7,14},{8,1},{9,9},{10... | collective-permute-start | bytes 3981320 | tf_op jit(solution)/shard_map/ppermute | solution.py:489
  246.8 11.9 %collective-permute-done.33 = bf16[3,192,768]{2,1,0:T(8,128)(2,1)S(1)} collective-permute-done((bf16[3,192,768]{2,1,0:T(8,128)(2,1)S(1)}, bf16[3,192,768]{2,1,0:T(8,128)(2,1)S(1)}, u32[]{:S(2)}, u32[]{:S(2)}) %collective-permute-start.33) | collective-permute-done | bytes 884768 | tf_op jit(solution)/shard_map/ppermute | solution.py:510
  259.0 2.9 collective-permute-done.35
  262.9 1.5 collective-permute-start.39
  264.3 2.1 collective-permute-start.40
  267.6 4.4 %place_early.2 = (f32[768,3072]{1,0:T(8,128)}, f32[3072,768]{1,0:T(8,128)}, f32[768,2304]{1,0:T(8,128)}, f32[768,768]{1,0:T(8,128)}) custom-call(s32[3]{0:T(128)S(1)} %copy-done.13, bf16[2,3,192,768]{3,2,1,0:T(8,128)(2,1)S(1)} %pad_maximum_fusion.2.source0_ref, bf16[2,3,192,768]{3,2,1,0:T(8,128)(2,1)S(1)} %pad_maximum_fusion.3.source1_ref), custom_call_target="tpu_custom_call" | custom-call | bytes 11000000 | tf_op jit(solution)/shard_map/place_early/pallas_call | solution.py:444
  272.1 4.4 %place_early.3 = (f32[768,3072]{1,0:T(8,128)}, f32[3072,768]{1,0:T(8,128)}, f32[768,2304]{1,0:T(8,128)}, f32[768,768]{1,0:T(8,128)}) custom-call(s32[3]{0:T(128)S(1)} %copy-done.13, bf16[2,3,192,768]{3,2,1,0:T(8,128)(2,1)S(1)} %collective-permute-done.36.source0_ref, ...), custom_call_target="tpu_custom_call", output_to_operand_aliasing={{0}: (3, {}), {1}: (4, {}), {2}: (5, {}), {3}: (6, {})} | custom-call | bytes 11000000 | tf_op jit(solution)/shard_map/place_early/pallas_call | solution.py:444
  276.5 8.9 %collective-permute-done.39.source0_ref = bf16[2,3,192,768]{3,2,1,0:T(8,128)(2,1)S(1)} collective-permute-done((bf16[2,3,192,768]{3,2,1,0:T(8,128)(2,1)S(1)}, bf16[2,3,192,768]{3,2,1,0:T(8,128)(2,1)S(1)}, u32[]{:S(2)}, u32[]{:S(2)}) %collective-permute-start.39) | collective-permute-done | bytes 1769504 | tf_op jit(solution)/shard_map/ppermute | solution.py:510
  285.5 1.5 collective-permute-done.40.source1_ref
  288.7 4.4 %place_late.2 = (f32[768,3072]{1,0:T(8,128)}, f32[3072,768]{1,0:T(8,128)}, f32[768,2304]{1,0:T(8,128)}, f32[768,768]{1,0:T(8,128)}) custom-call(s32[3]{0:T(128)S(1)} %copy-done.13, bf16[2,3,192,768]{3,2,1,0:T(8,128)(2,1)S(1)} %collective-permute-done.39.source0_ref, ...), custom_call_target="tpu_custom_call", output_to_operand_aliasing={{0}: (3, {}), {1}: (4, {}), {2}: (5, {}), {3}: (6, {})} | custom-call | bytes 11000000 | tf_op jit(solution)/shard_map/place_late/pallas_call | solution.py:444
  293.8 4.7 %place_late.3 = (f32[768,3072]{1,0:T(8,128)}, f32[3072,768]{1,0:T(8,128)}, f32[768,2304]{1,0:T(8,128)}, f32[768,768]{1,0:T(8,128)}) custom-call(s32[3]{0:T(128)S(1)} %copy-done.13, bf16[2,3,192,768]{3,2,1,0:T(8,128)(2,1)} %collective-permute-done.41.source0_ref, ...), custom_call_target="tpu_custom_call", output_to_operand_aliasing={{0}: (3, {}), {1}: (4, {}), {2}: (5, {}), {3}: (6, {})} | custom-call | bytes 11000000 | tf_op jit(solution)/shard_map/place_late/pallas_call | solution.py:444
  (222 shorter events, 43.0 us)
Async XLA Ops:
  3.0 19.3 %collective-permute-start.3 = (bf16[144,1664]{1,0:T(8,128)(2,1)S(1)}, bf16[144,1664]{1,0:T(8,128)(2,1)S(1)}, u32[]{:S(2)}, u32[]{:S(2)}) collective-permute-start(bf16[144,1664]{1,0:T(8,128)(2,1)S(1)} %get-tuple-element.304), channel_id=1, source_target_pairs={{1,10},{2,4},{3,8},{4,2},{6,0},{7,12},{8,3},{10,1},{11,13},{13,11}... | collective-permute-start | bytes 1437704 | tf_op jit(solution)/shard_map/ppermute | solution.py:480
  10.4 11.9 %collective-permute-start.2 = (bf16[144,1664]{1,0:T(8,128)(2,1)S(1)}, bf16[144,1664]{1,0:T(8,128)(2,1)}, u32[]{:S(2)}, u32[]{:S(2)}) collective-permute-start(bf16[144,1664]{1,0:T(8,128)(2,1)S(1)} %get-tuple-element.305), channel_id=1, source_target_pairs={{0,4},{1,8},{3,10},{4,0},{5,12},{6,2},{8,1},{9,13},{10,3},{12,5},{... | collective-permute-start | bytes 1437704 | tf_op jit(solution)/shard_map/ppermute | solution.py:480
  12.4 13.8 %collective-permute-start.1 = (bf16[144,1664]{1,0:T(8,128)(2,1)S(1)}, bf16[144,1664]{1,0:T(8,128)(2,1)}, u32[]{:S(2)}, u32[]{:S(2)}) collective-permute-start(bf16[144,1664]{1,0:T(8,128)(2,1)S(1)} %get-tuple-element.306), channel_id=1, source_target_pairs={{0,2},{2,0},{3,12},{5,10},{6,4},{7,8},{9,11},{10,5},{11,9},{12,3},... | collective-permute-start | bytes 1437704 | tf_op jit(solution)/shard_map/ppermute | solution.py:480
  13.7 18.9 %collective-permute-start = (bf16[144,1664]{1,0:T(8,128)(2,1)S(1)}, bf16[144,1664]{1,0:T(8,128)(2,1)S(1)}, u32[]{:S(2)}, u32[]{:S(2)}) collective-permute-start(bf16[144,1664]{1,0:T(8,128)(2,1)S(1)} %get-tuple-element.307), channel_id=1, source_target_pairs={{0,0},{1,12},{2,2},{4,4},{5,8},{7,10},{8,5},{9,9},{11,11},{12,1},{... | collective-permute-start | bytes 1437704 | tf_op jit(solution)/shard_map/ppermute | solution.py:480
  21.0 11.6 %copy-start.24 = (f32[768]{0:T(1024)S(1)}, f32[768]{0:T(1024)}, u32[]{:S(2)}) copy-start(f32[768]{0:T(1024)} %param.18) | copy-start | bytes 9220
  40.6 4.2 %collective-permute-start.4 = (bf16[576,1536]{1,0:T(8,128)(2,1)}, bf16[576,1536]{1,0:T(8,128)(2,1)}, u32[]{:S(2)}, u32[]{:S(2)}) collective-permute-start(bf16[576,1536]{1,0:T(8,128)(2,1)} %add_convert_fusion.ko_ref.vo_ref), channel_id=1, source_target_pairs={{0,8},{8,0},{1,9},{9,1},{2,10},{10,2},{3,11},{11,3},{4,12},{12,4},... | collective-permute-start | bytes 5308424 | tf_op jit(solution)/shard_map/ppermute | solution.py:523
  61.5 33.5 %copy-start.2 = (bf16[576,768]{1,0:T(8,128)(2,1)S(1)}, bf16[576,768]{1,0:T(8,128)(2,1)}, u32[]{:S(2)}) copy-start(bf16[576,768]{1,0:T(8,128)(2,1)} %get-tuple-element.161.att_ref) | copy-start | bytes 2654212
  94.5 20.7 %collective-permute-start.5 = (bf16[4,2,192,768]{3,2,1,0:T(8,128)(2,1)}, bf16[4,2,192,768]{3,2,1,0:T(8,128)(2,1)}, u32[]{:S(2)}, u32[]{:S(2)}) collective-permute-start(bf16[4,2,192,768]{3,2,1,0:T(8,128)(2,1)} %get-tuple-element.166), channel_id=1, source_target_pairs={{0,8},{8,0},{1,9},{9,1},{2,10},{10,2},{3,11},{11,3},{4,12},{12,4},... | collective-permute-start | bytes 7077896 | tf_op jit(solution)/shard_map/ppermute | solution.py:523
  94.8 20.4 %collective-permute-start.6 = (bf16[4,2,192,768]{3,2,1,0:T(8,128)(2,1)}, bf16[4,2,192,768]{3,2,1,0:T(8,128)(2,1)}, u32[]{:S(2)}, u32[]{:S(2)}) collective-permute-start(bf16[4,2,192,768]{3,2,1,0:T(8,128)(2,1)} %get-tuple-element.167), channel_id=1, source_target_pairs={{0,8},{8,0},{1,9},{9,1},{2,10},{10,2},{3,11},{11,3},{4,12},{12,4},... | collective-permute-start | bytes 7077896 | tf_op jit(solution)/shard_map/ppermute | solution.py:523
  95.0 20.1 %collective-permute-start.7 = (bf16[576,768]{1,0:T(8,128)(2,1)S(1)}, bf16[576,768]{1,0:T(8,128)(2,1)S(1)}, u32[]{:S(2)}, u32[]{:S(2)}) collective-permute-start(bf16[576,768]{1,0:T(8,128)(2,1)S(1)} %copy-done.2), channel_id=1, source_target_pairs={{0,8},{8,0},{1,9},{9,1},{2,10},{10,2},{3,11},{11,3},{4,12},{12,4},... | collective-permute-start | bytes 2654216 | tf_op jit(solution)/shard_map/ppermute | solution.py:523
  95.5 19.7 %collective-permute-start.8 = (bf16[576,768]{1,0:T(8,128)(2,1)}, bf16[576,768]{1,0:T(8,128)(2,1)S(1)}, u32[]{:S(2)}, u32[]{:S(2)}) collective-permute-start(bf16[576,768]{1,0:T(8,128)(2,1)} %get-tuple-element.168.gb_ref), channel_id=1, source_target_pairs={{0,8},{8,0},{1,9},{9,1},{2,10},{10,2},{3,11},{11,3},{4,12},{12,4},... | collective-permute-start | bytes 2654216 | tf_op jit(solution)/shard_map/ppermute | solution.py:523
  115.2 15.5 %collective-permute-start.9 = (bf16[4,576,768]{2,1,0:T(8,128)(2,1)}, bf16[4,576,768]{2,1,0:T(8,128)(2,1)S(1)}, u32[]{:S(2)}, u32[]{:S(2)}) collective-permute-start(bf16[4,576,768]{2,1,0:T(8,128)(2,1)} %get-tuple-element.170.other_ref), channel_id=1, source_target_pairs={{0,8},{8,0},{1,9},{9,1},{2,10},{10,2},{3,11},{11,3},{4,12},{12,4},... | collective-permute-start | bytes 10616840 | tf_op jit(solution)/shard_map/ppermute | solution.py:523
  115.5 15.2 %collective-permute-start.10 = (bf16[576,768]{1,0:T(8,128)(2,1)S(1)}, bf16[576,768]{1,0:T(8,128)(2,1)S(1)}, u32[]{:S(2)}, u32[]{:S(2)}) collective-permute-start(bf16[576,768]{1,0:T(8,128)(2,1)S(1)} %fusion.5.normed_ref), channel_id=1, source_target_pairs={{0,8},{8,0},{1,9},{9,1},{2,10},{10,2},{3,11},{11,3},{4,12},{12,4},... | collective-permute-start | bytes 2654216 | tf_op jit(solution)/shard_map/ppermute | solution.py:523
  115.8 9.5 %copy-start.16 = (bf16[4,2,192,768]{3,2,1,0:T(8,128)(2,1)S(1)}, bf16[4,2,192,768]{3,2,1,0:T(8,128)(2,1)}, u32[]{:S(2)}) copy-start(bf16[4,2,192,768]{3,2,1,0:T(8,128)(2,1)} %get-tuple-element.171) | copy-start | bytes 7077892
  115.8 16.8 %copy-start.4 = (bf16[576,768]{1,0:T(8,128)(2,1)S(1)}, bf16[576,768]{1,0:T(8,128)(2,1)}, u32[]{:S(2)}) copy-start(bf16[576,768]{1,0:T(8,128)(2,1)} %get-tuple-element.168.gb_ref) | copy-start | bytes 2654212
  118.8 37.2 %collective-permute-start.12 = (bf16[2,2,192,768]{3,2,1,0:T(8,128)(2,1)}, bf16[2,2,192,768]{3,2,1,0:T(8,128)(2,1)}, u32[]{:S(2)}, u32[]{:S(2)}) collective-permute-start(bf16[2,2,192,768]{3,2,1,0:T(8,128)(2,1)} %add_convert_fusion.1), channel_id=1, source_target_pairs={{0,2},{8,14},{2,0},{10,12},{4,6},{12,10},{6,4},{14,8},{32,34},{40,... | collective-permute-start | bytes 3538952 | tf_op jit(solution)/shard_map/ppermute | solution.py:510
  128.0 28.0 %collective-permute-start.11 = (bf16[2,2,192,768]{3,2,1,0:T(8,128)(2,1)}, bf16[2,2,192,768]{3,2,1,0:T(8,128)(2,1)}, u32[]{:S(2)}, u32[]{:S(2)}) collective-permute-start(bf16[2,2,192,768]{3,2,1,0:T(8,128)(2,1)} %add_convert_fusion.2), channel_id=1, source_target_pairs={{0,32},{8,104},{2,34},{10,106},{4,36},{12,108},{6,38},{14,110},{32... | collective-permute-start | bytes 3538952 | tf_op jit(solution)/shard_map/ppermute | solution.py:510
  144.2 11.8 %collective-permute-start.13 = (bf16[2,1,192,768]{3,2,1,0:T(8,128)(2,1)}, bf16[2,1,192,768]{3,2,1,0:T(8,128)(2,1)S(1)}, u32[]{:S(2)}, u32[]{:S(2)}) collective-permute-start(bf16[2,1,192,768]{3,2,1,0:T(8,128)(2,1)} %get-tuple-element.182), channel_id=1, source_target_pairs={{0,32},{8,104},{2,34},{10,106},{4,36},{12,108},{6,38},{14,110},{32... | collective-permute-start | bytes 1769480 | tf_op jit(solution)/shard_map/ppermute | solution.py:510
  144.2 11.8 %collective-permute-start.14 = (bf16[2,1,192,768]{3,2,1,0:T(8,128)(2,1)}, bf16[2,1,192,768]{3,2,1,0:T(8,128)(2,1)}, u32[]{:S(2)}, u32[]{:S(2)}) collective-permute-start(bf16[2,1,192,768]{3,2,1,0:T(8,128)(2,1)} %get-tuple-element.183), channel_id=1, source_target_pairs={{0,2},{8,14},{2,0},{10,12},{4,6},{12,10},{6,4},{14,8},{32,34},{40,... | collective-permute-start | bytes 1769480 | tf_op jit(solution)/shard_map/ppermute | solution.py:510
  147.2 11.9 %copy-start.10 = (bf16[2,1,192,768]{3,2,1,0:T(8,128)(2,1)S(1)}, bf16[2,1,192,768]{3,2,1,0:T(8,128)(2,1)}, u32[]{:S(2)}) copy-start(bf16[2,1,192,768]{3,2,1,0:T(8,128)(2,1)} %copy-done.9) | copy-start | bytes 1769476
  157.3 17.6 %collective-permute-start.16 = (bf16[1,192,768]{2,1,0:T(8,128)(2,1)S(1)}, bf16[1,192,768]{2,1,0:T(8,128)(2,1)S(1)}, u32[]{:S(2)}, u32[]{:S(2)}) collective-permute-start(bf16[1,192,768]{2,1,0:T(8,128)(2,1)S(1)} %fusion.19), channel_id=1, source_target_pairs={{0,6},{8,10},{2,4},{10,8},{4,2},{12,14},{6,0},{14,12},{32,38},{40,... | collective-permute-start | bytes 884744 | tf_op jit(solution)/shard_map/ppermute | solution.py:510
  159.2 15.8 %collective-permute-start.15 = (bf16[1,192,768]{2,1,0:T(8,128)(2,1)S(1)}, bf16[1,192,768]{2,1,0:T(8,128)(2,1)S(1)}, u32[]{:S(2)}, u32[]{:S(2)}) collective-permute-start(bf16[1,192,768]{2,1,0:T(8,128)(2,1)S(1)} %fusion.18), channel_id=1, source_target_pairs={{0,96},{8,40},{2,98},{10,42},{4,100},{12,44},{6,102},{14,46},{32,6... | collective-permute-start | bytes 884744 | tf_op jit(solution)/shard_map/ppermute | solution.py:510
  162.5 9.1 %collective-permute-start.18 = (bf16[2,192,768]{2,1,0:T(8,128)(2,1)S(1)}, bf16[2,192,768]{2,1,0:T(8,128)(2,1)S(1)}, u32[]{:S(2)}, u32[]{:S(2)}) collective-permute-start(bf16[2,192,768]{2,1,0:T(8,128)(2,1)S(1)} %fusion.9), channel_id=1, source_target_pairs={{0,6},{8,10},{2,4},{10,8},{4,2},{12,14},{6,0},{14,12},{32,38},{40,... | collective-permute-start | bytes 1769480 | tf_op jit(solution)/shard_map/ppermute | solution.py:510
  162.8 10.4 %collective-permute-start.17 = (bf16[2,192,768]{2,1,0:T(8,128)(2,1)S(1)}, bf16[2,192,768]{2,1,0:T(8,128)(2,1)S(1)}, u32[]{:S(2)}, u32[]{:S(2)}) collective-permute-start(bf16[2,192,768]{2,1,0:T(8,128)(2,1)S(1)} %fusion.8), channel_id=1, source_target_pairs={{0,96},{8,40},{2,98},{10,42},{4,100},{12,44},{6,102},{14,46},{32,6... | collective-permute-start | bytes 1769480 | tf_op jit(solution)/shard_map/ppermute | solution.py:510
  177.4 9.0 %collective-permute-start.20 = (bf16[320,768]{1,0:T(8,128)(2,1)S(1)}, bf16[320,768]{1,0:T(8,128)(2,1)S(1)}, u32[]{:S(2)}, u32[]{:S(2)}) collective-permute-start(bf16[320,768]{1,0:T(8,128)(2,1)S(1)} %pad_maximum_fusion.10), channel_id=1, source_target_pairs={{0,32},{8,104},{2,34},{10,106},{4,36},{12,108},{6,38},{14,110},{32... | collective-permute-start | bytes 1474568 | tf_op jit(solution)/shard_map/ppermute | solution.py:510
  178.8 8.4 %collective-permute-start.19 = (bf16[2,3,48,768]{3,2,1,0:T(8,128)(2,1)S(1)}, bf16[2,3,48,768]{3,2,1,0:T(8,128)(2,1)S(1)}, u32[]{:S(2)}, u32[]{:S(2)}) collective-permute-start(bf16[2,3,48,768]{3,2,1,0:T(8,128)(2,1)S(1)} %pad_maximum_fusion.12), channel_id=1, source_target_pairs={{0,16},{8,25},{2,18},{10,27},{4,20},{12,29},{6,22},{14,31},{32,48}... | collective-permute-start | bytes 1327112 | tf_op jit(solution)/shard_map/ppermute | solution.py:510
  187.3 5.7 %collective-permute-start.22 = (bf16[176,768]{1,0:T(8,128)(2,1)S(1)}, bf16[176,768]{1,0:T(8,128)(2,1)S(1)}, u32[]{:S(2)}, u32[]{:S(2)}) collective-permute-start(bf16[176,768]{1,0:T(8,128)(2,1)S(1)} %pad_maximum_fusion.16), channel_id=1, source_target_pairs={{0,96},{8,40},{2,98},{10,42},{4,100},{12,44},{6,102},{14,46},{32,6... | collective-permute-start | bytes 811016 | tf_op jit(solution)/shard_map/ppermute | solution.py:510
  188.2 18.3 %collective-permute-start.27 = (bf16[288,1536]{1,0:T(8,128)(2,1)}, bf16[288,1536]{1,0:T(8,128)(2,1)}, u32[]{:S(2)}, u32[]{:S(2)}) collective-permute-start(bf16[288,1536]{1,0:T(8,128)(2,1)} %pad_maximum_fusion.8), channel_id=1, source_target_pairs={{0,2},{8,14},{2,0},{10,12},{4,6},{12,10},{6,4},{14,8},{32,34},{40,... | collective-permute-start | bytes 2654216 | tf_op jit(solution)/shard_map/ppermute | solution.py:510
  190.2 4.8 %collective-permute-start.21 = (bf16[3,48,768]{2,1,0:T(8,128)(2,1)S(1)}, bf16[3,48,768]{2,1,0:T(8,128)(2,1)S(1)}, u32[]{:S(2)}, u32[]{:S(2)}) collective-permute-start(bf16[3,48,768]{2,1,0:T(8,128)(2,1)S(1)} %fusion.15), channel_id=1, source_target_pairs={{0,17},{8,24},{2,19},{10,26},{4,21},{12,28},{6,23},{14,30},{32,49}... | collective-permute-start | bytes 663560 | tf_op jit(solution)/shard_map/ppermute | solution.py:510
  195.2 9.3 %collective-permute-start.23 = (bf16[176,768]{1,0:T(8,128)(2,1)S(1)}, bf16[176,768]{1,0:T(8,128)(2,1)}, u32[]{:S(2)}, u32[]{:S(2)}) collective-permute-start(bf16[176,768]{1,0:T(8,128)(2,1)S(1)} %pad_maximum_fusion.17), channel_id=1, source_target_pairs={{0,2},{8,14},{2,0},{10,12},{4,6},{12,10},{6,4},{14,8},{32,34},{40,... | collective-permute-start | bytes 811016 | tf_op jit(solution)/shard_map/ppermute | solution.py:510
  196.0 10.2 %collective-permute-start.24 = (bf16[3,48,768]{2,1,0:T(8,128)(2,1)S(1)}, bf16[3,48,768]{2,1,0:T(8,128)(2,1)S(1)}, u32[]{:S(2)}, u32[]{:S(2)}) collective-permute-start(bf16[3,48,768]{2,1,0:T(8,128)(2,1)S(1)} %fusion.13), channel_id=1, source_target_pairs={{0,16},{8,25},{2,18},{10,27},{4,20},{12,29},{6,22},{14,31},{32,48}... | collective-permute-start | bytes 663560 | tf_op jit(solution)/shard_map/ppermute | solution.py:510
  206.5 5.4 %collective-permute-start.25 = (bf16[176,768]{1,0:T(8,128)(2,1)S(1)}, bf16[176,768]{1,0:T(8,128)(2,1)S(1)}, u32[]{:S(2)}, u32[]{:S(2)}) collective-permute-start(bf16[176,768]{1,0:T(8,128)(2,1)S(1)} %pad_maximum_fusion.18), channel_id=1, source_target_pairs={{0,6},{8,10},{2,4},{10,8},{4,2},{12,14},{6,0},{14,12},{32,38},{40,... | collective-permute-start | bytes 811016 | tf_op jit(solution)/shard_map/ppermute | solution.py:510
  207.8 4.9 %collective-permute-start.26 = (bf16[3,48,768]{2,1,0:T(8,128)(2,1)S(1)}, bf16[3,48,768]{2,1,0:T(8,128)(2,1)S(1)}, u32[]{:S(2)}, u32[]{:S(2)}) collective-permute-start(bf16[3,48,768]{2,1,0:T(8,128)(2,1)S(1)} %add.424), channel_id=1, source_target_pairs={{0,17},{8,24},{2,19},{10,26},{4,21},{12,28},{6,23},{14,30},{32,49}... | collective-permute-start | bytes 663560 | tf_op jit(solution)/shard_map/ppermute | solution.py:510
  212.9 5.7 %collective-permute-start.28 = (bf16[176,768]{1,0:T(8,128)(2,1)S(1)}, bf16[176,768]{1,0:T(8,128)(2,1)S(1)}, u32[]{:S(2)}, u32[]{:S(2)}) collective-permute-start(bf16[176,768]{1,0:T(8,128)(2,1)S(1)} %pad_maximum_fusion.19), channel_id=1, source_target_pairs={{0,17},{8,24},{2,19},{10,26},{4,21},{12,28},{6,23},{14,30},{32,49}... | collective-permute-start | bytes 811016 | tf_op jit(solution)/shard_map/ppermute | solution.py:510
  213.2 5.4 %collective-permute-start.29 = (bf16[3,48,768]{2,1,0:T(8,128)(2,1)S(1)}, bf16[3,48,768]{2,1,0:T(8,128)(2,1)S(1)}, u32[]{:S(2)}, u32[]{:S(2)}) collective-permute-start(bf16[3,48,768]{2,1,0:T(8,128)(2,1)S(1)} %add.429), channel_id=1, source_target_pairs={{0,96},{8,40},{2,98},{10,42},{4,100},{12,44},{6,102},{14,46},{32,6... | collective-permute-start | bytes 663560 | tf_op jit(solution)/shard_map/ppermute | solution.py:510
  214.1 18.7 %collective-permute-start.32 = (bf16[288,1536]{1,0:T(8,128)(2,1)S(1)}, bf16[288,1536]{1,0:T(8,128)(2,1)S(1)}, u32[]{:S(2)}, u32[]{:S(2)}) collective-permute-start(bf16[288,1536]{1,0:T(8,128)(2,1)S(1)} %pad_maximum_fusion.9), channel_id=1, source_target_pairs={{0,6},{8,10},{2,4},{10,8},{4,2},{12,14},{6,0},{14,12},{32,38},{40,... | collective-permute-start | bytes 2654216 | tf_op jit(solution)/shard_map/ppermute | solution.py:510
  218.7 13.9 %collective-permute-start.31 = (bf16[2,3,48,768]{3,2,1,0:T(8,128)(2,1)S(1)}, bf16[2,3,48,768]{3,2,1,0:T(8,128)(2,1)S(1)}, u32[]{:S(2)}, u32[]{:S(2)}) collective-permute-start(bf16[2,3,48,768]{3,2,1,0:T(8,128)(2,1)S(1)} %pad_maximum_fusion.15), channel_id=1, source_target_pairs={{0,32},{8,104},{2,34},{10,106},{4,36},{12,108},{6,38},{14,110},{32... | collective-permute-start | bytes 1327112 | tf_op jit(solution)/shard_map/ppermute | solution.py:510
  220.4 12.2 %collective-permute-start.30 = (bf16[320,768]{1,0:T(8,128)(2,1)S(1)}, bf16[320,768]{1,0:T(8,128)(2,1)S(1)}, u32[]{:S(2)}, u32[]{:S(2)}) collective-permute-start(bf16[320,768]{1,0:T(8,128)(2,1)S(1)} %pad_maximum_fusion.11), channel_id=1, source_target_pairs={{0,16},{8,25},{2,18},{10,27},{4,20},{12,29},{6,22},{14,31},{32,48}... | collective-permute-start | bytes 1474568 | tf_op jit(solution)/shard_map/ppermute | solution.py:510
  233.4 28.6 %collective-permute-start.35 = (bf16[3,144,1536]{2,1,0:T(8,128)(2,1)S(1)}, bf16[3,144,1536]{2,1,0:T(8,128)(2,1)S(1)}, u32[]{:S(2)}, u32[]{:S(2)}) collective-permute-start(bf16[3,144,1536]{2,1,0:T(8,128)(2,1)S(1)} %pad_maximum_fusion.5), channel_id=1, source_target_pairs={{0,0},{1,8},{2,2},{3,10},{4,4},{5,12},{6,6},{7,14},{8,1},{9,9},{10... | collective-permute-start | bytes 3981320 | tf_op jit(solution)/shard_map/ppermute | solution.py:489
  246.5 12.3 %collective-permute-start.33 = (bf16[3,192,768]{2,1,0:T(8,128)(2,1)S(1)}, bf16[3,192,768]{2,1,0:T(8,128)(2,1)S(1)}, u32[]{:S(2)}, u32[]{:S(2)}) collective-permute-start(bf16[3,192,768]{2,1,0:T(8,128)(2,1)S(1)} %bitcast.128), channel_id=1, source_target_pairs={{0,96},{8,40},{2,98},{10,42},{4,100},{12,44},{6,102},{14,46},{32,6... | collective-permute-start | bytes 2654216 | tf_op jit(solution)/shard_map/ppermute | solution.py:510
  246.6 12.4 %collective-permute-start.34 = (bf16[3,192,768]{2,1,0:T(8,128)(2,1)S(1)}, bf16[3,192,768]{2,1,0:T(8,128)(2,1)S(1)}, u32[]{:S(2)}, u32[]{:S(2)}) collective-permute-start(bf16[3,192,768]{2,1,0:T(8,128)(2,1)S(1)} %bitcast.130), channel_id=1, source_target_pairs={{0,6},{8,10},{2,4},{10,8},{4,2},{12,14},{6,0},{14,12},{32,38},{40,... | collective-permute-start | bytes 2654216 | tf_op jit(solution)/shard_map/ppermute | solution.py:510
  262.3 9.8 %collective-permute-start.36 = (bf16[2,3,192,768]{3,2,1,0:T(8,128)(2,1)S(1)}, bf16[2,3,192,768]{3,2,1,0:T(8,128)(2,1)S(1)}, u32[]{:S(2)}, u32[]{:S(2)}) collective-permute-start(bf16[2,3,192,768]{3,2,1,0:T(8,128)(2,1)S(1)} %pad_maximum_fusion.2.source0_ref), channel_id=1, source_target_pairs={{0,8},{8,0},{1,9},{9,1},{2,10},{10,2},{3,11},{11,3},{4,12},{12,4},... | collective-permute-start | bytes 5308424 | tf_op jit(solution)/shard_map/ppermute | solution.py:523
  262.4 9.7 %collective-permute-start.37 = (bf16[2,3,192,768]{3,2,1,0:T(8,128)(2,1)S(1)}, bf16[2,3,192,768]{3,2,1,0:T(8,128)(2,1)S(1)}, u32[]{:S(2)}, u32[]{:S(2)}) collective-permute-start(bf16[2,3,192,768]{3,2,1,0:T(8,128)(2,1)S(1)} %pad_maximum_fusion.3.source1_ref), channel_id=1, source_target_pairs={{0,8},{8,0},{1,9},{9,1},{2,10},{10,2},{3,11},{11,3},{4,12},{12,4},... | collective-permute-start | bytes 5308424 | tf_op jit(solution)/shard_map/ppermute | solution.py:523
  262.9 22.6 %collective-permute-start.39 = (bf16[2,3,192,768]{3,2,1,0:T(8,128)(2,1)S(1)}, bf16[2,3,192,768]{3,2,1,0:T(8,128)(2,1)S(1)}, u32[]{:S(2)}, u32[]{:S(2)}) collective-permute-start(bf16[2,3,192,768]{3,2,1,0:T(8,128)(2,1)S(1)} %pad_maximum_fusion.2.source0_ref), channel_id=1, source_target_pairs={{0,32},{8,104},{2,34},{10,106},{4,36},{12,108},{6,38},{14,110},{32... | collective-permute-start | bytes 5308424 | tf_op jit(solution)/shard_map/ppermute | solution.py:510
  264.3 22.6 %collective-permute-start.40 = (bf16[2,3,192,768]{3,2,1,0:T(8,128)(2,1)S(1)}, bf16[2,3,192,768]{3,2,1,0:T(8,128)(2,1)S(1)}, u32[]{:S(2)}, u32[]{:S(2)}) collective-permute-start(bf16[2,3,192,768]{3,2,1,0:T(8,128)(2,1)S(1)} %pad_maximum_fusion.3.source1_ref), channel_id=1, source_target_pairs={{0,2},{8,14},{2,0},{10,12},{4,6},{12,10},{6,4},{14,8},{32,34},{40,... | collective-permute-start | bytes 5308424 | tf_op jit(solution)/shard_map/ppermute | solution.py:510
  266.5 5.6 %collective-permute-start.38 = (f32[16,768]{1,0:T(8,128)S(1)}, f32[16,768]{1,0:T(8,128)S(1)}, u32[]{:S(2)}, u32[]{:S(2)}) collective-permute-start(f32[16,768]{1,0:T(8,128)S(1)} %fusion.37), channel_id=1, source_target_pairs={{0,8},{8,0},{1,9},{9,1},{2,10},{10,2},{3,11},{11,3},{4,12},{12,4},... | collective-permute-start | bytes 147464 | tf_op jit(solution)/shard_map/ppermute | solution.py:523
  286.9 6.8 %collective-permute-start.41 = (bf16[2,3,192,768]{3,2,1,0:T(8,128)(2,1)S(1)}, bf16[2,3,192,768]{3,2,1,0:T(8,128)(2,1)}, u32[]{:S(2)}, u32[]{:S(2)}) collective-permute-start(bf16[2,3,192,768]{3,2,1,0:T(8,128)(2,1)S(1)} %collective-permute-done.39.source0_ref), channel_id=1, source_target_pairs={{0,8},{8,0},{1,9},{9,1},{2,10},{10,2},{3,11},{11,3},{4,12},{12,4},... | collective-permute-start | bytes 5308424 | tf_op jit(solution)/shard_map/ppermute | solution.py:523
  286.9 6.8 %collective-permute-start.42 = (bf16[2,3,192,768]{3,2,1,0:T(8,128)(2,1)S(1)}, bf16[2,3,192,768]{3,2,1,0:T(8,128)(2,1)}, u32[]{:S(2)}, u32[]{:S(2)}) collective-permute-start(bf16[2,3,192,768]{3,2,1,0:T(8,128)(2,1)S(1)} %collective-permute-done.40.source1_ref), channel_id=1, source_target_pairs={{0,8},{8,0},{1,9},{9,1},{2,10},{10,2},{3,11},{11,3},{4,12},{12,4},... | collective-permute-start | bytes 5308424 | tf_op jit(solution)/shard_map/ppermute | solution.py:523
  (29 other events, 89.1 us)

commit v7 on v6

--- a/solution.py
+++ b/solution.py
@@ -473,11 +473,12 @@
     return pairs
 
 
-def to_scene(values, z, flip):
+def to_scene(arrays, z, flip):
     pieces = []
     for slot in range(SLOTS):
         scene = jnp.minimum(z ^ slot ^ flip, 2)
-        pieces.append(lax.ppermute(lax.dynamic_index_in_dim(values, scene, 0, keepdims=False), AXES, scene_pairs(slot)))
+        message = [lax.dynamic_index_in_dim(array, scene, 0, keepdims=False) for array in arrays]
+        pieces.append(lax.ppermute(jnp.concatenate(message, axis=1), AXES, scene_pairs(slot)))
     return pieces
 
 
@@ -568,7 +569,7 @@
 
     flip = jnp.where(xh == core, 0, 2)
     views = jnp.broadcast_to(view_counts.astype(bf16)[:, None, None], (3, BLK, LANES))
-    pieces = to_scene(jnp.concatenate([tokens, cotangent, views], axis=2), z, flip)
+    pieces = to_scene((tokens, cotangent, views), z, flip)
     vecs = jnp.concatenate([jnp.stack([out_bias, ln2_gain, ln2_shift, down_bias]), jnp.zeros((4, D), f32)])
     gains = jnp.broadcast_to(ln1_gain[None, :], (8, D))
     weight_q, weight_kv = qkv_weight[:, :D], qkv_weight[:, D:]
@@ -622,15 +623,18 @@
 
     away, grad_hidden = hold([away0, away1], grad_hidden)
     square_halved = meet_parts(away, 0, 0)
+    halved, grad_hidden = hold(halved, grad_hidden)
+    away = [add(mine[1], other[1], half[1]) for (mine, other), half in zip(pieces, halved)]
+    away, grad_hidden = hold(away, grad_hidden)
+    quartered = meet_parts(away, 0, 1)
     input_grad, small = input_gradient(
         grad_q, grad_own, arrived, qkv_weight, both, grad_hidden, gains, vec_grads, up_b_grad
     )
 
-    halved, square_halved, small, input_grad = hold(halved, square_halved, small, input_grad)
-    away = [add(mine[1], other[1], half[1]) for (mine, other), half in zip(pieces, halved)]
+    square_halved, small, input_grad = hold(square_halved, small, input_grad)
     square_away = [add(keep[1], half[1]) for keep, half in zip((keep0, keep1), square_halved)]
+    square_away, quartered = hold(square_away, quartered)
     square_quartered = meet_parts(square_away, 0, 1)
-    quartered = meet_parts(away, 0, 1)
 
     def ring_sum(pieces, halved, quartered):
         return [

time: 304 us -> 302 us (level)
  local copies, waits for them, and re-layouts: 20.9 us -> 26.1 us
  starting transfers between devices: 68.7 us -> 64.5 us
  waiting for transfers between devices: 77 us -> 73.7 us
    ppermute x26, starting transfers between devices: 34.5 us -> 26 us  [exchange(): return lax.ppermute(value, AXES, pairs)]
    ppermute x26, waiting for transfers between devices: 63.5 us -> 60.2 us  [exchange(): return lax.ppermute(value, AXES, pairs)]
    unnamed x65 -> x67, local copies, waits for them, and re-layouts: 9.26 us -> 9.96 us
  transfers between devices with their start and end apart: 43 -> 43, of which waited for: 18 -> 18; matrix products, arithmetic and copies ran while one was open for 8% -> 10% of each run, Pallas kernels for 16% -> 17%
where the time goes in v7:
time: 302 us; the launch traced here: 297 us
  Pallas kernels  103 us (34%)
  waiting for transfers between devices  73.7 us (24%)
  starting transfers between devices  64.5 us (21%)
  local copies, waits for them, and re-layouts  26.1 us (9%)
  other arithmetic  22.6 us (7%)
  matrix products  4.57 us (2%)
    ppermute x26, waiting for transfers between devices, exchange(): return lax.ppermute(value, AXES, pairs)  60.2 us
    pallas_call x1, Pallas kernels, feed_forward(): pl.pallas_call(feed_forward_kernel, grid_spec=pltpu.PrefetchScalarGridSpe...  33.1 us
    ppermute x26, starting transfers between devices, exchange(): return lax.ppermute(value, AXES, pairs)  26 us
    pallas_call x1, Pallas kernels, attention_backward(): pl.pallas_call(attention_backward_kernel, grid_spec=pltpu.PrefetchScalarG...  19.4 us
    pallas_call x4, Pallas kernels, place(): pl.pallas_call(functools.partial(place_kernel, mine, late), grid_spec=plt...  17.9 us
    ppermute x4, starting transfers between devices, to_scene(): lax.ppermute(jnp.concatenate(message, axis=1), AXES, scene_pairs(slot))  17.7 us
    convert_element_type x14, other arithmetic, add(): functools.reduce(jnp.add, [term.astype(f32) for term in terms]).astype(bf16)  16.3 us
    ppermute x1, starting transfers between devices, turn(): return lax.ppermute(values, AXES, pairs)  16 us
  transfers between devices with their start and end apart: 43, of which 18 were waited for; matrix products, arithmetic and copies ran while one was open for 10% of the time, Pallas kernels for 17%

profile of v7, /device:TPU:1, one launch (start us, length us, event | category | flops | bytes accessed | tf_op | source)
XLA Modules:
  0.0 297.3 jit_solution(18217633395530191842)
XLA Ops:
  2.6 1.7 dynamic-slice_bitcast_fusion.9
  4.4 6.0 %collective-permute-start.2 = (bf16[144,1664]{1,0:T(8,128)(2,1)S(1)}, bf16[144,1664]{1,0:T(8,128)(2,1)S(1)}, u32[]{:S(2)}, u32[]{:S(2)}) collective-permute-start(bf16[144,1664]{1,0:T(8,128)(2,1)S(1)} %maximum_maximum_fusion.2), channel_id=1, source_target_pairs={{0,4},{1,8},{3,10},{4,0},{5,12},{6,2},{8,1},{9,13},{10,3},{12,5},{... | collective-permute-start | bytes 1437704 | tf_op jit(solution)/shard_map/ppermute | solution.py:481
  11.2 5.2 %collective-permute-start = (bf16[144,1664]{1,0:T(8,128)(2,1)S(1)}, bf16[144,1664]{1,0:T(8,128)(2,1)S(1)}, u32[]{:S(2)}, u32[]{:S(2)}) collective-permute-start(bf16[144,1664]{1,0:T(8,128)(2,1)S(1)} %maximum_maximum_fusion), channel_id=1, source_target_pairs={{0,0},{1,12},{2,2},{4,4},{5,8},{7,10},{8,5},{9,9},{11,11},{12,1},{... | collective-permute-start | bytes 1437704 | tf_op jit(solution)/shard_map/ppermute | solution.py:481
  17.2 1.3 collective-permute-start.1
  19.2 5.2 %collective-permute-start.3 = (bf16[144,1664]{1,0:T(8,128)(2,1)S(1)}, bf16[144,1664]{1,0:T(8,128)(2,1)}, u32[]{:S(2)}, u32[]{:S(2)}) collective-permute-start(bf16[144,1664]{1,0:T(8,128)(2,1)S(1)} %maximum_maximum_fusion.3), channel_id=1, source_target_pairs={{1,10},{2,4},{3,8},{4,2},{6,0},{7,12},{8,3},{10,1},{11,13},{13,11}... | collective-permute-start | bytes 1437704 | tf_op jit(solution)/shard_map/ppermute | solution.py:481
  25.8 5.7 %collective-permute-done.1 = bf16[144,1664]{1,0:T(8,128)(2,1)} collective-permute-done((bf16[144,1664]{1,0:T(8,128)(2,1)S(1)}, bf16[144,1664]{1,0:T(8,128)(2,1)}, u32[]{:S(2)}, u32[]{:S(2)}) %collective-permute-start.1) | collective-permute-done | bytes 479264 | tf_op jit(solution)/shard_map/ppermute | solution.py:481
  31.5 4.3 %collective-permute-done.3 = bf16[144,1664]{1,0:T(8,128)(2,1)} collective-permute-done((bf16[144,1664]{1,0:T(8,128)(2,1)S(1)}, bf16[144,1664]{1,0:T(8,128)(2,1)}, u32[]{:S(2)}, u32[]{:S(2)}) %collective-permute-start.3) | collective-permute-done | bytes 479264 | tf_op jit(solution)/shard_map/ppermute | solution.py:481
  41.1 2.8 add_convert_fusion.ko_ref.vo_ref
  46.3 1.8 add_convert_fusion.3.q_ref
  49.1 15.9 %attention_forward.1 = (bf16[12,576,1152]{2,1,0:T(8,128)(2,1)}, f32[576,768]{1,0:T(8,128)}, f32[576,768]{1,0:T(8,128)}, bf16[576,768]{1,0:T(8,128)(2,1)}) custom-call(bf16[576,768]{1,0:T(8,128)(2,1)} %add_convert_fusion.3.q_ref, bf16[576,1536]{1,0:T(8,128)(2,1)} %add_convert_fusion.ko_ref.vo_ref, bf16[576,1536]{1,0:T(8,128)(2,1)} %add_convert_fusion.ko_ref.vo_ref, ...), custom_call_target="tpu_custom_call" | custom-call | flops 8153726976 | bytes 20000000 | tf_op jit(solution)/shard_map/attention_forward/pallas_call | solution.py:105
  65.0 33.1 %feed_forward.1 = (bf16[576,768]{1,0:T(8,128)(2,1)}, f32[576,768]{1,0:T(8,128)}, bf16[576,768]{1,0:T(8,128)(2,1)}, bf16[576,768]{1,0:T(8,128)(2,1)}, bf16[4,2,19...) custom-call(s32[3]{0:T(128)} %pad_add_fusion.1.at_ref, ...), custom_call_target="tpu_custom_call" | custom-call | flops 16307453952 | bytes 30000000 | tf_op jit(solution)/shard_map/feed_forward/pallas_call | solution.py:278
  99.6 19.4 %attention_backward.1 = (bf16[576,768]{1,0:T(8,128)(2,1)}, bf16[2,576,768]{2,1,0:T(8,128)(2,1)}, bf16[4,576,768]{2,1,0:T(8,128)(2,1)}) custom-call(s32[3]{0:T(128)} %pad_add_fusion.1.at_ref, bf16[576,768]{1,0:T(8,128)(2,1)} %add_convert_fusion.3.q_ref, bf16[576,1536]{1,0:T(8,128)(2,1)} %add_convert_fusion.ko_ref.vo_ref, ...), custom_call_target="tpu_custom_call" | custom-call | flops 16307453952 | bytes 25000000 | tf_op jit(solution)/shard_map/attention_backward/pallas_call | solution.py:165
  119.5 3.1 %add_convert_fusion.1 = bf16[2,2,192,768]{3,2,1,0:T(8,128)(2,1)} fusion(bf16[4,2,192,768]{3,2,1,0:T(8,128)(2,1)} %collective-permute-done.6, bf16[4,2,192,768]{3,2,1,0:T(8,128)(2,1)} %get-tuple-element.181), kind=kLoop, calls=%fused_computation.1 | loop fusion | flops 2359296 | bytes 3538944 | tf_op jit(solution)/shard_map/convert_element_type | solution.py:535
  122.6 2.7 add_convert_fusion.2
  125.3 2.7 collective-permute-start.13
  129.1 2.1 constant_dynamic-update-slice_fusion.1
  135.9 7.9 %squares.1 = (bf16[2,1,192,768]{3,2,1,0:T(8,128)(2,1)S(1)}, bf16[2,1,192,768]{3,2,1,0:T(8,128)(2,1)}, bf16[2,1,192,768]{3,2,1,0:T(8,128)(2,1)S(1)}, bf16[2,1,192,768]{3,2,1,0:T(8,128)(2,1)}) custom-call(s32[3]{0:T(128)S(1)} %copy-done.13, bf16[576,768]{1,0:T(8,128)(2,1)S(1)} %copy-done.1, bf16[2,576,768]{2,1,0:T(8,128)(2,1)S(1)} %copy-done, ...), custom_call_target="tpu_custom_call" | custom-call | flops 2717908992 | bytes 13000000 | tf_op jit(solution)/shard_map/squares/pallas_call | solution.py:339
  143.9 2.0 collective-permute-start.11
  145.9 1.7 collective-permute-start.12
  147.6 2.5 fusion.8
  150.1 2.4 fusion.9
  153.1 8.8 %input_gradient.1 = (bf16[576,768]{1,0:T(8,128)(2,1)}, f32[16,768]{1,0:T(8,128)}) custom-call(bf16[576,768]{1,0:T(8,128)(2,1)} %get-tuple-element.172.gq_ref, bf16[2,576,768]{2,1,0:T(8,128)(2,1)} %get-tuple-element.173.own_ref, bf16[4,576,768]{2,1,0:T(8,128)(2,1)} %collective-permute-done.9.arrived_ref.arrived_own_ref.arrived_gq_ref.swapped_ref, ...), custom_call_target="tpu_custom_call" | custom-call | flops 2038431744 | bytes 10000000 | tf_op jit(solution)/shard_map/input_gradient/pallas_call | solution.py:390
  164.2 1.9 fusion.6
  167.2 1.4 collective-permute-start.18
  169.7 2.0 fusion.7
  171.7 1.3 collective-permute-done.18
  174.5 1.4 collective-permute-start.20
  175.9 1.7 collective-permute-start.19
  177.6 5.8 %collective-permute-done.20 = bf16[320,768]{1,0:T(8,128)(2,1)S(1)} collective-permute-done((bf16[320,768]{1,0:T(8,128)(2,1)S(1)}, bf16[320,768]{1,0:T(8,128)(2,1)S(1)}, u32[]{:S(2)}, u32[]{:S(2)}) %collective-permute-start.20) | collective-permute-done | bytes 491552 | tf_op jit(solution)/shard_map/ppermute | solution.py:511
  184.5 1.9 collective-permute-start.27
  186.5 3.4 %collective-permute-done.22 = bf16[176,768]{1,0:T(8,128)(2,1)S(1)} collective-permute-done((bf16[176,768]{1,0:T(8,128)(2,1)S(1)}, bf16[176,768]{1,0:T(8,128)(2,1)S(1)}, u32[]{:S(2)}, u32[]{:S(2)}) %collective-permute-start.22) | collective-permute-done | bytes 270368 | tf_op jit(solution)/shard_map/ppermute | solution.py:511
  189.9 1.3 collective-permute-done.21
  192.5 1.8 collective-permute-start.24
  194.2 6.7 %collective-permute-done.23 = bf16[176,768]{1,0:T(8,128)(2,1)} collective-permute-done((bf16[176,768]{1,0:T(8,128)(2,1)S(1)}, bf16[176,768]{1,0:T(8,128)(2,1)}, u32[]{:S(2)}, u32[]{:S(2)}) %collective-permute-start.23) | collective-permute-done | bytes 270368 | tf_op jit(solution)/shard_map/ppermute | solution.py:511
  205.5 2.8 collective-permute-done.25
  210.6 1.4 collective-permute-start.29
  213.2 2.1 collective-permute-done.28
  215.7 1.5 collective-permute-start.31
  217.3 1.6 collective-permute-start.30
  219.1 10.4 %collective-permute-done.30 = bf16[320,768]{1,0:T(8,128)(2,1)S(1)} collective-permute-done((bf16[320,768]{1,0:T(8,128)(2,1)S(1)}, bf16[320,768]{1,0:T(8,128)(2,1)S(1)}, u32[]{:S(2)}, u32[]{:S(2)}) %collective-permute-start.30) | collective-permute-done | bytes 491552 | tf_op jit(solution)/shard_map/ppermute | solution.py:511
  230.3 16.0 %collective-permute-start.35 = (bf16[3,144,1536]{2,1,0:T(8,128)(2,1)S(1)}, bf16[3,144,1536]{2,1,0:T(8,128)(2,1)S(1)}, u32[]{:S(2)}, u32[]{:S(2)}) collective-permute-start(bf16[3,144,1536]{2,1,0:T(8,128)(2,1)S(1)} %pad_maximum_fusion.4), channel_id=1, source_target_pairs={{0,0},{1,8},{2,2},{3,10},{4,4},{5,12},{6,6},{7,14},{8,1},{9,9},{10... | collective-permute-start | bytes 3981320 | tf_op jit(solution)/shard_map/ppermute | solution.py:490
  246.5 11.8 %collective-permute-done.33 = bf16[3,192,768]{2,1,0:T(8,128)(2,1)S(1)} collective-permute-done((bf16[3,192,768]{2,1,0:T(8,128)(2,1)S(1)}, bf16[3,192,768]{2,1,0:T(8,128)(2,1)S(1)}, u32[]{:S(2)}, u32[]{:S(2)}) %collective-permute-start.33) | collective-permute-done | bytes 884768 | tf_op jit(solution)/shard_map/ppermute | solution.py:511
  258.4 3.4 %collective-permute-done.35 = bf16[3,144,1536]{2,1,0:T(8,128)(2,1)S(1)} collective-permute-done((bf16[3,144,1536]{2,1,0:T(8,128)(2,1)S(1)}, bf16[3,144,1536]{2,1,0:T(8,128)(2,1)S(1)}, u32[]{:S(2)}, u32[]{:S(2)}) %collective-permute-start.35) | collective-permute-done | bytes 1327136 | tf_op jit(solution)/shard_map/ppermute | solution.py:490
  264.3 4.4 %place_early.2 = (f32[768,3072]{1,0:T(8,128)}, f32[3072,768]{1,0:T(8,128)}, f32[768,2304]{1,0:T(8,128)}, f32[768,768]{1,0:T(8,128)}) custom-call(s32[3]{0:T(128)S(1)} %copy-done.13, bf16[2,3,192,768]{3,2,1,0:T(8,128)(2,1)S(1)} %pad_maximum_fusion.2.source0_ref, bf16[2,3,192,768]{3,2,1,0:T(8,128)(2,1)S(1)} %pad_maximum_fusion.3.source1_ref), custom_call_target="tpu_custom_call" | custom-call | bytes 11000000 | tf_op jit(solution)/shard_map/place_early/pallas_call | solution.py:444
  268.7 4.4 %place_early.3 = (f32[768,3072]{1,0:T(8,128)}, f32[3072,768]{1,0:T(8,128)}, f32[768,2304]{1,0:T(8,128)}, f32[768,768]{1,0:T(8,128)}) custom-call(s32[3]{0:T(128)S(1)} %copy-done.13, bf16[2,3,192,768]{3,2,1,0:T(8,128)(2,1)S(1)} %collective-permute-done.36.source0_ref, ...), custom_call_target="tpu_custom_call", output_to_operand_aliasing={{0}: (3, {}), {1}: (4, {}), {2}: (5, {}), {3}: (6, {})} | custom-call | bytes 11000000 | tf_op jit(solution)/shard_map/place_early/pallas_call | solution.py:444
  273.2 12.3 %collective-permute-done.39.source0_ref = bf16[2,3,192,768]{3,2,1,0:T(8,128)(2,1)S(1)} collective-permute-done((bf16[2,3,192,768]{3,2,1,0:T(8,128)(2,1)S(1)}, bf16[2,3,192,768]{3,2,1,0:T(8,128)(2,1)S(1)}, u32[]{:S(2)}, u32[]{:S(2)}) %collective-permute-start.39) | collective-permute-done | bytes 1769504 | tf_op jit(solution)/shard_map/ppermute | solution.py:511
  287.3 4.4 %place_late.2 = (f32[768,3072]{1,0:T(8,128)}, f32[3072,768]{1,0:T(8,128)}, f32[768,2304]{1,0:T(8,128)}, f32[768,768]{1,0:T(8,128)}) custom-call(s32[3]{0:T(128)S(1)} %copy-done.13, bf16[2,3,192,768]{3,2,1,0:T(8,128)(2,1)S(1)} %collective-permute-done.39.source0_ref, ...), custom_call_target="tpu_custom_call", output_to_operand_aliasing={{0}: (3, {}), {1}: (4, {}), {2}: (5, {}), {3}: (6, {})} | custom-call | bytes 11000000 | tf_op jit(solution)/shard_map/place_late/pallas_call | solution.py:444
  292.4 4.7 %place_late.3 = (f32[768,3072]{1,0:T(8,128)}, f32[3072,768]{1,0:T(8,128)}, f32[768,2304]{1,0:T(8,128)}, f32[768,768]{1,0:T(8,128)}) custom-call(s32[3]{0:T(128)S(1)} %copy-done.13, bf16[2,3,192,768]{3,2,1,0:T(8,128)(2,1)} %collective-permute-done.41.source0_ref, ...), custom_call_target="tpu_custom_call", output_to_operand_aliasing={{0}: (3, {}), {1}: (4, {}), {2}: (5, {}), {3}: (6, {})} | custom-call | bytes 11000000 | tf_op jit(solution)/shard_map/place_late/pallas_call | solution.py:444
  (235 shorter events, 44.5 us)
Async XLA Ops:
  4.4 21.5 %collective-permute-start.2 = (bf16[144,1664]{1,0:T(8,128)(2,1)S(1)}, bf16[144,1664]{1,0:T(8,128)(2,1)S(1)}, u32[]{:S(2)}, u32[]{:S(2)}) collective-permute-start(bf16[144,1664]{1,0:T(8,128)(2,1)S(1)} %maximum_maximum_fusion.2), channel_id=1, source_target_pairs={{0,4},{1,8},{3,10},{4,0},{5,12},{6,2},{8,1},{9,13},{10,3},{12,5},{... | collective-permute-start | bytes 1437704 | tf_op jit(solution)/shard_map/ppermute | solution.py:481
  11.2 14.7 %collective-permute-start = (bf16[144,1664]{1,0:T(8,128)(2,1)S(1)}, bf16[144,1664]{1,0:T(8,128)(2,1)S(1)}, u32[]{:S(2)}, u32[]{:S(2)}) collective-permute-start(bf16[144,1664]{1,0:T(8,128)(2,1)S(1)} %maximum_maximum_fusion), channel_id=1, source_target_pairs={{0,0},{1,12},{2,2},{4,4},{5,8},{7,10},{8,5},{9,9},{11,11},{12,1},{... | collective-permute-start | bytes 1437704 | tf_op jit(solution)/shard_map/ppermute | solution.py:481
  17.2 14.3 %collective-permute-start.1 = (bf16[144,1664]{1,0:T(8,128)(2,1)S(1)}, bf16[144,1664]{1,0:T(8,128)(2,1)}, u32[]{:S(2)}, u32[]{:S(2)}) collective-permute-start(bf16[144,1664]{1,0:T(8,128)(2,1)S(1)} %maximum_maximum_fusion.1), channel_id=1, source_target_pairs={{0,2},{2,0},{3,12},{5,10},{6,4},{7,8},{9,11},{10,5},{11,9},{12,3},... | collective-permute-start | bytes 1437704 | tf_op jit(solution)/shard_map/ppermute | solution.py:481
  19.2 16.6 %collective-permute-start.3 = (bf16[144,1664]{1,0:T(8,128)(2,1)S(1)}, bf16[144,1664]{1,0:T(8,128)(2,1)}, u32[]{:S(2)}, u32[]{:S(2)}) collective-permute-start(bf16[144,1664]{1,0:T(8,128)(2,1)S(1)} %maximum_maximum_fusion.3), channel_id=1, source_target_pairs={{1,10},{2,4},{3,8},{4,2},{6,0},{7,12},{8,3},{10,1},{11,13},{13,11}... | collective-permute-start | bytes 1437704 | tf_op jit(solution)/shard_map/ppermute | solution.py:481
  24.5 11.4 %copy-start.25 = (f32[768]{0:T(1024)S(1)}, f32[768]{0:T(1024)}, u32[]{:S(2)}) copy-start(f32[768]{0:T(1024)} %param.18) | copy-start | bytes 9220
  43.9 4.2 %collective-permute-start.4 = (bf16[576,1536]{1,0:T(8,128)(2,1)}, bf16[576,1536]{1,0:T(8,128)(2,1)}, u32[]{:S(2)}, u32[]{:S(2)}) collective-permute-start(bf16[576,1536]{1,0:T(8,128)(2,1)} %add_convert_fusion.ko_ref.vo_ref), channel_id=1, source_target_pairs={{0,8},{8,0},{1,9},{9,1},{2,10},{10,2},{3,11},{11,3},{4,12},{12,4},... | collective-permute-start | bytes 5308424 | tf_op jit(solution)/shard_map/ppermute | solution.py:524
  65.0 33.7 %copy-start.2 = (bf16[576,768]{1,0:T(8,128)(2,1)S(1)}, bf16[576,768]{1,0:T(8,128)(2,1)}, u32[]{:S(2)}) copy-start(bf16[576,768]{1,0:T(8,128)(2,1)} %get-tuple-element.169.att_ref) | copy-start | bytes 2654212
  98.1 20.9 %collective-permute-start.5 = (bf16[4,2,192,768]{3,2,1,0:T(8,128)(2,1)}, bf16[4,2,192,768]{3,2,1,0:T(8,128)(2,1)}, u32[]{:S(2)}, u32[]{:S(2)}) collective-permute-start(bf16[4,2,192,768]{3,2,1,0:T(8,128)(2,1)} %get-tuple-element.174), channel_id=1, source_target_pairs={{0,8},{8,0},{1,9},{9,1},{2,10},{10,2},{3,11},{11,3},{4,12},{12,4},... | collective-permute-start | bytes 7077896 | tf_op jit(solution)/shard_map/ppermute | solution.py:524
  98.5 20.5 %collective-permute-start.6 = (bf16[4,2,192,768]{3,2,1,0:T(8,128)(2,1)}, bf16[4,2,192,768]{3,2,1,0:T(8,128)(2,1)}, u32[]{:S(2)}, u32[]{:S(2)}) collective-permute-start(bf16[4,2,192,768]{3,2,1,0:T(8,128)(2,1)} %get-tuple-element.175), channel_id=1, source_target_pairs={{0,8},{8,0},{1,9},{9,1},{2,10},{10,2},{3,11},{11,3},{4,12},{12,4},... | collective-permute-start | bytes 7077896 | tf_op jit(solution)/shard_map/ppermute | solution.py:524
  98.7 20.3 %collective-permute-start.7 = (bf16[576,768]{1,0:T(8,128)(2,1)S(1)}, bf16[576,768]{1,0:T(8,128)(2,1)S(1)}, u32[]{:S(2)}, u32[]{:S(2)}) collective-permute-start(bf16[576,768]{1,0:T(8,128)(2,1)S(1)} %copy-done.2), channel_id=1, source_target_pairs={{0,8},{8,0},{1,9},{9,1},{2,10},{10,2},{3,11},{11,3},{4,12},{12,4},... | collective-permute-start | bytes 2654216 | tf_op jit(solution)/shard_map/ppermute | solution.py:524
  99.4 19.6 %collective-permute-start.8 = (bf16[576,768]{1,0:T(8,128)(2,1)}, bf16[576,768]{1,0:T(8,128)(2,1)S(1)}, u32[]{:S(2)}, u32[]{:S(2)}) collective-permute-start(bf16[576,768]{1,0:T(8,128)(2,1)} %get-tuple-element.176.gb_ref), channel_id=1, source_target_pairs={{0,8},{8,0},{1,9},{9,1},{2,10},{10,2},{3,11},{11,3},{4,12},{12,4},... | collective-permute-start | bytes 2654216 | tf_op jit(solution)/shard_map/ppermute | solution.py:524
  119.0 12.2 %collective-permute-start.9 = (bf16[4,576,768]{2,1,0:T(8,128)(2,1)}, bf16[4,576,768]{2,1,0:T(8,128)(2,1)}, u32[]{:S(2)}, u32[]{:S(2)}) collective-permute-start(bf16[4,576,768]{2,1,0:T(8,128)(2,1)} %get-tuple-element.178.other_ref), channel_id=1, source_target_pairs={{0,8},{8,0},{1,9},{9,1},{2,10},{10,2},{3,11},{11,3},{4,12},{12,4},... | collective-permute-start | bytes 10616840 | tf_op jit(solution)/shard_map/ppermute | solution.py:524
  122.5 21.4 %collective-permute-start.14 = (bf16[2,2,192,768]{3,2,1,0:T(8,128)(2,1)}, bf16[2,2,192,768]{3,2,1,0:T(8,128)(2,1)}, u32[]{:S(2)}, u32[]{:S(2)}) collective-permute-start(bf16[2,2,192,768]{3,2,1,0:T(8,128)(2,1)} %add_convert_fusion.1), channel_id=1, source_target_pairs={{0,2},{8,14},{2,0},{10,12},{4,6},{12,10},{6,4},{14,8},{32,34},{40,... | collective-permute-start | bytes 3538952 | tf_op jit(solution)/shard_map/ppermute | solution.py:511
  122.6 8.7 %copy-start.1 = (bf16[576,768]{1,0:T(8,128)(2,1)S(1)}, bf16[576,768]{1,0:T(8,128)(2,1)}, u32[]{:S(2)}) copy-start(bf16[576,768]{1,0:T(8,128)(2,1)} %get-tuple-element.172.gq_ref) | copy-start | bytes 2654212
  125.3 18.6 %collective-permute-start.13 = (bf16[2,2,192,768]{3,2,1,0:T(8,128)(2,1)}, bf16[2,2,192,768]{3,2,1,0:T(8,128)(2,1)}, u32[]{:S(2)}, u32[]{:S(2)}) collective-permute-start(bf16[2,2,192,768]{3,2,1,0:T(8,128)(2,1)} %add_convert_fusion.2), channel_id=1, source_target_pairs={{0,32},{8,104},{2,34},{10,106},{4,36},{12,108},{6,38},{14,110},{32... | collective-permute-start | bytes 3538952 | tf_op jit(solution)/shard_map/ppermute | solution.py:511
  128.0 3.3 %collective-permute-start.10 = (bf16[576,768]{1,0:T(8,128)(2,1)S(1)}, bf16[576,768]{1,0:T(8,128)(2,1)}, u32[]{:S(2)}, u32[]{:S(2)}) collective-permute-start(bf16[576,768]{1,0:T(8,128)(2,1)S(1)} %fusion.5.normed_ref), channel_id=1, source_target_pairs={{0,8},{8,0},{1,9},{9,1},{2,10},{10,2},{3,11},{11,3},{4,12},{12,4},... | collective-permute-start | bytes 2654216 | tf_op jit(solution)/shard_map/ppermute | solution.py:524
  143.9 18.0 %collective-permute-start.11 = (bf16[2,1,192,768]{3,2,1,0:T(8,128)(2,1)}, bf16[2,1,192,768]{3,2,1,0:T(8,128)(2,1)S(1)}, u32[]{:S(2)}, u32[]{:S(2)}) collective-permute-start(bf16[2,1,192,768]{3,2,1,0:T(8,128)(2,1)} %get-tuple-element.190), channel_id=1, source_target_pairs={{0,32},{8,104},{2,34},{10,106},{4,36},{12,108},{6,38},{14,110},{32... | collective-permute-start | bytes 1769480 | tf_op jit(solution)/shard_map/ppermute | solution.py:511
  145.9 16.1 %collective-permute-start.12 = (bf16[2,1,192,768]{3,2,1,0:T(8,128)(2,1)}, bf16[2,1,192,768]{3,2,1,0:T(8,128)(2,1)S(1)}, u32[]{:S(2)}, u32[]{:S(2)}) collective-permute-start(bf16[2,1,192,768]{3,2,1,0:T(8,128)(2,1)} %get-tuple-element.191), channel_id=1, source_target_pairs={{0,2},{8,14},{2,0},{10,12},{4,6},{12,10},{6,4},{14,8},{32,34},{40,... | collective-permute-start | bytes 1769480 | tf_op jit(solution)/shard_map/ppermute | solution.py:511
  152.5 11.6 %collective-permute-start.15 = (bf16[2,192,768]{2,1,0:T(8,128)(2,1)}, bf16[2,192,768]{2,1,0:T(8,128)(2,1)}, u32[]{:S(2)}, u32[]{:S(2)}) collective-permute-start(bf16[2,192,768]{2,1,0:T(8,128)(2,1)} %fusion.8), channel_id=1, source_target_pairs={{0,96},{8,40},{2,98},{10,42},{4,100},{12,44},{6,102},{14,46},{32,6... | collective-permute-start | bytes 1769480 | tf_op jit(solution)/shard_map/ppermute | solution.py:511
  152.9 11.2 %collective-permute-start.16 = (bf16[2,192,768]{2,1,0:T(8,128)(2,1)}, bf16[2,192,768]{2,1,0:T(8,128)(2,1)}, u32[]{:S(2)}, u32[]{:S(2)}) collective-permute-start(bf16[2,192,768]{2,1,0:T(8,128)(2,1)} %fusion.9), channel_id=1, source_target_pairs={{0,6},{8,10},{2,4},{10,8},{4,2},{12,14},{6,0},{14,12},{32,38},{40,... | collective-permute-start | bytes 1769480 | tf_op jit(solution)/shard_map/ppermute | solution.py:511
  153.1 8.9 %copy-start.10 = (bf16[2,1,192,768]{3,2,1,0:T(8,128)(2,1)S(1)}, bf16[2,1,192,768]{3,2,1,0:T(8,128)(2,1)}, u32[]{:S(2)}) copy-start(bf16[2,1,192,768]{3,2,1,0:T(8,128)(2,1)} %copy-done.9) | copy-start | bytes 1769476
  153.1 9.8 %copy-start.12 = (bf16[2,1,192,768]{3,2,1,0:T(8,128)(2,1)S(1)}, bf16[2,1,192,768]{3,2,1,0:T(8,128)(2,1)}, u32[]{:S(2)}) copy-start(bf16[2,1,192,768]{3,2,1,0:T(8,128)(2,1)} %copy-done.11) | copy-start | bytes 1769476
  166.0 5.7 %collective-permute-start.17 = (bf16[1,192,768]{2,1,0:T(8,128)(2,1)S(1)}, bf16[1,192,768]{2,1,0:T(8,128)(2,1)S(1)}, u32[]{:S(2)}, u32[]{:S(2)}) collective-permute-start(bf16[1,192,768]{2,1,0:T(8,128)(2,1)S(1)} %fusion.18), channel_id=1, source_target_pairs={{0,96},{8,40},{2,98},{10,42},{4,100},{12,44},{6,102},{14,46},{32,6... | collective-permute-start | bytes 884744 | tf_op jit(solution)/shard_map/ppermute | solution.py:511
  167.2 5.9 %collective-permute-start.18 = (bf16[1,192,768]{2,1,0:T(8,128)(2,1)S(1)}, bf16[1,192,768]{2,1,0:T(8,128)(2,1)S(1)}, u32[]{:S(2)}, u32[]{:S(2)}) collective-permute-start(bf16[1,192,768]{2,1,0:T(8,128)(2,1)S(1)} %fusion.19), channel_id=1, source_target_pairs={{0,6},{8,10},{2,4},{10,8},{4,2},{12,14},{6,0},{14,12},{32,38},{40,... | collective-permute-start | bytes 884744 | tf_op jit(solution)/shard_map/ppermute | solution.py:511
  174.5 9.0 %collective-permute-start.20 = (bf16[320,768]{1,0:T(8,128)(2,1)S(1)}, bf16[320,768]{1,0:T(8,128)(2,1)S(1)}, u32[]{:S(2)}, u32[]{:S(2)}) collective-permute-start(bf16[320,768]{1,0:T(8,128)(2,1)S(1)} %pad_maximum_fusion.9), channel_id=1, source_target_pairs={{0,32},{8,104},{2,34},{10,106},{4,36},{12,108},{6,38},{14,110},{32... | collective-permute-start | bytes 1474568 | tf_op jit(solution)/shard_map/ppermute | solution.py:511
  175.9 8.4 %collective-permute-start.19 = (bf16[2,3,48,768]{3,2,1,0:T(8,128)(2,1)S(1)}, bf16[2,3,48,768]{3,2,1,0:T(8,128)(2,1)S(1)}, u32[]{:S(2)}, u32[]{:S(2)}) collective-permute-start(bf16[2,3,48,768]{3,2,1,0:T(8,128)(2,1)S(1)} %pad_maximum_fusion.11), channel_id=1, source_target_pairs={{0,16},{8,25},{2,18},{10,27},{4,20},{12,29},{6,22},{14,31},{32,48}... | collective-permute-start | bytes 1327112 | tf_op jit(solution)/shard_map/ppermute | solution.py:511
  184.5 5.4 %collective-permute-start.22 = (bf16[176,768]{1,0:T(8,128)(2,1)S(1)}, bf16[176,768]{1,0:T(8,128)(2,1)S(1)}, u32[]{:S(2)}, u32[]{:S(2)}) collective-permute-start(bf16[176,768]{1,0:T(8,128)(2,1)S(1)} %pad_maximum_fusion.15), channel_id=1, source_target_pairs={{0,96},{8,40},{2,98},{10,42},{4,100},{12,44},{6,102},{14,46},{32,6... | collective-permute-start | bytes 811016 | tf_op jit(solution)/shard_map/ppermute | solution.py:511
  184.5 18.5 %collective-permute-start.27 = (bf16[288,1536]{1,0:T(8,128)(2,1)}, bf16[288,1536]{1,0:T(8,128)(2,1)}, u32[]{:S(2)}, u32[]{:S(2)}) collective-permute-start(bf16[288,1536]{1,0:T(8,128)(2,1)} %pad_maximum_fusion.7), channel_id=1, source_target_pairs={{0,2},{8,14},{2,0},{10,12},{4,6},{12,10},{6,4},{14,8},{32,34},{40,... | collective-permute-start | bytes 2654216 | tf_op jit(solution)/shard_map/ppermute | solution.py:511
  186.4 4.8 %collective-permute-start.21 = (bf16[3,48,768]{2,1,0:T(8,128)(2,1)S(1)}, bf16[3,48,768]{2,1,0:T(8,128)(2,1)S(1)}, u32[]{:S(2)}, u32[]{:S(2)}) collective-permute-start(bf16[3,48,768]{2,1,0:T(8,128)(2,1)S(1)} %fusion.15), channel_id=1, source_target_pairs={{0,17},{8,24},{2,19},{10,26},{4,21},{12,28},{6,23},{14,30},{32,49}... | collective-permute-start | bytes 663560 | tf_op jit(solution)/shard_map/ppermute | solution.py:511
  191.4 9.5 %collective-permute-start.23 = (bf16[176,768]{1,0:T(8,128)(2,1)S(1)}, bf16[176,768]{1,0:T(8,128)(2,1)}, u32[]{:S(2)}, u32[]{:S(2)}) collective-permute-start(bf16[176,768]{1,0:T(8,128)(2,1)S(1)} %pad_maximum_fusion.16), channel_id=1, source_target_pairs={{0,2},{8,14},{2,0},{10,12},{4,6},{12,10},{6,4},{14,8},{32,34},{40,... | collective-permute-start | bytes 811016 | tf_op jit(solution)/shard_map/ppermute | solution.py:511
  192.5 10.2 %collective-permute-start.24 = (bf16[3,48,768]{2,1,0:T(8,128)(2,1)S(1)}, bf16[3,48,768]{2,1,0:T(8,128)(2,1)S(1)}, u32[]{:S(2)}, u32[]{:S(2)}) collective-permute-start(bf16[3,48,768]{2,1,0:T(8,128)(2,1)S(1)} %fusion.13), channel_id=1, source_target_pairs={{0,16},{8,25},{2,18},{10,27},{4,20},{12,29},{6,22},{14,31},{32,48}... | collective-permute-start | bytes 663560 | tf_op jit(solution)/shard_map/ppermute | solution.py:511
  202.9 5.5 %collective-permute-start.25 = (bf16[176,768]{1,0:T(8,128)(2,1)S(1)}, bf16[176,768]{1,0:T(8,128)(2,1)S(1)}, u32[]{:S(2)}, u32[]{:S(2)}) collective-permute-start(bf16[176,768]{1,0:T(8,128)(2,1)S(1)} %pad_maximum_fusion.17), channel_id=1, source_target_pairs={{0,6},{8,10},{2,4},{10,8},{4,2},{12,14},{6,0},{14,12},{32,38},{40,... | collective-permute-start | bytes 811016 | tf_op jit(solution)/shard_map/ppermute | solution.py:511
  204.4 5.0 %collective-permute-start.26 = (bf16[3,48,768]{2,1,0:T(8,128)(2,1)S(1)}, bf16[3,48,768]{2,1,0:T(8,128)(2,1)S(1)}, u32[]{:S(2)}, u32[]{:S(2)}) collective-permute-start(bf16[3,48,768]{2,1,0:T(8,128)(2,1)S(1)} %add.433), channel_id=1, source_target_pairs={{0,17},{8,24},{2,19},{10,26},{4,21},{12,28},{6,23},{14,30},{32,49}... | collective-permute-start | bytes 663560 | tf_op jit(solution)/shard_map/ppermute | solution.py:511
  209.6 5.7 %collective-permute-start.28 = (bf16[176,768]{1,0:T(8,128)(2,1)S(1)}, bf16[176,768]{1,0:T(8,128)(2,1)S(1)}, u32[]{:S(2)}, u32[]{:S(2)}) collective-permute-start(bf16[176,768]{1,0:T(8,128)(2,1)S(1)} %pad_maximum_fusion.18), channel_id=1, source_target_pairs={{0,17},{8,24},{2,19},{10,26},{4,21},{12,28},{6,23},{14,30},{32,49}... | collective-permute-start | bytes 811016 | tf_op jit(solution)/shard_map/ppermute | solution.py:511
  210.6 5.1 %collective-permute-start.29 = (bf16[3,48,768]{2,1,0:T(8,128)(2,1)S(1)}, bf16[3,48,768]{2,1,0:T(8,128)(2,1)S(1)}, u32[]{:S(2)}, u32[]{:S(2)}) collective-permute-start(bf16[3,48,768]{2,1,0:T(8,128)(2,1)S(1)} %add.438), channel_id=1, source_target_pairs={{0,96},{8,40},{2,98},{10,42},{4,100},{12,44},{6,102},{14,46},{32,6... | collective-permute-start | bytes 663560 | tf_op jit(solution)/shard_map/ppermute | solution.py:511
  211.9 17.8 %collective-permute-start.32 = (bf16[288,1536]{1,0:T(8,128)(2,1)S(1)}, bf16[288,1536]{1,0:T(8,128)(2,1)S(1)}, u32[]{:S(2)}, u32[]{:S(2)}) collective-permute-start(bf16[288,1536]{1,0:T(8,128)(2,1)S(1)} %pad_maximum_fusion.8), channel_id=1, source_target_pairs={{0,6},{8,10},{2,4},{10,8},{4,2},{12,14},{6,0},{14,12},{32,38},{40,... | collective-permute-start | bytes 2654216 | tf_op jit(solution)/shard_map/ppermute | solution.py:511
  215.7 13.8 %collective-permute-start.31 = (bf16[2,3,48,768]{3,2,1,0:T(8,128)(2,1)S(1)}, bf16[2,3,48,768]{3,2,1,0:T(8,128)(2,1)S(1)}, u32[]{:S(2)}, u32[]{:S(2)}) collective-permute-start(bf16[2,3,48,768]{3,2,1,0:T(8,128)(2,1)S(1)} %pad_maximum_fusion.14), channel_id=1, source_target_pairs={{0,32},{8,104},{2,34},{10,106},{4,36},{12,108},{6,38},{14,110},{32... | collective-permute-start | bytes 1327112 | tf_op jit(solution)/shard_map/ppermute | solution.py:511
  217.3 12.2 %collective-permute-start.30 = (bf16[320,768]{1,0:T(8,128)(2,1)S(1)}, bf16[320,768]{1,0:T(8,128)(2,1)S(1)}, u32[]{:S(2)}, u32[]{:S(2)}) collective-permute-start(bf16[320,768]{1,0:T(8,128)(2,1)S(1)} %pad_maximum_fusion.10), channel_id=1, source_target_pairs={{0,16},{8,25},{2,18},{10,27},{4,20},{12,29},{6,22},{14,31},{32,48}... | collective-permute-start | bytes 1474568 | tf_op jit(solution)/shard_map/ppermute | solution.py:511
  230.3 31.4 %collective-permute-start.35 = (bf16[3,144,1536]{2,1,0:T(8,128)(2,1)S(1)}, bf16[3,144,1536]{2,1,0:T(8,128)(2,1)S(1)}, u32[]{:S(2)}, u32[]{:S(2)}) collective-permute-start(bf16[3,144,1536]{2,1,0:T(8,128)(2,1)S(1)} %pad_maximum_fusion.4), channel_id=1, source_target_pairs={{0,0},{1,8},{2,2},{3,10},{4,4},{5,12},{6,6},{7,14},{8,1},{9,9},{10... | collective-permute-start | bytes 3981320 | tf_op jit(solution)/shard_map/ppermute | solution.py:490
  246.3 12.0 %collective-permute-start.33 = (bf16[3,192,768]{2,1,0:T(8,128)(2,1)S(1)}, bf16[3,192,768]{2,1,0:T(8,128)(2,1)S(1)}, u32[]{:S(2)}, u32[]{:S(2)}) collective-permute-start(bf16[3,192,768]{2,1,0:T(8,128)(2,1)S(1)} %bitcast.140), channel_id=1, source_target_pairs={{0,96},{8,40},{2,98},{10,42},{4,100},{12,44},{6,102},{14,46},{32,6... | collective-permute-start | bytes 2654216 | tf_op jit(solution)/shard_map/ppermute | solution.py:511
  246.4 12.0 %collective-permute-start.34 = (bf16[3,192,768]{2,1,0:T(8,128)(2,1)S(1)}, bf16[3,192,768]{2,1,0:T(8,128)(2,1)S(1)}, u32[]{:S(2)}, u32[]{:S(2)}) collective-permute-start(bf16[3,192,768]{2,1,0:T(8,128)(2,1)S(1)} %bitcast.142), channel_id=1, source_target_pairs={{0,6},{8,10},{2,4},{10,8},{4,2},{12,14},{6,0},{14,12},{32,38},{40,... | collective-permute-start | bytes 2654216 | tf_op jit(solution)/shard_map/ppermute | solution.py:511
  262.1 6.6 %collective-permute-start.36 = (bf16[2,3,192,768]{3,2,1,0:T(8,128)(2,1)S(1)}, bf16[2,3,192,768]{3,2,1,0:T(8,128)(2,1)S(1)}, u32[]{:S(2)}, u32[]{:S(2)}) collective-permute-start(bf16[2,3,192,768]{3,2,1,0:T(8,128)(2,1)S(1)} %pad_maximum_fusion.2.source0_ref), channel_id=1, source_target_pairs={{0,8},{8,0},{1,9},{9,1},{2,10},{10,2},{3,11},{11,3},{4,12},{12,4},... | collective-permute-start | bytes 5308424 | tf_op jit(solution)/shard_map/ppermute | solution.py:524
  262.2 6.6 %collective-permute-start.37 = (bf16[2,3,192,768]{3,2,1,0:T(8,128)(2,1)S(1)}, bf16[2,3,192,768]{3,2,1,0:T(8,128)(2,1)S(1)}, u32[]{:S(2)}, u32[]{:S(2)}) collective-permute-start(bf16[2,3,192,768]{3,2,1,0:T(8,128)(2,1)S(1)} %pad_maximum_fusion.3.source1_ref), channel_id=1, source_target_pairs={{0,8},{8,0},{1,9},{9,1},{2,10},{10,2},{3,11},{11,3},{4,12},{12,4},... | collective-permute-start | bytes 5308424 | tf_op jit(solution)/shard_map/ppermute | solution.py:524
  262.7 22.8 %collective-permute-start.39 = (bf16[2,3,192,768]{3,2,1,0:T(8,128)(2,1)S(1)}, bf16[2,3,192,768]{3,2,1,0:T(8,128)(2,1)S(1)}, u32[]{:S(2)}, u32[]{:S(2)}) collective-permute-start(bf16[2,3,192,768]{3,2,1,0:T(8,128)(2,1)S(1)} %pad_maximum_fusion.2.source0_ref), channel_id=1, source_target_pairs={{0,32},{8,104},{2,34},{10,106},{4,36},{12,108},{6,38},{14,110},{32... | collective-permute-start | bytes 5308424 | tf_op jit(solution)/shard_map/ppermute | solution.py:511
  262.9 22.7 %collective-permute-start.40 = (bf16[2,3,192,768]{3,2,1,0:T(8,128)(2,1)S(1)}, bf16[2,3,192,768]{3,2,1,0:T(8,128)(2,1)S(1)}, u32[]{:S(2)}, u32[]{:S(2)}) collective-permute-start(bf16[2,3,192,768]{3,2,1,0:T(8,128)(2,1)S(1)} %pad_maximum_fusion.3.source1_ref), channel_id=1, source_target_pairs={{0,2},{8,14},{2,0},{10,12},{4,6},{12,10},{6,4},{14,8},{32,34},{40,... | collective-permute-start | bytes 5308424 | tf_op jit(solution)/shard_map/ppermute | solution.py:511
  263.0 5.7 %collective-permute-start.38 = (f32[16,768]{1,0:T(8,128)S(1)}, f32[16,768]{1,0:T(8,128)S(1)}, u32[]{:S(2)}, u32[]{:S(2)}) collective-permute-start(f32[16,768]{1,0:T(8,128)S(1)} %fusion.37), channel_id=1, source_target_pairs={{0,8},{8,0},{1,9},{9,1},{2,10},{10,2},{3,11},{11,3},{4,12},{12,4},... | collective-permute-start | bytes 147464 | tf_op jit(solution)/shard_map/ppermute | solution.py:524
  285.5 6.8 %collective-permute-start.41 = (bf16[2,3,192,768]{3,2,1,0:T(8,128)(2,1)S(1)}, bf16[2,3,192,768]{3,2,1,0:T(8,128)(2,1)}, u32[]{:S(2)}, u32[]{:S(2)}) collective-permute-start(bf16[2,3,192,768]{3,2,1,0:T(8,128)(2,1)S(1)} %collective-permute-done.39.source0_ref), channel_id=1, source_target_pairs={{0,8},{8,0},{1,9},{9,1},{2,10},{10,2},{3,11},{11,3},{4,12},{12,4},... | collective-permute-start | bytes 5308424 | tf_op jit(solution)/shard_map/ppermute | solution.py:524
  285.6 6.8 %collective-permute-start.42 = (bf16[2,3,192,768]{3,2,1,0:T(8,128)(2,1)S(1)}, bf16[2,3,192,768]{3,2,1,0:T(8,128)(2,1)}, u32[]{:S(2)}, u32[]{:S(2)}) collective-permute-start(bf16[2,3,192,768]{3,2,1,0:T(8,128)(2,1)S(1)} %collective-permute-done.40.source1_ref), channel_id=1, source_target_pairs={{0,8},{8,0},{1,9},{9,1},{2,10},{10,2},{3,11},{11,3},{4,12},{12,4},... | collective-permute-start | bytes 5308424 | tf_op jit(solution)/shard_map/ppermute | solution.py:524
  (30 other events, 88.4 us)

commit v8 on v7

--- a/solution.py
+++ b/solution.py
@@ -55,13 +55,26 @@
     return jnp.where((lane >= first) & (lane < last), 1.0, 0.0).astype(at)
 
 
-def attention_forward_kernel(q_ref, ko_ref, vo_ref, ks_ref, vs_ref, mask_ref, p_ref, o_ref, linv_ref, att_ref):
+def key_mask(at_ref):
+    core, z, flip, views = (at_ref[index] for index in (0, 3, 4, 5))
+    row = lax.broadcasted_iota(jnp.int32, (BLK, LANES), 0)
+    blocks = []
+    for part in range(2):
+        for slot in range(SLOTS):
+            turned = flip if part == 0 else 2 - flip
+            first = (2 * (z ^ slot ^ turned) + (core if part == 0 else 1 - core)) * BLK
+            usable = (row < views * VIEW_TOK - first) | (row >= VIEWS_MAX * VIEW_TOK - first)
+            blocks.append(jnp.where(usable, 0.0, masked_score).astype(bf16))
+    return jnp.concatenate(blocks, axis=0)
+
+
+def attention_forward_kernel(at_ref, q_ref, ko_ref, vo_ref, ks_ref, vs_ref, p_ref, o_ref, linv_ref, att_ref):
     half = [lane_row(bf16, 0, 64), lane_row(bf16, 64, 128)]
     unit = [lane_row(bf16, 64, 65), lane_row(bf16, 0, 1)]
     q = q_ref[...]
     k = jnp.concatenate([ko_ref[...], ks_ref[...]], axis=0)
     v = jnp.concatenate([vo_ref[...], vs_ref[...]], axis=0)
-    mask = mask_ref[...]
+    mask = key_mask(at_ref)
     lane = lax.broadcasted_iota(jnp.int32, (QROWS, LANES), 1)
     q_now = [q * half[h] + unit[h] for h in range(2)]
     k_now = [k * half[h] + mask * unit[h] for h in range(2)]
@@ -100,13 +113,15 @@
     return pl.BlockSpec((ROWS, LANES), lambda i, f=base: (0, f + i))
 
 
-def attention_forward(queries, own, sibling, mask):
-    col = head_columns
+def attention_forward(at, queries, own, sibling):
+    col = lambda base: pl.BlockSpec((ROWS, LANES), lambda i, at: (0, base + i))
     return pl.pallas_call(
         attention_forward_kernel,
-        grid=(PAIRS,),
-        in_specs=[col(0), col(0), col(PAIRS), col(0), col(PAIRS), pl.BlockSpec((KEYS, LANES), lambda i: (0, 0))],
-        out_specs=[pl.BlockSpec((2, ROWS, KEYS), lambda i: (i, 0, 0)), col(0), col(0), col(0)],
+        grid_spec=pltpu.PrefetchScalarGridSpec(
+            num_scalar_prefetch=1, grid=(PAIRS,),
+            in_specs=[col(0), col(0), col(PAIRS), col(0), col(PAIRS)],
+            out_specs=[pl.BlockSpec((2, ROWS, KEYS), lambda i, at: (i, 0, 0)), col(0), col(0), col(0)],
+        ),
         out_shape=[
             jax.ShapeDtypeStruct((HEADS, ROWS, KEYS), bf16),
             jax.ShapeDtypeStruct((ROWS, D), f32),
@@ -116,7 +131,7 @@
         compiler_params=pltpu.CompilerParams(vmem_limit_bytes=60 * MIB),
         cost_estimate=pl.CostEstimate(flops=16 * ROWS * KEYS * D, bytes_accessed=20_000_000, transcendentals=HEADS * ROWS * KEYS),
         name="attention_forward",
-    )(queries, own, own, sibling, sibling, mask)
+    )(at, queries, own, own, sibling, sibling)
 
 
 def attention_backward_kernel(
@@ -390,7 +405,7 @@
     return pl.pallas_call(
         input_grad_kernel,
         grid=(steps,),
-        in_specs=[rows, pair, pair, fixed(D, 3 * D), rows, rows, fixed(8, D), fixed(8, D), fixed(NF, 1, FCHUNK)],
+        in_specs=[rows, pair, pair, fixed(D, 3 * D), rows, rows, fixed(1, D), fixed(8, D), fixed(NF, 1, FCHUNK)],
         out_specs=[rows, fixed(16, D)],
         out_shape=[jax.ShapeDtypeStruct((ROWS, D), bf16), jax.ShapeDtypeStruct((16, D), f32)],
         scratch_shapes=[pltpu.VMEM((length, 3 * D), bf16)],
@@ -571,21 +586,16 @@
     views = jnp.broadcast_to(view_counts.astype(bf16)[:, None, None], (3, BLK, LANES))
     pieces = to_scene((tokens, cotangent, views), z, flip)
     vecs = jnp.concatenate([jnp.stack([out_bias, ln2_gain, ln2_shift, down_bias]), jnp.zeros((4, D), f32)])
-    gains = jnp.broadcast_to(ln1_gain[None, :], (8, D))
+    gains = ln1_gain.reshape(1, D)
     weight_q, weight_kv = qkv_weight[:, :D], qkv_weight[:, D:]
     pieces, vecs, gains, weight_q, weight_kv = hold(pieces, vecs, gains, weight_q, weight_kv)
     both = jnp.concatenate([piece[:, : 2 * D] for piece in pieces], axis=0)
     views = pieces[0][0, 2 * D].astype(f32)
     x = both[:, :D]
 
-    row = jnp.arange(ROWS, dtype=jnp.int32)
-    slot = row // BLK
-    position = jnp.concatenate([
-        (2 * (z ^ slot ^ flip) + core) * BLK + row % BLK,
-        (2 * (z ^ slot ^ (2 - flip)) + 1 - core) * BLK + row % BLK,
-    ])
-    usable = (position.astype(f32) < views * VIEW_TOK) | (position >= VIEWS_MAX * VIEW_TOK)
-    mask = jnp.broadcast_to(jnp.where(usable, 0.0, masked_score).astype(bf16)[:, None], (KEYS, LANES))
+    y = lax.axis_index("y")
+    x_place = lax.axis_index("xh") * 2 + lax.axis_index("xl")
+    at = jnp.stack([core, y, z, z, flip, views.astype(jnp.int32)]).astype(jnp.int32)
 
     source = x.astype(f32)
     centred = source - jnp.mean(source, axis=1, keepdims=True)
@@ -597,12 +607,9 @@
     sibling = swap(own)
     normed_other = swap(normed)
     queries = (product(weight_q) + query_bias).astype(bf16)
-    weights, heads_out, linv, attended = attention_forward(queries, own, sibling, mask)
+    weights, heads_out, linv, attended = attention_forward(at, queries, own, sibling)
 
     up_b = up_bias.reshape(NF, 1, FCHUNK)
-    y = lax.axis_index("y")
-    x_place = lax.axis_index("xh") * 2 + lax.axis_index("xl")
-    at = jnp.stack([core, y, z]).astype(jnp.int32)
     output, grad_hidden, grad_branch, grad_att, up_other, up_mine, down_other, down_mine, vec_grads, up_b_grad = (
         feed_forward(at, attended, both, out_weight, vecs, up_b, up_weight, down_weight)
     )

time: 302 us -> 301 us (level)
  transfers between devices with their start and end apart: 43 -> 43, of which waited for: 18 -> 19; matrix products, arithmetic and copies ran while one was open for 10% -> 10% of each run, Pallas kernels for 17% -> 17%
where the time goes in v8:
time: 301 us; the launch traced here: 296 us
  Pallas kernels  103 us (34%)
  waiting for transfers between devices  73.1 us (24%)
  starting transfers between devices  64.8 us (22%)
  local copies, waits for them, and re-layouts  25.8 us (9%)
  other arithmetic  22 us (7%)
  matrix products  4.57 us (2%)
    ppermute x26, waiting for transfers between devices, exchange(): return lax.ppermute(value, AXES, pairs)  60.1 us
    pallas_call x1, Pallas kernels, feed_forward(): pl.pallas_call(feed_forward_kernel, grid_spec=pltpu.PrefetchScalarGridSpe...  33.1 us
    ppermute x26, starting transfers between devices, exchange(): return lax.ppermute(value, AXES, pairs)  26.2 us
    pallas_call x1, Pallas kernels, attention_backward(): pl.pallas_call(attention_backward_kernel, grid_spec=pltpu.PrefetchScalarG...  19.3 us
    pallas_call x4, Pallas kernels, place(): pl.pallas_call(functools.partial(place_kernel, mine, late), grid_spec=plt...  17.9 us
    ppermute x4, starting transfers between devices, to_scene(): lax.ppermute(jnp.concatenate(message, axis=1), AXES, scene_pairs(slot))  17.7 us
    convert_element_type x14, other arithmetic, add(): functools.reduce(jnp.add, [term.astype(f32) for term in terms]).astype(bf16)  16.4 us
    pallas_call x1, Pallas kernels, attention_forward(): pl.pallas_call(attention_forward_kernel, grid_spec=pltpu.PrefetchScalarGr...  16.3 us
  transfers between devices with their start and end apart: 43, of which 19 were waited for; matrix products, arithmetic and copies ran while one was open for 10% of the time, Pallas kernels for 17%

profile of v8, /device:TPU:1, one launch (start us, length us, event | category | flops | bytes accessed | tf_op | source)
XLA Modules:
  0.0 296.2 jit_solution(6811589200378006753)
XLA Ops:
  2.6 1.7 dynamic-slice_bitcast_fusion.9
  4.4 6.0 %collective-permute-start.2 = (bf16[144,1664]{1,0:T(8,128)(2,1)S(1)}, bf16[144,1664]{1,0:T(8,128)(2,1)S(1)}, u32[]{:S(2)}, u32[]{:S(2)}) collective-permute-start(bf16[144,1664]{1,0:T(8,128)(2,1)S(1)} %maximum_maximum_fusion.2), channel_id=1, source_target_pairs={{0,4},{1,8},{3,10},{4,0},{5,12},{6,2},{8,1},{9,13},{10,3},{12,5},{... | collective-permute-start | bytes 1437704 | tf_op jit(solution)/shard_map/ppermute | solution.py:496
  11.2 5.2 %collective-permute-start = (bf16[144,1664]{1,0:T(8,128)(2,1)S(1)}, bf16[144,1664]{1,0:T(8,128)(2,1)S(1)}, u32[]{:S(2)}, u32[]{:S(2)}) collective-permute-start(bf16[144,1664]{1,0:T(8,128)(2,1)S(1)} %maximum_maximum_fusion), channel_id=1, source_target_pairs={{0,0},{1,12},{2,2},{4,4},{5,8},{7,10},{8,5},{9,9},{11,11},{12,1},{... | collective-permute-start | bytes 1437704 | tf_op jit(solution)/shard_map/ppermute | solution.py:496
  17.2 1.3 collective-permute-start.1
  19.2 5.2 %collective-permute-start.3 = (bf16[144,1664]{1,0:T(8,128)(2,1)S(1)}, bf16[144,1664]{1,0:T(8,128)(2,1)}, u32[]{:S(2)}, u32[]{:S(2)}) collective-permute-start(bf16[144,1664]{1,0:T(8,128)(2,1)S(1)} %maximum_maximum_fusion.3), channel_id=1, source_target_pairs={{1,10},{2,4},{3,8},{4,2},{6,0},{7,12},{8,3},{10,1},{11,13},{13,11}... | collective-permute-start | bytes 1437704 | tf_op jit(solution)/shard_map/ppermute | solution.py:496
  26.4 5.1 %collective-permute-done.1 = bf16[144,1664]{1,0:T(8,128)(2,1)} collective-permute-done((bf16[144,1664]{1,0:T(8,128)(2,1)S(1)}, bf16[144,1664]{1,0:T(8,128)(2,1)}, u32[]{:S(2)}, u32[]{:S(2)}) %collective-permute-start.1) | collective-permute-done | bytes 479264 | tf_op jit(solution)/shard_map/ppermute | solution.py:496
  31.5 4.3 %collective-permute-done.3 = bf16[144,1664]{1,0:T(8,128)(2,1)} collective-permute-done((bf16[144,1664]{1,0:T(8,128)(2,1)S(1)}, bf16[144,1664]{1,0:T(8,128)(2,1)}, u32[]{:S(2)}, u32[]{:S(2)}) %collective-permute-start.3) | collective-permute-done | bytes 479264 | tf_op jit(solution)/shard_map/ppermute | solution.py:496
  40.5 2.8 add_convert_fusion.ko_ref.vo_ref
  45.6 1.8 add_convert_fusion.3.q_ref
  47.5 16.3 %attention_forward.1 = (bf16[12,576,1152]{2,1,0:T(8,128)(2,1)}, f32[576,768]{1,0:T(8,128)}, f32[576,768]{1,0:T(8,128)}, bf16[576,768]{1,0:T(8,128)(2,1)}) custom-call(s32[6]{0:T(128)} %stack.115.at_ref, bf16[576,768]{1,0:T(8,128)(2,1)} %add_convert_fusion.3.q_ref, bf16[576,1536]{1,0:T(8,128)(2,1)} %add_convert_fusion.ko_ref.vo_ref, ...), custom_call_target="tpu_custom_call" | custom-call | flops 8153726976 | bytes 20000000 | tf_op jit(solution)/shard_map/attention_forward/pallas_call | solution.py:118
  63.8 33.1 %feed_forward.1 = (bf16[576,768]{1,0:T(8,128)(2,1)}, f32[576,768]{1,0:T(8,128)}, bf16[576,768]{1,0:T(8,128)(2,1)}, bf16[576,768]{1,0:T(8,128)(2,1)}, bf16[4,2,19...) custom-call(s32[6]{0:T(128)} %stack.115.at_ref, ...), custom_call_target="tpu_custom_call" | custom-call | flops 16307453952 | bytes 30000000 | tf_op jit(solution)/shard_map/feed_forward/pallas_call | solution.py:293
  98.5 19.3 %attention_backward.1 = (bf16[576,768]{1,0:T(8,128)(2,1)}, bf16[2,576,768]{2,1,0:T(8,128)(2,1)}, bf16[4,576,768]{2,1,0:T(8,128)(2,1)}) custom-call(s32[6]{0:T(128)} %stack.115.at_ref, bf16[576,768]{1,0:T(8,128)(2,1)} %add_convert_fusion.3.q_ref, bf16[576,1536]{1,0:T(8,128)(2,1)} %add_convert_fusion.ko_ref.vo_ref, ...), custom_call_target="tpu_custom_call" | custom-call | flops 16307453952 | bytes 25000000 | tf_op jit(solution)/shard_map/attention_backward/pallas_call | solution.py:180
  118.3 3.1 %add_convert_fusion.1 = bf16[2,2,192,768]{3,2,1,0:T(8,128)(2,1)} fusion(bf16[4,2,192,768]{3,2,1,0:T(8,128)(2,1)} %collective-permute-done.6, bf16[4,2,192,768]{3,2,1,0:T(8,128)(2,1)} %get-tuple-element.181), kind=kLoop, calls=%fused_computation.1 | loop fusion | flops 2359296 | bytes 3538944 | tf_op jit(solution)/shard_map/convert_element_type | solution.py:550
  121.5 2.7 add_convert_fusion.2
  124.2 2.7 collective-permute-start.13
  128.0 2.1 constant_dynamic-update-slice_fusion.1
  134.8 7.9 %squares.1 = (bf16[2,1,192,768]{3,2,1,0:T(8,128)(2,1)S(1)}, bf16[2,1,192,768]{3,2,1,0:T(8,128)(2,1)}, bf16[2,1,192,768]{3,2,1,0:T(8,128)(2,1)S(1)}, bf16[2,1,192,768]{3,2,1,0:T(8,128)(2,1)}) custom-call(s32[6]{0:T(128)S(1)} %copy-done.13, bf16[576,768]{1,0:T(8,128)(2,1)S(1)} %copy-done.1, bf16[2,576,768]{2,1,0:T(8,128)(2,1)S(1)} %copy-done, ...), custom_call_target="tpu_custom_call" | custom-call | flops 2717908992 | bytes 13000000 | tf_op jit(solution)/shard_map/squares/pallas_call | solution.py:354
  142.8 2.0 collective-permute-start.11
  144.8 1.7 collective-permute-start.12
  146.5 2.5 fusion.8
  149.0 2.4 fusion.9
  152.0 8.8 %input_gradient.1 = (bf16[576,768]{1,0:T(8,128)(2,1)}, f32[16,768]{1,0:T(8,128)}) custom-call(bf16[576,768]{1,0:T(8,128)(2,1)} %get-tuple-element.172.gq_ref, bf16[2,576,768]{2,1,0:T(8,128)(2,1)} %get-tuple-element.173.own_ref, bf16[4,576,768]{2,1,0:T(8,128)(2,1)} %collective-permute-done.9.arrived_ref.arrived_own_ref.arrived_gq_ref.swapped_ref, ...), custom_call_target="tpu_custom_call" | custom-call | flops 2038431744 | bytes 10000000 | tf_op jit(solution)/shard_map/input_gradient/pallas_call | solution.py:405
  163.0 1.9 fusion.6
  166.1 1.4 collective-permute-start.18
  168.7 2.0 fusion.7
  170.6 1.3 collective-permute-done.18
  173.4 1.5 collective-permute-start.20
  174.8 1.7 collective-permute-start.19
  176.6 5.8 %collective-permute-done.20 = bf16[320,768]{1,0:T(8,128)(2,1)S(1)} collective-permute-done((bf16[320,768]{1,0:T(8,128)(2,1)S(1)}, bf16[320,768]{1,0:T(8,128)(2,1)S(1)}, u32[]{:S(2)}, u32[]{:S(2)}) %collective-permute-start.20) | collective-permute-done | bytes 491552 | tf_op jit(solution)/shard_map/ppermute | solution.py:526
  183.5 1.8 collective-permute-start.27
  185.3 3.4 %collective-permute-done.22 = bf16[176,768]{1,0:T(8,128)(2,1)S(1)} collective-permute-done((bf16[176,768]{1,0:T(8,128)(2,1)S(1)}, bf16[176,768]{1,0:T(8,128)(2,1)S(1)}, u32[]{:S(2)}, u32[]{:S(2)}) %collective-permute-start.22) | collective-permute-done | bytes 270368 | tf_op jit(solution)/shard_map/ppermute | solution.py:526
  188.8 1.2 collective-permute-done.21
  191.4 1.8 collective-permute-start.24
  193.2 6.7 %collective-permute-done.23 = bf16[176,768]{1,0:T(8,128)(2,1)} collective-permute-done((bf16[176,768]{1,0:T(8,128)(2,1)S(1)}, bf16[176,768]{1,0:T(8,128)(2,1)}, u32[]{:S(2)}, u32[]{:S(2)}) %collective-permute-start.23) | collective-permute-done | bytes 270368 | tf_op jit(solution)/shard_map/ppermute | solution.py:526
  204.5 2.7 collective-permute-done.25
  209.5 1.4 collective-permute-start.29
  212.1 1.9 collective-permute-done.28
  214.7 1.5 collective-permute-start.31
  216.3 1.6 collective-permute-start.30
  218.0 10.4 %collective-permute-done.30 = bf16[320,768]{1,0:T(8,128)(2,1)S(1)} collective-permute-done((bf16[320,768]{1,0:T(8,128)(2,1)S(1)}, bf16[320,768]{1,0:T(8,128)(2,1)S(1)}, u32[]{:S(2)}, u32[]{:S(2)}) %collective-permute-start.30) | collective-permute-done | bytes 491552 | tf_op jit(solution)/shard_map/ppermute | solution.py:526
  229.3 16.0 %collective-permute-start.35 = (bf16[3,144,1536]{2,1,0:T(8,128)(2,1)S(1)}, bf16[3,144,1536]{2,1,0:T(8,128)(2,1)S(1)}, u32[]{:S(2)}, u32[]{:S(2)}) collective-permute-start(bf16[3,144,1536]{2,1,0:T(8,128)(2,1)S(1)} %pad_maximum_fusion.4), channel_id=1, source_target_pairs={{0,0},{1,8},{2,2},{3,10},{4,4},{5,12},{6,6},{7,14},{8,1},{9,9},{10... | collective-permute-start | bytes 3981320 | tf_op jit(solution)/shard_map/ppermute | solution.py:505
  245.5 11.8 %collective-permute-done.33 = bf16[3,192,768]{2,1,0:T(8,128)(2,1)S(1)} collective-permute-done((bf16[3,192,768]{2,1,0:T(8,128)(2,1)S(1)}, bf16[3,192,768]{2,1,0:T(8,128)(2,1)S(1)}, u32[]{:S(2)}, u32[]{:S(2)}) %collective-permute-start.33) | collective-permute-done | bytes 884768 | tf_op jit(solution)/shard_map/ppermute | solution.py:526
  257.4 3.4 %collective-permute-done.35 = bf16[3,144,1536]{2,1,0:T(8,128)(2,1)S(1)} collective-permute-done((bf16[3,144,1536]{2,1,0:T(8,128)(2,1)S(1)}, bf16[3,144,1536]{2,1,0:T(8,128)(2,1)S(1)}, u32[]{:S(2)}, u32[]{:S(2)}) %collective-permute-start.35) | collective-permute-done | bytes 1327136 | tf_op jit(solution)/shard_map/ppermute | solution.py:505
  263.2 4.4 %place_early.2 = (f32[768,3072]{1,0:T(8,128)}, f32[3072,768]{1,0:T(8,128)}, f32[768,2304]{1,0:T(8,128)}, f32[768,768]{1,0:T(8,128)}) custom-call(s32[6]{0:T(128)S(1)} %copy-done.13, bf16[2,3,192,768]{3,2,1,0:T(8,128)(2,1)S(1)} %pad_maximum_fusion.2.source0_ref, bf16[2,3,192,768]{3,2,1,0:T(8,128)(2,1)S(1)} %pad_maximum_fusion.3.source1_ref), custom_call_target="tpu_custom_call" | custom-call | bytes 11000000 | tf_op jit(solution)/shard_map/place_early/pallas_call | solution.py:459
  267.7 4.4 %place_early.3 = (f32[768,3072]{1,0:T(8,128)}, f32[3072,768]{1,0:T(8,128)}, f32[768,2304]{1,0:T(8,128)}, f32[768,768]{1,0:T(8,128)}) custom-call(s32[6]{0:T(128)S(1)} %copy-done.13, bf16[2,3,192,768]{3,2,1,0:T(8,128)(2,1)S(1)} %collective-permute-done.36.source0_ref, ...), custom_call_target="tpu_custom_call", output_to_operand_aliasing={{0}: (3, {}), {1}: (4, {}), {2}: (5, {}), {3}: (6, {})} | custom-call | bytes 11000000 | tf_op jit(solution)/shard_map/place_early/pallas_call | solution.py:459
  272.1 12.2 %collective-permute-done.39.source0_ref = bf16[2,3,192,768]{3,2,1,0:T(8,128)(2,1)S(1)} collective-permute-done((bf16[2,3,192,768]{3,2,1,0:T(8,128)(2,1)S(1)}, bf16[2,3,192,768]{3,2,1,0:T(8,128)(2,1)S(1)}, u32[]{:S(2)}, u32[]{:S(2)}) %collective-permute-start.39) | collective-permute-done | bytes 1769504 | tf_op jit(solution)/shard_map/ppermute | solution.py:526
  286.2 4.4 %place_late.2 = (f32[768,3072]{1,0:T(8,128)}, f32[3072,768]{1,0:T(8,128)}, f32[768,2304]{1,0:T(8,128)}, f32[768,768]{1,0:T(8,128)}) custom-call(s32[6]{0:T(128)S(1)} %copy-done.13, bf16[2,3,192,768]{3,2,1,0:T(8,128)(2,1)S(1)} %collective-permute-done.39.source0_ref, ...), custom_call_target="tpu_custom_call", output_to_operand_aliasing={{0}: (3, {}), {1}: (4, {}), {2}: (5, {}), {3}: (6, {})} | custom-call | bytes 11000000 | tf_op jit(solution)/shard_map/place_late/pallas_call | solution.py:459
  291.3 4.7 %place_late.3 = (f32[768,3072]{1,0:T(8,128)}, f32[3072,768]{1,0:T(8,128)}, f32[768,2304]{1,0:T(8,128)}, f32[768,768]{1,0:T(8,128)}) custom-call(s32[6]{0:T(128)S(1)} %copy-done.13, bf16[2,3,192,768]{3,2,1,0:T(8,128)(2,1)} %collective-permute-done.41.source0_ref, ...), custom_call_target="tpu_custom_call", output_to_operand_aliasing={{0}: (3, {}), {1}: (4, {}), {2}: (5, {}), {3}: (6, {})} | custom-call | bytes 11000000 | tf_op jit(solution)/shard_map/place_late/pallas_call | solution.py:459
  (232 shorter events, 44.1 us)
Async XLA Ops:
  4.4 22.0 %collective-permute-start.2 = (bf16[144,1664]{1,0:T(8,128)(2,1)S(1)}, bf16[144,1664]{1,0:T(8,128)(2,1)S(1)}, u32[]{:S(2)}, u32[]{:S(2)}) collective-permute-start(bf16[144,1664]{1,0:T(8,128)(2,1)S(1)} %maximum_maximum_fusion.2), channel_id=1, source_target_pairs={{0,4},{1,8},{3,10},{4,0},{5,12},{6,2},{8,1},{9,13},{10,3},{12,5},{... | collective-permute-start | bytes 1437704 | tf_op jit(solution)/shard_map/ppermute | solution.py:496
  11.2 15.2 %collective-permute-start = (bf16[144,1664]{1,0:T(8,128)(2,1)S(1)}, bf16[144,1664]{1,0:T(8,128)(2,1)S(1)}, u32[]{:S(2)}, u32[]{:S(2)}) collective-permute-start(bf16[144,1664]{1,0:T(8,128)(2,1)S(1)} %maximum_maximum_fusion), channel_id=1, source_target_pairs={{0,0},{1,12},{2,2},{4,4},{5,8},{7,10},{8,5},{9,9},{11,11},{12,1},{... | collective-permute-start | bytes 1437704 | tf_op jit(solution)/shard_map/ppermute | solution.py:496
  17.2 14.3 %collective-permute-start.1 = (bf16[144,1664]{1,0:T(8,128)(2,1)S(1)}, bf16[144,1664]{1,0:T(8,128)(2,1)}, u32[]{:S(2)}, u32[]{:S(2)}) collective-permute-start(bf16[144,1664]{1,0:T(8,128)(2,1)S(1)} %maximum_maximum_fusion.1), channel_id=1, source_target_pairs={{0,2},{2,0},{3,12},{5,10},{6,4},{7,8},{9,11},{10,5},{11,9},{12,3},... | collective-permute-start | bytes 1437704 | tf_op jit(solution)/shard_map/ppermute | solution.py:496
  19.2 16.6 %collective-permute-start.3 = (bf16[144,1664]{1,0:T(8,128)(2,1)S(1)}, bf16[144,1664]{1,0:T(8,128)(2,1)}, u32[]{:S(2)}, u32[]{:S(2)}) collective-permute-start(bf16[144,1664]{1,0:T(8,128)(2,1)S(1)} %maximum_maximum_fusion.3), channel_id=1, source_target_pairs={{1,10},{2,4},{3,8},{4,2},{6,0},{7,12},{8,3},{10,1},{11,13},{13,11}... | collective-permute-start | bytes 1437704 | tf_op jit(solution)/shard_map/ppermute | solution.py:496
  43.3 4.2 %collective-permute-start.4 = (bf16[576,1536]{1,0:T(8,128)(2,1)}, bf16[576,1536]{1,0:T(8,128)(2,1)}, u32[]{:S(2)}, u32[]{:S(2)}) collective-permute-start(bf16[576,1536]{1,0:T(8,128)(2,1)} %add_convert_fusion.ko_ref.vo_ref), channel_id=1, source_target_pairs={{0,8},{8,0},{1,9},{9,1},{2,10},{10,2},{3,11},{11,3},{4,12},{12,4},... | collective-permute-start | bytes 5308424 | tf_op jit(solution)/shard_map/ppermute | solution.py:539
  63.8 33.7 %copy-start.2 = (bf16[576,768]{1,0:T(8,128)(2,1)S(1)}, bf16[576,768]{1,0:T(8,128)(2,1)}, u32[]{:S(2)}) copy-start(bf16[576,768]{1,0:T(8,128)(2,1)} %get-tuple-element.169.att_ref) | copy-start | bytes 2654212
  96.9 20.9 %collective-permute-start.5 = (bf16[4,2,192,768]{3,2,1,0:T(8,128)(2,1)}, bf16[4,2,192,768]{3,2,1,0:T(8,128)(2,1)}, u32[]{:S(2)}, u32[]{:S(2)}) collective-permute-start(bf16[4,2,192,768]{3,2,1,0:T(8,128)(2,1)} %get-tuple-element.174), channel_id=1, source_target_pairs={{0,8},{8,0},{1,9},{9,1},{2,10},{10,2},{3,11},{11,3},{4,12},{12,4},... | collective-permute-start | bytes 7077896 | tf_op jit(solution)/shard_map/ppermute | solution.py:539
  97.4 20.5 %collective-permute-start.6 = (bf16[4,2,192,768]{3,2,1,0:T(8,128)(2,1)}, bf16[4,2,192,768]{3,2,1,0:T(8,128)(2,1)}, u32[]{:S(2)}, u32[]{:S(2)}) collective-permute-start(bf16[4,2,192,768]{3,2,1,0:T(8,128)(2,1)} %get-tuple-element.175), channel_id=1, source_target_pairs={{0,8},{8,0},{1,9},{9,1},{2,10},{10,2},{3,11},{11,3},{4,12},{12,4},... | collective-permute-start | bytes 7077896 | tf_op jit(solution)/shard_map/ppermute | solution.py:539
  97.5 20.3 %collective-permute-start.7 = (bf16[576,768]{1,0:T(8,128)(2,1)S(1)}, bf16[576,768]{1,0:T(8,128)(2,1)S(1)}, u32[]{:S(2)}, u32[]{:S(2)}) collective-permute-start(bf16[576,768]{1,0:T(8,128)(2,1)S(1)} %copy-done.2), channel_id=1, source_target_pairs={{0,8},{8,0},{1,9},{9,1},{2,10},{10,2},{3,11},{11,3},{4,12},{12,4},... | collective-permute-start | bytes 2654216 | tf_op jit(solution)/shard_map/ppermute | solution.py:539
  97.9 20.0 %collective-permute-start.8 = (bf16[576,768]{1,0:T(8,128)(2,1)}, bf16[576,768]{1,0:T(8,128)(2,1)S(1)}, u32[]{:S(2)}, u32[]{:S(2)}) collective-permute-start(bf16[576,768]{1,0:T(8,128)(2,1)} %get-tuple-element.176.gb_ref), channel_id=1, source_target_pairs={{0,8},{8,0},{1,9},{9,1},{2,10},{10,2},{3,11},{11,3},{4,12},{12,4},... | collective-permute-start | bytes 2654216 | tf_op jit(solution)/shard_map/ppermute | solution.py:539
  117.9 12.2 %collective-permute-start.9 = (bf16[4,576,768]{2,1,0:T(8,128)(2,1)}, bf16[4,576,768]{2,1,0:T(8,128)(2,1)}, u32[]{:S(2)}, u32[]{:S(2)}) collective-permute-start(bf16[4,576,768]{2,1,0:T(8,128)(2,1)} %get-tuple-element.178.other_ref), channel_id=1, source_target_pairs={{0,8},{8,0},{1,9},{9,1},{2,10},{10,2},{3,11},{11,3},{4,12},{12,4},... | collective-permute-start | bytes 10616840 | tf_op jit(solution)/shard_map/ppermute | solution.py:539
  121.4 21.4 %collective-permute-start.14 = (bf16[2,2,192,768]{3,2,1,0:T(8,128)(2,1)}, bf16[2,2,192,768]{3,2,1,0:T(8,128)(2,1)}, u32[]{:S(2)}, u32[]{:S(2)}) collective-permute-start(bf16[2,2,192,768]{3,2,1,0:T(8,128)(2,1)} %add_convert_fusion.1), channel_id=1, source_target_pairs={{0,2},{8,14},{2,0},{10,12},{4,6},{12,10},{6,4},{14,8},{32,34},{40,... | collective-permute-start | bytes 3538952 | tf_op jit(solution)/shard_map/ppermute | solution.py:526
  121.4 8.7 %copy-start.1 = (bf16[576,768]{1,0:T(8,128)(2,1)S(1)}, bf16[576,768]{1,0:T(8,128)(2,1)}, u32[]{:S(2)}) copy-start(bf16[576,768]{1,0:T(8,128)(2,1)} %get-tuple-element.172.gq_ref) | copy-start | bytes 2654212
  124.2 18.6 %collective-permute-start.13 = (bf16[2,2,192,768]{3,2,1,0:T(8,128)(2,1)}, bf16[2,2,192,768]{3,2,1,0:T(8,128)(2,1)}, u32[]{:S(2)}, u32[]{:S(2)}) collective-permute-start(bf16[2,2,192,768]{3,2,1,0:T(8,128)(2,1)} %add_convert_fusion.2), channel_id=1, source_target_pairs={{0,32},{8,104},{2,34},{10,106},{4,36},{12,108},{6,38},{14,110},{32... | collective-permute-start | bytes 3538952 | tf_op jit(solution)/shard_map/ppermute | solution.py:526
  126.9 3.3 %collective-permute-start.10 = (bf16[576,768]{1,0:T(8,128)(2,1)S(1)}, bf16[576,768]{1,0:T(8,128)(2,1)}, u32[]{:S(2)}, u32[]{:S(2)}) collective-permute-start(bf16[576,768]{1,0:T(8,128)(2,1)S(1)} %fusion.5.normed_ref), channel_id=1, source_target_pairs={{0,8},{8,0},{1,9},{9,1},{2,10},{10,2},{3,11},{11,3},{4,12},{12,4},... | collective-permute-start | bytes 2654216 | tf_op jit(solution)/shard_map/ppermute | solution.py:539
  142.8 8.6 %copy-start.11 = (bf16[2,1,192,768]{3,2,1,0:T(8,128)(2,1)}, bf16[2,1,192,768]{3,2,1,0:T(8,128)(2,1)S(1)}, u32[]{:S(2)}) copy-start(bf16[2,1,192,768]{3,2,1,0:T(8,128)(2,1)S(1)} %get-tuple-element.203) | copy-start | bytes 1769476
  142.8 18.0 %collective-permute-start.11 = (bf16[2,1,192,768]{3,2,1,0:T(8,128)(2,1)}, bf16[2,1,192,768]{3,2,1,0:T(8,128)(2,1)S(1)}, u32[]{:S(2)}, u32[]{:S(2)}) collective-permute-start(bf16[2,1,192,768]{3,2,1,0:T(8,128)(2,1)} %get-tuple-element.190), channel_id=1, source_target_pairs={{0,32},{8,104},{2,34},{10,106},{4,36},{12,108},{6,38},{14,110},{32... | collective-permute-start | bytes 1769480 | tf_op jit(solution)/shard_map/ppermute | solution.py:526
  144.8 16.0 %collective-permute-start.12 = (bf16[2,1,192,768]{3,2,1,0:T(8,128)(2,1)}, bf16[2,1,192,768]{3,2,1,0:T(8,128)(2,1)S(1)}, u32[]{:S(2)}, u32[]{:S(2)}) collective-permute-start(bf16[2,1,192,768]{3,2,1,0:T(8,128)(2,1)} %get-tuple-element.191), channel_id=1, source_target_pairs={{0,2},{8,14},{2,0},{10,12},{4,6},{12,10},{6,4},{14,8},{32,34},{40,... | collective-permute-start | bytes 1769480 | tf_op jit(solution)/shard_map/ppermute | solution.py:526
  151.4 11.6 %collective-permute-start.15 = (bf16[2,192,768]{2,1,0:T(8,128)(2,1)}, bf16[2,192,768]{2,1,0:T(8,128)(2,1)}, u32[]{:S(2)}, u32[]{:S(2)}) collective-permute-start(bf16[2,192,768]{2,1,0:T(8,128)(2,1)} %fusion.8), channel_id=1, source_target_pairs={{0,96},{8,40},{2,98},{10,42},{4,100},{12,44},{6,102},{14,46},{32,6... | collective-permute-start | bytes 1769480 | tf_op jit(solution)/shard_map/ppermute | solution.py:526
  151.8 11.2 %collective-permute-start.16 = (bf16[2,192,768]{2,1,0:T(8,128)(2,1)}, bf16[2,192,768]{2,1,0:T(8,128)(2,1)}, u32[]{:S(2)}, u32[]{:S(2)}) collective-permute-start(bf16[2,192,768]{2,1,0:T(8,128)(2,1)} %fusion.9), channel_id=1, source_target_pairs={{0,6},{8,10},{2,4},{10,8},{4,2},{12,14},{6,0},{14,12},{32,38},{40,... | collective-permute-start | bytes 1769480 | tf_op jit(solution)/shard_map/ppermute | solution.py:526
  152.0 8.9 %copy-start.10 = (bf16[2,1,192,768]{3,2,1,0:T(8,128)(2,1)S(1)}, bf16[2,1,192,768]{3,2,1,0:T(8,128)(2,1)}, u32[]{:S(2)}) copy-start(bf16[2,1,192,768]{3,2,1,0:T(8,128)(2,1)} %copy-done.9) | copy-start | bytes 1769476
  152.0 9.8 %copy-start.12 = (bf16[2,1,192,768]{3,2,1,0:T(8,128)(2,1)S(1)}, bf16[2,1,192,768]{3,2,1,0:T(8,128)(2,1)}, u32[]{:S(2)}) copy-start(bf16[2,1,192,768]{3,2,1,0:T(8,128)(2,1)} %copy-done.11) | copy-start | bytes 1769476
  164.9 5.7 %collective-permute-start.17 = (bf16[1,192,768]{2,1,0:T(8,128)(2,1)S(1)}, bf16[1,192,768]{2,1,0:T(8,128)(2,1)S(1)}, u32[]{:S(2)}, u32[]{:S(2)}) collective-permute-start(bf16[1,192,768]{2,1,0:T(8,128)(2,1)S(1)} %fusion.18), channel_id=1, source_target_pairs={{0,96},{8,40},{2,98},{10,42},{4,100},{12,44},{6,102},{14,46},{32,6... | collective-permute-start | bytes 884744 | tf_op jit(solution)/shard_map/ppermute | solution.py:526
  166.1 5.9 %collective-permute-start.18 = (bf16[1,192,768]{2,1,0:T(8,128)(2,1)S(1)}, bf16[1,192,768]{2,1,0:T(8,128)(2,1)S(1)}, u32[]{:S(2)}, u32[]{:S(2)}) collective-permute-start(bf16[1,192,768]{2,1,0:T(8,128)(2,1)S(1)} %fusion.19), channel_id=1, source_target_pairs={{0,6},{8,10},{2,4},{10,8},{4,2},{12,14},{6,0},{14,12},{32,38},{40,... | collective-permute-start | bytes 884744 | tf_op jit(solution)/shard_map/ppermute | solution.py:526
  173.4 9.0 %collective-permute-start.20 = (bf16[320,768]{1,0:T(8,128)(2,1)S(1)}, bf16[320,768]{1,0:T(8,128)(2,1)S(1)}, u32[]{:S(2)}, u32[]{:S(2)}) collective-permute-start(bf16[320,768]{1,0:T(8,128)(2,1)S(1)} %pad_maximum_fusion.9), channel_id=1, source_target_pairs={{0,32},{8,104},{2,34},{10,106},{4,36},{12,108},{6,38},{14,110},{32... | collective-permute-start | bytes 1474568 | tf_op jit(solution)/shard_map/ppermute | solution.py:526
  174.8 8.4 %collective-permute-start.19 = (bf16[2,3,48,768]{3,2,1,0:T(8,128)(2,1)S(1)}, bf16[2,3,48,768]{3,2,1,0:T(8,128)(2,1)S(1)}, u32[]{:S(2)}, u32[]{:S(2)}) collective-permute-start(bf16[2,3,48,768]{3,2,1,0:T(8,128)(2,1)S(1)} %pad_maximum_fusion.11), channel_id=1, source_target_pairs={{0,16},{8,25},{2,18},{10,27},{4,20},{12,29},{6,22},{14,31},{32,48}... | collective-permute-start | bytes 1327112 | tf_op jit(solution)/shard_map/ppermute | solution.py:526
  183.4 5.4 %collective-permute-start.22 = (bf16[176,768]{1,0:T(8,128)(2,1)S(1)}, bf16[176,768]{1,0:T(8,128)(2,1)S(1)}, u32[]{:S(2)}, u32[]{:S(2)}) collective-permute-start(bf16[176,768]{1,0:T(8,128)(2,1)S(1)} %pad_maximum_fusion.15), channel_id=1, source_target_pairs={{0,96},{8,40},{2,98},{10,42},{4,100},{12,44},{6,102},{14,46},{32,6... | collective-permute-start | bytes 811016 | tf_op jit(solution)/shard_map/ppermute | solution.py:526
  183.5 18.5 %collective-permute-start.27 = (bf16[288,1536]{1,0:T(8,128)(2,1)}, bf16[288,1536]{1,0:T(8,128)(2,1)}, u32[]{:S(2)}, u32[]{:S(2)}) collective-permute-start(bf16[288,1536]{1,0:T(8,128)(2,1)} %pad_maximum_fusion.7), channel_id=1, source_target_pairs={{0,2},{8,14},{2,0},{10,12},{4,6},{12,10},{6,4},{14,8},{32,34},{40,... | collective-permute-start | bytes 2654216 | tf_op jit(solution)/shard_map/ppermute | solution.py:526
  185.3 4.8 %collective-permute-start.21 = (bf16[3,48,768]{2,1,0:T(8,128)(2,1)S(1)}, bf16[3,48,768]{2,1,0:T(8,128)(2,1)S(1)}, u32[]{:S(2)}, u32[]{:S(2)}) collective-permute-start(bf16[3,48,768]{2,1,0:T(8,128)(2,1)S(1)} %fusion.15), channel_id=1, source_target_pairs={{0,17},{8,24},{2,19},{10,26},{4,21},{12,28},{6,23},{14,30},{32,49}... | collective-permute-start | bytes 663560 | tf_op jit(solution)/shard_map/ppermute | solution.py:526
  190.3 9.6 %collective-permute-start.23 = (bf16[176,768]{1,0:T(8,128)(2,1)S(1)}, bf16[176,768]{1,0:T(8,128)(2,1)}, u32[]{:S(2)}, u32[]{:S(2)}) collective-permute-start(bf16[176,768]{1,0:T(8,128)(2,1)S(1)} %pad_maximum_fusion.16), channel_id=1, source_target_pairs={{0,2},{8,14},{2,0},{10,12},{4,6},{12,10},{6,4},{14,8},{32,34},{40,... | collective-permute-start | bytes 811016 | tf_op jit(solution)/shard_map/ppermute | solution.py:526
  191.4 10.2 %collective-permute-start.24 = (bf16[3,48,768]{2,1,0:T(8,128)(2,1)S(1)}, bf16[3,48,768]{2,1,0:T(8,128)(2,1)S(1)}, u32[]{:S(2)}, u32[]{:S(2)}) collective-permute-start(bf16[3,48,768]{2,1,0:T(8,128)(2,1)S(1)} %fusion.13), channel_id=1, source_target_pairs={{0,16},{8,25},{2,18},{10,27},{4,20},{12,29},{6,22},{14,31},{32,48}... | collective-permute-start | bytes 663560 | tf_op jit(solution)/shard_map/ppermute | solution.py:526
  201.8 5.4 %collective-permute-start.25 = (bf16[176,768]{1,0:T(8,128)(2,1)S(1)}, bf16[176,768]{1,0:T(8,128)(2,1)S(1)}, u32[]{:S(2)}, u32[]{:S(2)}) collective-permute-start(bf16[176,768]{1,0:T(8,128)(2,1)S(1)} %pad_maximum_fusion.17), channel_id=1, source_target_pairs={{0,6},{8,10},{2,4},{10,8},{4,2},{12,14},{6,0},{14,12},{32,38},{40,... | collective-permute-start | bytes 811016 | tf_op jit(solution)/shard_map/ppermute | solution.py:526
  203.3 4.9 %collective-permute-start.26 = (bf16[3,48,768]{2,1,0:T(8,128)(2,1)S(1)}, bf16[3,48,768]{2,1,0:T(8,128)(2,1)S(1)}, u32[]{:S(2)}, u32[]{:S(2)}) collective-permute-start(bf16[3,48,768]{2,1,0:T(8,128)(2,1)S(1)} %add.376), channel_id=1, source_target_pairs={{0,17},{8,24},{2,19},{10,26},{4,21},{12,28},{6,23},{14,30},{32,49}... | collective-permute-start | bytes 663560 | tf_op jit(solution)/shard_map/ppermute | solution.py:526
  208.3 5.7 %collective-permute-start.28 = (bf16[176,768]{1,0:T(8,128)(2,1)S(1)}, bf16[176,768]{1,0:T(8,128)(2,1)S(1)}, u32[]{:S(2)}, u32[]{:S(2)}) collective-permute-start(bf16[176,768]{1,0:T(8,128)(2,1)S(1)} %pad_maximum_fusion.18), channel_id=1, source_target_pairs={{0,17},{8,24},{2,19},{10,26},{4,21},{12,28},{6,23},{14,30},{32,49}... | collective-permute-start | bytes 811016 | tf_op jit(solution)/shard_map/ppermute | solution.py:526
  209.5 5.1 %collective-permute-start.29 = (bf16[3,48,768]{2,1,0:T(8,128)(2,1)S(1)}, bf16[3,48,768]{2,1,0:T(8,128)(2,1)S(1)}, u32[]{:S(2)}, u32[]{:S(2)}) collective-permute-start(bf16[3,48,768]{2,1,0:T(8,128)(2,1)S(1)} %add.381), channel_id=1, source_target_pairs={{0,96},{8,40},{2,98},{10,42},{4,100},{12,44},{6,102},{14,46},{32,6... | collective-permute-start | bytes 663560 | tf_op jit(solution)/shard_map/ppermute | solution.py:526
  210.9 17.8 %collective-permute-start.32 = (bf16[288,1536]{1,0:T(8,128)(2,1)S(1)}, bf16[288,1536]{1,0:T(8,128)(2,1)S(1)}, u32[]{:S(2)}, u32[]{:S(2)}) collective-permute-start(bf16[288,1536]{1,0:T(8,128)(2,1)S(1)} %pad_maximum_fusion.8), channel_id=1, source_target_pairs={{0,6},{8,10},{2,4},{10,8},{4,2},{12,14},{6,0},{14,12},{32,38},{40,... | collective-permute-start | bytes 2654216 | tf_op jit(solution)/shard_map/ppermute | solution.py:526
  214.7 13.8 %collective-permute-start.31 = (bf16[2,3,48,768]{3,2,1,0:T(8,128)(2,1)S(1)}, bf16[2,3,48,768]{3,2,1,0:T(8,128)(2,1)S(1)}, u32[]{:S(2)}, u32[]{:S(2)}) collective-permute-start(bf16[2,3,48,768]{3,2,1,0:T(8,128)(2,1)S(1)} %pad_maximum_fusion.14), channel_id=1, source_target_pairs={{0,32},{8,104},{2,34},{10,106},{4,36},{12,108},{6,38},{14,110},{32... | collective-permute-start | bytes 1327112 | tf_op jit(solution)/shard_map/ppermute | solution.py:526
  216.3 12.2 %collective-permute-start.30 = (bf16[320,768]{1,0:T(8,128)(2,1)S(1)}, bf16[320,768]{1,0:T(8,128)(2,1)S(1)}, u32[]{:S(2)}, u32[]{:S(2)}) collective-permute-start(bf16[320,768]{1,0:T(8,128)(2,1)S(1)} %pad_maximum_fusion.10), channel_id=1, source_target_pairs={{0,16},{8,25},{2,18},{10,27},{4,20},{12,29},{6,22},{14,31},{32,48}... | collective-permute-start | bytes 1474568 | tf_op jit(solution)/shard_map/ppermute | solution.py:526
  229.3 31.5 %collective-permute-start.35 = (bf16[3,144,1536]{2,1,0:T(8,128)(2,1)S(1)}, bf16[3,144,1536]{2,1,0:T(8,128)(2,1)S(1)}, u32[]{:S(2)}, u32[]{:S(2)}) collective-permute-start(bf16[3,144,1536]{2,1,0:T(8,128)(2,1)S(1)} %pad_maximum_fusion.4), channel_id=1, source_target_pairs={{0,0},{1,8},{2,2},{3,10},{4,4},{5,12},{6,6},{7,14},{8,1},{9,9},{10... | collective-permute-start | bytes 3981320 | tf_op jit(solution)/shard_map/ppermute | solution.py:505
  245.3 12.0 %collective-permute-start.33 = (bf16[3,192,768]{2,1,0:T(8,128)(2,1)S(1)}, bf16[3,192,768]{2,1,0:T(8,128)(2,1)S(1)}, u32[]{:S(2)}, u32[]{:S(2)}) collective-permute-start(bf16[3,192,768]{2,1,0:T(8,128)(2,1)S(1)} %bitcast.141), channel_id=1, source_target_pairs={{0,96},{8,40},{2,98},{10,42},{4,100},{12,44},{6,102},{14,46},{32,6... | collective-permute-start | bytes 2654216 | tf_op jit(solution)/shard_map/ppermute | solution.py:526
  245.4 12.0 %collective-permute-start.34 = (bf16[3,192,768]{2,1,0:T(8,128)(2,1)S(1)}, bf16[3,192,768]{2,1,0:T(8,128)(2,1)S(1)}, u32[]{:S(2)}, u32[]{:S(2)}) collective-permute-start(bf16[3,192,768]{2,1,0:T(8,128)(2,1)S(1)} %bitcast.143), channel_id=1, source_target_pairs={{0,6},{8,10},{2,4},{10,8},{4,2},{12,14},{6,0},{14,12},{32,38},{40,... | collective-permute-start | bytes 2654216 | tf_op jit(solution)/shard_map/ppermute | solution.py:526
  261.1 6.6 %collective-permute-start.36 = (bf16[2,3,192,768]{3,2,1,0:T(8,128)(2,1)S(1)}, bf16[2,3,192,768]{3,2,1,0:T(8,128)(2,1)S(1)}, u32[]{:S(2)}, u32[]{:S(2)}) collective-permute-start(bf16[2,3,192,768]{3,2,1,0:T(8,128)(2,1)S(1)} %pad_maximum_fusion.2.source0_ref), channel_id=1, source_target_pairs={{0,8},{8,0},{1,9},{9,1},{2,10},{10,2},{3,11},{11,3},{4,12},{12,4},... | collective-permute-start | bytes 5308424 | tf_op jit(solution)/shard_map/ppermute | solution.py:539
  261.2 6.5 %collective-permute-start.37 = (bf16[2,3,192,768]{3,2,1,0:T(8,128)(2,1)S(1)}, bf16[2,3,192,768]{3,2,1,0:T(8,128)(2,1)S(1)}, u32[]{:S(2)}, u32[]{:S(2)}) collective-permute-start(bf16[2,3,192,768]{3,2,1,0:T(8,128)(2,1)S(1)} %pad_maximum_fusion.3.source1_ref), channel_id=1, source_target_pairs={{0,8},{8,0},{1,9},{9,1},{2,10},{10,2},{3,11},{11,3},{4,12},{12,4},... | collective-permute-start | bytes 5308424 | tf_op jit(solution)/shard_map/ppermute | solution.py:539
  261.7 22.6 %collective-permute-start.39 = (bf16[2,3,192,768]{3,2,1,0:T(8,128)(2,1)S(1)}, bf16[2,3,192,768]{3,2,1,0:T(8,128)(2,1)S(1)}, u32[]{:S(2)}, u32[]{:S(2)}) collective-permute-start(bf16[2,3,192,768]{3,2,1,0:T(8,128)(2,1)S(1)} %pad_maximum_fusion.2.source0_ref), channel_id=1, source_target_pairs={{0,32},{8,104},{2,34},{10,106},{4,36},{12,108},{6,38},{14,110},{32... | collective-permute-start | bytes 5308424 | tf_op jit(solution)/shard_map/ppermute | solution.py:526
  261.7 22.8 %collective-permute-start.40 = (bf16[2,3,192,768]{3,2,1,0:T(8,128)(2,1)S(1)}, bf16[2,3,192,768]{3,2,1,0:T(8,128)(2,1)S(1)}, u32[]{:S(2)}, u32[]{:S(2)}) collective-permute-start(bf16[2,3,192,768]{3,2,1,0:T(8,128)(2,1)S(1)} %pad_maximum_fusion.3.source1_ref), channel_id=1, source_target_pairs={{0,2},{8,14},{2,0},{10,12},{4,6},{12,10},{6,4},{14,8},{32,34},{40,... | collective-permute-start | bytes 5308424 | tf_op jit(solution)/shard_map/ppermute | solution.py:526
  262.0 5.7 %collective-permute-start.38 = (f32[16,768]{1,0:T(8,128)S(1)}, f32[16,768]{1,0:T(8,128)S(1)}, u32[]{:S(2)}, u32[]{:S(2)}) collective-permute-start(f32[16,768]{1,0:T(8,128)S(1)} %fusion.37), channel_id=1, source_target_pairs={{0,8},{8,0},{1,9},{9,1},{2,10},{10,2},{3,11},{11,3},{4,12},{12,4},... | collective-permute-start | bytes 147464 | tf_op jit(solution)/shard_map/ppermute | solution.py:539
  284.5 6.8 %collective-permute-start.41 = (bf16[2,3,192,768]{3,2,1,0:T(8,128)(2,1)S(1)}, bf16[2,3,192,768]{3,2,1,0:T(8,128)(2,1)}, u32[]{:S(2)}, u32[]{:S(2)}) collective-permute-start(bf16[2,3,192,768]{3,2,1,0:T(8,128)(2,1)S(1)} %collective-permute-done.39.source0_ref), channel_id=1, source_target_pairs={{0,8},{8,0},{1,9},{9,1},{2,10},{10,2},{3,11},{11,3},{4,12},{12,4},... | collective-permute-start | bytes 5308424 | tf_op jit(solution)/shard_map/ppermute | solution.py:539
  284.5 6.8 %collective-permute-start.42 = (bf16[2,3,192,768]{3,2,1,0:T(8,128)(2,1)S(1)}, bf16[2,3,192,768]{3,2,1,0:T(8,128)(2,1)}, u32[]{:S(2)}, u32[]{:S(2)}) collective-permute-start(bf16[2,3,192,768]{3,2,1,0:T(8,128)(2,1)S(1)} %collective-permute-done.40.source1_ref), channel_id=1, source_target_pairs={{0,8},{8,0},{1,9},{9,1},{2,10},{10,2},{3,11},{11,3},{4,12},{12,4},... | collective-permute-start | bytes 5308424 | tf_op jit(solution)/shard_map/ppermute | solution.py:539
  (30 other events, 80.9 us)
